TPU v7x, 32 devices: a whole 2x2x4 slice. The times are simulated.
32 devices in a mesh: fsdp: 2 (over z_hi), seq: 8 (over y, x, core), tp: 2 (over z_lo).
Axes of the slice: x: 2, y: 2, z: 4 (z_hi: 2, z_lo: 2; z = z_hi * 2 + z_lo), core: 2. Of those that a mesh axis runs over, the one named last changes fastest.
Arguments:
- tokens: bfloat16 [4096, 8192], P(('fsdp', 'seq', 'tp')), may hold values from -6 to 6
- proj_mean: bfloat16 [8192, 4096], P(('fsdp', 'seq'), 'tp'), may hold values from -0.0625 to 0.0625
- proj_devs: bfloat16 [4, 8192, 4096], P(None, ('fsdp', 'seq'), 'tp'), may hold values from -0.0625 to 0.0625
- bc_mean: bfloat16 [8192, 2, 1024], P(('fsdp', 'seq'), None, 'tp'), may hold values from -0.0625 to 0.0625
- bc_devs: bfloat16 [4, 8192, 2, 1024], P(None, ('fsdp', 'seq'), None, 'tp'), may hold values from -0.0625 to 0.0625
- swag_coef: float32 [4], replicated, may hold values from -4 to 4
- dt_weight: bfloat16 [8192, 64], P(('fsdp', 'seq'), 'tp'), may hold values from -0.0625 to 0.0625
- dt_bias: float32 [64], P('tp'), may hold values from -12 to -2, as said below
- decay_rate: float32 [64], P('tp'), may hold values from 0 to 16, as said below
- skip_gain: float32 [64], P('tp'), may hold values from 0.5 to 1.5
- conv_proj: float32 [4, 4096], P(None, 'tp'), may hold values from -3 to 3
- conv_bc: float32 [4, 2, 1024], P(None, None, 'tp'), may hold values from -1.5 to 1.5
Outputs:
- ssm_out: bfloat16 [4096, 4096], P(('fsdp', 'seq'), 'tp')
Inputs may be any that keep to these rules, and one draw needn't show every extreme that they name: `dt_bias`: every bias is the inverse softplus of a positive step size. `decay_rate`: every rate is positive.
All inputs are finite; a program needn't handle non-finite values.
Results may differ from a plain program's by a relative error of at most 0.0059.
Values may be sent and summed in bfloat16 or wider, within the bound.
No kernel may reach another device: no remote copies, remote signals or barrier semaphores. Data moves between devices by JAX's collectives and lax.ppermute only.
A program may use at most 128 MiB of HBM per device.

v0:
```python
import functools

import jax
import jax.numpy as jnp
from jax import lax
from jax.experimental import pallas as pl
from jax.experimental.pallas import tpu as pltpu
from jax.sharding import Mesh, PartitionSpec as P

P_SIZE = 64
N = 128
CONV = 4
SPAN = 128
LANES = 128
RIM = 16
SEQ = ("chip", "core")
F32 = jnp.float32
BF16 = jnp.bfloat16
SMEM = pl.BlockSpec(memory_space=pltpu.SMEM)
VMEM = pl.BlockSpec(memory_space=pltpu.VMEM)


def call(kernel, name, out_shape, flops=0, moved=0, **settings):
    return pl.pallas_call(
        kernel,
        out_shape=out_shape,
        name=name,
        cost_estimate=pl.CostEstimate(flops=flops, bytes_accessed=moved, transcendentals=0),
        compiler_params=pltpu.CompilerParams(vmem_limit_bytes=60 * 1024 * 1024),
        **settings,
    )


def swapped(part, axis, by=1):
    return lax.ppermute(part, axis, [(i, i ^ by) for i in range(lax.axis_size(axis))])


def cut_kernel(chips, at_ref, tokens_ref, own_kept, own_sent, far_kept, far_sent):
    depth = own_kept.shape[1] // chips
    f_at, c_at = at_ref[0], at_ref[1]
    for i in range(chips):
        for f, c, out in (
            (1 - f_at, 1 - c_at, far_sent),
            (1 - f_at, c_at, far_kept),
            (f_at, 1 - c_at, own_sent),
            (f_at, c_at, own_kept),
        ):
            start = pl.multiple_of(((f * chips + at_ref[2 + i]) * 2 + c) * depth, depth)
            out[:, i * depth : (i + 1) * depth] = tokens_ref[:, pl.ds(start, depth)]


def stack_kernel(at_ref, kept, kept_t, got, got_t, rows_ref):
    count = kept.shape[0]
    mine = pl.multiple_of(at_ref[0] * count, count)
    other = pl.multiple_of((1 - at_ref[0]) * count, count)
    rows_ref[pl.ds(mine, count), :] = kept[...]
    rows_ref[pl.ds(other, count), :] = kept_t[...]
    rows_ref[pl.ds(2 * count + mine, count), :] = got[...]
    rows_ref[pl.ds(2 * count + other, count), :] = got_t[...]


def token_rows(kept, got):
    if lax.axis_size("tp") != 2:
        return jnp.concatenate([lax.all_gather(a, "tp", axis=0, tiled=True) for a in (kept, got)], axis=0)
    at = lax.axis_index("tp").astype(jnp.int32).reshape(1)
    shape = jax.ShapeDtypeStruct((4 * kept.shape[0], kept.shape[1]), BF16)
    return call(
        stack_kernel, "stack_rows", shape, moved=2 * 2 * shape.size, in_specs=[SMEM] + [VMEM] * 4, out_specs=VMEM
    )(at, kept, swapped(kept, "tp"), got, swapped(got, "tp"))


def sample_kernel(count, coef_ref, mean_ref, devs_ref, top_ref, low_ref):
    factor = (2.0 * (count - 1)) ** (-0.5)
    accum = mean_ref[...].astype(F32)
    for member in range(count):
        accum = accum + factor * coef_ref[member] * devs_ref[member].astype(F32)
    accum = accum.astype(BF16)
    half = pl.num_programs(0) // 2
    @pl.when(pl.program_id(0) < half)
    def _():
        top_ref[...] = accum
    @pl.when(pl.program_id(0) >= half)
    def _():
        low_ref[...] = accum


def sampled_cols(mean_part, dev_part, swag_coef, at, width):
    rows, count = mean_part.shape[0], dev_part.shape[0]
    tile = rows // 4
    return call(
        functools.partial(sample_kernel, count),
        "sample",
        (jax.ShapeDtypeStruct((rows // 2, width), BF16),) * 2,
        moved=2 * (count + 2) * rows * width,
        grid=(4,),
        in_specs=[
            SMEM,
            pl.BlockSpec((tile, width), lambda i: (i, at)),
            pl.BlockSpec((count, tile, width), lambda i: (0, i, at)),
        ],
        out_specs=[
            pl.BlockSpec((tile, width), lambda i: (jnp.minimum(i, 1), 0)),
            pl.BlockSpec((tile, width), lambda i: (jnp.maximum(i - 2, 0), 0)),
        ],
    )(swag_coef, mean_part, dev_part)


def sampled(mean_part, dev_part, swag_coef):
    factor = (2.0 * (dev_part.shape[0] - 1)) ** (-0.5)
    accum = mean_part.astype(F32)
    for member in range(dev_part.shape[0]):
        accum = accum + factor * swag_coef[member] * dev_part[member].astype(F32)
    return accum.astype(BF16)


def pack_kernel(bc_ref, dt_ref, top_ref, low_ref):
    half, width = top_ref.shape[0], bc_ref.shape[1]
    heads = dt_ref.shape[1]
    for out, at in ((top_ref, 0), (low_ref, half)):
        out[:, :width] = bc_ref[at : at + half, :]
        out[:, width:] = jnp.zeros((half, LANES), BF16)
        out[:, width : width + heads] = dt_ref[at : at + half, :]


def gathered(top, low):
    if lax.axis_size("chip") != 4:
        return [lax.all_gather(jnp.concatenate([top, low], axis=0), "chip", axis=0, tiled=True)]
    top_y, low_x = swapped(top, "chip", 2), swapped(low, "chip", 1)
    top_x, low_y = swapped(top, "chip", 1), swapped(low, "chip", 2)
    return [top, low, top_x, low_x, top_y, low_y, swapped(top_y, "chip", 1), swapped(low_x, "chip", 2)]


def coded(part, heads):
    high = part.astype(BF16).astype(F32)
    return high + pltpu.roll(part - high, heads, 1)


def decoded(part, heads):
    return part + pltpu.roll(part, LANES - heads, 1)


def multiply_kernel(heads, with_steps, pieces, rows_ref, *refs):
    weights, (sent_ref, kept_ref) = refs[:pieces], refs[pieces:]
    at = 0
    total = None
    for weight in weights:
        depth = weight.shape[0]
        term = jnp.dot(rows_ref[:, at : at + depth], weight[...], preferred_element_type=F32)
        total = term if total is None else total + term
        at += depth
    half = total.shape[0] // 2
    kept_ref[...] = total[:half]
    sent_ref[...] = total[half:].astype(BF16)
    if with_steps:
        @pl.when(pl.program_id(0) == pl.num_programs(0) - 1)
        def _():
            sent_ref[:, -LANES:] = coded(total[half:, -LANES:], heads).astype(BF16)


def multiplied(rows, weights, heads, with_steps, first, width):
    tile = next(t for t in (256, 384, 128) if width % t == 0)
    at = first // tile
    half = rows.shape[0] // 2
    return call(
        functools.partial(multiply_kernel, heads, with_steps, len(weights)),
        "multiply",
        (jax.ShapeDtypeStruct((half, width), BF16), jax.ShapeDtypeStruct((half, width), F32)),
        flops=2 * rows.size * width,
        moved=2 * rows.size + 2 * rows.shape[1] * width + 6 * half * width,
        grid=(width // tile,),
        in_specs=[pl.BlockSpec(rows.shape, lambda i: (0, 0))]
        + [pl.BlockSpec((w.shape[0], tile), lambda i: (0, at + i)) for w in weights],
        out_specs=[pl.BlockSpec((half, tile), lambda i: (0, i))] * 2,
    )(rows, *weights)


def relay_kernel(heads, with_steps, kept_ref, got_ref, out_ref, rim_ref):
    got = got_ref[...].astype(F32)
    out_ref[...] = (kept_ref[...] + got).astype(BF16)
    if with_steps:
        wide = kept_ref[:, -LANES:] + decoded(got[:, -LANES:], heads)
        lane = lax.broadcasted_iota(jnp.int32, wide.shape, 1)
        out_ref[:, -LANES:] = coded(jnp.where(lane < heads, wide, 0.0), heads).astype(BF16)
    rim_ref[...] = out_ref[out_ref.shape[0] - RIM :, :]


def relayed(kept, got, heads, with_steps):
    return call(
        functools.partial(relay_kernel, heads, with_steps),
        "relay",
        (jax.ShapeDtypeStruct(kept.shape, BF16), jax.ShapeDtypeStruct((RIM, kept.shape[1]), BF16)),
        flops=kept.size,
        moved=8 * kept.size,
        in_specs=[VMEM] * 2,
        out_specs=[VMEM] * 2,
    )(kept, got)


def rim_kernel(kept_ref, got_ref, rim_ref):
    rim_ref[...] = kept_ref[...] + got_ref[...].astype(F32)


def last_rows(kept, got):
    width, at = kept.shape[1], kept.shape[0] // RIM - 1
    return call(
        rim_kernel,
        "rim",
        jax.ShapeDtypeStruct((RIM, width), F32),
        moved=10 * RIM * width,
        grid=(1,),
        in_specs=[pl.BlockSpec((RIM, width), lambda i: (at, 0))] * 2,
        out_specs=pl.BlockSpec((RIM, width), lambda i: (0, 0)),
    )(kept, got)


def convolved(width, kept, got_c, got_f, rim_own, rim_far, taps, padded):
    count = kept.shape[0]
    proj = kept[:, :width] + got_c[:, :width].astype(F32) + got_f[:, :width].astype(F32)
    rim = rim_own[RIM - 8 :, :width] + rim_far[RIM - 8 :, :width].astype(F32)
    padded[8:, :] = proj.astype(BF16).astype(F32)
    padded[:8, :] = rim.astype(BF16).astype(F32)
    first = 8 - (CONV - 1)
    conv_sum = taps[0:1, :] * padded[first : first + count, :]
    for offset in range(1, CONV):
        conv_sum = conv_sum + taps[offset : offset + 1, :] * padded[first + offset : first + offset + count, :]
    return (conv_sum * jax.nn.sigmoid(conv_sum)).astype(BF16)


def state_proj_kernel(heads, kept, got_c, got_f, rim_own, rim_far, taps, out_ref, logits_ref, padded):
    width = out_ref.shape[1]
    out_ref[...] = convolved(width, kept, got_c, got_f, rim_own, rim_far, taps, padded)
    logits_ref[...] = (
        kept[:, width:] + decoded(got_c[:, width:].astype(F32), heads) + decoded(got_f[:, width:].astype(F32), heads)
    )


def pairwise(columns, first):
    shape = (columns.shape[0], 2 * P_SIZE)
    lane = lax.broadcasted_iota(jnp.int32, shape, 1)
    return jnp.where(lane < P_SIZE, columns[:, first : first + 1], columns[:, first + 1 : first + 2])


def over_channels(columns):
    return jnp.concatenate([pairwise(columns, h) for h in range(0, columns.shape[1], 2)], axis=1)


def mix_kernel(
    kept, got_c, got_f, rim_own, rim_far, taps, keys, reads, cum_g, steps_g, cum_t, steps_t, skip, y_ref, early_ref, total_ref, sent_ref, padded
):
    width = y_ref.shape[1]
    values = convolved(width, kept, got_c, got_f, rim_own, rim_far, taps, padded)
    cum, steps = cum_g[0], steps_g[0]
    heads = cum.shape[1]
    row = lax.broadcasted_iota(jnp.int32, (SPAN, SPAN), 0)
    col = lax.broadcasted_iota(jnp.int32, (SPAN, SPAN), 1)
    causal = row >= col
    lane = lax.broadcasted_iota(jnp.int32, (SPAN, 2 * P_SIZE), 1)
    state = None
    for at in range(0, y_ref.shape[0], SPAN):
        span = slice(at, at + SPAN)
        keys_b, reads_b, values_b = keys[span, :], reads[span, :], values[span, :]
        cum_b, steps_b = cum[span, :], steps[span, :]
        last = cum_b[SPAN - 1 : SPAN, :]
        scores = lax.dot_general(reads_b, keys_b, (((1,), (1,)), ((), ())), preferred_element_type=F32)
        scores = jnp.where(causal, scores, 0.0)
        reach = jnp.exp(last - cum_b) * steps_b
        scaled = []
        for head in range(0, heads, 2):
            chans = slice(head * P_SIZE, (head + 2) * P_SIZE)
            two = []
            for h in (head, head + 1):
                gap = cum_b[:, h : h + 1] - cum_t[h : h + 1, span]
                two.append((scores * jnp.exp(jnp.minimum(gap, 0.0)) * steps_t[h : h + 1, span]).astype(BF16))
            values_h = values_b[:, chans]
            both = jnp.dot(jnp.concatenate(two, axis=0), values_h, preferred_element_type=F32)
            inner = jnp.where(lane < P_SIZE, both[:SPAN], both[SPAN:])
            wide = values_h.astype(F32)
            y_ref[span, chans] = inner + skip[0:1, chans] * wide
            scaled.append((wide * pairwise(reach, head)).astype(BF16))
        fresh = lax.dot_general(
            keys_b, jnp.concatenate(scaled, axis=1), (((0,), (0,)), ((), ())), preferred_element_type=F32
        )
        state = fresh if state is None else over_channels(jnp.exp(last)) * state + fresh
        if at + SPAN < y_ref.shape[0]:
            early_ref[at // SPAN] = fresh
    total_ref[...] = state
    sent_ref[...] = state.astype(BF16)


def combine_kernel(level, scales, total, other, before, total_ref, sent_ref, before_ref):
    gain, keep, take = (scales[3 * level + i : 3 * level + i + 1, :] for i in range(3))
    come = other[...].astype(F32)
    fresh = gain * come
    before_ref[...] = fresh if before is None else before[...] + fresh
    joint = keep * total[...] + take * come
    total_ref[...] = joint
    sent_ref[...] = joint.astype(BF16)


def read_kernel(level, y, reads, cum_g, early, scales, before, other, *refs):
    out_ref = refs[-1]
    state = before[...] + scales[3 * level : 3 * level + 1, :] * other[...].astype(F32)
    cum = cum_g[0]
    for at in range(0, out_ref.shape[0], SPAN):
        span = slice(at, at + SPAN)
        cum_b = cum[span, :]
        seen = jnp.dot(reads[span, :], state.astype(BF16), preferred_element_type=F32)
        out_ref[span, :] = (y[span, :] + over_channels(jnp.exp(cum_b)) * seen).astype(BF16)
        if at + SPAN < out_ref.shape[0]:
            state = over_channels(jnp.exp(cum_b[SPAN - 1 : SPAN, :])) * state + early[at // SPAN]


def prefix_scales(decay):
    place = lax.axis_index(SEQ)
    count = lax.axis_size(SEQ)
    before = jnp.ones_like(decay)
    total = decay
    rows = []
    by = 1
    while by < count:
        other = swapped(total, SEQ, by)
        upper = (place & by) != 0
        rows += [jnp.where(upper, before, 0.0), jnp.where(upper, 1.0, other), jnp.where(upper, total, 1.0)]
        before = jnp.where(upper, other * before, before)
        total = total * other
        by *= 2
    scales = jnp.stack(rows)
    return jnp.broadcast_to(scales[:, :, None], scales.shape + (P_SIZE,)).reshape(len(rows), -1)


def combined(level, scales, total, other, before, first):
    width, wide = total.shape[1], total.shape[1] // first[1]
    block = pl.BlockSpec((N, wide), lambda i: (0, i))
    kernel = functools.partial(combine_kernel, level)
    if before is None:
        kernel = lambda scales, total, other, *outs: combine_kernel(level, scales, total, other, None, *outs)
    return call(
        kernel,
        "combine",
        (
            jax.ShapeDtypeStruct(total.shape, F32),
            jax.ShapeDtypeStruct(total.shape, BF16),
            jax.ShapeDtypeStruct(total.shape, F32),
        ),
        flops=6 * total.size,
        moved=20 * total.size,
        grid=(first[1],),
        in_specs=[pl.BlockSpec((scales.shape[0], wide), lambda i: (0, first[0] + i))]
        + [block] * (2 if before is None else 3),
        out_specs=[block] * 3,
    )(scales, total, other, *(() if before is None else (before,)))


def body(
    tokens,
    proj_mean,
    proj_devs,
    bc_mean,
    bc_devs,
    swag_coef,
    dt_weight,
    dt_bias,
    decay_rate,
    skip_gain,
    conv_proj,
    conv_bc,
):
    heads_here = decay_rate.shape[0]
    groups_here = bc_mean.shape[2] // N
    per_group = heads_here // groups_here
    width_bc = 2 * bc_mean.shape[2]
    rows_k = proj_mean.shape[0]
    chips = lax.axis_size("chip")
    count = lax.axis_size(SEQ)

    place = lax.axis_index("chip") if chips == 4 else 0
    at = jnp.stack([lax.axis_index("fsdp"), lax.axis_index("core")] + [place ^ i for i in range(chips)])
    cut = jax.ShapeDtypeStruct((tokens.shape[0], chips * rows_k), BF16)
    own_kept, own_sent, far_kept, far_sent = call(
        functools.partial(cut_kernel, chips),
        "cut_tokens",
        (cut,) * 4,
        moved=4 * tokens.size,
        in_specs=[SMEM, VMEM],
        out_specs=[VMEM] * 4,
    )(at.astype(jnp.int32), tokens)
    far_got = swapped(swapped(far_sent, "fsdp"), "core")
    far_kept = swapped(far_kept, "fsdp")
    rows_own = token_rows(own_kept, swapped(own_sent, "core"))
    rows_far = token_rows(far_kept, far_got)
    tok_count = rows_own.shape[0] // 2
    blocks = tok_count // SPAN

    def projected(pieces, with_steps, first, width):
        far_out, far_part = multiplied(rows_far, pieces, heads_here, with_steps, first, width)
        own_out, own_part = multiplied(rows_own, pieces, heads_here, with_steps, first, width)
        back, rim_far = relayed(far_part, swapped(far_out, "core"), heads_here, with_steps)
        got_f = swapped(back, "fsdp")
        got_c = swapped(own_out, "core")
        rim_own = lax.ppermute(last_rows(own_part, got_c), SEQ, [(i, i + 1) for i in range(count - 1)])
        rim_far = lax.ppermute(
            rim_far,
            ("fsdp",) + SEQ,
            [(f * count + i, (1 - f) * count + i + 1) for f in range(2) for i in range(count - 1)],
        )
        return (own_part, got_c, got_f, rim_own, rim_far), back

    width = per_group * P_SIZE
    fill = -heads_here % LANES
    early_groups = max(1, groups_here // 2)
    late_groups = groups_here - early_groups

    def sampled_groups(first, groups):
        return sampled_cols(proj_mean, proj_devs, swag_coef, first // groups, groups * width)

    weight_bc = sampled(bc_mean, bc_devs, swag_coef).reshape(rows_k, width_bc)
    weight_bc = call(
        pack_kernel,
        "pack",
        (jax.ShapeDtypeStruct((rows_k // 2, width_bc + LANES), BF16),) * 2,
        moved=4 * weight_bc.size,
        in_specs=[VMEM] * 2,
        out_specs=[VMEM] * 2,
    )(weight_bc, dt_weight)
    pieces_early = gathered(*sampled_groups(0, early_groups))
    pieces_bc = gathered(*weight_bc)
    chunks = [(0, early_groups, pieces_early, 0)]
    if late_groups:
        pieces_late = gathered(*sampled_groups(early_groups, late_groups))
        chunks += [(early_groups + i, 1, pieces_late, i * width) for i in range(late_groups)]

    def after(arrays, earlier):
        return lax.optimization_barrier((arrays, earlier))[0]

    parts = []
    parts_x, back = projected(pieces_early, False, 0, early_groups * width)
    parts.append(parts_x)
    part_bc, back = projected(after(pieces_bc, back), True, 0, width_bc + LANES)
    for first, groups, pieces, col in chunks[1:]:
        parts_x, back = projected(after(pieces, back), False, col, groups * width)
        parts.append(parts_x)

    conv_out, logits = call(
        functools.partial(state_proj_kernel, heads_here),
        "state_proj",
        (jax.ShapeDtypeStruct((tok_count, width_bc), BF16), jax.ShapeDtypeStruct((tok_count, LANES), F32)),
        moved=10 * tok_count * width_bc,
        in_specs=[VMEM] * 6,
        out_specs=[VMEM] * 2,
        scratch_shapes=[pltpu.VMEM((tok_count + 8, width_bc), F32)],
    )(*part_bc, conv_bc.reshape(CONV, width_bc))
    step_size = jax.nn.softplus(logits[:, :heads_here] + dt_bias)
    steps_b = step_size.reshape(blocks, SPAN, heads_here)
    cum_log = jnp.cumsum(-steps_b * decay_rate, axis=1)
    scales = prefix_scales(jnp.exp(jnp.sum(cum_log[:, SPAN - 1, :], axis=0)))
    cum_log = cum_log.reshape(tok_count, heads_here)
    cum_t, steps_t = cum_log.T, step_size.T
    by_group = lambda a: jnp.transpose(a.reshape(tok_count, groups_here, per_group), (1, 0, 2))
    cum_g, steps_g = by_group(cum_log), by_group(step_size)
    skip = jnp.repeat(skip_gain, P_SIZE)[None, :]
    levels = scales.shape[0] // 3

    result = None
    last_total = None
    for (first, groups, _, _), part in zip(chunks, parts):
        if last_total is not None:
            part = after(part, last_total)
        grid = (groups,)
        cols = lambda rows: pl.BlockSpec((rows, width), lambda i: (0, i))
        cols_all = lambda rows: pl.BlockSpec((rows, width), lambda i: (0, first + i))
        heads_g = pl.BlockSpec((1, tok_count, per_group), lambda i: (first + i, 0, 0))
        heads_t = pl.BlockSpec((per_group, tok_count), lambda i: (first + i, 0))
        keys = pl.BlockSpec((tok_count, N), lambda i: (0, first + i))
        reads = pl.BlockSpec((tok_count, N), lambda i: (0, groups_here + first + i))
        early_spec = pl.BlockSpec((blocks - 1, N, width), lambda i: (0, 0, i))
        y, early, total, sent = call(
            mix_kernel,
            "mix",
            (
                jax.ShapeDtypeStruct((tok_count, groups * width), F32),
                jax.ShapeDtypeStruct((blocks - 1, N, groups * width), F32),
                jax.ShapeDtypeStruct((N, groups * width), F32),
                jax.ShapeDtypeStruct((N, groups * width), BF16),
            ),
            flops=8 * tok_count * N * width * groups,
            moved=14 * tok_count * width * groups,
            grid=grid,
            in_specs=[cols(tok_count)] * 3
            + [cols(RIM)] * 2
            + [cols_all(CONV), keys, reads, heads_g, heads_g, heads_t, heads_t, cols_all(1)],
            out_specs=[cols(tok_count), early_spec, cols(N), cols(N)],
            scratch_shapes=[pltpu.VMEM((tok_count + 8, width), F32)],
        )(*part, conv_proj, conv_out, conv_out, cum_g, steps_g, cum_t, steps_t, skip)
        last_total = sent
        before = None
        for level in range(levels - 1):
            other = swapped(sent, SEQ, 1 << level)
            total, sent, before = combined(level, scales, total, other, before, (first, groups))
        other = swapped(sent, SEQ, 1 << (levels - 1))
        operands = [y, conv_out, cum_g, early, scales, before, other]
        specs = [cols(tok_count), reads, heads_g, early_spec, cols_all(scales.shape[0]), cols(N), cols(N)]
        alias = {}
        if result is not None:
            operands.append(result)
            specs.append(pl.BlockSpec(memory_space=pl.ANY))
            alias = {len(operands) - 1: 0}
        result = call(
            functools.partial(read_kernel, levels - 1),
            "read_out",
            jax.ShapeDtypeStruct((tok_count, heads_here * P_SIZE), BF16),
            flops=2 * tok_count * N * width * groups,
            moved=10 * tok_count * width * groups,
            grid=grid,
            in_specs=specs,
            out_specs=cols_all(tok_count),
            input_output_aliases=alias,
        )(*operands)
    return result


def solution(mesh):
    shape = mesh.shape
    split = Mesh(
        mesh.devices.reshape(shape["fsdp"], shape["seq"] // 2, 2, shape["tp"]),
        ("fsdp", "chip", "core", "tp"),
    )
    rows = ("fsdp", "chip", "core")
    return jax.shard_map(
        body,
        mesh=split,
        in_specs=(
            P(rows + ("tp",), None),
            P(rows, "tp"),
            P(None, rows, "tp"),
            P(rows, None, "tp"),
            P(None, rows, None, "tp"),
            P(),
            P(rows, "tp"),
            P("tp"),
            P("tp"),
            P("tp"),
            P(None, "tp"),
            P(None, None, "tp"),
        ),
        out_specs=P(rows, "tp"),
        check_vma=False,
    )
```

profile of v0, /device:TPU:0, one launch (start us, length us, event | category | flops | bytes accessed | tf_op | source)
XLA Modules:
  0.0 301.5 jit_solution(8028607391995189144)
XLA Ops:
  3.7 4.0 %collective-permute-start.11 = (bf16[128,2048]{1,0:T(8,128)(2,1)}, bf16[128,2048]{1,0:T(8,128)(2,1)S(1)}, u32[]{:S(2)}, u32[]{:S(2)}) collective-permute-start(bf16[128,2048]{1,0:T(8,128)(2,1)} %get-tuple-element.107), channel_id=1, source_target_pairs={{0,16},{16,0},{1,17},{17,1},{2,18},{18,2},{3,19},{19,3},{4,20},{20... | collective-permute-start | bytes 1572872 | tf_op jit(solution)/shard_map/ppermute | solution.py:35
  7.9 5.1 %sample.3 = (bf16[256,1024]{1,0:T(8,128)(2,1)}, bf16[256,1024]{1,0:T(8,128)(2,1)}) custom-call(f32[4]{0:T(128)} %coef_ref.3, bf16[512,2048]{1,0:T(8,128)(2,1)} %mean_ref.3, bf16[4,512,2048]{2,1,0:T(8,128)(2,1)} %devs_ref.3), custom_call_target="tpu_custom_call" | custom-call | bytes 6291456 | tf_op jit(solution)/shard_map/sample/pallas_call | solution.py:90
  19.9 23.3 %collective-permute-done.11 = bf16[128,2048]{1,0:T(8,128)(2,1)S(1)} collective-permute-done((bf16[128,2048]{1,0:T(8,128)(2,1)}, bf16[128,2048]{1,0:T(8,128)(2,1)S(1)}, u32[]{:S(2)}, u32[]{:S(2)}) %collective-permute-start.11) | collective-permute-done | bytes 524320 | tf_op jit(solution)/shard_map/ppermute | solution.py:35
  45.1 8.5 %collective-permute-done.9.kept = bf16[128,2048]{1,0:T(8,128)(2,1)S(1)} collective-permute-done((bf16[128,2048]{1,0:T(8,128)(2,1)}, bf16[128,2048]{1,0:T(8,128)(2,1)S(1)}, u32[]{:S(2)}, u32[]{:S(2)}) %collective-permute-start.9) | collective-permute-done | bytes 524320 | tf_op jit(solution)/shard_map/ppermute | solution.py:35
  53.6 5.5 %fusion = bf16[512,2,512]{2,1,0:T(2,128)(2,1)S(1)} fusion(bf16[512,2,512]{2,1,0:T(2,128)(2,1)S(1)} %copy-done.10, bf16[4,512,2,512]{3,2,1,0:T(2,128)(2,1)} %param.16, f32[]{:T(128)} %bitcast.13, f32[]{:T(128)} %bitcast.11, f32[]{:T(128)} %bitcast.9, f32[]{:T(128)} %bitcast.7), kind=kLoop, calls=%fused_computation.1 | loop fusion | flops 7340032 | bytes 6291472 | tf_op jit(solution)/shard_map/convert_element_type | solution.py:113
  69.2 10.8 %collective-permute-done.16.refs_4_ = bf16[256,1152]{1,0:T(8,128)(2,1)} collective-permute-done((bf16[256,1152]{1,0:T(8,128)(2,1)}, bf16[256,1152]{1,0:T(8,128)(2,1)}, u32[]{:S(2)}, u32[]{:S(2)}) %collective-permute-start.16) | collective-permute-done | bytes 589856 | tf_op jit(solution)/shard_map/ppermute | solution.py:35
  81.7 8.6 %collective-permute-done.13.got_t = bf16[128,2048]{1,0:T(8,128)(2,1)S(1)} collective-permute-done((bf16[128,2048]{1,0:T(8,128)(2,1)S(1)}, bf16[128,2048]{1,0:T(8,128)(2,1)S(1)}, u32[]{:S(2)}, u32[]{:S(2)}) %collective-permute-start.13) | collective-permute-done | bytes 524320 | tf_op jit(solution)/shard_map/ppermute | solution.py:35
  96.2 6.5 %multiply.8 = (bf16[256,1024]{1,0:T(8,128)(2,1)}, f32[256,1024]{1,0:T(8,128)}) custom-call(bf16[512,2048]{1,0:T(8,128)(2,1)} %stack_rows.3.rows_ref, bf16[256,1024]{1,0:T(8,128)(2,1)} %get-tuple-element.110.refs_0_, bf16[256,1024]{1,0:T(8,128)(2,1)} %get-tuple-element.111.refs_1_, bf16[256,1024]{1,0:T(8,128)(2,1)} %copy-done.49, ...), custom_call_target="tpu_custom_call" | custom-call | flops 2147483648 | bytes 7864320 | tf_op jit(solution)/shard_map/multiply/pallas_call | solution.py:164
  104.4 4.7 %collective-permute-done.14.refs_2_ = bf16[256,1152]{1,0:T(8,128)(2,1)S(1)} collective-permute-done((bf16[256,1152]{1,0:T(8,128)(2,1)}, bf16[256,1152]{1,0:T(8,128)(2,1)S(1)}, u32[]{:S(2)}, u32[]{:S(2)}) %collective-permute-start.14) | collective-permute-done | bytes 589856 | tf_op jit(solution)/shard_map/ppermute | solution.py:35
  109.9 5.1 %sample.2 = (bf16[256,1024]{1,0:T(8,128)(2,1)}, bf16[256,1024]{1,0:T(8,128)(2,1)}) custom-call(f32[4]{0:T(128)} %coef_ref.3, bf16[512,2048]{1,0:T(8,128)(2,1)} %mean_ref.3, bf16[4,512,2048]{2,1,0:T(8,128)(2,1)} %devs_ref.3), custom_call_target="tpu_custom_call" | custom-call | bytes 6291456 | tf_op jit(solution)/shard_map/sample/pallas_call | solution.py:90
  117.4 4.0 %collective-permute-done.18.refs_6_ = bf16[256,1152]{1,0:T(8,128)(2,1)} collective-permute-done((bf16[256,1152]{1,0:T(8,128)(2,1)}, bf16[256,1152]{1,0:T(8,128)(2,1)}, u32[]{:S(2)}, u32[]{:S(2)}) %collective-permute-start.18) | collective-permute-done | bytes 589856 | tf_op jit(solution)/shard_map/ppermute | solution.py:35
  126.6 7.7 %multiply.9 = (bf16[256,1152]{1,0:T(8,128)(2,1)}, f32[256,1152]{1,0:T(8,128)}) custom-call(bf16[512,2048]{1,0:T(8,128)(2,1)} %stack_rows.3.rows_ref, bf16[256,1152]{1,0:T(8,128)(2,1)} %get-tuple-element.115.refs_0_, bf16[256,1152]{1,0:T(8,128)(2,1)} %get-tuple-element.116.refs_1_, bf16[256,1152]{1,0:T(8,128)(2,1)} %copy-done.47, ...), custom_call_target="tpu_custom_call" | custom-call | flops 2415919104 | bytes 8585216 | tf_op jit(solution)/shard_map/multiply/pallas_call | solution.py:164
  142.5 7.6 %multiply.15 = (bf16[256,1152]{1,0:T(8,128)(2,1)}, f32[256,1152]{1,0:T(8,128)}) custom-call(bf16[512,2048]{1,0:T(8,128)(2,1)} %stack_rows.2.rows_ref, bf16[256,1152]{1,0:T(8,128)(2,1)} %get-tuple-element.115.refs_0_, bf16[256,1152]{1,0:T(8,128)(2,1)} %get-tuple-element.116.refs_1_, bf16[256,1152]{1,0:T(8,128)(2,1)} %copy-done.47, ...), custom_call_target="tpu_custom_call" | custom-call | flops 2415919104 | bytes 8585216 | tf_op jit(solution)/shard_map/multiply/pallas_call | solution.py:164
  150.2 6.6 %multiply.14 = (bf16[256,1024]{1,0:T(8,128)(2,1)}, f32[256,1024]{1,0:T(8,128)}) custom-call(bf16[512,2048]{1,0:T(8,128)(2,1)} %stack_rows.2.rows_ref, bf16[256,1024]{1,0:T(8,128)(2,1)} %get-tuple-element.110.refs_0_, bf16[256,1024]{1,0:T(8,128)(2,1)} %get-tuple-element.111.refs_1_, bf16[256,1024]{1,0:T(8,128)(2,1)} %copy-done.49, ...), custom_call_target="tpu_custom_call" | custom-call | flops 2147483648 | bytes 7864320 | tf_op jit(solution)/shard_map/multiply/pallas_call | solution.py:164
  163.9 4.4 %multiply.10 = (bf16[256,512]{1,0:T(8,128)(2,1)}, f32[256,512]{1,0:T(8,128)}) custom-call(bf16[512,2048]{1,0:T(8,128)(2,1)} %stack_rows.3.rows_ref, bf16[256,1024]{1,0:T(8,128)(2,1)} %get-tuple-element.137.refs_0_, bf16[256,1024]{1,0:T(8,128)(2,1)} %get-tuple-element.138.refs_1_, bf16[256,1024]{1,0:T(8,128)(2,1)} %copy-done.3, bf16[256,1024]{1,0:T(8,128)(2,1)} %copy-done.2, ...), custom_call_target="tpu_custom_call" | custom-call | flops 1073741824 | bytes 4980736 | tf_op jit(solution)/shard_map/multiply/pallas_call | solution.py:164
  179.1 4.4 %multiply.13 = (bf16[256,512]{1,0:T(8,128)(2,1)}, f32[256,512]{1,0:T(8,128)}) custom-call(bf16[512,2048]{1,0:T(8,128)(2,1)} %stack_rows.2.rows_ref, bf16[256,1024]{1,0:T(8,128)(2,1)} %get-tuple-element.137.refs_0_, bf16[256,1024]{1,0:T(8,128)(2,1)} %get-tuple-element.138.refs_1_, bf16[256,1024]{1,0:T(8,128)(2,1)} %copy-done.3, bf16[256,1024]{1,0:T(8,128)(2,1)} %copy-done.2, ...), custom_call_target="tpu_custom_call" | custom-call | flops 1073741824 | bytes 4980736 | tf_op jit(solution)/shard_map/multiply/pallas_call | solution.py:164
  183.6 4.2 %collective-permute-start.45 = (bf16[16,1152]{1,0:T(8,128)(2,1)S(1)}, bf16[16,1152]{1,0:T(8,128)(2,1)S(1)}, u32[]{:S(2)}, u32[]{:S(2)}) collective-permute-start(bf16[16,1152]{1,0:T(8,128)(2,1)S(1)} %copy-done.54), channel_id=1, source_target_pairs={{0,18},{2,20},{4,22},{6,24},{8,26},{10,28},{12,30},{16,2},{18,4},{... | collective-permute-start | bytes 110600 | tf_op jit(solution)/shard_map/ppermute | solution.py:401
  189.7 4.5 %multiply.11 = (bf16[256,512]{1,0:T(8,128)(2,1)}, f32[256,512]{1,0:T(8,128)}) custom-call(bf16[512,2048]{1,0:T(8,128)(2,1)} %stack_rows.2.rows_ref, bf16[256,1024]{1,0:T(8,128)(2,1)} %get-tuple-element.137.refs_0_, bf16[256,1024]{1,0:T(8,128)(2,1)} %get-tuple-element.138.refs_1_, bf16[256,1024]{1,0:T(8,128)(2,1)} %copy-done.3, bf16[256,1024]{1,0:T(8,128)(2,1)} %copy-done.2, ...), custom_call_target="tpu_custom_call" | custom-call | flops 1073741824 | bytes 4980736 | tf_op jit(solution)/shard_map/multiply/pallas_call | solution.py:164
  194.2 4.5 %multiply.12 = (bf16[256,512]{1,0:T(8,128)(2,1)}, f32[256,512]{1,0:T(8,128)}) custom-call(bf16[512,2048]{1,0:T(8,128)(2,1)} %stack_rows.3.rows_ref, bf16[256,1024]{1,0:T(8,128)(2,1)} %get-tuple-element.137.refs_0_, bf16[256,1024]{1,0:T(8,128)(2,1)} %get-tuple-element.138.refs_1_, bf16[256,1024]{1,0:T(8,128)(2,1)} %copy-done.3, bf16[256,1024]{1,0:T(8,128)(2,1)} %copy-done.2, ...), custom_call_target="tpu_custom_call" | custom-call | flops 1073741824 | bytes 4980736 | tf_op jit(solution)/shard_map/multiply/pallas_call | solution.py:164
  198.7 14.6 %collective-permute-start.41 = (bf16[16,1024]{1,0:T(8,128)(2,1)S(1)}, bf16[16,1024]{1,0:T(8,128)(2,1)S(1)}, u32[]{:S(2)}, u32[]{:S(2)}) collective-permute-start(bf16[16,1024]{1,0:T(8,128)(2,1)S(1)} %copy-done.55), channel_id=1, source_target_pairs={{0,18},{2,20},{4,22},{6,24},{8,26},{10,28},{12,30},{16,2},{18,4},{... | collective-permute-start | bytes 98312 | tf_op jit(solution)/shard_map/ppermute | solution.py:401
  214.9 4.1 %state_proj.1 = (bf16[256,1024]{1,0:T(8,128)(2,1)}, f32[256,128]{1,0:T(8,128)}) custom-call(f32[256,1152]{1,0:T(8,128)} %get-tuple-element.157.kept_ref.kept, bf16[256,1152]{1,0:T(8,128)(2,1)} %collective-permute-done.42.got_ref.got_c, bf16[256,1152]{1,0:T(8,128)(2,1)} %collective-permute-done.43.got_f, f32[16,1152]{1,0:T(8,128)} %copy-done.32, ...), custom_call_target="tpu_custom_call" | custom-call | bytes 2621440 | tf_op jit(solution)/shard_map/state_proj/pallas_call | solution.py:443
  229.4 4.8 %mix.3 = (f32[256,1024]{1,0:T(8,128)}, f32[1,128,1024]{2,1,0:T(8,128)}, f32[128,1024]{1,0:T(8,128)}, bf16[128,1024]{1,0:T(8,128)(2,1)}) custom-call(f32[256,1024]{1,0:T(8,128)} %get-tuple-element.154.kept_ref.kept, bf16[256,1024]{1,0:T(8,128)(2,1)} %copy-done.7, bf16[256,1024]{1,0:T(8,128)(2,1)} %copy-done.12, f32[16,1024]{1,0:T(8,128)} %copy-done.33, ...), custom_call_target="tpu_custom_call" | custom-call | flops 268435456 | bytes 3670016 | tf_op jit(solution)/shard_map/mix/pallas_call | solution.py:476
  246.6 5.8 %collective-permute-start.37 = (bf16[16,512]{1,0:T(8,128)(2,1)S(1)}, bf16[16,512]{1,0:T(8,128)(2,1)S(1)}, u32[]{:S(2)}, u32[]{:S(2)}) collective-permute-start(bf16[16,512]{1,0:T(8,128)(2,1)S(1)} %copy-done.56), channel_id=1, source_target_pairs={{0,18},{2,20},{4,22},{6,24},{8,26},{10,28},{12,30},{16,2},{18,4},{... | collective-permute-start | bytes 49160 | tf_op jit(solution)/shard_map/ppermute | solution.py:401
  256.2 5.0 %collective-permute-start.33 = (bf16[16,512]{1,0:T(8,128)(2,1)S(1)}, bf16[16,512]{1,0:T(8,128)(2,1)S(1)}, u32[]{:S(2)}, u32[]{:S(2)}) collective-permute-start(bf16[16,512]{1,0:T(8,128)(2,1)S(1)} %copy-done.57), channel_id=1, source_target_pairs={{0,18},{2,20},{4,22},{6,24},{8,26},{10,28},{12,30},{16,2},{18,4},{... | collective-permute-start | bytes 49160 | tf_op jit(solution)/shard_map/ppermute | solution.py:401
  (270 shorter events, 133.8 us)
Async XLA Ops:
  3.7 39.5 %collective-permute-start.11 = (bf16[128,2048]{1,0:T(8,128)(2,1)}, bf16[128,2048]{1,0:T(8,128)(2,1)S(1)}, u32[]{:S(2)}, u32[]{:S(2)}) collective-permute-start(bf16[128,2048]{1,0:T(8,128)(2,1)} %get-tuple-element.107), channel_id=1, source_target_pairs={{0,16},{16,0},{1,17},{17,1},{2,18},{18,2},{3,19},{19,3},{4,20},{20... | collective-permute-start | bytes 1572872 | tf_op jit(solution)/shard_map/ppermute | solution.py:35
  7.8 45.8 %collective-permute-start.9 = (bf16[128,2048]{1,0:T(8,128)(2,1)}, bf16[128,2048]{1,0:T(8,128)(2,1)S(1)}, u32[]{:S(2)}, u32[]{:S(2)}) collective-permute-start(bf16[128,2048]{1,0:T(8,128)(2,1)} %get-tuple-element.106), channel_id=1, source_target_pairs={{0,16},{16,0},{1,17},{17,1},{2,18},{18,2},{3,19},{19,3},{4,20},{20... | collective-permute-start | bytes 1572872 | tf_op jit(solution)/shard_map/ppermute | solution.py:35
  13.0 50.6 %collective-permute-start.22 = (bf16[256,1024]{1,0:T(8,128)(2,1)}, bf16[256,1024]{1,0:T(8,128)(2,1)}, u32[]{:S(2)}, u32[]{:S(2)}) collective-permute-start(bf16[256,1024]{1,0:T(8,128)(2,1)} %get-tuple-element.110.refs_0_), channel_id=1, source_target_pairs={{0,8},{4,12},{8,0},{12,4},{1,9},{5,13},{9,1},{13,5},{2,10},{6,14},... | collective-permute-start | bytes 1572872 | tf_op jit(solution)/shard_map/ppermute | solution.py:35
  14.7 52.5 %collective-permute-start.20 = (bf16[256,1024]{1,0:T(8,128)(2,1)}, bf16[256,1024]{1,0:T(8,128)(2,1)S(1)}, u32[]{:S(2)}, u32[]{:S(2)}) collective-permute-start(bf16[256,1024]{1,0:T(8,128)(2,1)} %get-tuple-element.110.refs_0_), channel_id=1, source_target_pairs={{0,4},{4,0},{8,12},{12,8},{1,5},{5,1},{9,13},{13,9},{2,6},{6,2},{1... | collective-permute-start | bytes 1572872 | tf_op jit(solution)/shard_map/ppermute | solution.py:35
  16.2 48.9 %collective-permute-start.21 = (bf16[256,1024]{1,0:T(8,128)(2,1)}, bf16[256,1024]{1,0:T(8,128)(2,1)}, u32[]{:S(2)}, u32[]{:S(2)}) collective-permute-start(bf16[256,1024]{1,0:T(8,128)(2,1)} %get-tuple-element.111.refs_1_), channel_id=1, source_target_pairs={{0,4},{4,0},{8,12},{12,8},{1,5},{5,1},{9,13},{13,9},{2,6},{6,2},{1... | collective-permute-start | bytes 1572872 | tf_op jit(solution)/shard_map/ppermute | solution.py:35
  43.2 25.5 %collective-permute-start.23 = (bf16[256,1024]{1,0:T(8,128)(2,1)}, bf16[256,1024]{1,0:T(8,128)(2,1)}, u32[]{:S(2)}, u32[]{:S(2)}) collective-permute-start(bf16[256,1024]{1,0:T(8,128)(2,1)} %get-tuple-element.111.refs_1_), channel_id=1, source_target_pairs={{0,8},{4,12},{8,0},{12,4},{1,9},{5,13},{9,1},{13,5},{2,10},{6,14},... | collective-permute-start | bytes 1572872 | tf_op jit(solution)/shard_map/ppermute | solution.py:35
  65.9 24.3 %collective-permute-start.13 = (bf16[128,2048]{1,0:T(8,128)(2,1)S(1)}, bf16[128,2048]{1,0:T(8,128)(2,1)S(1)}, u32[]{:S(2)}, u32[]{:S(2)}) collective-permute-start(bf16[128,2048]{1,0:T(8,128)(2,1)S(1)} %collective-permute-done.12.got), channel_id=1, source_target_pairs={{0,1},{1,0},{2,3},{3,2},{4,5},{5,4},{6,7},{7,6},{8,9},{9,8},{10,11... | collective-permute-start | bytes 1572872 | tf_op jit(solution)/shard_map/ppermute | solution.py:35
  67.2 27.6 %collective-permute-start.24 = (bf16[256,1024]{1,0:T(8,128)(2,1)}, bf16[256,1024]{1,0:T(8,128)(2,1)}, u32[]{:S(2)}, u32[]{:S(2)}) collective-permute-start(bf16[256,1024]{1,0:T(8,128)(2,1)} %collective-permute-done.22.refs_4_), channel_id=1, source_target_pairs={{0,4},{4,0},{8,12},{12,8},{1,5},{5,1},{9,13},{13,9},{2,6},{6,2},{1... | collective-permute-start | bytes 1572872 | tf_op jit(solution)/shard_map/ppermute | solution.py:35
  68.7 26.7 %collective-permute-start.25 = (bf16[256,1024]{1,0:T(8,128)(2,1)}, bf16[256,1024]{1,0:T(8,128)(2,1)}, u32[]{:S(2)}, u32[]{:S(2)}) collective-permute-start(bf16[256,1024]{1,0:T(8,128)(2,1)} %collective-permute-done.21.refs_3_), channel_id=1, source_target_pairs={{0,8},{4,12},{8,0},{12,4},{1,9},{5,13},{9,1},{13,5},{2,10},{6,14},... | collective-permute-start | bytes 1572872 | tf_op jit(solution)/shard_map/ppermute | solution.py:35
  95.4 26.0 %collective-permute-start.18 = (bf16[256,1152]{1,0:T(8,128)(2,1)}, bf16[256,1152]{1,0:T(8,128)(2,1)}, u32[]{:S(2)}, u32[]{:S(2)}) collective-permute-start(bf16[256,1152]{1,0:T(8,128)(2,1)} %collective-permute-done.16.refs_4_), channel_id=1, source_target_pairs={{0,4},{4,0},{8,12},{12,8},{1,5},{5,1},{9,13},{13,9},{2,6},{6,2},{1... | collective-permute-start | bytes 1769480 | tf_op jit(solution)/shard_map/ppermute | solution.py:35
  109.1 25.2 %collective-permute-start = (bf16[128,2048]{1,0:T(8,128)(2,1)S(1)}, bf16[128,2048]{1,0:T(8,128)(2,1)S(1)}, u32[]{:S(2)}, u32[]{:S(2)}) collective-permute-start(bf16[128,2048]{1,0:T(8,128)(2,1)S(1)} %copy-done.11), channel_id=1, source_target_pairs={{0,1},{1,0},{2,3},{3,2},{4,5},{5,4},{6,7},{7,6},{8,9},{9,8},{10,11... | collective-permute-start | bytes 1572872 | tf_op jit(solution)/shard_map/ppermute | solution.py:35
  135.1 24.7 %collective-permute-start.6 = (bf16[256,1024]{1,0:T(8,128)(2,1)S(1)}, bf16[256,1024]{1,0:T(8,128)(2,1)S(1)}, u32[]{:S(2)}, u32[]{:S(2)}) collective-permute-start(bf16[256,1024]{1,0:T(8,128)(2,1)S(1)} %copy-done), channel_id=1, source_target_pairs={{0,8},{4,12},{8,0},{12,4},{1,9},{5,13},{9,1},{13,5},{2,10},{6,14},... | collective-permute-start | bytes 1572872 | tf_op jit(solution)/shard_map/ppermute | solution.py:35
  136.7 25.6 %collective-permute-start.7 = (bf16[256,1024]{1,0:T(8,128)(2,1)S(1)}, bf16[256,1024]{1,0:T(8,128)(2,1)S(1)}, u32[]{:S(2)}, u32[]{:S(2)}) collective-permute-start(bf16[256,1024]{1,0:T(8,128)(2,1)S(1)} %collective-permute-done.5.refs_4_), channel_id=1, source_target_pairs={{0,4},{4,0},{8,12},{12,8},{1,5},{5,1},{9,13},{13,9},{2,6},{6,2},{1... | collective-permute-start | bytes 1572872 | tf_op jit(solution)/shard_map/ppermute | solution.py:35
  138.2 24.1 %collective-permute-start.8 = (bf16[256,1024]{1,0:T(8,128)(2,1)S(1)}, bf16[256,1024]{1,0:T(8,128)(2,1)S(1)}, u32[]{:S(2)}, u32[]{:S(2)}) collective-permute-start(bf16[256,1024]{1,0:T(8,128)(2,1)S(1)} %collective-permute-done.4.refs_3_), channel_id=1, source_target_pairs={{0,8},{4,12},{8,0},{12,4},{1,9},{5,13},{9,1},{13,5},{2,10},{6,14},... | collective-permute-start | bytes 1572872 | tf_op jit(solution)/shard_map/ppermute | solution.py:35
  150.1 24.9 %collective-permute-start.42 = (bf16[256,1152]{1,0:T(8,128)(2,1)}, bf16[256,1152]{1,0:T(8,128)(2,1)}, u32[]{:S(2)}, u32[]{:S(2)}) collective-permute-start(bf16[256,1152]{1,0:T(8,128)(2,1)} %get-tuple-element.158), channel_id=1, source_target_pairs={{0,2},{2,0},{1,3},{3,1},{4,6},{6,4},{5,7},{7,5},{8,10},{10,8},{9,1... | collective-permute-start | bytes 1769480 | tf_op jit(solution)/shard_map/ppermute | solution.py:35
  159.8 55.0 %collective-permute-start.43 = (bf16[256,1152]{1,0:T(8,128)(2,1)}, bf16[256,1152]{1,0:T(8,128)(2,1)}, u32[]{:S(2)}, u32[]{:S(2)}) collective-permute-start(bf16[256,1152]{1,0:T(8,128)(2,1)} %get-tuple-element.125), channel_id=1, source_target_pairs={{0,16},{16,0},{1,17},{17,1},{2,18},{18,2},{3,19},{19,3},{4,20},{20... | collective-permute-start | bytes 1769480 | tf_op jit(solution)/shard_map/ppermute | solution.py:35
  172.1 52.3 %collective-permute-start.40 = (f32[16,1024]{1,0:T(8,128)}, f32[16,1024]{1,0:T(8,128)S(1)}, u32[]{:S(2)}, u32[]{:S(2)}) collective-permute-start(f32[16,1024]{1,0:T(8,128)} %rim.6), channel_id=1, source_target_pairs={{0,2},{2,4},{4,6},{6,8},{8,10},{10,12},{12,14},{1,3},{3,5},{5,7},{... | collective-permute-start | bytes 196616 | tf_op jit(solution)/shard_map/ppermute | solution.py:400
  174.5 53.5 %collective-permute-start.39 = (bf16[256,1024]{1,0:T(8,128)(2,1)}, bf16[256,1024]{1,0:T(8,128)(2,1)S(1)}, u32[]{:S(2)}, u32[]{:S(2)}) collective-permute-start(bf16[256,1024]{1,0:T(8,128)(2,1)} %get-tuple-element.114), channel_id=1, source_target_pairs={{0,16},{16,0},{1,17},{17,1},{2,18},{18,2},{3,19},{19,3},{4,20},{20... | collective-permute-start | bytes 1572872 | tf_op jit(solution)/shard_map/ppermute | solution.py:35
  176.5 36.8 %collective-permute-start.44 = (f32[16,1152]{1,0:T(8,128)}, f32[16,1152]{1,0:T(8,128)S(1)}, u32[]{:S(2)}, u32[]{:S(2)}) collective-permute-start(f32[16,1152]{1,0:T(8,128)} %rim.7), channel_id=1, source_target_pairs={{0,2},{2,4},{4,6},{6,8},{8,10},{10,12},{12,14},{1,3},{3,5},{5,7},{... | collective-permute-start | bytes 221192 | tf_op jit(solution)/shard_map/ppermute | solution.py:400
  198.7 29.0 %collective-permute-start.41 = (bf16[16,1024]{1,0:T(8,128)(2,1)S(1)}, bf16[16,1024]{1,0:T(8,128)(2,1)S(1)}, u32[]{:S(2)}, u32[]{:S(2)}) collective-permute-start(bf16[16,1024]{1,0:T(8,128)(2,1)S(1)} %copy-done.55), channel_id=1, source_target_pairs={{0,18},{2,20},{4,22},{6,24},{8,26},{10,28},{12,30},{16,2},{18,4},{... | collective-permute-start | bytes 98312 | tf_op jit(solution)/shard_map/ppermute | solution.py:401
  213.4 29.8 %collective-permute-start.34 = (bf16[256,512]{1,0:T(8,128)(2,1)S(1)}, bf16[256,512]{1,0:T(8,128)(2,1)S(1)}, u32[]{:S(2)}, u32[]{:S(2)}) collective-permute-start(bf16[256,512]{1,0:T(8,128)(2,1)S(1)} %copy-done.51), channel_id=1, source_target_pairs={{0,2},{2,0},{1,3},{3,1},{4,6},{6,4},{5,7},{7,5},{8,10},{10,8},{9,1... | collective-permute-start | bytes 786440 | tf_op jit(solution)/shard_map/ppermute | solution.py:35
  224.4 36.8 %collective-permute-start.35 = (bf16[256,512]{1,0:T(8,128)(2,1)S(1)}, bf16[256,512]{1,0:T(8,128)(2,1)S(1)}, u32[]{:S(2)}, u32[]{:S(2)}) collective-permute-start(bf16[256,512]{1,0:T(8,128)(2,1)S(1)} %copy-done.50), channel_id=1, source_target_pairs={{0,16},{16,0},{1,17},{17,1},{2,18},{18,2},{3,19},{19,3},{4,20},{20... | collective-permute-start | bytes 786440 | tf_op jit(solution)/shard_map/ppermute | solution.py:35
  238.0 28.4 %collective-permute-start.31 = (bf16[256,512]{1,0:T(8,128)(2,1)}, bf16[256,512]{1,0:T(8,128)(2,1)S(1)}, u32[]{:S(2)}, u32[]{:S(2)}) collective-permute-start(bf16[256,512]{1,0:T(8,128)(2,1)} %get-tuple-element.149), channel_id=1, source_target_pairs={{0,16},{16,0},{1,17},{17,1},{2,18},{18,2},{3,19},{19,3},{4,20},{20... | collective-permute-start | bytes 786440 | tf_op jit(solution)/shard_map/ppermute | solution.py:35
  242.1 29.1 %collective-permute-start.56 = (bf16[128,1024]{1,0:T(8,128)(2,1)}, bf16[128,1024]{1,0:T(8,128)(2,1)S(1)}, u32[]{:S(2)}, u32[]{:S(2)}) collective-permute-start(bf16[128,1024]{1,0:T(8,128)(2,1)} %get-tuple-element.195), channel_id=1, source_target_pairs={{0,4},{2,6},{4,0},{6,2},{8,12},{10,14},{12,8},{14,10},{1,5},{3,7},... | collective-permute-start | bytes 786440 | tf_op jit(solution)/shard_map/ppermute | solution.py:35
  (92 other events, 867.2 us)
where the time goes:
time: 303 us; the launch traced here: 301 us
  Pallas kernels  118 us (39%)
  starting transfers between devices  90.2 us (30%)
  waiting for transfers between devices  61.1 us (20%)
  local copies, waits for them, and re-layouts  22.3 us (7%)
  other arithmetic  6.48 us (2%)
  between operations  3.22 us (1%)
    ppermute x50, waiting for transfers between devices, swapped(): lax.ppermute(part, axis, [(i, i ^ by) for i in range(lax.axis_size(axis))])  61 us
    ppermute x50, starting transfers between devices, swapped(): lax.ppermute(part, axis, [(i, i ^ by) for i in range(lax.axis_size(axis))])  52 us
    pallas_call x8, Pallas kernels, multiplied(): call(functools.partial(multiply_kernel, heads, with_steps, len(weights)),...  46.1 us
    ppermute x4, starting transfers between devices, projected(): lax.ppermute(rim_far, ('fsdp',) + SEQ, [(f * count + i, (1 - f) * count +...  29.6 us
    unnamed x120, local copies, waits for them, and re-layouts  16.1 us
    pallas_call x6, Pallas kernels, combined(): call(kernel, 'combine', (jax.ShapeDtypeStruct(total.shape, F32), jax.Shap...  12.2 us
    pallas_call x3, Pallas kernels, body(): call(mix_kernel, 'mix', (jax.ShapeDtypeStruct((tok_count, groups * width)...  11.9 us
    pallas_call x2, Pallas kernels, sampled_cols(): call(functools.partial(sample_kernel, count), 'sample', (jax.ShapeDtypeSt...  10.2 us
  transfers between devices with their start and end apart: 58, of which 8 were waited for; matrix products, arithmetic and copies ran while one was open for 5% of the time, Pallas kernels for 37%

commit v1 on v0

v1 whole, which is shorter than its diff:
```python
import functools

import jax
import jax.numpy as jnp
from jax import lax
from jax.experimental import pallas as pl
from jax.experimental.pallas import tpu as pltpu
from jax.sharding import Mesh, PartitionSpec as P

P_SIZE = 64
N = 128
CONV = 4
SPAN = 128
LANES = 128
RIM = 16
SEQ = ("chip", "core")
F32 = jnp.float32
BF16 = jnp.bfloat16
SMEM = pl.BlockSpec(memory_space=pltpu.SMEM)
VMEM = pl.BlockSpec(memory_space=pltpu.VMEM)


def call(kernel, name, out_shape, flops=0, moved=0, small=False, **settings):
    return pl.pallas_call(
        kernel,
        out_shape=out_shape,
        name=name,
        cost_estimate=pl.CostEstimate(flops=flops // 50, bytes_accessed=moved // 50, transcendentals=0),
        compiler_params=pltpu.CompilerParams(vmem_limit_bytes=(12 if small else 60) * 1024 * 1024),
        **settings,
    )


def swapped(part, axis, by=1):
    return lax.ppermute(part, axis, [(i, i ^ by) for i in range(lax.axis_size(axis))])


def cut_kernel(chips, at_ref, tokens_ref, own_ref, far_kept, far_sent):
    depth = far_kept.shape[1] // chips
    rows = far_kept.shape[0]
    f_at, c_at = at_ref[0], at_ref[1]
    for i in range(chips):
        cols = slice(i * depth, (i + 1) * depth)

        def taken(f, c):
            start = pl.multiple_of(((f * chips + at_ref[3 + i]) * 2 + c) * depth, depth)
            return tokens_ref[:, pl.ds(start, depth)]

        far_sent[:, cols] = taken(1 - f_at, 1 - c_at)
        far_kept[:, cols] = taken(1 - f_at, c_at)
        own_ref[:rows, cols] = taken(f_at, c_at)
        own_ref[rows:, cols] = taken(f_at, 1 - c_at)


def stack_kernel(chips, shares, at_ref, *refs):
    pieces, (rows_ref, tail_ref) = refs[:-2], refs[-2:]
    count = pieces[0].shape[0]
    half = shares * count
    depth = tail_ref.shape[1] // chips
    for at in range(2):
        for share in range(shares):
            place = (at_ref[2] if share == 0 else 1 - at_ref[2]) if shares == 2 else 0
            start = pl.multiple_of(at * half + place * count, count)
            rows_ref[pl.ds(start, count), :] = pieces[at * shares + share][...]
    last = pl.multiple_of((2 - at_ref[1]) * half - RIM, RIM)
    for i in range(chips):
        start = pl.multiple_of(at_ref[3 + i] * depth, depth)
        tail_ref[:, pl.ds(start, depth)] = rows_ref[pl.ds(last, RIM), i * depth : (i + 1) * depth]


def append_kernel(chips, at_ref, tail_ref, rows_ref, out_ref):
    depth = tail_ref.shape[1] // chips
    for i in range(chips):
        start = pl.multiple_of(at_ref[3 + i] * depth, depth)
        out_ref[:, i * depth : (i + 1) * depth] = tail_ref[:, pl.ds(start, depth)]


def token_rows(at, chips, pieces, specs):
    count, depth = specs[0].block_shape
    rows = len(pieces) * count + RIM
    rows_ext, tail = call(
        functools.partial(stack_kernel, chips, len(pieces) // 2),
        "stack_rows",
        (jax.ShapeDtypeStruct((rows, depth), BF16), jax.ShapeDtypeStruct((RIM, depth), BF16)),
        moved=4 * rows * depth,
        grid=(1,),
        in_specs=[SMEM] + specs,
        out_specs=[pl.BlockSpec((rows, depth), lambda i: (0, 0)), pl.BlockSpec((RIM, depth), lambda i: (0, 0))],
    )(at, *pieces)
    tail = lax.ppermute(tail, "chip", [(i, i + 1) for i in range(chips - 1)])
    last = rows // RIM - 1
    return call(
        functools.partial(append_kernel, chips),
        "append_rows",
        jax.ShapeDtypeStruct((rows, depth), BF16),
        moved=4 * RIM * depth,
        grid=(1,),
        in_specs=[SMEM, pl.BlockSpec((RIM, depth), lambda i: (0, 0)), pl.BlockSpec(memory_space=pl.ANY)],
        out_specs=pl.BlockSpec((RIM, depth), lambda i: (last, 0)),
        input_output_aliases={2: 0},
    )(at, tail, rows_ext)


def sample_kernel(count, coef_ref, mean_ref, devs_ref, out_ref):
    factor = (2.0 * (count - 1)) ** (-0.5)
    accum = mean_ref[...].astype(F32)
    for member in range(count):
        accum = accum + factor * coef_ref[member] * devs_ref[member].astype(F32)
    out_ref[...] = accum.astype(BF16)


def sampled_cols(mean_part, dev_part, swag_coef, at, width):
    rows, count = mean_part.shape[0], dev_part.shape[0]
    tile = rows // 4
    return call(
        functools.partial(sample_kernel, count),
        "sample",
        jax.ShapeDtypeStruct((rows, width), BF16),
        moved=2 * (count + 2) * rows * width,
        grid=(4,),
        in_specs=[
            SMEM,
            pl.BlockSpec((tile, width), lambda i: (i, at)),
            pl.BlockSpec((count, tile, width), lambda i: (0, i, at)),
        ],
        out_specs=pl.BlockSpec((tile, width), lambda i: (i, 0)),
    )(swag_coef, mean_part, dev_part)


def sampled(mean_part, dev_part, swag_coef):
    factor = (2.0 * (dev_part.shape[0] - 1)) ** (-0.5)
    accum = mean_part.astype(F32)
    for member in range(dev_part.shape[0]):
        accum = accum + factor * swag_coef[member] * dev_part[member].astype(F32)
    return accum.astype(BF16)


def pack_kernel(bc_ref, dt_ref, out_ref):
    width, heads = bc_ref.shape[1], dt_ref.shape[1]
    out_ref[:, :width] = bc_ref[...]
    out_ref[:, width:] = jnp.zeros((out_ref.shape[0], LANES), BF16)
    out_ref[:, width : width + heads] = dt_ref[...]


def swapped_both(weight):
    return swapped(weight, "chip", 1), swapped(weight, "chip", 2)


def gathered(weight, both, by_x):
    if both is None:
        return [lax.all_gather(weight, "chip", axis=0, tiled=True)]
    return [weight, both[0], both[1], swapped(both[1], "chip", 1) if by_x else swapped(both[0], "chip", 2)]


def coded(part, heads):
    high = part.astype(BF16).astype(F32)
    return high + pltpu.roll(part - high, heads, 1)


def decoded(part, heads):
    return part + pltpu.roll(part, LANES - heads, 1)


def multiply_kernel(heads, with_steps, pieces, at_ref, far_ref, own_ref, *refs):
    weights, (sent_ref, kept_ref) = refs[:pieces], refs[pieces:]
    second = at_ref[1] == 1
    for k, rows_ref in enumerate((far_ref, own_ref)):
        at = 0
        total = None
        for weight in weights:
            depth = weight.shape[0]
            term = jnp.dot(rows_ref[:, at : at + depth], weight[...], preferred_element_type=F32)
            total = term if total is None else total + term
            at += depth
        half = (total.shape[0] - RIM) // 2
        before = total[2 * half :]
        kept_ref[k, :half, :] = total[:half]
        kept_ref[k, half:, :] = jnp.where(second, total[2 * half - RIM : 2 * half], before)
        sent_ref[k, :half, :] = total[half : 2 * half].astype(BF16)
        sent_ref[k, half:, :] = jnp.where(second, before, total[half - RIM : half]).astype(BF16)
        if with_steps:
            @pl.when(pl.program_id(0) == pl.num_programs(0) - 1)
            def _():
                sent_ref[k, :half, -LANES:] = coded(total[half : 2 * half, -LANES:], heads).astype(BF16)


def multiplied(at, rows_far, rows_own, weights, heads, with_steps, first, width):
    tile = next(t for t in (256, 384, 128) if width % t == 0)
    col = first // tile
    half = (rows_far.shape[0] - RIM) // 2 + RIM
    return call(
        functools.partial(multiply_kernel, heads, with_steps, len(weights)),
        "multiply",
        (jax.ShapeDtypeStruct((2, half, width), BF16), jax.ShapeDtypeStruct((2, half, width), F32)),
        flops=4 * rows_far.size * width,
        moved=4 * rows_far.size + 2 * rows_far.shape[1] * width + 12 * half * width,
        grid=(width // tile,),
        in_specs=[SMEM]
        + [pl.BlockSpec(rows_far.shape, lambda i: (0, 0))] * 2
        + [pl.BlockSpec((w.shape[0], tile), lambda i: (0, col + i)) for w in weights],
        out_specs=[pl.BlockSpec((2, half, tile), lambda i: (0, 0, i))] * 2,
    )(at, rows_far, rows_own, *weights)


def relay_kernel(heads, with_steps, kept_ref, got_ref, out_ref):
    kept, got = kept_ref[0], got_ref[0].astype(F32)
    out_ref[...] = (kept + got).astype(BF16)
    if with_steps:
        wide = kept[:, -LANES:] + decoded(got[:, -LANES:], heads)
        lane = lax.broadcasted_iota(jnp.int32, wide.shape, 1)
        out_ref[:, -LANES:] = coded(jnp.where(lane < heads, wide, 0.0), heads).astype(BF16)


def relayed(kept, got, heads, with_steps):
    rows, width = kept.shape[1:]
    return call(
        functools.partial(relay_kernel, heads, with_steps),
        "relay",
        jax.ShapeDtypeStruct((rows, width), BF16),
        moved=8 * rows * width,
        small=True,
        grid=(1,),
        in_specs=[pl.BlockSpec((1, rows, width), lambda i: (0, 0, 0))] * 2,
        out_specs=pl.BlockSpec((rows, width), lambda i: (0, 0)),
    )(kept, got)


def convolved(width, kept, got_c, got_f, taps, padded):
    count = padded.shape[0] - 8
    proj = kept[0, :, :width] + got_c[0, :, :width].astype(F32) + got_f[:, :width].astype(F32)
    proj = proj.astype(BF16).astype(F32)
    padded[8:, :] = proj[:count]
    padded[:8, :] = proj[count + RIM - 8 :]
    first = 8 - (CONV - 1)
    conv_sum = taps[0:1, :] * padded[first : first + count, :]
    for offset in range(1, CONV):
        conv_sum = conv_sum + taps[offset : offset + 1, :] * padded[first + offset : first + offset + count, :]
    return (conv_sum * jax.nn.sigmoid(conv_sum)).astype(BF16)


def state_proj_kernel(heads, kept, got_c, got_f, taps, out_ref, logits_ref, padded):
    count, width = out_ref.shape
    out_ref[...] = convolved(width, kept, got_c, got_f, taps, padded)
    logits_ref[...] = (
        kept[0, :count, width:]
        + decoded(got_c[0, :count, width:].astype(F32), heads)
        + decoded(got_f[:count, width:].astype(F32), heads)
    )


def pairwise(columns, first):
    shape = (columns.shape[0], 2 * P_SIZE)
    lane = lax.broadcasted_iota(jnp.int32, shape, 1)
    return jnp.where(lane < P_SIZE, columns[:, first : first + 1], columns[:, first + 1 : first + 2])


def over_channels(columns):
    return jnp.concatenate([pairwise(columns, h) for h in range(0, columns.shape[1], 2)], axis=1)


def mix_kernel(
    kept, got_c, got_f, taps, keys, reads, cum_g, steps_g, cum_t, steps_t, skip, y_ref, early_ref, total_ref, sent_ref, padded
):
    width = y_ref.shape[1]
    values = convolved(width, kept, got_c, got_f, taps, padded)
    cum, steps = cum_g[0], steps_g[0]
    heads = cum.shape[1]
    row = lax.broadcasted_iota(jnp.int32, (SPAN, SPAN), 0)
    col = lax.broadcasted_iota(jnp.int32, (SPAN, SPAN), 1)
    causal = row >= col
    lane = lax.broadcasted_iota(jnp.int32, (SPAN, 2 * P_SIZE), 1)
    state = None
    for at in range(0, y_ref.shape[0], SPAN):
        span = slice(at, at + SPAN)
        keys_b, reads_b, values_b = keys[span, :], reads[span, :], values[span, :]
        cum_b, steps_b = cum[span, :], steps[span, :]
        last = cum_b[SPAN - 1 : SPAN, :]
        scores = lax.dot_general(reads_b, keys_b, (((1,), (1,)), ((), ())), preferred_element_type=F32)
        scores = jnp.where(causal, scores, 0.0)
        reach = jnp.exp(last - cum_b) * steps_b
        scaled = []
        for head in range(0, heads, 2):
            chans = slice(head * P_SIZE, (head + 2) * P_SIZE)
            two = []
            for h in (head, head + 1):
                gap = cum_b[:, h : h + 1] - cum_t[h : h + 1, span]
                two.append((scores * jnp.exp(jnp.minimum(gap, 0.0)) * steps_t[h : h + 1, span]).astype(BF16))
            values_h = values_b[:, chans]
            both = jnp.dot(jnp.concatenate(two, axis=0), values_h, preferred_element_type=F32)
            inner = jnp.where(lane < P_SIZE, both[:SPAN], both[SPAN:])
            wide = values_h.astype(F32)
            y_ref[span, chans] = inner + skip[0:1, chans] * wide
            scaled.append((wide * pairwise(reach, head)).astype(BF16))
        fresh = lax.dot_general(
            keys_b, jnp.concatenate(scaled, axis=1), (((0,), (0,)), ((), ())), preferred_element_type=F32
        )
        state = fresh if state is None else over_channels(jnp.exp(last)) * state + fresh
        if at + SPAN < y_ref.shape[0]:
            early_ref[at // SPAN] = fresh
    total_ref[...] = state
    sent_ref[...] = state.astype(BF16)


def combine_kernel(level, scales, total, other, before, total_ref, sent_ref, before_ref):
    gain, keep, take = (scales[3 * level + i : 3 * level + i + 1, :] for i in range(3))
    come = other[...].astype(F32)
    fresh = gain * come
    before_ref[...] = fresh if before is None else before[...] + fresh
    joint = keep * total[...] + take * come
    total_ref[...] = joint
    sent_ref[...] = joint.astype(BF16)


def read_kernel(level, y, reads, cum_g, early, scales, before, other, *refs):
    out_ref = refs[-1]
    state = before[...] + scales[3 * level : 3 * level + 1, :] * other[...].astype(F32)
    cum = cum_g[0]
    for at in range(0, out_ref.shape[0], SPAN):
        span = slice(at, at + SPAN)
        cum_b = cum[span, :]
        seen = jnp.dot(reads[span, :], state.astype(BF16), preferred_element_type=F32)
        out_ref[span, :] = (y[span, :] + over_channels(jnp.exp(cum_b)) * seen).astype(BF16)
        if at + SPAN < out_ref.shape[0]:
            state = over_channels(jnp.exp(cum_b[SPAN - 1 : SPAN, :])) * state + early[at // SPAN]


def prefix_scales(decay):
    place = lax.axis_index(SEQ)
    count = lax.axis_size(SEQ)
    before = jnp.ones_like(decay)
    total = decay
    rows = []
    by = 1
    while by < count:
        other = swapped(total, SEQ, by)
        upper = (place & by) != 0
        rows += [jnp.where(upper, before, 0.0), jnp.where(upper, 1.0, other), jnp.where(upper, total, 1.0)]
        before = jnp.where(upper, other * before, before)
        total = total * other
        by *= 2
    scales = jnp.stack(rows)
    return jnp.broadcast_to(scales[:, :, None], scales.shape + (P_SIZE,)).reshape(len(rows), -1)


def combined(level, scales, total, other, before, first):
    width, wide = total.shape[1], total.shape[1] // first[1]
    block = pl.BlockSpec((N, wide), lambda i: (0, i))
    kernel = functools.partial(combine_kernel, level)
    if before is None:
        kernel = lambda scales, total, other, *outs: combine_kernel(level, scales, total, other, None, *outs)
    return call(
        kernel,
        "combine",
        (
            jax.ShapeDtypeStruct(total.shape, F32),
            jax.ShapeDtypeStruct(total.shape, BF16),
            jax.ShapeDtypeStruct(total.shape, F32),
        ),
        flops=6 * total.size,
        moved=20 * total.size,
        small=True,
        grid=(first[1],),
        in_specs=[pl.BlockSpec((scales.shape[0], wide), lambda i: (0, first[0] + i))]
        + [block] * (2 if before is None else 3),
        out_specs=[block] * 3,
    )(scales, total, other, *(() if before is None else (before,)))


def body(
    tokens,
    proj_mean,
    proj_devs,
    bc_mean,
    bc_devs,
    swag_coef,
    dt_weight,
    dt_bias,
    decay_rate,
    skip_gain,
    conv_proj,
    conv_bc,
):
    heads_here = decay_rate.shape[0]
    groups_here = bc_mean.shape[2] // N
    per_group = heads_here // groups_here
    width_bc = 2 * bc_mean.shape[2]
    rows_k = proj_mean.shape[0]
    chips = lax.axis_size("chip")
    count = lax.axis_size(SEQ)

    def after(arrays, earlier):
        return lax.optimization_barrier((arrays, earlier))[0]

    width = per_group * P_SIZE
    early_groups = max(1, groups_here // 2)
    late = list(range(early_groups, groups_here))

    plane = chips == 4
    place = lax.axis_index("chip") if plane else 0
    at = jnp.stack([lax.axis_index(a) for a in ("fsdp", "core", "tp")] + [place ^ i for i in range(chips)]).astype(jnp.int32)
    share, depth = tokens.shape[0], chips * rows_k
    own, far_kept, far_sent = call(
        functools.partial(cut_kernel, chips),
        "cut_tokens",
        (jax.ShapeDtypeStruct((2 * share, depth), BF16),) + (jax.ShapeDtypeStruct((share, depth), BF16),) * 2,
        moved=4 * tokens.size,
        in_specs=[SMEM, VMEM],
        out_specs=[VMEM] * 3,
    )(at, tokens)
    far_sent, far_kept = swapped(far_sent, "fsdp"), swapped(far_kept, "fsdp")

    weights = [sampled_cols(proj_mean, proj_devs, swag_coef, 0, early_groups * width)]
    both = [swapped_both(weights[0]) if plane else None]
    weight_bc = sampled(bc_mean, bc_devs, swag_coef).reshape(rows_k, width_bc)
    weights.append(
        call(
            pack_kernel,
            "pack",
            jax.ShapeDtypeStruct((rows_k, width_bc + LANES), BF16),
            moved=4 * weight_bc.size,
            in_specs=[VMEM] * 2,
            out_specs=VMEM,
        )(weight_bc, dt_weight)
    )
    both.append(swapped_both(weights[1]) if plane else None)
    for j, g in enumerate(late):
        mean_part = proj_mean
        if plane and j < 2:
            mean_part = after(proj_mean, (both[j], weights[-1]))
        weights.append(sampled_cols(mean_part, proj_devs, swag_coef, g, width))
        both.append(swapped_both(weights[-1]) if plane else None)
        if j == 0:
            far_sent, far_kept = after((far_sent, far_kept), weights[-1])
    pieces = [gathered(w, b, j % 2 == 0) for j, (w, b) in enumerate(zip(weights, both))]

    if lax.axis_size("tp") == 2:
        low = pl.BlockSpec((share, depth), lambda i: (0, 0))
        high = pl.BlockSpec((share, depth), lambda i: (1, 0))
        own_t = swapped(own, "tp")
        own_pieces = (own, own_t, swapped(own, "core"), swapped(own_t, "core"))
        rows_own = token_rows(at, chips, own_pieces, [low, low, high, high])
        sent_t = swapped(far_sent, "tp")
        far_pieces = (far_kept, swapped(far_kept, "tp"), swapped(far_sent, "core"), swapped(sent_t, "core"))
        rows_far = token_rows(at, chips, far_pieces, [low] * 4)
    else:
        whole = lambda a: lax.all_gather(a, "tp", axis=0, tiled=True)
        spec = pl.BlockSpec((share * lax.axis_size("tp"), depth), lambda i: (0, 0))
        rows_own = token_rows(at, chips, (whole(own[:share]), whole(swapped(own[share:], "core"))), [spec] * 2)
        rows_far = token_rows(at, chips, (whole(far_kept), whole(swapped(far_sent, "core"))), [spec] * 2)
    tok_count = (rows_own.shape[0] - RIM) // 2
    blocks = tok_count // SPAN

    def projected(pieces, with_steps, width):
        sent, kept = multiplied(at, rows_far, rows_own, pieces, heads_here, with_steps, 0, width)
        got = swapped(sent, "core")
        back = relayed(kept, got, heads_here, with_steps)
        return (kept, got, swapped(back, "fsdp")), back

    parts = []
    back = None
    for j, chunk in enumerate(pieces):
        if back is not None:
            chunk = after(chunk, back)
        part, back = projected(chunk, j == 1, weights[j].shape[1])
        parts.append(part)
    part_bc = parts.pop(1)
    chunks = [(0, early_groups)] + [(g, 1) for g in late]

    rows_ext = tok_count + RIM
    specs_of = lambda width: [pl.BlockSpec((1, rows_ext, width), lambda i: (1, 0, i))] * 2 + [
        pl.BlockSpec((rows_ext, width), lambda i: (0, i))
    ]
    whole_of = lambda *shape: pl.BlockSpec(shape, lambda i: (0,) * len(shape))
    conv_out, logits = call(
        functools.partial(state_proj_kernel, heads_here),
        "state_proj",
        (jax.ShapeDtypeStruct((tok_count, width_bc), BF16), jax.ShapeDtypeStruct((tok_count, LANES), F32)),
        moved=10 * tok_count * width_bc,
        grid=(1,),
        in_specs=specs_of(width_bc + LANES) + [whole_of(CONV, width_bc)],
        out_specs=[whole_of(tok_count, width_bc), whole_of(tok_count, LANES)],
        scratch_shapes=[pltpu.VMEM((tok_count + 8, width_bc), F32)],
    )(*part_bc, conv_bc.reshape(CONV, width_bc))
    step_size = jax.nn.softplus(logits[:, :heads_here] + dt_bias)
    steps_b = step_size.reshape(blocks, SPAN, heads_here)
    cum_log = jnp.cumsum(-steps_b * decay_rate, axis=1)
    scales = prefix_scales(jnp.exp(jnp.sum(cum_log[:, SPAN - 1, :], axis=0)))
    cum_log = cum_log.reshape(tok_count, heads_here)
    cum_t, steps_t = cum_log.T, step_size.T
    by_group = lambda a: jnp.transpose(a.reshape(tok_count, groups_here, per_group), (1, 0, 2))
    cum_g, steps_g = by_group(cum_log), by_group(step_size)
    skip = jnp.repeat(skip_gain, P_SIZE)[None, :]
    levels = scales.shape[0] // 3

    result = None
    last_total = None
    for (first, groups), part in zip(chunks, parts):
        if last_total is not None:
            part = after(part, last_total)
        grid = (groups,)
        cols = lambda rows: pl.BlockSpec((rows, width), lambda i: (0, i))
        cols_all = lambda rows: pl.BlockSpec((rows, width), lambda i: (0, first + i))
        heads_g = pl.BlockSpec((1, tok_count, per_group), lambda i: (first + i, 0, 0))
        heads_t = pl.BlockSpec((per_group, tok_count), lambda i: (first + i, 0))
        keys = pl.BlockSpec((tok_count, N), lambda i: (0, first + i))
        reads = pl.BlockSpec((tok_count, N), lambda i: (0, groups_here + first + i))
        early_spec = pl.BlockSpec((blocks - 1, N, width), lambda i: (0, 0, i))
        y, early, total, sent = call(
            mix_kernel,
            "mix",
            (
                jax.ShapeDtypeStruct((tok_count, groups * width), F32),
                jax.ShapeDtypeStruct((blocks - 1, N, groups * width), F32),
                jax.ShapeDtypeStruct((N, groups * width), F32),
                jax.ShapeDtypeStruct((N, groups * width), BF16),
            ),
            flops=8 * tok_count * N * width * groups,
            moved=14 * tok_count * width * groups,
            grid=grid,
            in_specs=specs_of(width)
            + [cols_all(CONV), keys, reads, heads_g, heads_g, heads_t, heads_t, cols_all(1)],
            out_specs=[cols(tok_count), early_spec, cols(N), cols(N)],
            scratch_shapes=[pltpu.VMEM((tok_count + 8, width), F32)],
        )(*part, conv_proj, conv_out, conv_out, cum_g, steps_g, cum_t, steps_t, skip)
        last_total = sent
        before = None
        for level in range(levels - 1):
            other = swapped(sent, SEQ, 1 << level)
            total, sent, before = combined(level, scales, total, other, before, (first, groups))
        other = swapped(sent, SEQ, 1 << (levels - 1))
        operands = [y, conv_out, cum_g, early, scales, before, other]
        specs = [cols(tok_count), reads, heads_g, early_spec, cols_all(scales.shape[0]), cols(N), cols(N)]
        alias = {}
        if result is not None:
            operands.append(result)
            specs.append(pl.BlockSpec(memory_space=pl.ANY))
            alias = {len(operands) - 1: 0}
        result = call(
            functools.partial(read_kernel, levels - 1),
            "read_out",
            jax.ShapeDtypeStruct((tok_count, heads_here * P_SIZE), BF16),
            flops=2 * tok_count * N * width * groups,
            moved=10 * tok_count * width * groups,
            small=True,
            grid=grid,
            in_specs=specs,
            out_specs=cols_all(tok_count),
            input_output_aliases=alias,
        )(*operands)
    return result


def solution(mesh):
    shape = mesh.shape
    split = Mesh(
        mesh.devices.reshape(shape["fsdp"], shape["seq"] // 2, 2, shape["tp"]),
        ("fsdp", "chip", "core", "tp"),
    )
    rows = ("fsdp", "chip", "core")
    return jax.shard_map(
        body,
        mesh=split,
        in_specs=(
            P(rows + ("tp",), None),
            P(rows, "tp"),
            P(None, rows, "tp"),
            P(rows, None, "tp"),
            P(None, rows, None, "tp"),
            P(),
            P(rows, "tp"),
            P("tp"),
            P("tp"),
            P("tp"),
            P(None, "tp"),
            P(None, None, "tp"),
        ),
        out_specs=P(rows, "tp"),
        check_vma=False,
    )
```

time: 303 us -> 296 us (0.977)
  waiting for transfers between devices: 61.1 us -> 133 us
  starting transfers between devices: 90.2 us -> 49.2 us
  Pallas kernels: 118 us -> 85.6 us
  local copies, waits for them, and re-layouts: 22.3 us -> 17.6 us
    ppermute x50 -> x41, waiting for transfers between devices: 61 us -> 132 us  [swapped(): lax.ppermute(part, axis, [(i, i ^ by) for i in range(lax.axis_size(axis))])]
    ppermute x8 -> x2, starting transfers between devices: 38.3 us -> 6.64 us  [token_rows(): tail = lax.ppermute(tail, 'chip', [(i, i + 1) for i in range(chips - 1)])]
    pallas_call x8 -> x4, Pallas kernels: 46.1 us -> 33.7 us  [multiplied(): call(functools.partial(multiply_kernel, heads, with_steps, len(weights)),...]
    ppermute x50 -> x41, starting transfers between devices: 52 us -> 42.5 us  [swapped(): lax.ppermute(part, axis, [(i, i ^ by) for i in range(lax.axis_size(axis))])]
    pallas_call x6, Pallas kernels: 12.2 us -> 3.36 us  [combined(): call(kernel, 'combine', (jax.ShapeDtypeStruct(total.shape, F32), jax.Shap...]
    pallas_call x14 -> x13, Pallas kernels: 36.1 us -> 28.5 us  [the longest x3 12.3 us: sampled_cols(): call(functools.partial(sample_kernel, count), 'sample', jax.ShapeDtypeStr...]
    unnamed x120 -> x84, local copies, waits for them, and re-layouts: 16.1 us -> 12.1 us
    pallas_call x3, Pallas kernels: 7.75 us -> 4.03 us  [body(): call(functools.partial(read_kernel, levels - 1), 'read_out', jax.ShapeDty...]
  transfers between devices with their start and end apart: 58 -> 43, of which waited for: 8 -> 21; matrix products, arithmetic and copies ran while one was open for 5% -> 5% of each run, Pallas kernels for 37% -> 24%
where the time goes in v1:
time: 296 us; the launch traced here: 295 us
  waiting for transfers between devices  133 us (45%)
  Pallas kernels  85.6 us (29%)
  starting transfers between devices  49.2 us (17%)
  local copies, waits for them, and re-layouts  17.6 us (6%)
  other arithmetic  6.29 us (2%)
  between operations  2.98 us (1%)
    ppermute x41, waiting for transfers between devices, swapped(): lax.ppermute(part, axis, [(i, i ^ by) for i in range(lax.axis_size(axis))])  132 us
    ppermute x41, starting transfers between devices, swapped(): lax.ppermute(part, axis, [(i, i ^ by) for i in range(lax.axis_size(axis))])  42.5 us
    pallas_call x4, Pallas kernels, multiplied(): call(functools.partial(multiply_kernel, heads, with_steps, len(weights)),...  33.7 us
    pallas_call x3, Pallas kernels, sampled_cols(): call(functools.partial(sample_kernel, count), 'sample', jax.ShapeDtypeStr...  12.3 us
    unnamed x84, local copies, waits for them, and re-layouts  12.1 us
    pallas_call x3, Pallas kernels, body(): call(mix_kernel, 'mix', (jax.ShapeDtypeStruct((tok_count, groups * width)...  11.9 us
    ppermute x2, starting transfers between devices, token_rows(): tail = lax.ppermute(tail, 'chip', [(i, i + 1) for i in range(chips - 1)])  6.64 us
    pallas_call x2, Pallas kernels, token_rows(): call(functools.partial(stack_kernel, chips, len(pieces) // 2), 'stack_row...  6.12 us
  transfers between devices with their start and end apart: 43, of which 21 were waited for; matrix products, arithmetic and copies ran while one was open for 5% of the time, Pallas kernels for 24%

profile of v1, /device:TPU:0, one launch (start us, length us, event | category | flops | bytes accessed | tf_op | source)
XLA Modules:
  0.0 294.6 jit_solution(14429292023419185577)
XLA Ops:
  6.8 4.6 %sample.3.refs_0_ = bf16[512,1024]{1,0:T(8,128)(2,1)} custom-call(f32[4]{0:T(128)} %coef_ref.5, bf16[512,2048]{1,0:T(8,128)(2,1)} %mean_ref.3, bf16[4,512,2048]{2,1,0:T(8,128)(2,1)} %devs_ref.5), custom_call_target="tpu_custom_call" | custom-call | bytes 125829 | tf_op jit(solution)/shard_map/sample/pallas_call | solution.py:115
  20.2 21.4 %collective-permute-done.9.refs_1_ = bf16[256,2048]{1,0:T(8,128)(2,1)} collective-permute-done((bf16[256,2048]{1,0:T(8,128)(2,1)}, bf16[256,2048]{1,0:T(8,128)(2,1)}, u32[]{:S(2)}, u32[]{:S(2)}) %collective-permute-start.9) | collective-permute-done | bytes 1048608 | tf_op jit(solution)/shard_map/ppermute | solution.py:35
  43.4 5.3 %fusion = bf16[512,2,512]{2,1,0:T(2,128)(2,1)S(1)} fusion(bf16[512,2,512]{2,1,0:T(2,128)(2,1)S(1)} %copy-done.25, bf16[4,512,2,512]{3,2,1,0:T(2,128)(2,1)} %param.16, f32[]{:T(128)} %bitcast.13, f32[]{:T(128)} %bitcast.11, f32[]{:T(128)} %bitcast.9, f32[]{:T(128)} %bitcast.7), kind=kLoop, calls=%fused_computation.1 | loop fusion | flops 7340032 | bytes 6291472 | tf_op jit(solution)/shard_map/convert_element_type | solution.py:135
  54.7 3.8 %sample.4.refs_0_ = bf16[512,512]{1,0:T(8,128)(2,1)} custom-call(f32[4]{0:T(128)} %coef_ref.5, bf16[512,2048]{1,0:T(8,128)(2,1)} %mean_ref.3, bf16[4,512,2048]{2,1,0:T(8,128)(2,1)} %devs_ref.5), custom_call_target="tpu_custom_call" | custom-call | bytes 62914 | tf_op jit(solution)/shard_map/sample/pallas_call | solution.py:115
  58.5 8.5 %collective-permute-done.1.refs_0_ = bf16[128,2048]{1,0:T(8,128)(2,1)S(1)} collective-permute-done((bf16[128,2048]{1,0:T(8,128)(2,1)}, bf16[128,2048]{1,0:T(8,128)(2,1)S(1)}, u32[]{:S(2)}, u32[]{:S(2)}) %collective-permute-start.1) | collective-permute-done | bytes 524320 | tf_op jit(solution)/shard_map/ppermute | solution.py:35
  70.4 11.8 %collective-permute-done.6 = bf16[128,2048]{1,0:T(8,128)(2,1)} collective-permute-done((bf16[128,2048]{1,0:T(8,128)(2,1)}, bf16[128,2048]{1,0:T(8,128)(2,1)}, u32[]{:S(2)}, u32[]{:S(2)}) %collective-permute-start.6) | collective-permute-done | bytes 524320 | tf_op jit(solution)/shard_map/ppermute | solution.py:35
  85.8 5.7 %collective-permute-done.4.refs_1_ = bf16[128,2048]{1,0:T(8,128)(2,1)S(1)} collective-permute-done((bf16[128,2048]{1,0:T(8,128)(2,1)S(1)}, bf16[128,2048]{1,0:T(8,128)(2,1)S(1)}, u32[]{:S(2)}, u32[]{:S(2)}) %collective-permute-start.4) | collective-permute-done | bytes 524320 | tf_op jit(solution)/shard_map/ppermute | solution.py:35
  98.4 3.6 %collective-permute-start.8 = (bf16[16,2048]{1,0:T(8,128)(2,1)}, bf16[16,2048]{1,0:T(8,128)(2,1)S(1)}, u32[]{:S(2)}, u32[]{:S(2)}) collective-permute-start(bf16[16,2048]{1,0:T(8,128)(2,1)} %get-tuple-element.76), channel_id=1, source_target_pairs={{0,4},{4,8},{8,12},{1,5},{5,9},{9,13},{2,6},{6,10},{10,14},{3,7},{... | collective-permute-start | bytes 196616 | tf_op jit(solution)/shard_map/ppermute | solution.py:90
  109.4 9.1 %multiply.4 = (bf16[2,272,1024]{2,1,0:T(8,128)(2,1)}, f32[2,272,1024]{2,1,0:T(8,128)}) custom-call(s32[7]{0:T(128)} %stack.59.at_ref, bf16[528,2048]{1,0:T(8,128)(2,1)} %append_rows.2.far_ref, bf16[528,2048]{1,0:T(8,128)(2,1)} %append_rows.3.own_ref, bf16[512,1024]{1,0:T(8,128)(2,1)} %sample.3.refs_0_, bf16[512,1024]{1,0:T(8,128)(2,1)} %collective-permute-done.2.refs_1_, ...), custom_call_target="tpu_custom_call" | custom-call | flops 88583696 | bytes 237240 | tf_op jit(solution)/shard_map/multiply/pallas_call | solution.py:191
  124.4 6.7 %collective-permute-done.14.refs_2_ = bf16[512,1152]{1,0:T(8,128)(2,1)S(1)} collective-permute-done((bf16[512,1152]{1,0:T(8,128)(2,1)S(1)}, bf16[512,1152]{1,0:T(8,128)(2,1)S(1)}, u32[]{:S(2)}, u32[]{:S(2)}) %collective-permute-start.14) | collective-permute-done | bytes 1179680 | tf_op jit(solution)/shard_map/ppermute | solution.py:35
  131.1 22.3 %collective-permute-done.21.refs_3_ = bf16[512,1152]{1,0:T(8,128)(2,1)} collective-permute-done((bf16[512,1152]{1,0:T(8,128)(2,1)S(1)}, bf16[512,1152]{1,0:T(8,128)(2,1)}, u32[]{:S(2)}, u32[]{:S(2)}) %collective-permute-start.21) | collective-permute-done | bytes 1179680 | tf_op jit(solution)/shard_map/ppermute | solution.py:35
  153.5 12.1 %multiply.5 = (bf16[2,272,1152]{2,1,0:T(8,128)(2,1)}, f32[2,272,1152]{2,1,0:T(8,128)}) custom-call(s32[7]{0:T(128)} %stack.59.at_ref, bf16[528,2048]{1,0:T(8,128)(2,1)} %append_rows.2.far_ref, bf16[528,2048]{1,0:T(8,128)(2,1)} %append_rows.3.own_ref, bf16[512,1152]{1,0:T(8,128)(2,1)} %pack.1.refs_0_, bf16[512,1152]{1,0:T(8,128)(2,1)} %copy-done.22, ...), custom_call_target="tpu_custom_call" | custom-call | flops 99656664 | bytes 256081 | tf_op jit(solution)/shard_map/multiply/pallas_call | solution.py:191
  168.3 12.7 %collective-permute-done.19.refs_2_ = bf16[512,512]{1,0:T(8,128)(2,1)S(1)} collective-permute-done((bf16[512,512]{1,0:T(8,128)(2,1)}, bf16[512,512]{1,0:T(8,128)(2,1)S(1)}, u32[]{:S(2)}, u32[]{:S(2)}) %collective-permute-start.19) | collective-permute-done | bytes 524320 | tf_op jit(solution)/shard_map/ppermute | solution.py:35
  181.1 3.9 %sample.5.refs_0_ = bf16[512,512]{1,0:T(8,128)(2,1)} custom-call(f32[4]{0:T(128)} %coef_ref.5, bf16[512,2048]{1,0:T(8,128)(2,1)} %mean_ref.3, bf16[4,512,2048]{2,1,0:T(8,128)(2,1)} %devs_ref.5), custom_call_target="tpu_custom_call" | custom-call | bytes 62914 | tf_op jit(solution)/shard_map/sample/pallas_call | solution.py:115
  188.3 3.9 %collective-permute-start.30 = (bf16[272,1152]{1,0:T(8,128)(2,1)S(1)}, bf16[272,1152]{1,0:T(8,128)(2,1)S(1)}, u32[]{:S(2)}, u32[]{:S(2)}) collective-permute-start(bf16[272,1152]{1,0:T(8,128)(2,1)S(1)} %relay.5), channel_id=1, source_target_pairs={{0,16},{16,0},{1,17},{17,1},{2,18},{18,2},{3,19},{19,3},{4,20},{20... | collective-permute-start | bytes 1880072 | tf_op jit(solution)/shard_map/ppermute | solution.py:35
  192.2 3.7 %collective-permute-done.20.refs_3_ = bf16[512,512]{1,0:T(8,128)(2,1)} collective-permute-done((bf16[512,512]{1,0:T(8,128)(2,1)S(1)}, bf16[512,512]{1,0:T(8,128)(2,1)}, u32[]{:S(2)}, u32[]{:S(2)}) %collective-permute-start.20) | collective-permute-done | bytes 524320 | tf_op jit(solution)/shard_map/ppermute | solution.py:35
  195.9 6.2 %multiply.6 = (bf16[2,272,512]{2,1,0:T(8,128)(2,1)}, f32[2,272,512]{2,1,0:T(8,128)}) custom-call(s32[7]{0:T(128)} %stack.59.at_ref, bf16[528,2048]{1,0:T(8,128)(2,1)} %append_rows.2.far_ref, bf16[528,2048]{1,0:T(8,128)(2,1)} %append_rows.3.own_ref, bf16[512,512]{1,0:T(8,128)(2,1)} %sample.4.refs_0_, bf16[512,512]{1,0:T(8,128)(2,1)} %collective-permute-done.18.refs_1_, ...), custom_call_target="tpu_custom_call" | custom-call | flops 44291848 | bytes 161873 | tf_op jit(solution)/shard_map/multiply/pallas_call | solution.py:191
  209.0 3.8 %collective-permute-start.29 = (bf16[272,1024]{1,0:T(8,128)(2,1)S(1)}, bf16[272,1024]{1,0:T(8,128)(2,1)}, u32[]{:S(2)}, u32[]{:S(2)}) collective-permute-start(bf16[272,1024]{1,0:T(8,128)(2,1)S(1)} %copy-done.11), channel_id=1, source_target_pairs={{0,16},{16,0},{1,17},{17,1},{2,18},{18,2},{3,19},{19,3},{4,20},{20... | collective-permute-start | bytes 1671176 | tf_op jit(solution)/shard_map/ppermute | solution.py:35
  217.0 10.8 %collective-permute-done.17.refs_3_ = bf16[512,512]{1,0:T(8,128)(2,1)} collective-permute-done((bf16[512,512]{1,0:T(8,128)(2,1)}, bf16[512,512]{1,0:T(8,128)(2,1)}, u32[]{:S(2)}, u32[]{:S(2)}) %collective-permute-start.17) | collective-permute-done | bytes 524320 | tf_op jit(solution)/shard_map/ppermute | solution.py:35
  227.8 6.3 %multiply.7 = (bf16[2,272,512]{2,1,0:T(8,128)(2,1)}, f32[2,272,512]{2,1,0:T(8,128)}) custom-call(s32[7]{0:T(128)} %stack.59.at_ref, bf16[528,2048]{1,0:T(8,128)(2,1)} %append_rows.2.far_ref, bf16[528,2048]{1,0:T(8,128)(2,1)} %append_rows.3.own_ref, bf16[512,512]{1,0:T(8,128)(2,1)} %sample.5.refs_0_, bf16[512,512]{1,0:T(8,128)(2,1)} %collective-permute-done.15.refs_1_, ...), custom_call_target="tpu_custom_call" | custom-call | flops 44291848 | bytes 161873 | tf_op jit(solution)/shard_map/multiply/pallas_call | solution.py:191
  234.2 4.0 %collective-permute-done.30.got_f = bf16[272,1152]{1,0:T(8,128)(2,1)S(1)} collective-permute-done((bf16[272,1152]{1,0:T(8,128)(2,1)S(1)}, bf16[272,1152]{1,0:T(8,128)(2,1)S(1)}, u32[]{:S(2)}, u32[]{:S(2)}) %collective-permute-start.30) | collective-permute-done | bytes 626720 | tf_op jit(solution)/shard_map/ppermute | solution.py:35
  239.0 4.1 %state_proj.1 = (bf16[256,1024]{1,0:T(8,128)(2,1)}, f32[256,128]{1,0:T(8,128)}) custom-call(f32[2,272,1152]{2,1,0:T(8,128)} %get-tuple-element.88.kept_ref.kept, bf16[2,272,1152]{2,1,0:T(8,128)(2,1)} %collective-permute-done.24.got_ref.got_c, bf16[272,1152]{1,0:T(8,128)(2,1)} %copy-done.26, f32[4,1024]{1,0:T(4,128)} %bitcast.81), custom_call_target="tpu_custom_call" | custom-call | bytes 52428 | tf_op jit(solution)/shard_map/state_proj/pallas_call | solution.py:474
  250.2 4.9 %mix.3 = (f32[256,1024]{1,0:T(8,128)}, f32[1,128,1024]{2,1,0:T(8,128)}, f32[128,1024]{1,0:T(8,128)}, bf16[128,1024]{1,0:T(8,128)(2,1)}) custom-call(f32[2,272,1024]{2,1,0:T(8,128)} %get-tuple-element.82.kept_ref.kept, bf16[2,272,1024]{2,1,0:T(8,128)(2,1)} %copy-done.4, bf16[272,1024]{1,0:T(8,128)(2,1)} %collective-permute-done.29.got_f, f32[4,2048]{1,0:T(4,128)} %taps.5, ...), custom_call_target="tpu_custom_call" | custom-call | flops 5368709 | bytes 73400 | tf_op jit(solution)/shard_map/mix/pallas_call | solution.py:508
  267.3 5.8 %collective-permute-done.27.got_f = bf16[272,512]{1,0:T(8,128)(2,1)S(1)} collective-permute-done((bf16[272,512]{1,0:T(8,128)(2,1)S(1)}, bf16[272,512]{1,0:T(8,128)(2,1)S(1)}, u32[]{:S(2)}, u32[]{:S(2)}) %collective-permute-start.27) | collective-permute-done | bytes 278560 | tf_op jit(solution)/shard_map/ppermute | solution.py:35
  (199 shorter events, 106.6 us)
Async XLA Ops:
  3.8 37.8 %collective-permute-start.9 = (bf16[256,2048]{1,0:T(8,128)(2,1)}, bf16[256,2048]{1,0:T(8,128)(2,1)}, u32[]{:S(2)}, u32[]{:S(2)}) collective-permute-start(bf16[256,2048]{1,0:T(8,128)(2,1)} %get-tuple-element.78.refs_0_), channel_id=1, source_target_pairs={{0,1},{1,0},{2,3},{3,2},{4,5},{5,4},{6,7},{7,6},{8,9},{9,8},{10,11... | collective-permute-start | bytes 3145736 | tf_op jit(solution)/shard_map/ppermute | solution.py:35
  11.5 31.9 %collective-permute-start.3 = (bf16[512,1024]{1,0:T(8,128)(2,1)}, bf16[512,1024]{1,0:T(8,128)(2,1)}, u32[]{:S(2)}, u32[]{:S(2)}) collective-permute-start(bf16[512,1024]{1,0:T(8,128)(2,1)} %sample.3.refs_0_), channel_id=1, source_target_pairs={{0,8},{4,12},{8,0},{12,4},{1,9},{5,13},{9,1},{13,5},{2,10},{6,14},... | collective-permute-start | bytes 3145736 | tf_op jit(solution)/shard_map/ppermute | solution.py:35
  13.0 40.2 %collective-permute-start.2 = (bf16[512,1024]{1,0:T(8,128)(2,1)}, bf16[512,1024]{1,0:T(8,128)(2,1)}, u32[]{:S(2)}, u32[]{:S(2)}) collective-permute-start(bf16[512,1024]{1,0:T(8,128)(2,1)} %sample.3.refs_0_), channel_id=1, source_target_pairs={{0,4},{4,0},{8,12},{12,8},{1,5},{5,1},{9,13},{13,9},{2,6},{6,2},{1... | collective-permute-start | bytes 3145736 | tf_op jit(solution)/shard_map/ppermute | solution.py:35
  14.5 53.9 %collective-permute-start.10 = (bf16[256,2048]{1,0:T(8,128)(2,1)S(1)}, bf16[256,2048]{1,0:T(8,128)(2,1)}, u32[]{:S(2)}, u32[]{:S(2)}) collective-permute-start(bf16[256,2048]{1,0:T(8,128)(2,1)S(1)} %copy-done.24), channel_id=1, source_target_pairs={{0,2},{2,0},{1,3},{3,1},{4,6},{6,4},{5,7},{7,5},{8,10},{10,8},{9,1... | collective-permute-start | bytes 3145736 | tf_op jit(solution)/shard_map/ppermute | solution.py:35
  14.5 44.0 %collective-permute-start = (bf16[128,2048]{1,0:T(8,128)(2,1)}, bf16[128,2048]{1,0:T(8,128)(2,1)}, u32[]{:S(2)}, u32[]{:S(2)}) collective-permute-start(bf16[128,2048]{1,0:T(8,128)(2,1)} %get-tuple-element.71), channel_id=1, source_target_pairs={{0,16},{16,0},{1,17},{17,1},{2,18},{18,2},{3,19},{19,3},{4,20},{20... | collective-permute-start | bytes 1572872 | tf_op jit(solution)/shard_map/ppermute | solution.py:35
  41.6 25.5 %collective-permute-start.1 = (bf16[128,2048]{1,0:T(8,128)(2,1)}, bf16[128,2048]{1,0:T(8,128)(2,1)S(1)}, u32[]{:S(2)}, u32[]{:S(2)}) collective-permute-start(bf16[128,2048]{1,0:T(8,128)(2,1)} %get-tuple-element.72), channel_id=1, source_target_pairs={{0,16},{16,0},{1,17},{17,1},{2,18},{18,2},{3,19},{19,3},{4,20},{20... | collective-permute-start | bytes 1572872 | tf_op jit(solution)/shard_map/ppermute | solution.py:35
  43.4 38.8 %collective-permute-start.11 = (bf16[256,2048]{1,0:T(8,128)(2,1)}, bf16[256,2048]{1,0:T(8,128)(2,1)}, u32[]{:S(2)}, u32[]{:S(2)}) collective-permute-start(bf16[256,2048]{1,0:T(8,128)(2,1)} %collective-permute-done.9.refs_1_), channel_id=1, source_target_pairs={{0,2},{2,0},{1,3},{3,1},{4,6},{6,4},{5,7},{7,5},{8,10},{10,8},{9,1... | collective-permute-start | bytes 3145736 | tf_op jit(solution)/shard_map/ppermute | solution.py:35
  53.2 48.9 %collective-permute-start.13 = (bf16[512,1152]{1,0:T(8,128)(2,1)}, bf16[512,1152]{1,0:T(8,128)(2,1)S(1)}, u32[]{:S(2)}, u32[]{:S(2)}) collective-permute-start(bf16[512,1152]{1,0:T(8,128)(2,1)} %pack.1.refs_0_), channel_id=1, source_target_pairs={{0,4},{4,0},{8,12},{12,8},{1,5},{5,1},{9,13},{13,9},{2,6},{6,2},{1... | collective-permute-start | bytes 3538952 | tf_op jit(solution)/shard_map/ppermute | solution.py:35
  67.0 15.2 %collective-permute-start.6 = (bf16[128,2048]{1,0:T(8,128)(2,1)}, bf16[128,2048]{1,0:T(8,128)(2,1)}, u32[]{:S(2)}, u32[]{:S(2)}) collective-permute-start(bf16[128,2048]{1,0:T(8,128)(2,1)} %collective-permute-done), channel_id=1, source_target_pairs={{0,1},{1,0},{2,3},{3,2},{4,5},{5,4},{6,7},{7,6},{8,9},{9,8},{10,11... | collective-permute-start | bytes 1572872 | tf_op jit(solution)/shard_map/ppermute | solution.py:35
  67.0 42.3 %collective-permute-start.22 = (bf16[512,1024]{1,0:T(8,128)(2,1)}, bf16[512,1024]{1,0:T(8,128)(2,1)}, u32[]{:S(2)}, u32[]{:S(2)}) collective-permute-start(bf16[512,1024]{1,0:T(8,128)(2,1)} %collective-permute-done.3.refs_2_), channel_id=1, source_target_pairs={{0,4},{4,0},{8,12},{12,8},{1,5},{5,1},{9,13},{13,9},{2,6},{6,2},{1... | collective-permute-start | bytes 3145736 | tf_op jit(solution)/shard_map/ppermute | solution.py:35
  68.4 23.1 %collective-permute-start.4 = (bf16[128,2048]{1,0:T(8,128)(2,1)S(1)}, bf16[128,2048]{1,0:T(8,128)(2,1)S(1)}, u32[]{:S(2)}, u32[]{:S(2)}) collective-permute-start(bf16[128,2048]{1,0:T(8,128)(2,1)S(1)} %collective-permute-done.1.refs_0_), channel_id=1, source_target_pairs={{0,1},{1,0},{2,3},{3,2},{4,5},{5,4},{6,7},{7,6},{8,9},{9,8},{10,11... | collective-permute-start | bytes 1572872 | tf_op jit(solution)/shard_map/ppermute | solution.py:35
  102.0 29.2 %collective-permute-start.14 = (bf16[512,1152]{1,0:T(8,128)(2,1)S(1)}, bf16[512,1152]{1,0:T(8,128)(2,1)S(1)}, u32[]{:S(2)}, u32[]{:S(2)}) collective-permute-start(bf16[512,1152]{1,0:T(8,128)(2,1)S(1)} %copy-done.20), channel_id=1, source_target_pairs={{0,8},{4,12},{8,0},{12,4},{1,9},{5,13},{9,1},{13,5},{2,10},{6,14},... | collective-permute-start | bytes 3538952 | tf_op jit(solution)/shard_map/ppermute | solution.py:35
  102.1 51.4 %collective-permute-start.21 = (bf16[512,1152]{1,0:T(8,128)(2,1)S(1)}, bf16[512,1152]{1,0:T(8,128)(2,1)}, u32[]{:S(2)}, u32[]{:S(2)}) collective-permute-start(bf16[512,1152]{1,0:T(8,128)(2,1)S(1)} %collective-permute-done.13.refs_1_), channel_id=1, source_target_pairs={{0,8},{4,12},{8,0},{12,4},{1,9},{5,13},{9,1},{13,5},{2,10},{6,14},... | collective-permute-start | bytes 3538952 | tf_op jit(solution)/shard_map/ppermute | solution.py:35
  165.5 21.3 %collective-permute-start.24 = (bf16[2,272,1152]{2,1,0:T(8,128)(2,1)}, bf16[2,272,1152]{2,1,0:T(8,128)(2,1)}, u32[]{:S(2)}, u32[]{:S(2)}) collective-permute-start(bf16[2,272,1152]{2,1,0:T(8,128)(2,1)} %get-tuple-element.89), channel_id=1, source_target_pairs={{0,2},{2,0},{1,3},{3,1},{4,6},{6,4},{5,7},{7,5},{8,10},{10,8},{9,1... | collective-permute-start | bytes 3760136 | tf_op jit(solution)/shard_map/ppermute | solution.py:35
  165.6 15.4 %collective-permute-start.19 = (bf16[512,512]{1,0:T(8,128)(2,1)}, bf16[512,512]{1,0:T(8,128)(2,1)S(1)}, u32[]{:S(2)}, u32[]{:S(2)}) collective-permute-start(bf16[512,512]{1,0:T(8,128)(2,1)} %sample.4.refs_0_), channel_id=1, source_target_pairs={{0,8},{4,12},{8,0},{12,4},{1,9},{5,13},{9,1},{13,5},{2,10},{6,14},... | collective-permute-start | bytes 1572872 | tf_op jit(solution)/shard_map/ppermute | solution.py:35
  168.3 23.9 %collective-permute-start.18 = (bf16[512,512]{1,0:T(8,128)(2,1)}, bf16[512,512]{1,0:T(8,128)(2,1)}, u32[]{:S(2)}, u32[]{:S(2)}) collective-permute-start(bf16[512,512]{1,0:T(8,128)(2,1)} %sample.4.refs_0_), channel_id=1, source_target_pairs={{0,4},{4,0},{8,12},{12,8},{1,5},{5,1},{9,13},{13,9},{2,6},{6,2},{1... | collective-permute-start | bytes 1572872 | tf_op jit(solution)/shard_map/ppermute | solution.py:35
  181.0 14.9 %collective-permute-start.20 = (bf16[512,512]{1,0:T(8,128)(2,1)S(1)}, bf16[512,512]{1,0:T(8,128)(2,1)}, u32[]{:S(2)}, u32[]{:S(2)}) collective-permute-start(bf16[512,512]{1,0:T(8,128)(2,1)S(1)} %collective-permute-done.19.refs_2_), channel_id=1, source_target_pairs={{0,4},{4,0},{8,12},{12,8},{1,5},{5,1},{9,13},{13,9},{2,6},{6,2},{1... | collective-permute-start | bytes 1572872 | tf_op jit(solution)/shard_map/ppermute | solution.py:35
  185.0 21.1 %collective-permute-start.15 = (bf16[512,512]{1,0:T(8,128)(2,1)}, bf16[512,512]{1,0:T(8,128)(2,1)}, u32[]{:S(2)}, u32[]{:S(2)}) collective-permute-start(bf16[512,512]{1,0:T(8,128)(2,1)} %sample.5.refs_0_), channel_id=1, source_target_pairs={{0,4},{4,0},{8,12},{12,8},{1,5},{5,1},{9,13},{13,9},{2,6},{6,2},{1... | collective-permute-start | bytes 1572872 | tf_op jit(solution)/shard_map/ppermute | solution.py:35
  188.3 49.9 %collective-permute-start.30 = (bf16[272,1152]{1,0:T(8,128)(2,1)S(1)}, bf16[272,1152]{1,0:T(8,128)(2,1)S(1)}, u32[]{:S(2)}, u32[]{:S(2)}) collective-permute-start(bf16[272,1152]{1,0:T(8,128)(2,1)S(1)} %relay.5), channel_id=1, source_target_pairs={{0,16},{16,0},{1,17},{17,1},{2,18},{18,2},{3,19},{19,3},{4,20},{20... | collective-permute-start | bytes 1880072 | tf_op jit(solution)/shard_map/ppermute | solution.py:35
  202.1 14.9 %collective-permute-start.16 = (bf16[512,512]{1,0:T(8,128)(2,1)S(1)}, bf16[512,512]{1,0:T(8,128)(2,1)}, u32[]{:S(2)}, u32[]{:S(2)}) collective-permute-start(bf16[512,512]{1,0:T(8,128)(2,1)S(1)} %copy-done.21), channel_id=1, source_target_pairs={{0,8},{4,12},{8,0},{12,4},{1,9},{5,13},{9,1},{13,5},{2,10},{6,14},... | collective-permute-start | bytes 1572872 | tf_op jit(solution)/shard_map/ppermute | solution.py:35
  206.1 21.7 %collective-permute-start.17 = (bf16[512,512]{1,0:T(8,128)(2,1)}, bf16[512,512]{1,0:T(8,128)(2,1)}, u32[]{:S(2)}, u32[]{:S(2)}) collective-permute-start(bf16[512,512]{1,0:T(8,128)(2,1)} %collective-permute-done.15.refs_1_), channel_id=1, source_target_pairs={{0,8},{4,12},{8,0},{12,4},{1,9},{5,13},{9,1},{13,5},{2,10},{6,14},... | collective-permute-start | bytes 1572872 | tf_op jit(solution)/shard_map/ppermute | solution.py:35
  209.0 41.2 %collective-permute-start.29 = (bf16[272,1024]{1,0:T(8,128)(2,1)S(1)}, bf16[272,1024]{1,0:T(8,128)(2,1)}, u32[]{:S(2)}, u32[]{:S(2)}) collective-permute-start(bf16[272,1024]{1,0:T(8,128)(2,1)S(1)} %copy-done.11), channel_id=1, source_target_pairs={{0,16},{16,0},{1,17},{17,1},{2,18},{18,2},{3,19},{19,3},{4,20},{20... | collective-permute-start | bytes 1671176 | tf_op jit(solution)/shard_map/ppermute | solution.py:35
  214.4 49.3 %collective-permute-start.28 = (bf16[272,512]{1,0:T(8,128)(2,1)S(1)}, bf16[272,512]{1,0:T(8,128)(2,1)}, u32[]{:S(2)}, u32[]{:S(2)}) collective-permute-start(bf16[272,512]{1,0:T(8,128)(2,1)S(1)} %relay.6), channel_id=1, source_target_pairs={{0,16},{16,0},{1,17},{17,1},{2,18},{18,2},{3,19},{19,3},{4,20},{20... | collective-permute-start | bytes 835592 | tf_op jit(solution)/shard_map/ppermute | solution.py:35
  234.2 26.2 %collective-permute-start.26 = (bf16[2,272,512]{2,1,0:T(8,128)(2,1)}, bf16[2,272,512]{2,1,0:T(8,128)(2,1)S(1)}, u32[]{:S(2)}, u32[]{:S(2)}) collective-permute-start(bf16[2,272,512]{2,1,0:T(8,128)(2,1)} %get-tuple-element.101), channel_id=1, source_target_pairs={{0,2},{2,0},{1,3},{3,1},{4,6},{6,4},{5,7},{7,5},{8,10},{10,8},{9,1... | collective-permute-start | bytes 1671176 | tf_op jit(solution)/shard_map/ppermute | solution.py:35
  (59 other events, 524.6 us)

commit v2 on v1

--- a/solution.py
+++ b/solution.py
@@ -20,13 +20,13 @@
 VMEM = pl.BlockSpec(memory_space=pltpu.VMEM)
 
 
-def call(kernel, name, out_shape, flops=0, moved=0, small=False, **settings):
+def call(kernel, name, out_shape, flops=0, moved=0, vmem=60, **settings):
     return pl.pallas_call(
         kernel,
         out_shape=out_shape,
         name=name,
         cost_estimate=pl.CostEstimate(flops=flops // 50, bytes_accessed=moved // 50, transcendentals=0),
-        compiler_params=pltpu.CompilerParams(vmem_limit_bytes=(12 if small else 60) * 1024 * 1024),
+        compiler_params=pltpu.CompilerParams(vmem_limit_bytes=vmem * 1024 * 1024),
         **settings,
     )
 
@@ -35,70 +35,44 @@
     return lax.ppermute(part, axis, [(i, i ^ by) for i in range(lax.axis_size(axis))])
 
 
-def cut_kernel(chips, at_ref, tokens_ref, own_ref, far_kept, far_sent):
-    depth = far_kept.shape[1] // chips
-    rows = far_kept.shape[0]
+def cut_kernel(chips, at_ref, tokens_ref, far_ref, own_ref):
+    depth = far_ref.shape[1] // chips
+    rows = tokens_ref.shape[0]
     f_at, c_at = at_ref[0], at_ref[1]
     for i in range(chips):
-        cols = slice(i * depth, (i + 1) * depth)
-
-        def taken(f, c):
-            start = pl.multiple_of(((f * chips + at_ref[3 + i]) * 2 + c) * depth, depth)
-            return tokens_ref[:, pl.ds(start, depth)]
-
-        far_sent[:, cols] = taken(1 - f_at, 1 - c_at)
-        far_kept[:, cols] = taken(1 - f_at, c_at)
-        own_ref[:rows, cols] = taken(f_at, c_at)
-        own_ref[rows:, cols] = taken(f_at, 1 - c_at)
-
-
-def stack_kernel(chips, shares, at_ref, *refs):
-    pieces, (rows_ref, tail_ref) = refs[:-2], refs[-2:]
-    count = pieces[0].shape[0]
-    half = shares * count
-    depth = tail_ref.shape[1] // chips
-    for at in range(2):
-        for share in range(shares):
-            place = (at_ref[2] if share == 0 else 1 - at_ref[2]) if shares == 2 else 0
-            start = pl.multiple_of(at * half + place * count, count)
-            rows_ref[pl.ds(start, count), :] = pieces[at * shares + share][...]
-    last = pl.multiple_of((2 - at_ref[1]) * half - RIM, RIM)
-    for i in range(chips):
-        start = pl.multiple_of(at_ref[3 + i] * depth, depth)
-        tail_ref[:, pl.ds(start, depth)] = rows_ref[pl.ds(last, RIM), i * depth : (i + 1) * depth]
-
-
-def append_kernel(chips, at_ref, tail_ref, rows_ref, out_ref):
-    depth = tail_ref.shape[1] // chips
-    for i in range(chips):
-        start = pl.multiple_of(at_ref[3 + i] * depth, depth)
-        out_ref[:, i * depth : (i + 1) * depth] = tail_ref[:, pl.ds(start, depth)]
-
-
-def token_rows(at, chips, pieces, specs):
-    count, depth = specs[0].block_shape
-    rows = len(pieces) * count + RIM
-    rows_ext, tail = call(
-        functools.partial(stack_kernel, chips, len(pieces) // 2),
+        for out, f in ((far_ref, 1 - f_at), (own_ref, f_at)):
+            for k, c in enumerate((c_at, 1 - c_at)):
+                start = pl.multiple_of(((f * chips + at_ref[3 + i]) * 2 + c) * depth, depth)
+                out[k * rows : (k + 1) * rows, i * depth : (i + 1) * depth] = tokens_ref[:, pl.ds(start, depth)]
+
+
+def stack_kernel(at_ref, kept, kept_t, got, got_t, rows_ref):
+    count = kept.shape[0]
+    mine = pl.multiple_of(at_ref[2] * count, count)
+    other = pl.multiple_of((1 - at_ref[2]) * count, count)
+    rows_ref[pl.ds(mine, count), :] = kept[...]
+    rows_ref[pl.ds(other, count), :] = kept_t[...]
+    rows_ref[pl.ds(2 * count + mine, count), :] = got[...]
+    rows_ref[pl.ds(2 * count + other, count), :] = got_t[...]
+
+
+def token_rows(at, cut, cut_t):
+    share, depth = cut.shape[0] // 2, cut.shape[1]
+    if cut_t is None:
+        parts = (cut[:share], swapped(cut[share:], "core"))
+        return jnp.concatenate([lax.all_gather(a, "tp", axis=0, tiled=True) for a in parts], axis=0)
+    low = pl.BlockSpec((share, depth), lambda i: (0, 0))
+    high = pl.BlockSpec((share, depth), lambda i: (1, 0))
+    return call(
+        stack_kernel,
         "stack_rows",
-        (jax.ShapeDtypeStruct((rows, depth), BF16), jax.ShapeDtypeStruct((RIM, depth), BF16)),
-        moved=4 * rows * depth,
+        jax.ShapeDtypeStruct((4 * share, depth), BF16),
+        moved=16 * share * depth,
+        vmem=40,
         grid=(1,),
-        in_specs=[SMEM] + specs,
-        out_specs=[pl.BlockSpec((rows, depth), lambda i: (0, 0)), pl.BlockSpec((RIM, depth), lambda i: (0, 0))],
-    )(at, *pieces)
-    tail = lax.ppermute(tail, "chip", [(i, i + 1) for i in range(chips - 1)])
-    last = rows // RIM - 1
-    return call(
-        functools.partial(append_kernel, chips),
-        "append_rows",
-        jax.ShapeDtypeStruct((rows, depth), BF16),
-        moved=4 * RIM * depth,
-        grid=(1,),
-        in_specs=[SMEM, pl.BlockSpec((RIM, depth), lambda i: (0, 0)), pl.BlockSpec(memory_space=pl.ANY)],
-        out_specs=pl.BlockSpec((RIM, depth), lambda i: (last, 0)),
-        input_output_aliases={2: 0},
-    )(at, tail, rows_ext)
+        in_specs=[SMEM, low, low, high, high],
+        out_specs=pl.BlockSpec((4 * share, depth), lambda i: (0, 0)),
+    )(at, cut, cut_t, swapped(cut, "core"), swapped(cut_t, "core"))
 
 
 def sample_kernel(count, coef_ref, mean_ref, devs_ref, out_ref):
@@ -142,14 +116,13 @@
     out_ref[:, width : width + heads] = dt_ref[...]
 
 
-def swapped_both(weight):
-    return swapped(weight, "chip", 1), swapped(weight, "chip", 2)
-
-
-def gathered(weight, both, by_x):
-    if both is None:
-        return [lax.all_gather(weight, "chip", axis=0, tiled=True)]
-    return [weight, both[0], both[1], swapped(both[1], "chip", 1) if by_x else swapped(both[0], "chip", 2)]
+def gathered(weight):
+    if lax.axis_size("chip") != 4:
+        return [lax.all_gather(weight, "chip", axis=0, tiled=True)], ()
+    half = weight.shape[0] // 2
+    by_x, by_y = swapped(weight, "chip", 1), swapped(weight, "chip", 2)
+    halves = (by_y[:half], by_x[half:])
+    return [weight, by_x, by_y, swapped(halves[0], "chip", 1), swapped(halves[1], "chip", 2)], halves
 
 
 def coded(part, heads):
@@ -161,39 +134,41 @@
     return part + pltpu.roll(part, LANES - heads, 1)
 
 
-def multiply_kernel(heads, with_steps, pieces, at_ref, far_ref, own_ref, *refs):
+def multiply_kernel(heads, with_steps, chips, pieces, at_ref, far_ref, own_ref, *refs):
     weights, (sent_ref, kept_ref) = refs[:pieces], refs[pieces:]
-    second = at_ref[1] == 1
+    half = far_ref.shape[0] // 2
+    if pieces == 1:
+        depth = far_ref.shape[1] // chips
+        parts = [weights[0].at[pl.ds(pl.multiple_of(at_ref[3 + i] * depth, depth), depth), :] for i in range(chips)]
+    else:
+        parts = weights
     for k, rows_ref in enumerate((far_ref, own_ref)):
         at = 0
         total = None
-        for weight in weights:
-            depth = weight.shape[0]
-            term = jnp.dot(rows_ref[:, at : at + depth], weight[...], preferred_element_type=F32)
+        for part in parts:
+            depth = part.shape[0]
+            term = jnp.dot(rows_ref[:, at : at + depth], part[...], preferred_element_type=F32)
             total = term if total is None else total + term
             at += depth
-        half = (total.shape[0] - RIM) // 2
-        before = total[2 * half :]
-        kept_ref[k, :half, :] = total[:half]
-        kept_ref[k, half:, :] = jnp.where(second, total[2 * half - RIM : 2 * half], before)
-        sent_ref[k, :half, :] = total[half : 2 * half].astype(BF16)
-        sent_ref[k, half:, :] = jnp.where(second, before, total[half - RIM : half]).astype(BF16)
+        kept_ref[k] = total[:half]
+        sent_ref[k] = total[half:].astype(BF16)
         if with_steps:
             @pl.when(pl.program_id(0) == pl.num_programs(0) - 1)
             def _():
-                sent_ref[k, :half, -LANES:] = coded(total[half : 2 * half, -LANES:], heads).astype(BF16)
+                sent_ref[k, :, -LANES:] = coded(total[half:, -LANES:], heads).astype(BF16)
 
 
 def multiplied(at, rows_far, rows_own, weights, heads, with_steps, first, width):
     tile = next(t for t in (256, 384, 128) if width % t == 0)
     col = first // tile
-    half = (rows_far.shape[0] - RIM) // 2 + RIM
+    half = rows_far.shape[0] // 2
     return call(
-        functools.partial(multiply_kernel, heads, with_steps, len(weights)),
+        functools.partial(multiply_kernel, heads, with_steps, lax.axis_size("chip"), len(weights)),
         "multiply",
         (jax.ShapeDtypeStruct((2, half, width), BF16), jax.ShapeDtypeStruct((2, half, width), F32)),
         flops=4 * rows_far.size * width,
         moved=4 * rows_far.size + 2 * rows_far.shape[1] * width + 12 * half * width,
+        vmem=40,
         grid=(width // tile,),
         in_specs=[SMEM]
         + [pl.BlockSpec(rows_far.shape, lambda i: (0, 0))] * 2
@@ -218,19 +193,38 @@
         "relay",
         jax.ShapeDtypeStruct((rows, width), BF16),
         moved=8 * rows * width,
-        small=True,
+        vmem=12,
         grid=(1,),
         in_specs=[pl.BlockSpec((1, rows, width), lambda i: (0, 0, 0))] * 2,
         out_specs=pl.BlockSpec((rows, width), lambda i: (0, 0)),
     )(kept, got)
 
 
-def convolved(width, kept, got_c, got_f, taps, padded):
+def rim_kernel(kept, got_c, got_f, rim_ref):
+    rim_ref[...] = (kept[0] + got_c[0].astype(F32) + got_f[...].astype(F32)).astype(BF16)
+
+
+def rows_before(kept, got_c, got_f):
+    rows, width = got_f.shape
+    at = rows // RIM - 1
+    rim = call(
+        rim_kernel,
+        "rim",
+        jax.ShapeDtypeStruct((RIM, width), BF16),
+        moved=10 * RIM * width,
+        vmem=12,
+        grid=(1,),
+        in_specs=[pl.BlockSpec((1, RIM, width), lambda i: (1, at, 0))] * 2 + [pl.BlockSpec((RIM, width), lambda i: (at, 0))],
+        out_specs=pl.BlockSpec((RIM, width), lambda i: (0, 0)),
+    )(kept, got_c, got_f)
+    return lax.ppermute(rim, SEQ, [(i, i + 1) for i in range(lax.axis_size(SEQ) - 1)])
+
+
+def convolved(width, kept, got_c, got_f, rim, taps, padded):
     count = padded.shape[0] - 8
     proj = kept[0, :, :width] + got_c[0, :, :width].astype(F32) + got_f[:, :width].astype(F32)
-    proj = proj.astype(BF16).astype(F32)
-    padded[8:, :] = proj[:count]
-    padded[:8, :] = proj[count + RIM - 8 :]
+    padded[8:, :] = proj.astype(BF16).astype(F32)
+    padded[:8, :] = rim[:, :width].astype(F32)[RIM - 8 :]
     first = 8 - (CONV - 1)
     conv_sum = taps[0:1, :] * padded[first : first + count, :]
     for offset in range(1, CONV):
@@ -238,13 +232,13 @@
     return (conv_sum * jax.nn.sigmoid(conv_sum)).astype(BF16)
 
 
-def state_proj_kernel(heads, kept, got_c, got_f, taps, out_ref, logits_ref, padded):
+def state_proj_kernel(heads, kept, got_c, got_f, rim, taps, out_ref, logits_ref, padded):
     count, width = out_ref.shape
-    out_ref[...] = convolved(width, kept, got_c, got_f, taps, padded)
+    out_ref[...] = convolved(width, kept, got_c, got_f, rim, taps, padded)
     logits_ref[...] = (
-        kept[0, :count, width:]
-        + decoded(got_c[0, :count, width:].astype(F32), heads)
-        + decoded(got_f[:count, width:].astype(F32), heads)
+        kept[0, :, width:]
+        + decoded(got_c[0, :, width:].astype(F32), heads)
+        + decoded(got_f[:, width:].astype(F32), heads)
     )
 
 
@@ -259,10 +253,10 @@
 
 
 def mix_kernel(
-    kept, got_c, got_f, taps, keys, reads, cum_g, steps_g, cum_t, steps_t, skip, y_ref, early_ref, total_ref, sent_ref, padded
+    kept, got_c, got_f, rim, taps, keys, reads, cum_g, steps_g, cum_t, steps_t, skip, y_ref, early_ref, total_ref, sent_ref, padded
 ):
     width = y_ref.shape[1]
-    values = convolved(width, kept, got_c, got_f, taps, padded)
+    values = convolved(width, kept, got_c, got_f, rim, taps, padded)
     cum, steps = cum_g[0], steps_g[0]
     heads = cum.shape[1]
     row = lax.broadcasted_iota(jnp.int32, (SPAN, SPAN), 0)
@@ -358,7 +352,7 @@
         ),
         flops=6 * total.size,
         moved=20 * total.size,
-        small=True,
+        vmem=12,
         grid=(first[1],),
         in_specs=[pl.BlockSpec((scales.shape[0], wide), lambda i: (0, first[0] + i))]
         + [block] * (2 if before is None else 3),
@@ -395,80 +389,65 @@
     early_groups = max(1, groups_here // 2)
     late = list(range(early_groups, groups_here))
 
-    plane = chips == 4
-    place = lax.axis_index("chip") if plane else 0
+    place = lax.axis_index("chip") if chips == 4 else 0
     at = jnp.stack([lax.axis_index(a) for a in ("fsdp", "core", "tp")] + [place ^ i for i in range(chips)]).astype(jnp.int32)
-    share, depth = tokens.shape[0], chips * rows_k
-    own, far_kept, far_sent = call(
+    cut = jax.ShapeDtypeStruct((2 * tokens.shape[0], chips * rows_k), BF16)
+    far, own = call(
         functools.partial(cut_kernel, chips),
         "cut_tokens",
-        (jax.ShapeDtypeStruct((2 * share, depth), BF16),) + (jax.ShapeDtypeStruct((share, depth), BF16),) * 2,
+        (cut,) * 2,
         moved=4 * tokens.size,
         in_specs=[SMEM, VMEM],
-        out_specs=[VMEM] * 3,
+        out_specs=[VMEM] * 2,
     )(at, tokens)
-    far_sent, far_kept = swapped(far_sent, "fsdp"), swapped(far_kept, "fsdp")
-
-    weights = [sampled_cols(proj_mean, proj_devs, swag_coef, 0, early_groups * width)]
-    both = [swapped_both(weights[0]) if plane else None]
+    far = swapped(far, "fsdp")
+
+    gather = lambda a: [lax.all_gather(a, "chip", axis=0, tiled=True)]
+    weights_early = sampled_cols(proj_mean, proj_devs, swag_coef, 0, early_groups * width)
+    pieces_early = gather(weights_early)
     weight_bc = sampled(bc_mean, bc_devs, swag_coef).reshape(rows_k, width_bc)
-    weights.append(
-        call(
-            pack_kernel,
-            "pack",
-            jax.ShapeDtypeStruct((rows_k, width_bc + LANES), BF16),
-            moved=4 * weight_bc.size,
-            in_specs=[VMEM] * 2,
-            out_specs=VMEM,
-        )(weight_bc, dt_weight)
-    )
-    both.append(swapped_both(weights[1]) if plane else None)
-    for j, g in enumerate(late):
-        mean_part = proj_mean
-        if plane and j < 2:
-            mean_part = after(proj_mean, (both[j], weights[-1]))
-        weights.append(sampled_cols(mean_part, proj_devs, swag_coef, g, width))
-        both.append(swapped_both(weights[-1]) if plane else None)
-        if j == 0:
-            far_sent, far_kept = after((far_sent, far_kept), weights[-1])
-    pieces = [gathered(w, b, j % 2 == 0) for j, (w, b) in enumerate(zip(weights, both))]
-
-    if lax.axis_size("tp") == 2:
-        low = pl.BlockSpec((share, depth), lambda i: (0, 0))
-        high = pl.BlockSpec((share, depth), lambda i: (1, 0))
-        own_t = swapped(own, "tp")
-        own_pieces = (own, own_t, swapped(own, "core"), swapped(own_t, "core"))
-        rows_own = token_rows(at, chips, own_pieces, [low, low, high, high])
-        sent_t = swapped(far_sent, "tp")
-        far_pieces = (far_kept, swapped(far_kept, "tp"), swapped(far_sent, "core"), swapped(sent_t, "core"))
-        rows_far = token_rows(at, chips, far_pieces, [low] * 4)
-    else:
-        whole = lambda a: lax.all_gather(a, "tp", axis=0, tiled=True)
-        spec = pl.BlockSpec((share * lax.axis_size("tp"), depth), lambda i: (0, 0))
-        rows_own = token_rows(at, chips, (whole(own[:share]), whole(swapped(own[share:], "core"))), [spec] * 2)
-        rows_far = token_rows(at, chips, (whole(far_kept), whole(swapped(far_sent, "core"))), [spec] * 2)
-    tok_count = (rows_own.shape[0] - RIM) // 2
+    weight_bc = call(
+        pack_kernel,
+        "pack",
+        jax.ShapeDtypeStruct((rows_k, width_bc + LANES), BF16),
+        moved=4 * weight_bc.size,
+        in_specs=[VMEM] * 2,
+        out_specs=VMEM,
+    )(weight_bc, dt_weight)
+    pieces_bc, halves_bc = gathered(weight_bc)
+    chunks = [(0, early_groups, pieces_early, 0)]
+    if late:
+        weights_late = sampled_cols(proj_mean, proj_devs, swag_coef, early_groups // len(late), len(late) * width)
+        pieces_late = gather(weights_late)
+        chunks += [(g, 1, pieces_late, i * width) for i, g in enumerate(late)]
+        far = after(far, weights_late)
+
+    two_shares = lax.axis_size("tp") == 2
+    rows_own = token_rows(at, own, swapped(own, "tp") if two_shares else None)
+    far_t = swapped(far, "tp") if two_shares else None
+    far, far_t = after((far, far_t), (rows_own, halves_bc))
+    rows_far = token_rows(at, far, far_t)
+    tok_count = rows_own.shape[0] // 2
     blocks = tok_count // SPAN
 
-    def projected(pieces, with_steps, width):
-        sent, kept = multiplied(at, rows_far, rows_own, pieces, heads_here, with_steps, 0, width)
+    def projected(pieces, with_steps, first, width):
+        sent, kept = multiplied(at, rows_far, rows_own, pieces, heads_here, with_steps, first, width)
         got = swapped(sent, "core")
         back = relayed(kept, got, heads_here, with_steps)
         return (kept, got, swapped(back, "fsdp")), back
 
-    parts = []
-    back = None
-    for j, chunk in enumerate(pieces):
-        if back is not None:
-            chunk = after(chunk, back)
-        part, back = projected(chunk, j == 1, weights[j].shape[1])
+    part_bc, back = projected(pieces_bc, True, 0, width_bc + LANES)
+    parts = [part_bc]
+    for j, (_, groups, pieces, col) in enumerate(chunks):
+        earlier = (back, parts[j - 1][2]) if j else back
+        part, back = projected(after(pieces, earlier), False, col, groups * width)
         parts.append(part)
-    part_bc = parts.pop(1)
-    chunks = [(0, early_groups)] + [(g, 1) for g in late]
-
-    rows_ext = tok_count + RIM
-    specs_of = lambda width: [pl.BlockSpec((1, rows_ext, width), lambda i: (1, 0, i))] * 2 + [
-        pl.BlockSpec((rows_ext, width), lambda i: (0, i))
+    parts = [part + (rows_before(*part),) for part in parts]
+    part_bc = parts.pop(0)
+
+    specs_of = lambda width: [pl.BlockSpec((1, tok_count, width), lambda i: (1, 0, i))] * 2 + [
+        pl.BlockSpec((tok_count, width), lambda i: (0, i)),
+        pl.BlockSpec((RIM, width), lambda i: (0, i)),
     ]
     whole_of = lambda *shape: pl.BlockSpec(shape, lambda i: (0,) * len(shape))
     conv_out, logits = call(
@@ -494,7 +473,7 @@
 
     result = None
     last_total = None
-    for (first, groups), part in zip(chunks, parts):
+    for (first, groups, _, _), part in zip(chunks, parts):
         if last_total is not None:
             part = after(part, last_total)
         grid = (groups,)
@@ -541,7 +520,7 @@
             jax.ShapeDtypeStruct((tok_count, heads_here * P_SIZE), BF16),
             flops=2 * tok_count * N * width * groups,
             moved=10 * tok_count * width * groups,
-            small=True,
+            vmem=12,
             grid=grid,
             in_specs=specs,
             out_specs=cols_all(tok_count),

time: 296 us -> 305 us (1.030)
  local copies, waits for them, and re-layouts: 17.6 us -> 38.2 us
  Pallas kernels: 85.6 us -> 70 us
  between operations: 2.98 us -> 16.5 us
  starting transfers between devices: 49.2 us -> 36.3 us
    unnamed x84 -> x114, local copies, waits for them, and re-layouts: 12.1 us -> 28.9 us
    pallas_call x9 -> x11, Pallas kernels: 45.9 us -> 29.8 us  [the longest x4 23.2 us: multiplied(): call(functools.partial(multiply_kernel, heads, with_steps, lax.axis_size(...]
    ppermute x41 -> x31, starting transfers between devices: 42.5 us -> 28.7 us  [swapped(): lax.ppermute(part, axis, [(i, i ^ by) for i in range(lax.axis_size(axis))])]
    ppermute x41 -> x31, waiting for transfers between devices: 132 us -> 136 us  [swapped(): lax.ppermute(part, axis, [(i, i ^ by) for i in range(lax.axis_size(axis))])]
    pallas_call x3 -> x2, Pallas kernels: 12.3 us -> 9.26 us  [sampled_cols(): call(functools.partial(sample_kernel, count), 'sample', jax.ShapeDtypeStr...]
    ppermute x2 -> x4, starting transfers between devices: 6.64 us -> 7.52 us  [rows_before(): lax.ppermute(rim, SEQ, [(i, i + 1) for i in range(lax.axis_size(SEQ) - 1)])]
  transfers between devices with their start and end apart: 43 -> 37, of which waited for: 21 -> 16; matrix products, arithmetic and copies ran while one was open for 5% -> 6% of each run, Pallas kernels for 24% -> 19%
where the time goes in v2:
time: 305 us; the launch traced here: 303 us
  waiting for transfers between devices  136 us (45%)
  Pallas kernels  70 us (23%)
  local copies, waits for them, and re-layouts  38.2 us (13%)
  starting transfers between devices  36.3 us (12%)
  between operations  16.5 us (5%)
  other arithmetic  6.3 us (2%)
    ppermute x31, waiting for transfers between devices, swapped(): lax.ppermute(part, axis, [(i, i ^ by) for i in range(lax.axis_size(axis))])  136 us
    unnamed x114, local copies, waits for them, and re-layouts  28.9 us
    ppermute x31, starting transfers between devices, swapped(): lax.ppermute(part, axis, [(i, i ^ by) for i in range(lax.axis_size(axis))])  28.7 us
    pallas_call x4, Pallas kernels, multiplied(): call(functools.partial(multiply_kernel, heads, with_steps, lax.axis_size(...  23.2 us
    pallas_call x3, Pallas kernels, body(): call(mix_kernel, 'mix', (jax.ShapeDtypeStruct((tok_count, groups * width)...  11.9 us
    pallas_call x2, Pallas kernels, sampled_cols(): call(functools.partial(sample_kernel, count), 'sample', jax.ShapeDtypeStr...  9.26 us
    ppermute x4, starting transfers between devices, rows_before(): lax.ppermute(rim, SEQ, [(i, i + 1) for i in range(lax.axis_size(SEQ) - 1)])  7.52 us
  transfers between devices with their start and end apart: 37, of which 16 were waited for; matrix products, arithmetic and copies ran while one was open for 6% of the time, Pallas kernels for 19%

profile of v2, /device:TPU:0, one launch (start us, length us, event | category | flops | bytes accessed | tf_op | source)
XLA Modules:
  0.0 303.3 jit_solution(12588049885722769395)
XLA Ops:
  6.5 4.6 %sample.3 = bf16[512,1024]{1,0:T(8,128)(2,1)} custom-call(f32[4]{0:T(128)} %coef_ref.3, bf16[512,2048]{1,0:T(8,128)(2,1)} %mean_ref.3, bf16[4,512,2048]{2,1,0:T(8,128)(2,1)} %devs_ref.3), custom_call_target="tpu_custom_call" | custom-call | bytes 125829 | tf_op jit(solution)/shard_map/sample/pallas_call | solution.py:89
  11.2 4.6 %sample.2 = bf16[512,1024]{1,0:T(8,128)(2,1)} custom-call(f32[4]{0:T(128)} %coef_ref.3, bf16[512,2048]{1,0:T(8,128)(2,1)} %mean_ref.3, bf16[4,512,2048]{2,1,0:T(8,128)(2,1)} %devs_ref.3), custom_call_target="tpu_custom_call" | custom-call | bytes 125829 | tf_op jit(solution)/shard_map/sample/pallas_call | solution.py:89
  16.5 3.1 %cut_tokens.1 = (bf16[256,2048]{1,0:T(8,128)(2,1)}, bf16[256,2048]{1,0:T(8,128)(2,1)}) custom-call(s32[7]{0:T(128)} %stack.59.at_ref, bf16[128,8192]{1,0:T(8,128)(2,1)} %tokens_ref.1), custom_call_target="tpu_custom_call" | custom-call | bytes 83886 | tf_op jit(solution)/shard_map/cut_tokens/pallas_call | solution.py:395
  19.6 3.0 collective-permute-start.2
  28.4 5.3 %fusion = bf16[512,2,512]{2,1,0:T(2,128)(2,1)S(1)} fusion(bf16[512,2,512]{2,1,0:T(2,128)(2,1)S(1)} %copy-done.44, bf16[4,512,2,512]{3,2,1,0:T(2,128)(2,1)} %param.16, f32[]{:T(128)} %bitcast.13, f32[]{:T(128)} %bitcast.11, f32[]{:T(128)} %bitcast.9, f32[]{:T(128)} %bitcast.7), kind=kLoop, calls=%fused_computation.1 | loop fusion | flops 7340032 | bytes 6291472 | tf_op jit(solution)/shard_map/convert_element_type | solution.py:109
  41.2 29.7 %collective-permute-done.kept = bf16[256,2048]{1,0:T(8,128)(2,1)S(1)} collective-permute-done((bf16[256,2048]{1,0:T(8,128)(2,1)}, bf16[256,2048]{1,0:T(8,128)(2,1)S(1)}, u32[]{:S(2)}, u32[]{:S(2)}) %collective-permute-start) | collective-permute-done | bytes 1048608 | tf_op jit(solution)/shard_map/ppermute | solution.py:35
  71.4 16.6 %collective-permute-done.5.refs_2_ = bf16[512,1152]{1,0:T(8,128)(2,1)S(1)} collective-permute-done((bf16[512,1152]{1,0:T(8,128)(2,1)}, bf16[512,1152]{1,0:T(8,128)(2,1)S(1)}, u32[]{:S(2)}, u32[]{:S(2)}) %collective-permute-start.5) | collective-permute-done | bytes 1179680 | tf_op jit(solution)/shard_map/ppermute | solution.py:35
  91.2 5.2 %collective-permute-done.1.kept_t = bf16[256,2048]{1,0:T(8,128)(2,1)S(1)} collective-permute-done((bf16[256,2048]{1,0:T(8,128)(2,1)S(1)}, bf16[256,2048]{1,0:T(8,128)(2,1)S(1)}, u32[]{:S(2)}, u32[]{:S(2)}) %collective-permute-start.1) | collective-permute-done | bytes 1048608 | tf_op jit(solution)/shard_map/ppermute | solution.py:35
  101.3 21.9 %collective-permute-done.10.refs_4_ = bf16[256,1152]{1,0:T(8,128)(2,1)S(1)} collective-permute-done((bf16[256,1152]{1,0:T(8,128)(2,1)S(1)}, bf16[256,1152]{1,0:T(8,128)(2,1)S(1)}, u32[]{:S(2)}, u32[]{:S(2)}) %collective-permute-start.10) | collective-permute-done | bytes 589856 | tf_op jit(solution)/shard_map/ppermute | solution.py:35
  123.2 8.9 %multiply.4 = (bf16[2,256,1152]{2,1,0:T(8,128)(2,1)S(1)}, f32[2,256,1152]{2,1,0:T(8,128)S(1)}) custom-call(s32[7]{0:T(128)S(1)} %copy-done.43, bf16[512,2048]{1,0:T(8,128)(2,1)S(1)} %stack_rows.3.far_ref, bf16[512,2048]{1,0:T(8,128)(2,1)S(1)} %stack_rows.2.own_ref, bf16[512,1152]{1,0:T(8,128)(2,1)S(1)} %copy-done.20, ...), custom_call_target="tpu_custom_call" | custom-call | flops 96636768 | bytes 249036 | tf_op jit(solution)/shard_map/multiply/pallas_call | solution.py:165
  141.4 6.3 %multiply.5 = (bf16[2,256,1024]{2,1,0:T(8,128)(2,1)S(1)}, f32[2,256,1024]{2,1,0:T(8,128)S(1)}) custom-call(s32[7]{0:T(128)S(1)} %copy-done.43, bf16[512,2048]{1,0:T(8,128)(2,1)S(1)} %copy-done.1, bf16[512,2048]{1,0:T(8,128)(2,1)S(1)} %stack_rows.2.own_ref, bf16[2048,1024]{1,0:T(8,128)(2,1)S(1)} %copy-done.21), custom_call_target="tpu_custom_call" | custom-call | flops 85899344 | bytes 230686 | tf_op jit(solution)/shard_map/multiply/pallas_call | solution.py:165
  152.9 24.2 %collective-permute-done.13.got_f = bf16[256,1152]{1,0:T(8,128)(2,1)S(1)} collective-permute-done((bf16[256,1152]{1,0:T(8,128)(2,1)S(1)}, bf16[256,1152]{1,0:T(8,128)(2,1)S(1)}, u32[]{:S(2)}, u32[]{:S(2)}) %collective-permute-start.13) | collective-permute-done | bytes 589856 | tf_op jit(solution)/shard_map/ppermute | solution.py:35
  181.7 4.0 %multiply.6 = (bf16[2,256,512]{2,1,0:T(8,128)(2,1)}, f32[2,256,512]{2,1,0:T(8,128)S(1)}) custom-call(s32[7]{0:T(128)S(1)} %copy-done.43, bf16[512,2048]{1,0:T(8,128)(2,1)S(1)} %copy-done.2, bf16[512,2048]{1,0:T(8,128)(2,1)S(1)} %stack_rows.2.own_ref, bf16[2048,1024]{1,0:T(8,128)(2,1)S(1)} %copy-done.10), custom_call_target="tpu_custom_call" | custom-call | flops 42949672 | bytes 157286 | tf_op jit(solution)/shard_map/multiply/pallas_call | solution.py:165
  190.5 4.1 %state_proj.1 = (bf16[256,1024]{1,0:T(8,128)(2,1)}, f32[256,128]{1,0:T(8,128)}) custom-call(f32[2,256,1152]{2,1,0:T(8,128)} %copy-done.6, bf16[2,256,1152]{2,1,0:T(8,128)(2,1)} %copy-done.12, bf16[256,1152]{1,0:T(8,128)(2,1)} %copy-done.22, bf16[16,1152]{1,0:T(8,128)(2,1)} %copy-done.45, f32[4,1024]{1,0:T(4,128)} %bitcast.81), custom_call_target="tpu_custom_call" | custom-call | bytes 52428 | tf_op jit(solution)/shard_map/state_proj/pallas_call | solution.py:453
  198.3 14.2 %collective-permute-done.15.got_f = bf16[256,1024]{1,0:T(8,128)(2,1)} collective-permute-done((bf16[256,1024]{1,0:T(8,128)(2,1)}, bf16[256,1024]{1,0:T(8,128)(2,1)}, u32[]{:S(2)}, u32[]{:S(2)}) %collective-permute-start.15) | collective-permute-done | bytes 524320 | tf_op jit(solution)/shard_map/ppermute | solution.py:35
  216.2 4.0 %multiply.7 = (bf16[2,256,512]{2,1,0:T(8,128)(2,1)}, f32[2,256,512]{2,1,0:T(8,128)S(1)}) custom-call(s32[7]{0:T(128)S(1)} %copy-done.43, bf16[512,2048]{1,0:T(8,128)(2,1)S(1)} %copy-done.3, bf16[512,2048]{1,0:T(8,128)(2,1)S(1)} %stack_rows.2.own_ref, bf16[2048,1024]{1,0:T(8,128)(2,1)S(1)} %copy-done.11), custom_call_target="tpu_custom_call" | custom-call | flops 42949672 | bytes 157286 | tf_op jit(solution)/shard_map/multiply/pallas_call | solution.py:165
  233.0 4.9 %mix.3 = (f32[256,1024]{1,0:T(8,128)}, f32[1,128,1024]{2,1,0:T(8,128)}, f32[128,1024]{1,0:T(8,128)}, bf16[128,1024]{1,0:T(8,128)(2,1)}) custom-call(f32[2,256,1024]{2,1,0:T(8,128)} %copy-done.8, bf16[2,256,1024]{2,1,0:T(8,128)(2,1)} %copy-done.13, bf16[256,1024]{1,0:T(8,128)(2,1)} %collective-permute-done.15.got_f, bf16[16,1024]{1,0:T(8,128)(2,1)} %copy-done.46, ...), custom_call_target="tpu_custom_call" | custom-call | flops 5368709 | bytes 73400 | tf_op jit(solution)/shard_map/mix/pallas_call | solution.py:487
  238.9 2.9 collective-permute-start.25
  243.5 2.9 collective-permute-start.17
  251.1 9.8 %collective-permute-done.19.got_f = bf16[256,512]{1,0:T(8,128)(2,1)S(1)} collective-permute-done((bf16[256,512]{1,0:T(8,128)(2,1)S(1)}, bf16[256,512]{1,0:T(8,128)(2,1)S(1)}, u32[]{:S(2)}, u32[]{:S(2)}) %collective-permute-start.19) | collective-permute-done | bytes 262176 | tf_op jit(solution)/shard_map/ppermute | solution.py:35
  263.6 2.9 collective-permute-done.17.got_f
  269.8 3.5 %mix.4 = (f32[256,512]{1,0:T(8,128)}, f32[1,128,512]{2,1,0:T(8,128)}, f32[128,512]{1,0:T(8,128)}, bf16[128,512]{1,0:T(8,128)(2,1)}) custom-call(f32[2,256,512]{2,1,0:T(8,128)} %copy-done.15, bf16[2,256,512]{2,1,0:T(8,128)(2,1)} %collective-permute-done.14.got_ref.got_c, bf16[256,512]{1,0:T(8,128)(2,1)} %copy-done.29, bf16[16,512]{1,0:T(8,128)(2,1)} %copy-done.50, ...), custom_call_target="tpu_custom_call" | custom-call | flops 2684354 | bytes 36700 | tf_op jit(solution)/shard_map/mix/pallas_call | solution.py:487
  274.2 3.5 %mix.5 = (f32[256,512]{1,0:T(8,128)}, f32[1,128,512]{2,1,0:T(8,128)}, f32[128,512]{1,0:T(8,128)}, bf16[128,512]{1,0:T(8,128)(2,1)}) custom-call(f32[2,256,512]{2,1,0:T(8,128)} %copy-done.18, bf16[2,256,512]{2,1,0:T(8,128)(2,1)} %collective-permute-done.16.got_ref.got_c, bf16[256,512]{1,0:T(8,128)(2,1)} %copy-done.28, bf16[16,512]{1,0:T(8,128)(2,1)} %copy-done.49, ...), custom_call_target="tpu_custom_call" | custom-call | flops 2684354 | bytes 36700 | tf_op jit(solution)/shard_map/mix/pallas_call | solution.py:487
  283.6 3.2 %collective-permute-done.30.other = bf16[128,512]{1,0:T(8,128)(2,1)S(1)} collective-permute-done((bf16[128,512]{1,0:T(8,128)(2,1)S(1)}, bf16[128,512]{1,0:T(8,128)(2,1)S(1)}, u32[]{:S(2)}, u32[]{:S(2)}) %collective-permute-start.30) | collective-permute-done | bytes 131104 | tf_op jit(solution)/shard_map/ppermute | solution.py:35
  (222 shorter events, 93.6 us)
Async XLA Ops:
  6.5 131.1 %all-gather.5.cloned.1.call-start = ((), (), s32[]{:S(2)}) async-start(), calls=%async_computation.1 | async-start | bytes 5242880 | tf_op jit(solution)/shard_map/all_gather | solution.py:405
  11.2 166.7 %all-gather.3.cloned.1.call-start = ((), (), s32[]{:S(2)}) async-start(), calls=%async_computation | async-start | bytes 5242880 | tf_op jit(solution)/shard_map/all_gather | solution.py:405
  19.6 51.3 %collective-permute-start.2 = (bf16[256,2048]{1,0:T(8,128)(2,1)}, bf16[256,2048]{1,0:T(8,128)(2,1)S(1)}, u32[]{:S(2)}, u32[]{:S(2)}) collective-permute-start(bf16[256,2048]{1,0:T(8,128)(2,1)} %get-tuple-element.60.kept), channel_id=1, source_target_pairs={{0,1},{1,0},{2,3},{3,2},{4,5},{5,4},{6,7},{7,6},{8,9},{9,8},{10,11... | collective-permute-start | bytes 3145736 | tf_op jit(solution)/shard_map/ppermute | solution.py:35
  22.6 48.2 %collective-permute-start = (bf16[256,2048]{1,0:T(8,128)(2,1)}, bf16[256,2048]{1,0:T(8,128)(2,1)S(1)}, u32[]{:S(2)}, u32[]{:S(2)}) collective-permute-start(bf16[256,2048]{1,0:T(8,128)(2,1)} %get-tuple-element.58), channel_id=1, source_target_pairs={{0,16},{16,0},{1,17},{17,1},{2,18},{18,2},{3,19},{19,3},{4,20},{20... | collective-permute-start | bytes 3145736 | tf_op jit(solution)/shard_map/ppermute | solution.py:35
  38.1 49.8 %collective-permute-start.5 = (bf16[512,1152]{1,0:T(8,128)(2,1)}, bf16[512,1152]{1,0:T(8,128)(2,1)S(1)}, u32[]{:S(2)}, u32[]{:S(2)}) collective-permute-start(bf16[512,1152]{1,0:T(8,128)(2,1)} %pack.1.refs_0_), channel_id=1, source_target_pairs={{0,8},{4,12},{8,0},{12,4},{1,9},{5,13},{9,1},{13,5},{2,10},{6,14},... | collective-permute-start | bytes 3538952 | tf_op jit(solution)/shard_map/ppermute | solution.py:35
  39.7 49.5 %collective-permute-start.6 = (bf16[512,1152]{1,0:T(8,128)(2,1)}, bf16[512,1152]{1,0:T(8,128)(2,1)S(1)}, u32[]{:S(2)}, u32[]{:S(2)}) collective-permute-start(bf16[512,1152]{1,0:T(8,128)(2,1)} %pack.1.refs_0_), channel_id=1, source_target_pairs={{0,4},{4,0},{8,12},{12,8},{1,5},{5,1},{9,13},{13,9},{2,6},{6,2},{1... | collective-permute-start | bytes 3538952 | tf_op jit(solution)/shard_map/ppermute | solution.py:35
  41.2 48.1 %collective-permute-start.3 = (bf16[256,2048]{1,0:T(8,128)(2,1)S(1)}, bf16[256,2048]{1,0:T(8,128)(2,1)S(1)}, u32[]{:S(2)}, u32[]{:S(2)}) collective-permute-start(bf16[256,2048]{1,0:T(8,128)(2,1)S(1)} %copy-done.24), channel_id=1, source_target_pairs={{0,2},{2,0},{1,3},{3,1},{4,6},{6,4},{5,7},{7,5},{8,10},{10,8},{9,1... | collective-permute-start | bytes 3145736 | tf_op jit(solution)/shard_map/ppermute | solution.py:35
  70.9 18.4 %collective-permute-start.4 = (bf16[256,2048]{1,0:T(8,128)(2,1)S(1)}, bf16[256,2048]{1,0:T(8,128)(2,1)S(1)}, u32[]{:S(2)}, u32[]{:S(2)}) collective-permute-start(bf16[256,2048]{1,0:T(8,128)(2,1)S(1)} %collective-permute-done.2.kept_t), channel_id=1, source_target_pairs={{0,2},{2,0},{1,3},{3,1},{4,6},{6,4},{5,7},{7,5},{8,10},{10,8},{9,1... | collective-permute-start | bytes 3145736 | tf_op jit(solution)/shard_map/ppermute | solution.py:35
  70.9 25.6 %collective-permute-start.1 = (bf16[256,2048]{1,0:T(8,128)(2,1)S(1)}, bf16[256,2048]{1,0:T(8,128)(2,1)S(1)}, u32[]{:S(2)}, u32[]{:S(2)}) collective-permute-start(bf16[256,2048]{1,0:T(8,128)(2,1)S(1)} %collective-permute-done.kept), channel_id=1, source_target_pairs={{0,1},{1,0},{2,3},{3,2},{4,5},{5,4},{6,7},{7,6},{8,9},{9,8},{10,11... | collective-permute-start | bytes 3145736 | tf_op jit(solution)/shard_map/ppermute | solution.py:35
  97.0 26.2 %collective-permute-start.10 = (bf16[256,1152]{1,0:T(8,128)(2,1)S(1)}, bf16[256,1152]{1,0:T(8,128)(2,1)S(1)}, u32[]{:S(2)}, u32[]{:S(2)}) collective-permute-start(bf16[256,1152]{1,0:T(8,128)(2,1)S(1)} %slice.49), channel_id=1, source_target_pairs={{0,8},{4,12},{8,0},{12,4},{1,9},{5,13},{9,1},{13,5},{2,10},{6,14},... | collective-permute-start | bytes 1769480 | tf_op jit(solution)/shard_map/ppermute | solution.py:35
  98.5 24.7 %collective-permute-start.9 = (bf16[256,1152]{1,0:T(8,128)(2,1)S(1)}, bf16[256,1152]{1,0:T(8,128)(2,1)S(1)}, u32[]{:S(2)}, u32[]{:S(2)}) collective-permute-start(bf16[256,1152]{1,0:T(8,128)(2,1)S(1)} %slice.48), channel_id=1, source_target_pairs={{0,4},{4,0},{8,12},{12,8},{1,5},{5,1},{9,13},{13,9},{2,6},{6,2},{1... | collective-permute-start | bytes 1769480 | tf_op jit(solution)/shard_map/ppermute | solution.py:35
  147.9 29.1 %collective-permute-start.13 = (bf16[256,1152]{1,0:T(8,128)(2,1)S(1)}, bf16[256,1152]{1,0:T(8,128)(2,1)S(1)}, u32[]{:S(2)}, u32[]{:S(2)}) collective-permute-start(bf16[256,1152]{1,0:T(8,128)(2,1)S(1)} %copy-done.32), channel_id=1, source_target_pairs={{0,16},{16,0},{1,17},{17,1},{2,18},{18,2},{3,19},{19,3},{4,20},{20... | collective-permute-start | bytes 1769480 | tf_op jit(solution)/shard_map/ppermute | solution.py:35
  185.6 11.6 %collective-permute-start.14 = (bf16[2,256,512]{2,1,0:T(8,128)(2,1)}, bf16[2,256,512]{2,1,0:T(8,128)(2,1)}, u32[]{:S(2)}, u32[]{:S(2)}) collective-permute-start(bf16[2,256,512]{2,1,0:T(8,128)(2,1)} %get-tuple-element.70), channel_id=1, source_target_pairs={{0,2},{2,0},{1,3},{3,1},{4,6},{6,4},{5,7},{7,5},{8,10},{10,8},{9,1... | collective-permute-start | bytes 1572872 | tf_op jit(solution)/shard_map/ppermute | solution.py:35
  185.6 26.8 %collective-permute-start.15 = (bf16[256,1024]{1,0:T(8,128)(2,1)}, bf16[256,1024]{1,0:T(8,128)(2,1)}, u32[]{:S(2)}, u32[]{:S(2)}) collective-permute-start(bf16[256,1024]{1,0:T(8,128)(2,1)} %relay.5), channel_id=1, source_target_pairs={{0,16},{16,0},{1,17},{17,1},{2,18},{18,2},{3,19},{19,3},{4,20},{20... | collective-permute-start | bytes 1572872 | tf_op jit(solution)/shard_map/ppermute | solution.py:35
  221.2 20.6 %collective-permute-start.16 = (bf16[2,256,512]{2,1,0:T(8,128)(2,1)}, bf16[2,256,512]{2,1,0:T(8,128)(2,1)}, u32[]{:S(2)}, u32[]{:S(2)}) collective-permute-start(bf16[2,256,512]{2,1,0:T(8,128)(2,1)} %get-tuple-element.73), channel_id=1, source_target_pairs={{0,2},{2,0},{1,3},{3,1},{4,6},{6,4},{5,7},{7,5},{8,10},{10,8},{9,1... | collective-permute-start | bytes 1572872 | tf_op jit(solution)/shard_map/ppermute | solution.py:35
  221.2 9.8 %collective-permute-start.23 = (f32[32]{0:T(128)S(1)}, f32[32]{0:T(128)S(1)}, u32[]{:S(2)}, u32[]{:S(2)}) collective-permute-start(f32[32]{0:T(128)S(1)} %exp.16), channel_id=1, source_target_pairs={{0,2},{2,0},{4,6},{6,4},{8,10},{10,8},{12,14},{14,12},{1,3},{3,1},... | collective-permute-start | bytes 392 | tf_op jit(solution)/shard_map/ppermute | solution.py:35
  231.0 7.9 %collective-permute-start.24 = (f32[32]{0:T(128)S(1)}, f32[32]{0:T(128)S(1)}, u32[]{:S(2)}, u32[]{:S(2)}) collective-permute-start(f32[32]{0:T(128)S(1)} %get-tuple-element.114), channel_id=1, source_target_pairs={{0,4},{2,6},{4,0},{6,2},{8,12},{10,14},{12,8},{14,10},{1,5},{3,7},... | collective-permute-start | bytes 392 | tf_op jit(solution)/shard_map/ppermute | solution.py:35
  237.9 10.4 %collective-permute-start.32 = (bf16[128,1024]{1,0:T(8,128)(2,1)}, bf16[128,1024]{1,0:T(8,128)(2,1)}, u32[]{:S(2)}, u32[]{:S(2)}) collective-permute-start(bf16[128,1024]{1,0:T(8,128)(2,1)} %get-tuple-element.76), channel_id=1, source_target_pairs={{0,2},{2,0},{4,6},{6,4},{8,10},{10,8},{12,14},{14,12},{1,3},{3,1},... | collective-permute-start | bytes 786440 | tf_op jit(solution)/shard_map/ppermute | solution.py:35
  238.9 7.5 %collective-permute-start.25 = (f32[32]{0:T(128)S(1)}, f32[32]{0:T(128)S(1)}, u32[]{:S(2)}, u32[]{:S(2)}) collective-permute-start(f32[32]{0:T(128)S(1)} %get-tuple-element.112), channel_id=1, source_target_pairs={{0,8},{2,10},{4,12},{6,14},{8,0},{10,2},{12,4},{14,6},{1,9},{3,11}... | collective-permute-start | bytes 392 | tf_op jit(solution)/shard_map/ppermute | solution.py:35
  241.8 19.2 %collective-permute-start.19 = (bf16[256,512]{1,0:T(8,128)(2,1)S(1)}, bf16[256,512]{1,0:T(8,128)(2,1)S(1)}, u32[]{:S(2)}, u32[]{:S(2)}) collective-permute-start(bf16[256,512]{1,0:T(8,128)(2,1)S(1)} %relay.6), channel_id=1, source_target_pairs={{0,16},{16,0},{1,17},{17,1},{2,18},{18,2},{3,19},{19,3},{4,20},{20... | collective-permute-start | bytes 786440 | tf_op jit(solution)/shard_map/ppermute | solution.py:35
  243.5 23.0 %collective-permute-start.17 = (bf16[256,512]{1,0:T(8,128)(2,1)}, bf16[256,512]{1,0:T(8,128)(2,1)S(1)}, u32[]{:S(2)}, u32[]{:S(2)}) collective-permute-start(bf16[256,512]{1,0:T(8,128)(2,1)} %relay.7), channel_id=1, source_target_pairs={{0,16},{16,0},{1,17},{17,1},{2,18},{18,2},{3,19},{19,3},{4,20},{20... | collective-permute-start | bytes 786440 | tf_op jit(solution)/shard_map/ppermute | solution.py:35
  250.9 27.2 %collective-permute-start.33 = (bf16[128,1024]{1,0:T(8,128)(2,1)}, bf16[128,1024]{1,0:T(8,128)(2,1)S(1)}, u32[]{:S(2)}, u32[]{:S(2)}) collective-permute-start(bf16[128,1024]{1,0:T(8,128)(2,1)} %get-tuple-element.107), channel_id=1, source_target_pairs={{0,4},{2,6},{4,0},{6,2},{8,12},{10,14},{12,8},{14,10},{1,5},{3,7},... | collective-permute-start | bytes 786440 | tf_op jit(solution)/shard_map/ppermute | solution.py:35
  261.7 7.5 %collective-permute-start.20 = (bf16[16,512]{1,0:T(8,128)(2,1)S(1)}, bf16[16,512]{1,0:T(8,128)(2,1)S(1)}, u32[]{:S(2)}, u32[]{:S(2)}) collective-permute-start(bf16[16,512]{1,0:T(8,128)(2,1)S(1)} %rim.5), channel_id=1, source_target_pairs={{0,2},{2,4},{4,6},{6,8},{8,10},{10,12},{12,14},{1,3},{3,5},{5,7},{... | collective-permute-start | bytes 49160 | tf_op jit(solution)/shard_map/ppermute | solution.py:220
  279.2 11.2 %collective-permute-start.34 = (bf16[128,1024]{1,0:T(8,128)(2,1)S(1)}, bf16[128,1024]{1,0:T(8,128)(2,1)S(1)}, u32[]{:S(2)}, u32[]{:S(2)}) collective-permute-start(bf16[128,1024]{1,0:T(8,128)(2,1)S(1)} %get-tuple-element.110), channel_id=1, source_target_pairs={{0,8},{2,10},{4,12},{6,14},{8,0},{10,2},{12,4},{14,6},{1,9},{3,11}... | collective-permute-start | bytes 786440 | tf_op jit(solution)/shard_map/ppermute | solution.py:35
  (68 other events, 528.8 us)
Sparse Core Ops, SparseCore 0:
  11.3 77.0 all-gather.4
  90.2 61.9 all-gather.2

commit v3 on v2

--- a/solution.py
+++ b/solution.py
@@ -35,44 +35,45 @@
     return lax.ppermute(part, axis, [(i, i ^ by) for i in range(lax.axis_size(axis))])
 
 
-def cut_kernel(chips, at_ref, tokens_ref, far_ref, own_ref):
-    depth = far_ref.shape[1] // chips
+def cut_kernel(chips, at_ref, tokens_ref, far_sent, far_kept, own_ref):
+    depth = far_kept.shape[1] // chips
     rows = tokens_ref.shape[0]
     f_at, c_at = at_ref[0], at_ref[1]
     for i in range(chips):
-        for out, f in ((far_ref, 1 - f_at), (own_ref, f_at)):
-            for k, c in enumerate((c_at, 1 - c_at)):
-                start = pl.multiple_of(((f * chips + at_ref[3 + i]) * 2 + c) * depth, depth)
-                out[k * rows : (k + 1) * rows, i * depth : (i + 1) * depth] = tokens_ref[:, pl.ds(start, depth)]
-
-
-def stack_kernel(at_ref, kept, kept_t, got, got_t, rows_ref):
-    count = kept.shape[0]
-    mine = pl.multiple_of(at_ref[2] * count, count)
-    other = pl.multiple_of((1 - at_ref[2]) * count, count)
-    rows_ref[pl.ds(mine, count), :] = kept[...]
-    rows_ref[pl.ds(other, count), :] = kept_t[...]
-    rows_ref[pl.ds(2 * count + mine, count), :] = got[...]
-    rows_ref[pl.ds(2 * count + other, count), :] = got_t[...]
-
-
-def token_rows(at, cut, cut_t):
-    share, depth = cut.shape[0] // 2, cut.shape[1]
-    if cut_t is None:
-        parts = (cut[:share], swapped(cut[share:], "core"))
-        return jnp.concatenate([lax.all_gather(a, "tp", axis=0, tiled=True) for a in parts], axis=0)
-    low = pl.BlockSpec((share, depth), lambda i: (0, 0))
-    high = pl.BlockSpec((share, depth), lambda i: (1, 0))
+        cols = slice(i * depth, (i + 1) * depth)
+
+        def taken(f, c):
+            start = pl.multiple_of(((f * chips + at_ref[3 + i]) * 2 + c) * depth, depth)
+            return tokens_ref[:, pl.ds(start, depth)]
+
+        far_sent[:, cols] = taken(1 - f_at, 1 - c_at)
+        far_kept[:, cols] = taken(1 - f_at, c_at)
+        own_ref[:rows, cols] = taken(f_at, c_at)
+        own_ref[rows:, cols] = taken(f_at, 1 - c_at)
+
+
+def stack_kernel(at_ref, *refs):
+    pieces, rows_ref = refs[:-1], refs[-1]
+    count = pieces[0].shape[0]
+    for k in range(0, len(pieces), 2):
+        rows_ref[pl.ds(pl.multiple_of((k + at_ref[2]) * count, count), count), :] = pieces[k][...]
+        rows_ref[pl.ds(pl.multiple_of((k + 1 - at_ref[2]) * count, count), count), :] = pieces[k + 1][...]
+
+
+def token_rows(at, kept, kept_t, got, got_t, own, own_t, own_c, own_tc):
+    count, depth = kept.shape
+    low = pl.BlockSpec((count, depth), lambda i: (0, 0))
+    high = pl.BlockSpec((count, depth), lambda i: (1, 0))
     return call(
         stack_kernel,
         "stack_rows",
-        jax.ShapeDtypeStruct((4 * share, depth), BF16),
-        moved=16 * share * depth,
+        jax.ShapeDtypeStruct((8 * count, depth), BF16),
+        moved=32 * count * depth,
         vmem=40,
         grid=(1,),
-        in_specs=[SMEM, low, low, high, high],
-        out_specs=pl.BlockSpec((4 * share, depth), lambda i: (0, 0)),
-    )(at, cut, cut_t, swapped(cut, "core"), swapped(cut_t, "core"))
+        in_specs=[SMEM] + [low] * 6 + [high] * 2,
+        out_specs=pl.BlockSpec((8 * count, depth), lambda i: (0, 0)),
+    )(at, kept, kept_t, got, got_t, own, own_t, own_c, own_tc)
 
 
 def sample_kernel(count, coef_ref, mean_ref, devs_ref, out_ref):
@@ -116,13 +117,17 @@
     out_ref[:, width : width + heads] = dt_ref[...]
 
 
-def gathered(weight):
-    if lax.axis_size("chip") != 4:
-        return [lax.all_gather(weight, "chip", axis=0, tiled=True)], ()
-    half = weight.shape[0] // 2
-    by_x, by_y = swapped(weight, "chip", 1), swapped(weight, "chip", 2)
-    halves = (by_y[:half], by_x[half:])
-    return [weight, by_x, by_y, swapped(halves[0], "chip", 1), swapped(halves[1], "chip", 2)], halves
+def sent_straight(weight):
+    return swapped(weight, "chip", 1), swapped(weight, "chip", 2)
+
+
+def corner_halves(straight):
+    half = straight[0].shape[0] // 2
+    return straight[1][:half], straight[0][half:]
+
+
+def sent_on(halves):
+    return swapped(halves[0], "chip", 1), swapped(halves[1], "chip", 2)
 
 
 def coded(part, heads):
@@ -134,60 +139,60 @@
     return part + pltpu.roll(part, LANES - heads, 1)
 
 
-def multiply_kernel(heads, with_steps, chips, pieces, at_ref, far_ref, own_ref, *refs):
-    weights, (sent_ref, kept_ref) = refs[:pieces], refs[pieces:]
-    half = far_ref.shape[0] // 2
-    if pieces == 1:
-        depth = far_ref.shape[1] // chips
-        parts = [weights[0].at[pl.ds(pl.multiple_of(at_ref[3 + i] * depth, depth), depth), :] for i in range(chips)]
-    else:
-        parts = weights
-    for k, rows_ref in enumerate((far_ref, own_ref)):
-        at = 0
-        total = None
-        for part in parts:
-            depth = part.shape[0]
-            term = jnp.dot(rows_ref[:, at : at + depth], part[...], preferred_element_type=F32)
-            total = term if total is None else total + term
-            at += depth
-        kept_ref[k] = total[:half]
-        sent_ref[k] = total[half:].astype(BF16)
+def multiply_kernel(heads, with_steps, pieces, rows_ref, *refs):
+    weights, (first_ref, second_ref, sent_ref, kept_ref) = refs[:pieces], refs[pieces:]
+    at = 0
+    total = None
+    for weight in weights:
+        depth = weight.shape[0]
+        term = jnp.dot(rows_ref[:, at : at + depth], weight[...], preferred_element_type=F32)
+        total = term if total is None else total + term
+        at += depth
+    half = total.shape[0] // 4
+    kept_ref[0] = total[:half]
+    kept_ref[1] = total[2 * half : 3 * half]
+    for out, first in ((first_ref, half), (second_ref, half + half // 2), (sent_ref, 3 * half)):
+        sent = total[first : first + out.shape[0]]
+        out[...] = sent.astype(BF16)
         if with_steps:
             @pl.when(pl.program_id(0) == pl.num_programs(0) - 1)
             def _():
-                sent_ref[k, :, -LANES:] = coded(total[half:, -LANES:], heads).astype(BF16)
-
-
-def multiplied(at, rows_far, rows_own, weights, heads, with_steps, first, width):
+                out[:, -LANES:] = coded(sent[:, -LANES:], heads).astype(BF16)
+
+
+def multiplied(rows, weights, heads, with_steps):
+    width = weights[0].shape[1]
     tile = next(t for t in (256, 384, 128) if width % t == 0)
-    col = first // tile
-    half = rows_far.shape[0] // 2
+    half = rows.shape[0] // 4
+    sent = lambda count: jax.ShapeDtypeStruct((count, width), BF16)
     return call(
-        functools.partial(multiply_kernel, heads, with_steps, lax.axis_size("chip"), len(weights)),
+        functools.partial(multiply_kernel, heads, with_steps, len(weights)),
         "multiply",
-        (jax.ShapeDtypeStruct((2, half, width), BF16), jax.ShapeDtypeStruct((2, half, width), F32)),
-        flops=4 * rows_far.size * width,
-        moved=4 * rows_far.size + 2 * rows_far.shape[1] * width + 12 * half * width,
-        vmem=40,
+        (sent(half // 2), sent(half // 2), sent(half), jax.ShapeDtypeStruct((2, half, width), F32)),
+        flops=2 * rows.size * width,
+        moved=2 * rows.size + 2 * rows.shape[1] * width + 12 * half * width,
         grid=(width // tile,),
-        in_specs=[SMEM]
-        + [pl.BlockSpec(rows_far.shape, lambda i: (0, 0))] * 2
-        + [pl.BlockSpec((w.shape[0], tile), lambda i: (0, col + i)) for w in weights],
-        out_specs=[pl.BlockSpec((2, half, tile), lambda i: (0, 0, i))] * 2,
-    )(at, rows_far, rows_own, *weights)
-
-
-def relay_kernel(heads, with_steps, kept_ref, got_ref, out_ref):
-    kept, got = kept_ref[0], got_ref[0].astype(F32)
-    out_ref[...] = (kept + got).astype(BF16)
-    if with_steps:
-        wide = kept[:, -LANES:] + decoded(got[:, -LANES:], heads)
-        lane = lax.broadcasted_iota(jnp.int32, wide.shape, 1)
-        out_ref[:, -LANES:] = coded(jnp.where(lane < heads, wide, 0.0), heads).astype(BF16)
-
-
-def relayed(kept, got, heads, with_steps):
+        in_specs=[pl.BlockSpec(rows.shape, lambda i: (0, 0))]
+        + [pl.BlockSpec((w.shape[0], tile), lambda i: (0, i)) for w in weights],
+        out_specs=[pl.BlockSpec((count, tile), lambda i: (0, i)) for count in (half // 2, half // 2, half)]
+        + [pl.BlockSpec((2, half, tile), lambda i: (0, 0, i))],
+    )(rows, *weights)
+
+
+def relay_kernel(heads, with_steps, kept_ref, first_ref, second_ref, out_ref):
+    half = first_ref.shape[0]
+    for got_ref, rows in ((first_ref, slice(0, half)), (second_ref, slice(half, 2 * half))):
+        kept, got = kept_ref[0, rows, :], got_ref[...].astype(F32)
+        out_ref[rows, :] = (kept + got).astype(BF16)
+        if with_steps:
+            wide = kept[:, -LANES:] + decoded(got[:, -LANES:], heads)
+            lane = lax.broadcasted_iota(jnp.int32, wide.shape, 1)
+            out_ref[rows, -LANES:] = coded(jnp.where(lane < heads, wide, 0.0), heads).astype(BF16)
+
+
+def relayed(kept, first, second, heads, with_steps):
     rows, width = kept.shape[1:]
+    half = pl.BlockSpec((rows // 2, width), lambda i: (0, 0))
     return call(
         functools.partial(relay_kernel, heads, with_steps),
         "relay",
@@ -195,13 +200,13 @@
         moved=8 * rows * width,
         vmem=12,
         grid=(1,),
-        in_specs=[pl.BlockSpec((1, rows, width), lambda i: (0, 0, 0))] * 2,
+        in_specs=[pl.BlockSpec((1, rows, width), lambda i: (0, 0, 0)), half, half],
         out_specs=pl.BlockSpec((rows, width), lambda i: (0, 0)),
-    )(kept, got)
+    )(kept, first, second)
 
 
 def rim_kernel(kept, got_c, got_f, rim_ref):
-    rim_ref[...] = (kept[0] + got_c[0].astype(F32) + got_f[...].astype(F32)).astype(BF16)
+    rim_ref[...] = (kept[0] + got_c[...].astype(F32) + got_f[...].astype(F32)).astype(BF16)
 
 
 def rows_before(kept, got_c, got_f):
@@ -214,7 +219,7 @@
         moved=10 * RIM * width,
         vmem=12,
         grid=(1,),
-        in_specs=[pl.BlockSpec((1, RIM, width), lambda i: (1, at, 0))] * 2 + [pl.BlockSpec((RIM, width), lambda i: (at, 0))],
+        in_specs=[pl.BlockSpec((1, RIM, width), lambda i: (1, at, 0))] + [pl.BlockSpec((RIM, width), lambda i: (at, 0))] * 2,
         out_specs=pl.BlockSpec((RIM, width), lambda i: (0, 0)),
     )(kept, got_c, got_f)
     return lax.ppermute(rim, SEQ, [(i, i + 1) for i in range(lax.axis_size(SEQ) - 1)])
@@ -222,7 +227,7 @@
 
 def convolved(width, kept, got_c, got_f, rim, taps, padded):
     count = padded.shape[0] - 8
-    proj = kept[0, :, :width] + got_c[0, :, :width].astype(F32) + got_f[:, :width].astype(F32)
+    proj = kept[0, :, :width] + got_c[:, :width].astype(F32) + got_f[:, :width].astype(F32)
     padded[8:, :] = proj.astype(BF16).astype(F32)
     padded[:8, :] = rim[:, :width].astype(F32)[RIM - 8 :]
     first = 8 - (CONV - 1)
@@ -232,14 +237,31 @@
     return (conv_sum * jax.nn.sigmoid(conv_sum)).astype(BF16)
 
 
-def state_proj_kernel(heads, kept, got_c, got_f, rim, taps, out_ref, logits_ref, padded):
+def state_proj_kernel(
+    heads, kept, got_c, got_f, rim, taps, bias, rate, out_ref, cum_ref, steps_ref, cum_t_ref, steps_t_ref, decay_ref, padded
+):
     count, width = out_ref.shape
     out_ref[...] = convolved(width, kept, got_c, got_f, rim, taps, padded)
-    logits_ref[...] = (
-        kept[0, :, width:]
-        + decoded(got_c[0, :, width:].astype(F32), heads)
-        + decoded(got_f[:, width:].astype(F32), heads)
-    )
+    logits = kept[0, :, width:] + decoded(got_c[:, width:].astype(F32), heads) + decoded(got_f[:, width:].astype(F32), heads)
+    steps = jax.nn.softplus(logits + bias[...])
+    row = lax.broadcasted_iota(jnp.int32, (SPAN, SPAN), 0)
+    col = lax.broadcasted_iota(jnp.int32, (SPAN, SPAN), 1)
+    causal = jnp.where(row >= col, 1.0, 0.0)
+    groups, per_group = cum_ref.shape[0], cum_ref.shape[2]
+    through = jnp.zeros((1, LANES), F32)
+    for at in range(0, count, SPAN):
+        span = slice(at, at + SPAN)
+        steps_b = steps[span, :]
+        cum = jnp.dot(
+            causal, -steps_b * rate[...], precision=lax.Precision.HIGHEST, preferred_element_type=F32
+        )
+        through = through + cum[SPAN - 1 : SPAN, :]
+        cum_t_ref[:, span] = jnp.transpose(cum)[:heads]
+        steps_t_ref[:, span] = jnp.transpose(steps_b)[:heads]
+        for g in range(groups):
+            cum_ref[g, span, :] = cum[:, g * per_group : (g + 1) * per_group]
+            steps_ref[g, span, :] = steps_b[:, g * per_group : (g + 1) * per_group]
+    decay_ref[...] = jnp.exp(through)[:, :heads]
 
 
 def pairwise(columns, first):
@@ -387,95 +409,118 @@
 
     width = per_group * P_SIZE
     early_groups = max(1, groups_here // 2)
+    fill = -heads_here % LANES
     late = list(range(early_groups, groups_here))
 
-    place = lax.axis_index("chip") if chips == 4 else 0
+    plane = chips == 4
+    two_shares = lax.axis_size("tp") == 2
+    place = lax.axis_index("chip") if plane else 0
     at = jnp.stack([lax.axis_index(a) for a in ("fsdp", "core", "tp")] + [place ^ i for i in range(chips)]).astype(jnp.int32)
-    cut = jax.ShapeDtypeStruct((2 * tokens.shape[0], chips * rows_k), BF16)
-    far, own = call(
+    share, depth = tokens.shape[0], chips * rows_k
+    cut = lambda rows: jax.ShapeDtypeStruct((rows, depth), BF16)
+    far_sent, far_kept, own = call(
         functools.partial(cut_kernel, chips),
         "cut_tokens",
-        (cut,) * 2,
+        (cut(share), cut(share), cut(2 * share)),
         moved=4 * tokens.size,
         in_specs=[SMEM, VMEM],
-        out_specs=[VMEM] * 2,
+        out_specs=[VMEM] * 3,
     )(at, tokens)
-    far = swapped(far, "fsdp")
-
-    gather = lambda a: [lax.all_gather(a, "chip", axis=0, tiled=True)]
-    weights_early = sampled_cols(proj_mean, proj_devs, swag_coef, 0, early_groups * width)
-    pieces_early = gather(weights_early)
+    proj_mean = after(proj_mean, own)
+    far_sent = swapped(far_sent, "fsdp")
+    far_kept = swapped(after(far_kept, far_sent), "fsdp")
+    bc_mean = after(bc_mean, far_sent)
+
+    weight_early = sampled_cols(proj_mean, proj_devs, swag_coef, 0, early_groups * width)
     weight_bc = sampled(bc_mean, bc_devs, swag_coef).reshape(rows_k, width_bc)
     weight_bc = call(
         pack_kernel,
         "pack",
         jax.ShapeDtypeStruct((rows_k, width_bc + LANES), BF16),
         moved=4 * weight_bc.size,
+        vmem=12,
         in_specs=[VMEM] * 2,
         out_specs=VMEM,
     )(weight_bc, dt_weight)
-    pieces_bc, halves_bc = gathered(weight_bc)
-    chunks = [(0, early_groups, pieces_early, 0)]
+    weight_late = None
     if late:
-        weights_late = sampled_cols(proj_mean, proj_devs, swag_coef, early_groups // len(late), len(late) * width)
-        pieces_late = gather(weights_late)
-        chunks += [(g, 1, pieces_late, i * width) for i, g in enumerate(late)]
-        far = after(far, weights_late)
-
-    two_shares = lax.axis_size("tp") == 2
-    rows_own = token_rows(at, own, swapped(own, "tp") if two_shares else None)
-    far_t = swapped(far, "tp") if two_shares else None
-    far, far_t = after((far, far_t), (rows_own, halves_bc))
-    rows_far = token_rows(at, far, far_t)
-    tok_count = rows_own.shape[0] // 2
+        weight_late = sampled_cols(proj_mean, proj_devs, swag_coef, early_groups // len(late), len(late) * width)
+    tok_count = share * lax.axis_size("tp")
     blocks = tok_count // SPAN
 
-    def projected(pieces, with_steps, first, width):
-        sent, kept = multiplied(at, rows_far, rows_own, pieces, heads_here, with_steps, first, width)
-        got = swapped(sent, "core")
-        back = relayed(kept, got, heads_here, with_steps)
-        return (kept, got, swapped(back, "fsdp")), back
-
-    part_bc, back = projected(pieces_bc, True, 0, width_bc + LANES)
-    parts = [part_bc]
-    for j, (_, groups, pieces, col) in enumerate(chunks):
-        earlier = (back, parts[j - 1][2]) if j else back
-        part, back = projected(after(pieces, earlier), False, col, groups * width)
-        parts.append(part)
-    parts = [part + (rows_before(*part),) for part in parts]
-    part_bc = parts.pop(0)
-
-    specs_of = lambda width: [pl.BlockSpec((1, tok_count, width), lambda i: (1, 0, i))] * 2 + [
+    def partial_sums(rows, pieces, with_steps, earlier=()):
+        first, second, sent, kept = multiplied(rows, pieces, heads_here, with_steps)
+        first, second = after((first, second), earlier)
+        back = relayed(kept, swapped(first, "core"), swapped(second, "core"), heads_here, with_steps)
+        return (kept, swapped(after(sent, back), "core")), back
+
+    if plane and two_shares:
+        early = [weight_early, *sent_straight(weight_early)]
+        early += sent_on(corner_halves(early[1:]))
+        own_t = swapped(own, "tp")
+        own_c, own_tc = swapped(own, "core"), swapped(own_t, "core")
+        far_sent = after(far_sent, own_t)
+        sent_t = swapped(far_sent, "tp")
+        got, got_t = swapped(far_sent, "core"), swapped(sent_t, "core")
+        far_kept = after(far_kept, (own_c, own_tc, got_t, weight_late))
+        kept_t = swapped(far_kept, "tp")
+        weight_bc = after(weight_bc, (early[3:], far_kept))
+        bc = [weight_bc, *sent_straight(weight_bc)]
+        rows = token_rows(at, far_kept, kept_t, got, got_t, own, own_t, own_c, own_tc)
+        part, back = partial_sums(rows, early, False)
+        bc += sent_on(corner_halves(after(bc[1:], back)))
+        got = swapped(back, "fsdp")
+        weight_late = after(weight_late, (back, bc[3:]))
+        part_bc, back_bc = partial_sums(rows, bc, True, got)
+        got_bc = swapped(after(back_bc, got), "fsdp")
+        straight = sent_straight(weight_late)
+        corners = sent_on(after(corner_halves(straight), got))
+        part_late, back_late = partial_sums(rows, after([weight_late, *straight, *corners], back_bc), False)
+        got_late = swapped(after(back_late, got_bc), "fsdp")
+        got_bc = after(got_bc, back_late)
+    else:
+        whole = lambda a, axis: lax.all_gather(a, axis, axis=0, tiled=True)
+        ranges = [far_kept, swapped(far_sent, "core"), own[:share], swapped(own[share:], "core")]
+        rows = jnp.concatenate([whole(r, "tp") for r in ranges], axis=0)
+        part, back = partial_sums(rows, [whole(weight_early, "chip")], False)
+        part_bc, back_bc = partial_sums(rows, [whole(weight_bc, "chip")], True)
+        got, got_bc = swapped(back, "fsdp"), swapped(back_bc, "fsdp")
+        if late:
+            part_late, back_late = partial_sums(rows, [whole(weight_late, "chip")], False)
+            got_late = swapped(back_late, "fsdp")
+    parts = [part + (got,)]
+    if late:
+        parts.append(part_late + (got_late,))
+    part_bc += (got_bc,)
+
+    specs_of = lambda width: [pl.BlockSpec((1, tok_count, width), lambda i: (1, 0, i))] + [
+        pl.BlockSpec((tok_count, width), lambda i: (0, i)),
         pl.BlockSpec((tok_count, width), lambda i: (0, i)),
         pl.BlockSpec((RIM, width), lambda i: (0, i)),
     ]
     whole_of = lambda *shape: pl.BlockSpec(shape, lambda i: (0,) * len(shape))
-    conv_out, logits = call(
+    by_group = (groups_here, tok_count, per_group)
+    by_head = (heads_here, tok_count)
+    conv_out, cum_g, steps_g, cum_t, steps_t, decay = call(
         functools.partial(state_proj_kernel, heads_here),
         "state_proj",
-        (jax.ShapeDtypeStruct((tok_count, width_bc), BF16), jax.ShapeDtypeStruct((tok_count, LANES), F32)),
+        (jax.ShapeDtypeStruct((tok_count, width_bc), BF16),)
+        + tuple(jax.ShapeDtypeStruct(a, F32) for a in (by_group, by_group, by_head, by_head, (1, heads_here))),
         moved=10 * tok_count * width_bc,
         grid=(1,),
-        in_specs=specs_of(width_bc + LANES) + [whole_of(CONV, width_bc)],
-        out_specs=[whole_of(tok_count, width_bc), whole_of(tok_count, LANES)],
+        in_specs=specs_of(width_bc + LANES) + [whole_of(CONV, width_bc)] + [whole_of(1, LANES)] * 2,
+        out_specs=[whole_of(*a) for a in ((tok_count, width_bc), by_group, by_group, by_head, by_head, (1, heads_here))],
         scratch_shapes=[pltpu.VMEM((tok_count + 8, width_bc), F32)],
-    )(*part_bc, conv_bc.reshape(CONV, width_bc))
-    step_size = jax.nn.softplus(logits[:, :heads_here] + dt_bias)
-    steps_b = step_size.reshape(blocks, SPAN, heads_here)
-    cum_log = jnp.cumsum(-steps_b * decay_rate, axis=1)
-    scales = prefix_scales(jnp.exp(jnp.sum(cum_log[:, SPAN - 1, :], axis=0)))
-    cum_log = cum_log.reshape(tok_count, heads_here)
-    cum_t, steps_t = cum_log.T, step_size.T
-    by_group = lambda a: jnp.transpose(a.reshape(tok_count, groups_here, per_group), (1, 0, 2))
-    cum_g, steps_g = by_group(cum_log), by_group(step_size)
+    )(*part_bc, rows_before(*part_bc), conv_bc.reshape(CONV, width_bc), jnp.pad(dt_bias, (0, fill))[None], jnp.pad(decay_rate, (0, fill))[None])
+    scales = prefix_scales(decay[0])
     skip = jnp.repeat(skip_gain, P_SIZE)[None, :]
     levels = scales.shape[0] // 3
 
     result = None
-    last_total = None
-    for (first, groups, _, _), part in zip(chunks, parts):
-        if last_total is not None:
-            part = after(part, last_total)
+    for first, groups, part in zip((0, early_groups), (early_groups, len(late)), parts):
+        if first:
+            part = after(part, first_total)
+        part = part + (rows_before(*part),)
         grid = (groups,)
         cols = lambda rows: pl.BlockSpec((rows, width), lambda i: (0, i))
         cols_all = lambda rows: pl.BlockSpec((rows, width), lambda i: (0, first + i))
@@ -501,8 +546,8 @@
             out_specs=[cols(tok_count), early_spec, cols(N), cols(N)],
             scratch_shapes=[pltpu.VMEM((tok_count + 8, width), F32)],
         )(*part, conv_proj, conv_out, conv_out, cum_g, steps_g, cum_t, steps_t, skip)
-        last_total = sent
         before = None
+        first_total = total
         for level in range(levels - 1):
             other = swapped(sent, SEQ, 1 << level)
             total, sent, before = combined(level, scales, total, other, before, (first, groups))

time: 305 us -> 256 us (0.84)
  waiting for transfers between devices: 136 us -> 108 us
  local copies, waits for them, and re-layouts: 38.2 us -> 20.5 us
  starting transfers between devices: 36.3 us -> 50.1 us
  between operations: 16.5 us -> 2.94 us
    ppermute x31 -> x42, waiting for transfers between devices: 136 us -> 108 us  [swapped(): lax.ppermute(part, axis, [(i, i ^ by) for i in range(lax.axis_size(axis))])]
    unnamed x114 -> x85, local copies, waits for them, and re-layouts: 28.9 us -> 11 us
    ppermute x31 -> x42, starting transfers between devices: 28.7 us -> 43.2 us  [swapped(): lax.ppermute(part, axis, [(i, i ^ by) for i in range(lax.axis_size(axis))])]
    pallas_call x7 -> x5, Pallas kernels: 27.6 us -> 33.7 us  [the longest x3 29.2 us: multiplied(): call(functools.partial(multiply_kernel, heads, with_steps, len(weights)),...]
    slice x2 -> x6, local copies, waits for them, and re-layouts: 0.09 us -> 5.98 us  [corner_halves(): return (straight[1][:half], straight[0][half:])]
    pallas_call x3 -> x2, Pallas kernels: 11.9 us -> 9.8 us  [body(): call(mix_kernel, 'mix', (jax.ShapeDtypeStruct((tok_count, groups * width)...]
    ppermute x4 -> x3, starting transfers between devices: 7.52 us -> 6.95 us  [rows_before(): lax.ppermute(rim, SEQ, [(i, i + 1) for i in range(lax.axis_size(SEQ) - 1)])]
  transfers between devices with their start and end apart: 37 -> 45, of which waited for: 16 -> 20; matrix products, arithmetic and copies ran while one was open for 6% -> 5% of each run, Pallas kernels for 19% -> 25%
where the time goes in v3:
time: 256 us; the launch traced here: 255 us
  waiting for transfers between devices  108 us (42%)
  Pallas kernels  68.8 us (27%)
  starting transfers between devices  50.1 us (20%)
  local copies, waits for them, and re-layouts  20.5 us (8%)
  other arithmetic  5.37 us (2%)
  between operations  2.94 us (1%)
    ppermute x42, waiting for transfers between devices, swapped(): lax.ppermute(part, axis, [(i, i ^ by) for i in range(lax.axis_size(axis))])  108 us
    ppermute x42, starting transfers between devices, swapped(): lax.ppermute(part, axis, [(i, i ^ by) for i in range(lax.axis_size(axis))])  43.2 us
    pallas_call x3, Pallas kernels, multiplied(): call(functools.partial(multiply_kernel, heads, with_steps, len(weights)),...  29.2 us
    unnamed x85, local copies, waits for them, and re-layouts  11 us
    pallas_call x2, Pallas kernels, body(): call(mix_kernel, 'mix', (jax.ShapeDtypeStruct((tok_count, groups * width)...  9.8 us
    pallas_call x2, Pallas kernels, sampled_cols(): call(functools.partial(sample_kernel, count), 'sample', jax.ShapeDtypeStr...  9.25 us
    ppermute x3, starting transfers between devices, rows_before(): lax.ppermute(rim, SEQ, [(i, i + 1) for i in range(lax.axis_size(SEQ) - 1)])  6.95 us
    slice x6, local copies, waits for them, and re-layouts, corner_halves(): return (straight[1][:half], straight[0][half:])  5.98 us
  transfers between devices with their start and end apart: 45, of which 20 were waited for; matrix products, arithmetic and copies ran while one was open for 5% of the time, Pallas kernels for 25%

profile of v3, /device:TPU:0, one launch (start us, length us, event | category | flops | bytes accessed | tf_op | source)
XLA Modules:
  0.0 255.2 jit_solution(5620879969503107039)
XLA Ops:
  0.7 3.1 %cut_tokens.1 = (bf16[128,2048]{1,0:T(8,128)(2,1)}, bf16[128,2048]{1,0:T(8,128)(2,1)}, bf16[256,2048]{1,0:T(8,128)(2,1)}) custom-call(s32[7]{0:T(128)} %stack.59.at_ref, bf16[128,8192]{1,0:T(8,128)(2,1)} %tokens_ref.1), custom_call_target="tpu_custom_call" | custom-call | bytes 83886 | tf_op jit(solution)/shard_map/cut_tokens/pallas_call | solution.py:421
  6.8 4.6 %sample.3.refs_0_ = bf16[512,1024]{1,0:T(8,128)(2,1)} custom-call(f32[4]{0:T(128)} %coef_ref.3, bf16[512,2048]{1,0:T(8,128)(2,1)} %mean_ref.1, bf16[4,512,2048]{2,1,0:T(8,128)(2,1)} %devs_ref.3), custom_call_target="tpu_custom_call" | custom-call | bytes 125829 | tf_op jit(solution)/shard_map/sample/pallas_call | solution.py:90
  17.0 23.6 %collective-permute-done = bf16[128,2048]{1,0:T(8,128)(2,1)S(1)} collective-permute-done((bf16[128,2048]{1,0:T(8,128)(2,1)S(1)}, bf16[128,2048]{1,0:T(8,128)(2,1)S(1)}, u32[]{:S(2)}, u32[]{:S(2)}) %collective-permute-start) | collective-permute-done | bytes 524320 | tf_op jit(solution)/shard_map/ppermute | solution.py:35
  40.6 3.4 %collective-permute-start.1 = (bf16[128,2048]{1,0:T(8,128)(2,1)}, bf16[128,2048]{1,0:T(8,128)(2,1)S(1)}, u32[]{:S(2)}, u32[]{:S(2)}) collective-permute-start(bf16[128,2048]{1,0:T(8,128)(2,1)} %get-tuple-element.77), channel_id=1, source_target_pairs={{0,16},{16,0},{1,17},{17,1},{2,18},{18,2},{3,19},{19,3},{4,20},{20... | collective-permute-start | bytes 1572872 | tf_op jit(solution)/shard_map/ppermute | solution.py:35
  44.7 4.6 %sample.2.refs_0_ = bf16[512,1024]{1,0:T(8,128)(2,1)} custom-call(f32[4]{0:T(128)} %coef_ref.3, bf16[512,2048]{1,0:T(8,128)(2,1)} %mean_ref.1, bf16[4,512,2048]{2,1,0:T(8,128)(2,1)} %devs_ref.3), custom_call_target="tpu_custom_call" | custom-call | bytes 125829 | tf_op jit(solution)/shard_map/sample/pallas_call | solution.py:90
  56.4 10.1 %collective-permute-done.1.refs_0_ = bf16[128,2048]{1,0:T(8,128)(2,1)S(1)} collective-permute-done((bf16[128,2048]{1,0:T(8,128)(2,1)}, bf16[128,2048]{1,0:T(8,128)(2,1)S(1)}, u32[]{:S(2)}, u32[]{:S(2)}) %collective-permute-start.1) | collective-permute-done | bytes 524320 | tf_op jit(solution)/shard_map/ppermute | solution.py:35
  68.1 5.4 %fusion = bf16[512,2,512]{2,1,0:T(2,128)(2,1)S(1)} fusion(bf16[512,2,512]{2,1,0:T(2,128)(2,1)S(1)} %copy-done.23, bf16[4,512,2,512]{3,2,1,0:T(2,128)(2,1)} %param.16, f32[]{:T(128)} %bitcast.13, f32[]{:T(128)} %bitcast.11, f32[]{:T(128)} %bitcast.9, f32[]{:T(128)} %bitcast.7), kind=kLoop, calls=%fused_computation.1 | loop fusion | flops 7340032 | bytes 6291472 | tf_op jit(solution)/shard_map/convert_element_type | solution.py:110
  73.9 4.8 %collective-permute-done.12.refs_4_ = bf16[256,1024]{1,0:T(8,128)(2,1)S(1)} collective-permute-done((bf16[256,1024]{1,0:T(8,128)(2,1)S(1)}, bf16[256,1024]{1,0:T(8,128)(2,1)S(1)}, u32[]{:S(2)}, u32[]{:S(2)}) %collective-permute-start.12) | collective-permute-done | bytes 524320 | tf_op jit(solution)/shard_map/ppermute | solution.py:35
  83.6 12.4 %collective-permute-done.7.refs_1_ = bf16[128,2048]{1,0:T(8,128)(2,1)S(1)} collective-permute-done((bf16[128,2048]{1,0:T(8,128)(2,1)S(1)}, bf16[128,2048]{1,0:T(8,128)(2,1)S(1)}, u32[]{:S(2)}, u32[]{:S(2)}) %collective-permute-start.7) | collective-permute-done | bytes 524320 | tf_op jit(solution)/shard_map/ppermute | solution.py:35
  99.5 8.8 %multiply.3 = (bf16[128,1024]{1,0:T(8,128)(2,1)}, bf16[128,1024]{1,0:T(8,128)(2,1)}, bf16[256,1024]{1,0:T(8,128)(2,1)}, f32[2,256,1024]{2,1,0:T(8,128)}) custom-call(bf16[1024,2048]{1,0:T(8,128)(2,1)} %copy-done, bf16[512,1024]{1,0:T(8,128)(2,1)} %sample.3.refs_0_, bf16[512,1024]{1,0:T(8,128)(2,1)} %collective-permute-done.9.refs_1_, ...), custom_call_target="tpu_custom_call" | custom-call | flops 85899344 | bytes 230686 | tf_op jit(solution)/shard_map/multiply/pallas_call | solution.py:168
  115.6 14.3 %collective-permute-done.18.refs_4_ = bf16[256,1152]{1,0:T(8,128)(2,1)S(1)} collective-permute-done((bf16[256,1152]{1,0:T(8,128)(2,1)S(1)}, bf16[256,1152]{1,0:T(8,128)(2,1)S(1)}, u32[]{:S(2)}, u32[]{:S(2)}) %collective-permute-start.18) | collective-permute-done | bytes 589856 | tf_op jit(solution)/shard_map/ppermute | solution.py:35
  134.1 11.6 %multiply.4 = (bf16[128,1152]{1,0:T(8,128)(2,1)}, bf16[128,1152]{1,0:T(8,128)(2,1)}, bf16[256,1152]{1,0:T(8,128)(2,1)}, f32[2,256,1152]{2,1,0:T(8,128)}) custom-call(bf16[1024,2048]{1,0:T(8,128)(2,1)} %copy-done, bf16[512,1152]{1,0:T(8,128)(2,1)} %copy-done.9, bf16[512,1152]{1,0:T(8,128)(2,1)} %collective-permute-done.15.refs_1_, ...), custom_call_target="tpu_custom_call" | custom-call | flops 96636768 | bytes 249036 | tf_op jit(solution)/shard_map/multiply/pallas_call | solution.py:168
  145.7 10.9 %collective-permute-done.21.got_f = bf16[256,1024]{1,0:T(8,128)(2,1)S(1)} collective-permute-done((bf16[256,1024]{1,0:T(8,128)(2,1)S(1)}, bf16[256,1024]{1,0:T(8,128)(2,1)S(1)}, u32[]{:S(2)}, u32[]{:S(2)}) %collective-permute-start.21) | collective-permute-done | bytes 524320 | tf_op jit(solution)/shard_map/ppermute | solution.py:35
  164.1 8.3 %collective-permute-done.22.refs_3_ = bf16[256,1024]{1,0:T(8,128)(2,1)S(1)} collective-permute-done((bf16[256,1024]{1,0:T(8,128)(2,1)S(1)}, bf16[256,1024]{1,0:T(8,128)(2,1)S(1)}, u32[]{:S(2)}, u32[]{:S(2)}) %collective-permute-start.22) | collective-permute-done | bytes 524320 | tf_op jit(solution)/shard_map/ppermute | solution.py:35
  174.5 8.8 %multiply.5 = (bf16[128,1024]{1,0:T(8,128)(2,1)}, bf16[128,1024]{1,0:T(8,128)(2,1)}, bf16[256,1024]{1,0:T(8,128)(2,1)}, f32[2,256,1024]{2,1,0:T(8,128)}) custom-call(bf16[1024,2048]{1,0:T(8,128)(2,1)} %copy-done, bf16[512,1024]{1,0:T(8,128)(2,1)} %sample.2.refs_0_, bf16[512,1024]{1,0:T(8,128)(2,1)} %collective-permute-done.19.refs_1_, ...), custom_call_target="tpu_custom_call" | custom-call | flops 85899344 | bytes 230686 | tf_op jit(solution)/shard_map/multiply/pallas_call | solution.py:168
  187.9 4.1 %collective-permute-done.29.got_f = bf16[256,1152]{1,0:T(8,128)(2,1)S(1)} collective-permute-done((bf16[256,1152]{1,0:T(8,128)(2,1)}, bf16[256,1152]{1,0:T(8,128)(2,1)S(1)}, u32[]{:S(2)}, u32[]{:S(2)}) %collective-permute-start.29) | collective-permute-done | bytes 589856 | tf_op jit(solution)/shard_map/ppermute | solution.py:35
  193.5 3.1 %collective-permute-start.32 = (bf16[16,1024]{1,0:T(8,128)(2,1)}, bf16[16,1024]{1,0:T(8,128)(2,1)}, u32[]{:S(2)}, u32[]{:S(2)}) collective-permute-start(bf16[16,1024]{1,0:T(8,128)(2,1)} %rim.3), channel_id=1, source_target_pairs={{0,2},{2,4},{4,6},{6,8},{8,10},{10,12},{12,14},{1,3},{3,5},{5,7},{... | collective-permute-start | bytes 98312 | tf_op jit(solution)/shard_map/ppermute | solution.py:225
  202.4 4.6 %state_proj.1 = (bf16[256,1024]{1,0:T(8,128)(2,1)}, f32[4,256,8]{2,1,0:T(8,128)}, f32[4,256,8]{2,1,0:T(8,128)}, f32[32,256]{1,0:T(8,128)}, f32[32,256]{1,0:T(8,128)}, /*index=5*/f32[1,32]{1,0:T(1,128)}) custom-call(f32[2,256,1152]{2,1,0:T(8,128)} %get-tuple-element.94.kept_ref.kept, bf16[256,1152]{1,0:T(8,128)(2,1)} %copy-done.11, ...), custom_call_target="tpu_custom_call" | custom-call | bytes 52428 | tf_op jit(solution)/shard_map/state_proj/pallas_call | solution.py:504
  207.4 4.9 %mix.2 = (f32[256,1024]{1,0:T(8,128)}, f32[1,128,1024]{2,1,0:T(8,128)}, f32[128,1024]{1,0:T(8,128)}, bf16[128,1024]{1,0:T(8,128)(2,1)}) custom-call(f32[2,256,1024]{2,1,0:T(8,128)} %get-tuple-element.82.kept_ref.kept, bf16[256,1024]{1,0:T(8,128)(2,1)} %collective-permute-done.31.got_c, bf16[256,1024]{1,0:T(8,128)(2,1)} %copy-done.12, ...), custom_call_target="tpu_custom_call" | custom-call | flops 5368709 | bytes 73400 | tf_op jit(solution)/shard_map/mix/pallas_call | solution.py:532
  222.2 4.9 %mix.3 = (f32[256,1024]{1,0:T(8,128)}, f32[1,128,1024]{2,1,0:T(8,128)}, f32[128,1024]{1,0:T(8,128)}, bf16[128,1024]{1,0:T(8,128)(2,1)}) custom-call(f32[2,256,1024]{2,1,0:T(8,128)} %get-tuple-element.124.kept_ref.kept, bf16[256,1024]{1,0:T(8,128)(2,1)} %collective-permute-done.28.got_c, bf16[256,1024]{1,0:T(8,128)(2,1)} %collective-permute-done.30.got_f, ...), custom_call_target="tpu_custom_call" | custom-call | flops 5368709 | bytes 73400 | tf_op jit(solution)/shard_map/mix/pallas_call | solution.py:532
  232.8 4.7 %collective-permute-done.43.other = bf16[128,1024]{1,0:T(8,128)(2,1)S(1)} collective-permute-done((bf16[128,1024]{1,0:T(8,128)(2,1)S(1)}, bf16[128,1024]{1,0:T(8,128)(2,1)S(1)}, u32[]{:S(2)}, u32[]{:S(2)}) %collective-permute-start.43) | collective-permute-done | bytes 262176 | tf_op jit(solution)/shard_map/ppermute | solution.py:35
  238.6 3.5 %collective-permute-start.44 = (bf16[128,1024]{1,0:T(8,128)(2,1)S(1)}, bf16[128,1024]{1,0:T(8,128)(2,1)S(1)}, u32[]{:S(2)}, u32[]{:S(2)}) collective-permute-start(bf16[128,1024]{1,0:T(8,128)(2,1)S(1)} %get-tuple-element.144), channel_id=1, source_target_pairs={{0,8},{2,10},{4,12},{6,14},{8,0},{10,2},{12,4},{14,6},{1,9},{3,11}... | collective-permute-start | bytes 786440 | tf_op jit(solution)/shard_map/ppermute | solution.py:35
  244.0 3.3 %collective-permute-start.41 = (bf16[128,1024]{1,0:T(8,128)(2,1)S(1)}, bf16[128,1024]{1,0:T(8,128)(2,1)S(1)}, u32[]{:S(2)}, u32[]{:S(2)}) collective-permute-start(bf16[128,1024]{1,0:T(8,128)(2,1)S(1)} %get-tuple-element.136), channel_id=1, source_target_pairs={{0,8},{2,10},{4,12},{6,14},{8,0},{10,2},{12,4},{14,6},{1,9},{3,11}... | collective-permute-start | bytes 786440 | tf_op jit(solution)/shard_map/ppermute | solution.py:35
  249.7 3.8 %collective-permute-done.41.other = bf16[128,1024]{1,0:T(8,128)(2,1)S(1)} collective-permute-done((bf16[128,1024]{1,0:T(8,128)(2,1)S(1)}, bf16[128,1024]{1,0:T(8,128)(2,1)S(1)}, u32[]{:S(2)}, u32[]{:S(2)}) %collective-permute-start.41) | collective-permute-done | bytes 262176 | tf_op jit(solution)/shard_map/ppermute | solution.py:35
  (194 shorter events, 80.6 us)
Async XLA Ops:
  3.8 40.3 %collective-permute-start.3 = (bf16[256,2048]{1,0:T(8,128)(2,1)}, bf16[256,2048]{1,0:T(8,128)(2,1)S(1)}, u32[]{:S(2)}, u32[]{:S(2)}) collective-permute-start(bf16[256,2048]{1,0:T(8,128)(2,1)} %get-tuple-element.78.refs_4_), channel_id=1, source_target_pairs={{0,1},{1,0},{2,3},{3,2},{4,5},{5,4},{6,7},{7,6},{8,9},{9,8},{10,11... | collective-permute-start | bytes 3145736 | tf_op jit(solution)/shard_map/ppermute | solution.py:35
  11.4 32.8 %collective-permute-start.10 = (bf16[512,1024]{1,0:T(8,128)(2,1)}, bf16[512,1024]{1,0:T(8,128)(2,1)}, u32[]{:S(2)}, u32[]{:S(2)}) collective-permute-start(bf16[512,1024]{1,0:T(8,128)(2,1)} %sample.3.refs_0_), channel_id=1, source_target_pairs={{0,8},{4,12},{8,0},{12,4},{1,9},{5,13},{9,1},{13,5},{2,10},{6,14},... | collective-permute-start | bytes 3145736 | tf_op jit(solution)/shard_map/ppermute | solution.py:35
  12.9 27.7 %collective-permute-start = (bf16[128,2048]{1,0:T(8,128)(2,1)S(1)}, bf16[128,2048]{1,0:T(8,128)(2,1)S(1)}, u32[]{:S(2)}, u32[]{:S(2)}) collective-permute-start(bf16[128,2048]{1,0:T(8,128)(2,1)S(1)} %copy-done.40), channel_id=1, source_target_pairs={{0,16},{16,0},{1,17},{17,1},{2,18},{18,2},{3,19},{19,3},{4,20},{20... | collective-permute-start | bytes 1572872 | tf_op jit(solution)/shard_map/ppermute | solution.py:35
  15.5 38.2 %collective-permute-start.9 = (bf16[512,1024]{1,0:T(8,128)(2,1)}, bf16[512,1024]{1,0:T(8,128)(2,1)}, u32[]{:S(2)}, u32[]{:S(2)}) collective-permute-start(bf16[512,1024]{1,0:T(8,128)(2,1)} %sample.3.refs_0_), channel_id=1, source_target_pairs={{0,4},{4,0},{8,12},{12,8},{1,5},{5,1},{9,13},{13,9},{2,6},{6,2},{1... | collective-permute-start | bytes 3145736 | tf_op jit(solution)/shard_map/ppermute | solution.py:35
  40.6 25.9 %collective-permute-start.1 = (bf16[128,2048]{1,0:T(8,128)(2,1)}, bf16[128,2048]{1,0:T(8,128)(2,1)S(1)}, u32[]{:S(2)}, u32[]{:S(2)}) collective-permute-start(bf16[128,2048]{1,0:T(8,128)(2,1)} %get-tuple-element.77), channel_id=1, source_target_pairs={{0,16},{16,0},{1,17},{17,1},{2,18},{18,2},{3,19},{19,3},{4,20},{20... | collective-permute-start | bytes 1572872 | tf_op jit(solution)/shard_map/ppermute | solution.py:35
  44.0 24.0 %collective-permute-start.5 = (bf16[128,2048]{1,0:T(8,128)(2,1)S(1)}, bf16[128,2048]{1,0:T(8,128)(2,1)}, u32[]{:S(2)}, u32[]{:S(2)}) collective-permute-start(bf16[128,2048]{1,0:T(8,128)(2,1)S(1)} %collective-permute-done), channel_id=1, source_target_pairs={{0,1},{1,0},{2,3},{3,2},{4,5},{5,4},{6,7},{7,6},{8,9},{9,8},{10,11... | collective-permute-start | bytes 1572872 | tf_op jit(solution)/shard_map/ppermute | solution.py:35
  44.2 29.6 %collective-permute-start.2 = (bf16[256,2048]{1,0:T(8,128)(2,1)S(1)}, bf16[256,2048]{1,0:T(8,128)(2,1)}, u32[]{:S(2)}, u32[]{:S(2)}) collective-permute-start(bf16[256,2048]{1,0:T(8,128)(2,1)S(1)} %copy-done.15), channel_id=1, source_target_pairs={{0,2},{2,0},{1,3},{3,1},{4,6},{6,4},{5,7},{7,5},{8,10},{10,8},{9,1... | collective-permute-start | bytes 3145736 | tf_op jit(solution)/shard_map/ppermute | solution.py:35
  44.2 29.6 %collective-permute-start.4 = (bf16[256,2048]{1,0:T(8,128)(2,1)S(1)}, bf16[256,2048]{1,0:T(8,128)(2,1)}, u32[]{:S(2)}, u32[]{:S(2)}) collective-permute-start(bf16[256,2048]{1,0:T(8,128)(2,1)S(1)} %collective-permute-done.3.refs_5_), channel_id=1, source_target_pairs={{0,2},{2,0},{1,3},{3,1},{4,6},{6,4},{5,7},{7,5},{8,10},{10,8},{9,1... | collective-permute-start | bytes 3145736 | tf_op jit(solution)/shard_map/ppermute | solution.py:35
  53.7 20.1 %collective-permute-start.11 = (bf16[256,1024]{1,0:T(8,128)(2,1)S(1)}, bf16[256,1024]{1,0:T(8,128)(2,1)S(1)}, u32[]{:S(2)}, u32[]{:S(2)}) collective-permute-start(bf16[256,1024]{1,0:T(8,128)(2,1)S(1)} %slice.56), channel_id=1, source_target_pairs={{0,4},{4,0},{8,12},{12,8},{1,5},{5,1},{9,13},{13,9},{2,6},{6,2},{1... | collective-permute-start | bytes 1572872 | tf_op jit(solution)/shard_map/ppermute | solution.py:35
  78.7 33.5 %collective-permute-start.16 = (bf16[512,1152]{1,0:T(8,128)(2,1)S(1)}, bf16[512,1152]{1,0:T(8,128)(2,1)}, u32[]{:S(2)}, u32[]{:S(2)}) collective-permute-start(bf16[512,1152]{1,0:T(8,128)(2,1)S(1)} %pack.1.refs_0_), channel_id=1, source_target_pairs={{0,8},{4,12},{8,0},{12,4},{1,9},{5,13},{9,1},{13,5},{2,10},{6,14},... | collective-permute-start | bytes 3538952 | tf_op jit(solution)/shard_map/ppermute | solution.py:35
  80.2 31.9 %collective-permute-start.15 = (bf16[512,1152]{1,0:T(8,128)(2,1)S(1)}, bf16[512,1152]{1,0:T(8,128)(2,1)}, u32[]{:S(2)}, u32[]{:S(2)}) collective-permute-start(bf16[512,1152]{1,0:T(8,128)(2,1)S(1)} %pack.1.refs_0_), channel_id=1, source_target_pairs={{0,4},{4,0},{8,12},{12,8},{1,5},{5,1},{9,13},{13,9},{2,6},{6,2},{1... | collective-permute-start | bytes 3538952 | tf_op jit(solution)/shard_map/ppermute | solution.py:35
  81.7 14.3 %collective-permute-start.7 = (bf16[128,2048]{1,0:T(8,128)(2,1)S(1)}, bf16[128,2048]{1,0:T(8,128)(2,1)S(1)}, u32[]{:S(2)}, u32[]{:S(2)}) collective-permute-start(bf16[128,2048]{1,0:T(8,128)(2,1)S(1)} %collective-permute-done.1.refs_0_), channel_id=1, source_target_pairs={{0,1},{1,0},{2,3},{3,2},{4,5},{5,4},{6,7},{7,6},{8,9},{9,8},{10,11... | collective-permute-start | bytes 1572872 | tf_op jit(solution)/shard_map/ppermute | solution.py:35
  114.4 15.4 %collective-permute-start.18 = (bf16[256,1152]{1,0:T(8,128)(2,1)S(1)}, bf16[256,1152]{1,0:T(8,128)(2,1)S(1)}, u32[]{:S(2)}, u32[]{:S(2)}) collective-permute-start(bf16[256,1152]{1,0:T(8,128)(2,1)S(1)} %slice.53), channel_id=1, source_target_pairs={{0,8},{4,12},{8,0},{12,4},{1,9},{5,13},{9,1},{13,5},{2,10},{6,14},... | collective-permute-start | bytes 1769480 | tf_op jit(solution)/shard_map/ppermute | solution.py:35
  115.0 15.1 %collective-permute-start.17 = (bf16[256,1152]{1,0:T(8,128)(2,1)S(1)}, bf16[256,1152]{1,0:T(8,128)(2,1)S(1)}, u32[]{:S(2)}, u32[]{:S(2)}) collective-permute-start(bf16[256,1152]{1,0:T(8,128)(2,1)S(1)} %slice.52), channel_id=1, source_target_pairs={{0,4},{4,0},{8,12},{12,8},{1,5},{5,1},{9,13},{13,9},{2,6},{6,2},{1... | collective-permute-start | bytes 1769480 | tf_op jit(solution)/shard_map/ppermute | solution.py:35
  130.1 27.0 %collective-permute-start.20 = (bf16[512,1024]{1,0:T(8,128)(2,1)S(1)}, bf16[512,1024]{1,0:T(8,128)(2,1)S(1)}, u32[]{:S(2)}, u32[]{:S(2)}) collective-permute-start(bf16[512,1024]{1,0:T(8,128)(2,1)S(1)} %copy-done.21), channel_id=1, source_target_pairs={{0,8},{4,12},{8,0},{12,4},{1,9},{5,13},{9,1},{13,5},{2,10},{6,14},... | collective-permute-start | bytes 3145736 | tf_op jit(solution)/shard_map/ppermute | solution.py:35
  131.6 25.5 %collective-permute-start.19 = (bf16[512,1024]{1,0:T(8,128)(2,1)S(1)}, bf16[512,1024]{1,0:T(8,128)(2,1)}, u32[]{:S(2)}, u32[]{:S(2)}) collective-permute-start(bf16[512,1024]{1,0:T(8,128)(2,1)S(1)} %copy-done.21), channel_id=1, source_target_pairs={{0,4},{4,0},{8,12},{12,8},{1,5},{5,1},{9,13},{13,9},{2,6},{6,2},{1... | collective-permute-start | bytes 3145736 | tf_op jit(solution)/shard_map/ppermute | solution.py:35
  132.2 24.4 %collective-permute-start.21 = (bf16[256,1024]{1,0:T(8,128)(2,1)S(1)}, bf16[256,1024]{1,0:T(8,128)(2,1)S(1)}, u32[]{:S(2)}, u32[]{:S(2)}) collective-permute-start(bf16[256,1024]{1,0:T(8,128)(2,1)S(1)} %relay.3), channel_id=1, source_target_pairs={{0,16},{16,0},{1,17},{17,1},{2,18},{18,2},{3,19},{19,3},{4,20},{20... | collective-permute-start | bytes 1572872 | tf_op jit(solution)/shard_map/ppermute | solution.py:35
  163.6 28.4 %collective-permute-start.29 = (bf16[256,1152]{1,0:T(8,128)(2,1)}, bf16[256,1152]{1,0:T(8,128)(2,1)S(1)}, u32[]{:S(2)}, u32[]{:S(2)}) collective-permute-start(bf16[256,1152]{1,0:T(8,128)(2,1)} %relay.4), channel_id=1, source_target_pairs={{0,16},{16,0},{1,17},{17,1},{2,18},{18,2},{3,19},{19,3},{4,20},{20... | collective-permute-start | bytes 1769480 | tf_op jit(solution)/shard_map/ppermute | solution.py:35
  163.6 33.0 %collective-permute-start.33 = (bf16[256,1152]{1,0:T(8,128)(2,1)}, bf16[256,1152]{1,0:T(8,128)(2,1)S(1)}, u32[]{:S(2)}, u32[]{:S(2)}) collective-permute-start(bf16[256,1152]{1,0:T(8,128)(2,1)} %get-tuple-element.116), channel_id=1, source_target_pairs={{0,2},{2,0},{1,3},{3,1},{4,6},{6,4},{5,7},{7,5},{8,10},{10,8},{9,1... | collective-permute-start | bytes 1769480 | tf_op jit(solution)/shard_map/ppermute | solution.py:35
  163.6 28.4 %collective-permute-start.31 = (bf16[256,1024]{1,0:T(8,128)(2,1)}, bf16[256,1024]{1,0:T(8,128)(2,1)}, u32[]{:S(2)}, u32[]{:S(2)}) collective-permute-start(bf16[256,1024]{1,0:T(8,128)(2,1)} %get-tuple-element.114), channel_id=1, source_target_pairs={{0,2},{2,0},{1,3},{3,1},{4,6},{6,4},{5,7},{7,5},{8,10},{10,8},{9,1... | collective-permute-start | bytes 1572872 | tf_op jit(solution)/shard_map/ppermute | solution.py:35
  192.0 22.6 %collective-permute-start.28 = (bf16[256,1024]{1,0:T(8,128)(2,1)}, bf16[256,1024]{1,0:T(8,128)(2,1)}, u32[]{:S(2)}, u32[]{:S(2)}) collective-permute-start(bf16[256,1024]{1,0:T(8,128)(2,1)} %get-tuple-element.110), channel_id=1, source_target_pairs={{0,2},{2,0},{1,3},{3,1},{4,6},{6,4},{5,7},{7,5},{8,10},{10,8},{9,1... | collective-permute-start | bytes 1572872 | tf_op jit(solution)/shard_map/ppermute | solution.py:35
  192.0 25.3 %collective-permute-start.30 = (bf16[256,1024]{1,0:T(8,128)(2,1)}, bf16[256,1024]{1,0:T(8,128)(2,1)}, u32[]{:S(2)}, u32[]{:S(2)}) collective-permute-start(bf16[256,1024]{1,0:T(8,128)(2,1)} %relay.5), channel_id=1, source_target_pairs={{0,16},{16,0},{1,17},{17,1},{2,18},{18,2},{3,19},{19,3},{4,20},{20... | collective-permute-start | bytes 1572872 | tf_op jit(solution)/shard_map/ppermute | solution.py:35
  193.5 13.9 %collective-permute-start.32 = (bf16[16,1024]{1,0:T(8,128)(2,1)}, bf16[16,1024]{1,0:T(8,128)(2,1)}, u32[]{:S(2)}, u32[]{:S(2)}) collective-permute-start(bf16[16,1024]{1,0:T(8,128)(2,1)} %rim.3), channel_id=1, source_target_pairs={{0,2},{2,4},{4,6},{6,8},{8,10},{10,12},{12,14},{1,3},{3,5},{5,7},{... | collective-permute-start | bytes 98312 | tf_op jit(solution)/shard_map/ppermute | solution.py:225
  212.3 15.4 %collective-permute-start.42 = (bf16[128,1024]{1,0:T(8,128)(2,1)}, bf16[128,1024]{1,0:T(8,128)(2,1)S(1)}, u32[]{:S(2)}, u32[]{:S(2)}) collective-permute-start(bf16[128,1024]{1,0:T(8,128)(2,1)} %get-tuple-element.139), channel_id=1, source_target_pairs={{0,2},{2,0},{4,6},{6,4},{8,10},{10,8},{12,14},{14,12},{1,3},{3,1},... | collective-permute-start | bytes 786440 | tf_op jit(solution)/shard_map/ppermute | solution.py:35
  (62 other events, 532.3 us)

commit v4 on v3

--- a/solution.py
+++ b/solution.py
@@ -121,13 +121,15 @@
     return swapped(weight, "chip", 1), swapped(weight, "chip", 2)
 
 
-def corner_halves(straight):
-    half = straight[0].shape[0] // 2
-    return straight[1][:half], straight[0][half:]
-
-
-def sent_on(halves):
-    return swapped(halves[0], "chip", 1), swapped(halves[1], "chip", 2)
+def corner_parts(straight, each):
+    rows = straight[0].shape[0] // (2 * each)
+    cut = lambda a, i: a[i * rows : (i + 1) * rows]
+    return [cut(straight[1], i) for i in range(each)] + [cut(straight[0], each + i) for i in range(each)]
+
+
+def sent_on(parts):
+    each = len(parts) // 2
+    return [swapped(a, "chip", 1) for a in parts[:each]] + [swapped(a, "chip", 2) for a in parts[each:]]
 
 
 def coded(part, heads):
@@ -141,13 +143,8 @@
 
 def multiply_kernel(heads, with_steps, pieces, rows_ref, *refs):
     weights, (first_ref, second_ref, sent_ref, kept_ref) = refs[:pieces], refs[pieces:]
-    at = 0
-    total = None
-    for weight in weights:
-        depth = weight.shape[0]
-        term = jnp.dot(rows_ref[:, at : at + depth], weight[...], preferred_element_type=F32)
-        total = term if total is None else total + term
-        at += depth
+    joined = jnp.concatenate([weight[...] for weight in weights], axis=0)
+    total = jnp.dot(rows_ref[...], joined, preferred_element_type=F32)
     half = total.shape[0] // 4
     kept_ref[0] = total[:half]
     kept_ref[1] = total[2 * half : 3 * half]
@@ -162,7 +159,7 @@
 
 def multiplied(rows, weights, heads, with_steps):
     width = weights[0].shape[1]
-    tile = next(t for t in (256, 384, 128) if width % t == 0)
+    tile = next(t for t in (512, 384, 128) if width % t == 0)
     half = rows.shape[0] // 4
     sent = lambda count: jax.ShapeDtypeStruct((count, width), BF16)
     return call(
@@ -243,12 +240,12 @@
     count, width = out_ref.shape
     out_ref[...] = convolved(width, kept, got_c, got_f, rim, taps, padded)
     logits = kept[0, :, width:] + decoded(got_c[:, width:].astype(F32), heads) + decoded(got_f[:, width:].astype(F32), heads)
-    steps = jax.nn.softplus(logits + bias[...])
+    steps = jax.nn.softplus(logits[:, :heads] + bias[...])
     row = lax.broadcasted_iota(jnp.int32, (SPAN, SPAN), 0)
     col = lax.broadcasted_iota(jnp.int32, (SPAN, SPAN), 1)
     causal = jnp.where(row >= col, 1.0, 0.0)
     groups, per_group = cum_ref.shape[0], cum_ref.shape[2]
-    through = jnp.zeros((1, LANES), F32)
+    through = jnp.zeros((1, heads), F32)
     for at in range(0, count, SPAN):
         span = slice(at, at + SPAN)
         steps_b = steps[span, :]
@@ -256,12 +253,13 @@
             causal, -steps_b * rate[...], precision=lax.Precision.HIGHEST, preferred_element_type=F32
         )
         through = through + cum[SPAN - 1 : SPAN, :]
-        cum_t_ref[:, span] = jnp.transpose(cum)[:heads]
-        steps_t_ref[:, span] = jnp.transpose(steps_b)[:heads]
+        cum_t_ref[:, span] = jnp.transpose(cum)
+        steps_t_ref[:, span] = jnp.transpose(steps_b)
         for g in range(groups):
             cum_ref[g, span, :] = cum[:, g * per_group : (g + 1) * per_group]
             steps_ref[g, span, :] = steps_b[:, g * per_group : (g + 1) * per_group]
-    decay_ref[...] = jnp.exp(through)[:, :heads]
+    for g in range(groups):
+        decay_ref[g] = jnp.exp(through)[:, g * per_group : (g + 1) * per_group]
 
 
 def pairwise(columns, first):
@@ -275,7 +273,7 @@
 
 
 def mix_kernel(
-    kept, got_c, got_f, rim, taps, keys, reads, cum_g, steps_g, cum_t, steps_t, skip, y_ref, early_ref, total_ref, sent_ref, padded
+    kept, got_c, got_f, rim, taps, keys, reads, cum_g, steps_g, cum_t, steps_t, skip, decay, y_ref, early_ref, total_ref, decays_ref, sent_ref, padded
 ):
     width = y_ref.shape[1]
     values = convolved(width, kept, got_c, got_f, rim, taps, padded)
@@ -285,6 +283,7 @@
     col = lax.broadcasted_iota(jnp.int32, (SPAN, SPAN), 1)
     causal = row >= col
     lane = lax.broadcasted_iota(jnp.int32, (SPAN, 2 * P_SIZE), 1)
+    gain = over_channels(skip[0])
     state = None
     for at in range(0, y_ref.shape[0], SPAN):
         span = slice(at, at + SPAN)
@@ -305,7 +304,7 @@
             both = jnp.dot(jnp.concatenate(two, axis=0), values_h, preferred_element_type=F32)
             inner = jnp.where(lane < P_SIZE, both[:SPAN], both[SPAN:])
             wide = values_h.astype(F32)
-            y_ref[span, chans] = inner + skip[0:1, chans] * wide
+            y_ref[span, chans] = inner + gain[:, chans] * wide
             scaled.append((wide * pairwise(reach, head)).astype(BF16))
         fresh = lax.dot_general(
             keys_b, jnp.concatenate(scaled, axis=1), (((0,), (0,)), ((), ())), preferred_element_type=F32
@@ -314,22 +313,42 @@
         if at + SPAN < y_ref.shape[0]:
             early_ref[at // SPAN] = fresh
     total_ref[...] = state
-    sent_ref[...] = state.astype(BF16)
-
-
-def combine_kernel(level, scales, total, other, before, total_ref, sent_ref, before_ref):
-    gain, keep, take = (scales[3 * level + i : 3 * level + i + 1, :] for i in range(3))
-    come = other[...].astype(F32)
-    fresh = gain * come
-    before_ref[...] = fresh if before is None else before[...] + fresh
-    joint = keep * total[...] + take * come
+    wide = over_channels(decay[0])
+    decays_ref[0:1, :] = wide
+    decays_ref[1:2, :] = jnp.ones_like(wide)
+    pack_state(sent_ref, state, wide)
+
+
+def pack_state(sent_ref, state, decay):
+    sent_ref[:N, :] = state.astype(BF16)
+    high = decay.astype(BF16).astype(F32)
+    row = lax.broadcasted_iota(jnp.int32, (RIM, decay.shape[1]), 0)
+    sent_ref[N:, :] = jnp.where(row == 0, high, jnp.where(row == 1, decay - high, 0.0)).astype(BF16)
+
+
+def unpack_state(got_ref):
+    rows = got_ref[N:, :].astype(F32)
+    return got_ref[:N, :].astype(F32), rows[0:1, :] + rows[1:2, :]
+
+
+def combine_kernel(level, place_ref, total, decays, other, *refs):
+    before, (total_ref, decays_ref, sent_ref, before_ref) = refs[:-4], refs[-4:]
+    come, decay = unpack_state(other)
+    whole, part = decays[0:1, :], decays[1:2, :]
+    upper = (place_ref[0] >> level) & 1 == 1
+    fresh = jnp.where(upper, part, 0.0) * come
+    before_ref[...] = before[0][...] + fresh if before else fresh
+    joint = jnp.where(upper, 1.0, decay) * total[...] + jnp.where(upper, whole, 1.0) * come
     total_ref[...] = joint
-    sent_ref[...] = joint.astype(BF16)
-
-
-def read_kernel(level, y, reads, cum_g, early, scales, before, other, *refs):
+    decays_ref[0:1, :] = whole * decay
+    decays_ref[1:2, :] = jnp.where(upper, decay * part, part)
+    pack_state(sent_ref, joint, whole * decay)
+
+
+def read_kernel(level, place_ref, y, reads, cum_g, early, decays, before, other, *refs):
     out_ref = refs[-1]
-    state = before[...] + scales[3 * level : 3 * level + 1, :] * other[...].astype(F32)
+    upper = (place_ref[0] >> level) & 1 == 1
+    state = before[...] + jnp.where(upper, decays[1:2, :], 0.0) * unpack_state(other)[0]
     cum = cum_g[0]
     for at in range(0, out_ref.shape[0], SPAN):
         span = slice(at, at + SPAN)
@@ -340,46 +359,21 @@
             state = over_channels(jnp.exp(cum_b[SPAN - 1 : SPAN, :])) * state + early[at // SPAN]
 
 
-def prefix_scales(decay):
-    place = lax.axis_index(SEQ)
-    count = lax.axis_size(SEQ)
-    before = jnp.ones_like(decay)
-    total = decay
-    rows = []
-    by = 1
-    while by < count:
-        other = swapped(total, SEQ, by)
-        upper = (place & by) != 0
-        rows += [jnp.where(upper, before, 0.0), jnp.where(upper, 1.0, other), jnp.where(upper, total, 1.0)]
-        before = jnp.where(upper, other * before, before)
-        total = total * other
-        by *= 2
-    scales = jnp.stack(rows)
-    return jnp.broadcast_to(scales[:, :, None], scales.shape + (P_SIZE,)).reshape(len(rows), -1)
-
-
-def combined(level, scales, total, other, before, first):
-    width, wide = total.shape[1], total.shape[1] // first[1]
-    block = pl.BlockSpec((N, wide), lambda i: (0, i))
-    kernel = functools.partial(combine_kernel, level)
-    if before is None:
-        kernel = lambda scales, total, other, *outs: combine_kernel(level, scales, total, other, None, *outs)
+def combined(level, place, total, decays, other, before, groups):
+    width = total.shape[1] // groups
+    block = lambda rows: pl.BlockSpec((rows, width), lambda i: (0, i))
+    shape = lambda rows, dtype: jax.ShapeDtypeStruct((rows, total.shape[1]), dtype)
     return call(
-        kernel,
+        functools.partial(combine_kernel, level),
         "combine",
-        (
-            jax.ShapeDtypeStruct(total.shape, F32),
-            jax.ShapeDtypeStruct(total.shape, BF16),
-            jax.ShapeDtypeStruct(total.shape, F32),
-        ),
+        (shape(N, F32), shape(8, F32), shape(N + RIM, BF16), shape(N, F32)),
         flops=6 * total.size,
         moved=20 * total.size,
         vmem=12,
-        grid=(first[1],),
-        in_specs=[pl.BlockSpec((scales.shape[0], wide), lambda i: (0, first[0] + i))]
-        + [block] * (2 if before is None else 3),
-        out_specs=[block] * 3,
-    )(scales, total, other, *(() if before is None else (before,)))
+        grid=(groups,),
+        in_specs=[SMEM, block(N), block(8), block(N + RIM)] + [block(N)] * len(before),
+        out_specs=[block(N), block(8), block(N + RIM), block(N)],
+    )(place, total, decays, other, *before)
 
 
 def body(
@@ -456,25 +450,26 @@
 
     if plane and two_shares:
         early = [weight_early, *sent_straight(weight_early)]
-        early += sent_on(corner_halves(early[1:]))
+        early += sent_on(corner_parts(early[1:], 1))
         own_t = swapped(own, "tp")
-        own_c, own_tc = swapped(own, "core"), swapped(own_t, "core")
         far_sent = after(far_sent, own_t)
         sent_t = swapped(far_sent, "tp")
         got, got_t = swapped(far_sent, "core"), swapped(sent_t, "core")
-        far_kept = after(far_kept, (own_c, own_tc, got_t, weight_late))
+        far_kept = after(far_kept, (got_t, weight_bc, weight_late))
+        own, own_t = after((own, own_t), far_kept)
+        own_c, own_tc = swapped(own, "core"), swapped(own_t, "core")
         kept_t = swapped(far_kept, "tp")
         weight_bc = after(weight_bc, (early[3:], far_kept))
         bc = [weight_bc, *sent_straight(weight_bc)]
         rows = token_rows(at, far_kept, kept_t, got, got_t, own, own_t, own_c, own_tc)
         part, back = partial_sums(rows, early, False)
-        bc += sent_on(corner_halves(after(bc[1:], back)))
+        bc += sent_on(corner_parts(after(bc[1:], back), 1))
         got = swapped(back, "fsdp")
-        weight_late = after(weight_late, (back, bc[3:]))
+        weight_late = after(weight_late, (back, bc[1:3]))
         part_bc, back_bc = partial_sums(rows, bc, True, got)
         got_bc = swapped(after(back_bc, got), "fsdp")
         straight = sent_straight(weight_late)
-        corners = sent_on(after(corner_halves(straight), got))
+        corners = sent_on(after(corner_parts(straight, 2), back_bc))
         part_late, back_late = partial_sums(rows, after([weight_late, *straight, *corners], back_bc), False)
         got_late = swapped(after(back_late, got_bc), "fsdp")
         got_bc = after(got_bc, back_late)
@@ -501,20 +496,21 @@
     whole_of = lambda *shape: pl.BlockSpec(shape, lambda i: (0,) * len(shape))
     by_group = (groups_here, tok_count, per_group)
     by_head = (heads_here, tok_count)
+    by_decay = (groups_here, 1, per_group)
     conv_out, cum_g, steps_g, cum_t, steps_t, decay = call(
         functools.partial(state_proj_kernel, heads_here),
         "state_proj",
         (jax.ShapeDtypeStruct((tok_count, width_bc), BF16),)
-        + tuple(jax.ShapeDtypeStruct(a, F32) for a in (by_group, by_group, by_head, by_head, (1, heads_here))),
+        + tuple(jax.ShapeDtypeStruct(a, F32) for a in (by_group, by_group, by_head, by_head, by_decay)),
         moved=10 * tok_count * width_bc,
         grid=(1,),
-        in_specs=specs_of(width_bc + LANES) + [whole_of(CONV, width_bc)] + [whole_of(1, LANES)] * 2,
-        out_specs=[whole_of(*a) for a in ((tok_count, width_bc), by_group, by_group, by_head, by_head, (1, heads_here))],
+        in_specs=specs_of(width_bc + LANES) + [whole_of(CONV, width_bc)] + [whole_of(1, heads_here)] * 2,
+        out_specs=[whole_of(*a) for a in ((tok_count, width_bc), by_group, by_group, by_head, by_head, by_decay)],
         scratch_shapes=[pltpu.VMEM((tok_count + 8, width_bc), F32)],
-    )(*part_bc, rows_before(*part_bc), conv_bc.reshape(CONV, width_bc), jnp.pad(dt_bias, (0, fill))[None], jnp.pad(decay_rate, (0, fill))[None])
-    scales = prefix_scales(decay[0])
-    skip = jnp.repeat(skip_gain, P_SIZE)[None, :]
-    levels = scales.shape[0] // 3
+    )(*part_bc, rows_before(*part_bc), conv_bc.reshape(CONV, width_bc), dt_bias[None], decay_rate[None])
+    skip = skip_gain.reshape(by_decay)
+    levels = count.bit_length() - 1
+    seq_place = (2 * lax.axis_index("chip") + lax.axis_index("core")).astype(jnp.int32).reshape(1)
 
     result = None
     for first, groups, part in zip((0, early_groups), (early_groups, len(late)), parts):
@@ -526,34 +522,37 @@
         cols_all = lambda rows: pl.BlockSpec((rows, width), lambda i: (0, first + i))
         heads_g = pl.BlockSpec((1, tok_count, per_group), lambda i: (first + i, 0, 0))
         heads_t = pl.BlockSpec((per_group, tok_count), lambda i: (first + i, 0))
+        heads_1 = pl.BlockSpec((1, 1, per_group), lambda i: (first + i, 0, 0))
         keys = pl.BlockSpec((tok_count, N), lambda i: (0, first + i))
         reads = pl.BlockSpec((tok_count, N), lambda i: (0, groups_here + first + i))
         early_spec = pl.BlockSpec((blocks - 1, N, width), lambda i: (0, 0, i))
-        y, early, total, sent = call(
+        y, early, total, decays, sent = call(
             mix_kernel,
             "mix",
             (
                 jax.ShapeDtypeStruct((tok_count, groups * width), F32),
                 jax.ShapeDtypeStruct((blocks - 1, N, groups * width), F32),
                 jax.ShapeDtypeStruct((N, groups * width), F32),
-                jax.ShapeDtypeStruct((N, groups * width), BF16),
+                jax.ShapeDtypeStruct((8, groups * width), F32),
+                jax.ShapeDtypeStruct((N + RIM, groups * width), BF16),
             ),
             flops=8 * tok_count * N * width * groups,
             moved=14 * tok_count * width * groups,
             grid=grid,
-            in_specs=specs_of(width)
-            + [cols_all(CONV), keys, reads, heads_g, heads_g, heads_t, heads_t, cols_all(1)],
-            out_specs=[cols(tok_count), early_spec, cols(N), cols(N)],
+            in_specs=specs_of(width) + [cols_all(CONV), keys, reads, heads_g, heads_g, heads_t, heads_t, heads_1, heads_1],
+            out_specs=[cols(tok_count), early_spec, cols(N), cols(8), cols(N + RIM)],
             scratch_shapes=[pltpu.VMEM((tok_count + 8, width), F32)],
-        )(*part, conv_proj, conv_out, conv_out, cum_g, steps_g, cum_t, steps_t, skip)
-        before = None
-        first_total = total
+        )(*part, conv_proj, conv_out, conv_out, cum_g, steps_g, cum_t, steps_t, skip, decay)
+        before = ()
+        first_total = None
         for level in range(levels - 1):
             other = swapped(sent, SEQ, 1 << level)
-            total, sent, before = combined(level, scales, total, other, before, (first, groups))
+            total, decays, sent, fresh = combined(level, seq_place, total, decays, other, before, groups)
+            before = (fresh,)
+            first_total = total if first_total is None else first_total
         other = swapped(sent, SEQ, 1 << (levels - 1))
-        operands = [y, conv_out, cum_g, early, scales, before, other]
-        specs = [cols(tok_count), reads, heads_g, early_spec, cols_all(scales.shape[0]), cols(N), cols(N)]
+        operands = [seq_place, y, conv_out, cum_g, early, decays, *before, other]
+        specs = [SMEM, cols(tok_count), reads, heads_g, early_spec, cols(8), cols(N), cols(N + RIM)]
         alias = {}
         if result is not None:
             operands.append(result)

time: 256 us -> 263 us (1.027)
  waiting for transfers between devices: 108 us -> 115 us
    ppermute x42 -> x41, waiting for transfers between devices: 108 us -> 114 us  [swapped(): lax.ppermute(part, axis, [(i, i ^ by) for i in range(lax.axis_size(axis))])]
    unnamed x85 -> x89, local copies, waits for them, and re-layouts: 11 us -> 14.9 us
    ppermute x42 -> x41, starting transfers between devices: 43.2 us -> 43.9 us  [swapped(): lax.ppermute(part, axis, [(i, i ^ by) for i in range(lax.axis_size(axis))])]
  transfers between devices with their start and end apart: 45 -> 44, of which waited for: 20 -> 22; matrix products, arithmetic and copies ran while one was open for 5% -> 4% of each run, Pallas kernels for 25% -> 22%
where the time goes in v4:
time: 263 us; the launch traced here: 262 us
  waiting for transfers between devices  115 us (44%)
  Pallas kernels  67.9 us (26%)
  starting transfers between devices  50.3 us (19%)
  local copies, waits for them, and re-layouts  20.5 us (8%)
  other arithmetic  5.35 us (2%)
  between operations  3.08 us (1%)
    ppermute x41, waiting for transfers between devices, swapped(): lax.ppermute(part, axis, [(i, i ^ by) for i in range(lax.axis_size(axis))])  114 us
    ppermute x41, starting transfers between devices, swapped(): lax.ppermute(part, axis, [(i, i ^ by) for i in range(lax.axis_size(axis))])  43.9 us
    pallas_call x3, Pallas kernels, multiplied(): call(functools.partial(multiply_kernel, heads, with_steps, len(weights)),...  29.4 us
    unnamed x89, local copies, waits for them, and re-layouts  14.9 us
    pallas_call x2, Pallas kernels, body(): call(mix_kernel, 'mix', (jax.ShapeDtypeStruct((tok_count, groups * width)...  10.1 us
    pallas_call x2, Pallas kernels, sampled_cols(): call(functools.partial(sample_kernel, count), 'sample', jax.ShapeDtypeStr...  9.24 us
    ppermute x3, starting transfers between devices, rows_before(): lax.ppermute(rim, SEQ, [(i, i + 1) for i in range(lax.axis_size(SEQ) - 1)])  6.39 us
    convert_element_type x1, other arithmetic, sampled(): return accum.astype(BF16)  5.35 us
  transfers between devices with their start and end apart: 44, of which 22 were waited for; matrix products, arithmetic and copies ran while one was open for 4% of the time, Pallas kernels for 22%

profile of v4, /device:TPU:0, one launch (start us, length us, event | category | flops | bytes accessed | tf_op | source)
XLA Modules:
  0.0 262.1 jit_solution(7943202458209403668)
XLA Ops:
  0.6 3.1 %cut_tokens.1 = (bf16[128,2048]{1,0:T(8,128)(2,1)}, bf16[128,2048]{1,0:T(8,128)(2,1)}, bf16[256,2048]{1,0:T(8,128)(2,1)}) custom-call(s32[7]{0:T(128)} %stack.31.at_ref, bf16[128,8192]{1,0:T(8,128)(2,1)} %tokens_ref.1), custom_call_target="tpu_custom_call" | custom-call | bytes 83886 | tf_op jit(solution)/shard_map/cut_tokens/pallas_call | solution.py:415
  3.7 3.0 %collective-permute-start.2 = (bf16[256,2048]{1,0:T(8,128)(2,1)}, bf16[256,2048]{1,0:T(8,128)(2,1)S(1)}, u32[]{:S(2)}, u32[]{:S(2)}) collective-permute-start(bf16[256,2048]{1,0:T(8,128)(2,1)} %get-tuple-element.95.refs_4_), channel_id=1, source_target_pairs={{0,1},{1,0},{2,3},{3,2},{4,5},{5,4},{6,7},{7,6},{8,9},{9,8},{10,11... | collective-permute-start | bytes 3145736 | tf_op jit(solution)/shard_map/ppermute | solution.py:35
  6.7 4.6 %sample.3.refs_0_ = bf16[512,1024]{1,0:T(8,128)(2,1)} custom-call(f32[4]{0:T(128)} %coef_ref.3, bf16[512,2048]{1,0:T(8,128)(2,1)} %mean_ref.1, bf16[4,512,2048]{2,1,0:T(8,128)(2,1)} %devs_ref.3), custom_call_target="tpu_custom_call" | custom-call | bytes 125829 | tf_op jit(solution)/shard_map/sample/pallas_call | solution.py:90
  12.9 2.6 collective-permute-start
  17.0 23.6 %collective-permute-done = bf16[128,2048]{1,0:T(8,128)(2,1)} collective-permute-done((bf16[128,2048]{1,0:T(8,128)(2,1)S(1)}, bf16[128,2048]{1,0:T(8,128)(2,1)}, u32[]{:S(2)}, u32[]{:S(2)}) %collective-permute-start) | collective-permute-done | bytes 524320 | tf_op jit(solution)/shard_map/ppermute | solution.py:35
  41.3 2.9 %collective-permute-start.3 = (bf16[128,2048]{1,0:T(8,128)(2,1)}, bf16[128,2048]{1,0:T(8,128)(2,1)}, u32[]{:S(2)}, u32[]{:S(2)}) collective-permute-start(bf16[128,2048]{1,0:T(8,128)(2,1)} %collective-permute-done), channel_id=1, source_target_pairs={{0,1},{1,0},{2,3},{3,2},{4,5},{5,4},{6,7},{7,6},{8,9},{9,8},{10,11... | collective-permute-start | bytes 1572872 | tf_op jit(solution)/shard_map/ppermute | solution.py:35
  44.2 4.6 %sample.2.refs_0_ = bf16[512,1024]{1,0:T(8,128)(2,1)} custom-call(f32[4]{0:T(128)} %coef_ref.3, bf16[512,2048]{1,0:T(8,128)(2,1)} %mean_ref.1, bf16[4,512,2048]{2,1,0:T(8,128)(2,1)} %devs_ref.3), custom_call_target="tpu_custom_call" | custom-call | bytes 125829 | tf_op jit(solution)/shard_map/sample/pallas_call | solution.py:90
  56.9 5.4 %fusion = bf16[512,2,512]{2,1,0:T(2,128)(2,1)S(1)} fusion(bf16[512,2,512]{2,1,0:T(2,128)(2,1)S(1)} %copy-done.27, bf16[4,512,2,512]{3,2,1,0:T(2,128)(2,1)} %param.16, f32[]{:T(128)} %bitcast.14, f32[]{:T(128)} %bitcast.12, f32[]{:T(128)} %bitcast.10, f32[]{:T(128)} %bitcast.8), kind=kLoop, calls=%fused_computation.1 | loop fusion | flops 7340032 | bytes 6291472 | tf_op jit(solution)/shard_map/convert_element_type | solution.py:110
  63.2 13.7 %collective-permute-done.1.refs_0_ = bf16[128,2048]{1,0:T(8,128)(2,1)S(1)} collective-permute-done((bf16[128,2048]{1,0:T(8,128)(2,1)}, bf16[128,2048]{1,0:T(8,128)(2,1)S(1)}, u32[]{:S(2)}, u32[]{:S(2)}) %collective-permute-start.1) | collective-permute-done | bytes 524320 | tf_op jit(solution)/shard_map/ppermute | solution.py:35
  80.6 13.3 %collective-permute-done.5.refs_1_ = bf16[128,2048]{1,0:T(8,128)(2,1)S(1)} collective-permute-done((bf16[128,2048]{1,0:T(8,128)(2,1)S(1)}, bf16[128,2048]{1,0:T(8,128)(2,1)S(1)}, u32[]{:S(2)}, u32[]{:S(2)}) %collective-permute-start.5) | collective-permute-done | bytes 524320 | tf_op jit(solution)/shard_map/ppermute | solution.py:35
  96.8 8.9 %multiply.3 = (bf16[128,1024]{1,0:T(8,128)(2,1)}, bf16[128,1024]{1,0:T(8,128)(2,1)}, bf16[256,1024]{1,0:T(8,128)(2,1)}, f32[2,256,1024]{2,1,0:T(8,128)}) custom-call(bf16[1024,2048]{1,0:T(8,128)(2,1)} %copy-done, bf16[512,1024]{1,0:T(8,128)(2,1)} %sample.3.refs_0_, bf16[512,1024]{1,0:T(8,128)(2,1)} %copy-done.25, bf16[512,1024]{1,0:T(8,128)(2,1)} %copy-done.24, ...), custom_call_target="tpu_custom_call" | custom-call | flops 85899344 | bytes 230686 | tf_op jit(solution)/shard_map/multiply/pallas_call | solution.py:165
  116.2 31.2 %collective-permute-done.20.refs_4_ = bf16[256,1152]{1,0:T(8,128)(2,1)S(1)} collective-permute-done((bf16[256,1152]{1,0:T(8,128)(2,1)S(1)}, bf16[256,1152]{1,0:T(8,128)(2,1)S(1)}, u32[]{:S(2)}, u32[]{:S(2)}) %collective-permute-start.20) | collective-permute-done | bytes 589856 | tf_op jit(solution)/shard_map/ppermute | solution.py:35
  148.3 11.6 %multiply.4 = (bf16[128,1152]{1,0:T(8,128)(2,1)}, bf16[128,1152]{1,0:T(8,128)(2,1)}, bf16[256,1152]{1,0:T(8,128)(2,1)}, f32[2,256,1152]{2,1,0:T(8,128)}) custom-call(bf16[1024,2048]{1,0:T(8,128)(2,1)} %copy-done, bf16[512,1152]{1,0:T(8,128)(2,1)} %copy-done.9, bf16[512,1152]{1,0:T(8,128)(2,1)} %collective-permute-done.15.refs_1_, ...), custom_call_target="tpu_custom_call" | custom-call | flops 96636768 | bytes 249036 | tf_op jit(solution)/shard_map/multiply/pallas_call | solution.py:165
  170.9 4.8 %collective-permute-done.24.refs_3_ = bf16[128,1024]{1,0:T(8,128)(2,1)S(1)} collective-permute-done((bf16[128,1024]{1,0:T(8,128)(2,1)S(1)}, bf16[128,1024]{1,0:T(8,128)(2,1)S(1)}, u32[]{:S(2)}, u32[]{:S(2)}) %collective-permute-start.24) | collective-permute-done | bytes 262176 | tf_op jit(solution)/shard_map/ppermute | solution.py:35
  175.7 4.8 %collective-permute-done.25.refs_4_ = bf16[128,1024]{1,0:T(8,128)(2,1)S(1)} collective-permute-done((bf16[128,1024]{1,0:T(8,128)(2,1)S(1)}, bf16[128,1024]{1,0:T(8,128)(2,1)S(1)}, u32[]{:S(2)}, u32[]{:S(2)}) %collective-permute-start.25) | collective-permute-done | bytes 262176 | tf_op jit(solution)/shard_map/ppermute | solution.py:35
  182.7 8.9 %multiply.5 = (bf16[128,1024]{1,0:T(8,128)(2,1)}, bf16[128,1024]{1,0:T(8,128)(2,1)}, bf16[256,1024]{1,0:T(8,128)(2,1)}, f32[2,256,1024]{2,1,0:T(8,128)}) custom-call(bf16[1024,2048]{1,0:T(8,128)(2,1)} %copy-done, bf16[512,1024]{1,0:T(8,128)(2,1)} %sample.2.refs_0_, bf16[512,1024]{1,0:T(8,128)(2,1)} %collective-permute-done.17.refs_1_, ...), custom_call_target="tpu_custom_call" | custom-call | flops 85899344 | bytes 230686 | tf_op jit(solution)/shard_map/multiply/pallas_call | solution.py:165
  202.7 2.7 %collective-permute-start.34 = (bf16[16,1024]{1,0:T(8,128)(2,1)S(1)}, bf16[16,1024]{1,0:T(8,128)(2,1)S(1)}, u32[]{:S(2)}, u32[]{:S(2)}) collective-permute-start(bf16[16,1024]{1,0:T(8,128)(2,1)S(1)} %rim.3), channel_id=1, source_target_pairs={{0,2},{2,4},{4,6},{6,8},{8,10},{10,12},{12,14},{1,3},{3,5},{5,7},{... | collective-permute-start | bytes 98312 | tf_op jit(solution)/shard_map/ppermute | solution.py:222
  207.2 4.6 %state_proj.1 = (bf16[256,1024]{1,0:T(8,128)(2,1)}, f32[4,256,8]{2,1,0:T(8,128)}, f32[4,256,8]{2,1,0:T(8,128)}, f32[32,256]{1,0:T(8,128)}, f32[32,256]{1,0:T(8,128)}, /*index=5*/f32[4,1,8]{2,1,0:T(1,128)}) custom-call(f32[2,256,1152]{2,1,0:T(8,128)} %get-tuple-element.106.kept_ref.kept, bf16[256,1152]{1,0:T(8,128)(2,1)} %copy-done.11, ...), custom_call_target="tpu_custom_call" | custom-call | bytes 52428 | tf_op jit(solution)/shard_map/state_proj/pallas_call | solution.py:500
  212.4 5.1 %mix.2 = (f32[256,1024]{1,0:T(8,128)}, f32[1,128,1024]{2,1,0:T(8,128)}, f32[128,1024]{1,0:T(8,128)}, f32[8,1024]{1,0:T(8,128)}, bf16[144,1024]{1,0:T(8,128)(2,1)}) custom-call(f32[2,256,1024]{2,1,0:T(8,128)} %get-tuple-element.97.kept_ref.kept, bf16[256,1024]{1,0:T(8,128)(2,1)} %collective-permute-done.33.got_c, bf16[256,1024]{1,0:T(8,128)(2,1)} %copy-done.12, ...), custom_call_target="tpu_custom_call" | custom-call | flops 5368709 | bytes 73400 | tf_op jit(solution)/shard_map/mix/pallas_call | solution.py:529
  227.4 5.0 %mix.3 = (f32[256,1024]{1,0:T(8,128)}, f32[1,128,1024]{2,1,0:T(8,128)}, f32[128,1024]{1,0:T(8,128)}, f32[8,1024]{1,0:T(8,128)}, bf16[144,1024]{1,0:T(8,128)(2,1)}) custom-call(f32[2,256,1024]{2,1,0:T(8,128)} %get-tuple-element.146.kept_ref.kept, bf16[256,1024]{1,0:T(8,128)(2,1)} %collective-permute-done.30.got_c, ...), custom_call_target="tpu_custom_call" | custom-call | flops 5368709 | bytes 73400 | tf_op jit(solution)/shard_map/mix/pallas_call | solution.py:529
  239.9 3.9 %collective-permute-done.42.other = bf16[144,1024]{1,0:T(8,128)(2,1)S(1)} collective-permute-done((bf16[144,1024]{1,0:T(8,128)(2,1)S(1)}, bf16[144,1024]{1,0:T(8,128)(2,1)S(1)}, u32[]{:S(2)}, u32[]{:S(2)}) %collective-permute-start.42) | collective-permute-done | bytes 294944 | tf_op jit(solution)/shard_map/ppermute | solution.py:35
  244.8 2.8 %collective-permute-start.43 = (bf16[144,1024]{1,0:T(8,128)(2,1)S(1)}, bf16[144,1024]{1,0:T(8,128)(2,1)S(1)}, u32[]{:S(2)}, u32[]{:S(2)}) collective-permute-start(bf16[144,1024]{1,0:T(8,128)(2,1)S(1)} %get-tuple-element.168), channel_id=1, source_target_pairs={{0,8},{2,10},{4,12},{6,14},{8,0},{10,2},{12,4},{14,6},{1,9},{3,11}... | collective-permute-start | bytes 884744 | tf_op jit(solution)/shard_map/ppermute | solution.py:35
  250.9 2.6 collective-permute-start.41
  255.8 4.5 %collective-permute-done.41.other = bf16[144,1024]{1,0:T(8,128)(2,1)S(1)} collective-permute-done((bf16[144,1024]{1,0:T(8,128)(2,1)S(1)}, bf16[144,1024]{1,0:T(8,128)(2,1)S(1)}, u32[]{:S(2)}, u32[]{:S(2)}) %collective-permute-start.41) | collective-permute-done | bytes 294944 | tf_op jit(solution)/shard_map/ppermute | solution.py:35
  (186 shorter events, 80.9 us)
Async XLA Ops:
  3.7 37.6 %collective-permute-start.2 = (bf16[256,2048]{1,0:T(8,128)(2,1)}, bf16[256,2048]{1,0:T(8,128)(2,1)S(1)}, u32[]{:S(2)}, u32[]{:S(2)}) collective-permute-start(bf16[256,2048]{1,0:T(8,128)(2,1)} %get-tuple-element.95.refs_4_), channel_id=1, source_target_pairs={{0,1},{1,0},{2,3},{3,2},{4,5},{5,4},{6,7},{7,6},{8,9},{9,8},{10,11... | collective-permute-start | bytes 3145736 | tf_op jit(solution)/shard_map/ppermute | solution.py:35
  11.4 42.3 %collective-permute-start.10 = (bf16[512,1024]{1,0:T(8,128)(2,1)}, bf16[512,1024]{1,0:T(8,128)(2,1)S(1)}, u32[]{:S(2)}, u32[]{:S(2)}) collective-permute-start(bf16[512,1024]{1,0:T(8,128)(2,1)} %sample.3.refs_0_), channel_id=1, source_target_pairs={{0,8},{4,12},{8,0},{12,4},{1,9},{5,13},{9,1},{13,5},{2,10},{6,14},... | collective-permute-start | bytes 3145736 | tf_op jit(solution)/shard_map/ppermute | solution.py:35
  12.9 27.7 %collective-permute-start = (bf16[128,2048]{1,0:T(8,128)(2,1)S(1)}, bf16[128,2048]{1,0:T(8,128)(2,1)}, u32[]{:S(2)}, u32[]{:S(2)}) collective-permute-start(bf16[128,2048]{1,0:T(8,128)(2,1)S(1)} %copy-done.42), channel_id=1, source_target_pairs={{0,16},{16,0},{1,17},{17,1},{2,18},{18,2},{3,19},{19,3},{4,20},{20... | collective-permute-start | bytes 1572872 | tf_op jit(solution)/shard_map/ppermute | solution.py:35
  15.5 39.8 %collective-permute-start.9 = (bf16[512,1024]{1,0:T(8,128)(2,1)}, bf16[512,1024]{1,0:T(8,128)(2,1)S(1)}, u32[]{:S(2)}, u32[]{:S(2)}) collective-permute-start(bf16[512,1024]{1,0:T(8,128)(2,1)} %sample.3.refs_0_), channel_id=1, source_target_pairs={{0,4},{4,0},{8,12},{12,8},{1,5},{5,1},{9,13},{13,9},{2,6},{6,2},{1... | collective-permute-start | bytes 3145736 | tf_op jit(solution)/shard_map/ppermute | solution.py:35
  41.3 15.6 %collective-permute-start.3 = (bf16[128,2048]{1,0:T(8,128)(2,1)}, bf16[128,2048]{1,0:T(8,128)(2,1)}, u32[]{:S(2)}, u32[]{:S(2)}) collective-permute-start(bf16[128,2048]{1,0:T(8,128)(2,1)} %collective-permute-done), channel_id=1, source_target_pairs={{0,1},{1,0},{2,3},{3,2},{4,5},{5,4},{6,7},{7,6},{8,9},{9,8},{10,11... | collective-permute-start | bytes 1572872 | tf_op jit(solution)/shard_map/ppermute | solution.py:35
  52.1 24.8 %collective-permute-start.1 = (bf16[128,2048]{1,0:T(8,128)(2,1)}, bf16[128,2048]{1,0:T(8,128)(2,1)S(1)}, u32[]{:S(2)}, u32[]{:S(2)}) collective-permute-start(bf16[128,2048]{1,0:T(8,128)(2,1)} %get-tuple-element.89), channel_id=1, source_target_pairs={{0,16},{16,0},{1,17},{17,1},{2,18},{18,2},{3,19},{19,3},{4,20},{20... | collective-permute-start | bytes 1572872 | tf_op jit(solution)/shard_map/ppermute | solution.py:35
  53.7 23.8 %collective-permute-start.11 = (bf16[256,1024]{1,0:T(8,128)(2,1)S(1)}, bf16[256,1024]{1,0:T(8,128)(2,1)S(1)}, u32[]{:S(2)}, u32[]{:S(2)}) collective-permute-start(bf16[256,1024]{1,0:T(8,128)(2,1)S(1)} %slice.64), channel_id=1, source_target_pairs={{0,4},{4,0},{8,12},{12,8},{1,5},{5,1},{9,13},{13,9},{2,6},{6,2},{1... | collective-permute-start | bytes 1572872 | tf_op jit(solution)/shard_map/ppermute | solution.py:35
  55.3 22.2 %collective-permute-start.12 = (bf16[256,1024]{1,0:T(8,128)(2,1)S(1)}, bf16[256,1024]{1,0:T(8,128)(2,1)S(1)}, u32[]{:S(2)}, u32[]{:S(2)}) collective-permute-start(bf16[256,1024]{1,0:T(8,128)(2,1)S(1)} %slice.65), channel_id=1, source_target_pairs={{0,8},{4,12},{8,0},{12,4},{1,9},{5,13},{9,1},{13,5},{2,10},{6,14},... | collective-permute-start | bytes 1572872 | tf_op jit(solution)/shard_map/ppermute | solution.py:35
  56.9 20.1 %collective-permute-start.4 = (bf16[128,2048]{1,0:T(8,128)(2,1)}, bf16[128,2048]{1,0:T(8,128)(2,1)S(1)}, u32[]{:S(2)}, u32[]{:S(2)}) collective-permute-start(bf16[128,2048]{1,0:T(8,128)(2,1)} %collective-permute-done.3), channel_id=1, source_target_pairs={{0,2},{2,0},{1,3},{3,1},{4,6},{6,4},{5,7},{7,5},{8,10},{10,8},{9,1... | collective-permute-start | bytes 1572872 | tf_op jit(solution)/shard_map/ppermute | solution.py:35
  62.7 17.9 %collective-permute-start.6 = (bf16[128,2048]{1,0:T(8,128)(2,1)}, bf16[128,2048]{1,0:T(8,128)(2,1)S(1)}, u32[]{:S(2)}, u32[]{:S(2)}) collective-permute-start(bf16[128,2048]{1,0:T(8,128)(2,1)} %collective-permute-done), channel_id=1, source_target_pairs={{0,2},{2,0},{1,3},{3,1},{4,6},{6,4},{5,7},{7,5},{8,10},{10,8},{9,1... | collective-permute-start | bytes 1572872 | tf_op jit(solution)/shard_map/ppermute | solution.py:35
  77.0 17.0 %collective-permute-start.7 = (bf16[256,2048]{1,0:T(8,128)(2,1)S(1)}, bf16[256,2048]{1,0:T(8,128)(2,1)S(1)}, u32[]{:S(2)}, u32[]{:S(2)}) collective-permute-start(bf16[256,2048]{1,0:T(8,128)(2,1)S(1)} %copy-done.15), channel_id=1, source_target_pairs={{0,2},{2,0},{1,3},{3,1},{4,6},{6,4},{5,7},{7,5},{8,10},{10,8},{9,1... | collective-permute-start | bytes 3145736 | tf_op jit(solution)/shard_map/ppermute | solution.py:35
  77.0 16.9 %collective-permute-start.8 = (bf16[256,2048]{1,0:T(8,128)(2,1)S(1)}, bf16[256,2048]{1,0:T(8,128)(2,1)S(1)}, u32[]{:S(2)}, u32[]{:S(2)}) collective-permute-start(bf16[256,2048]{1,0:T(8,128)(2,1)S(1)} %collective-permute-done.2.refs_5_), channel_id=1, source_target_pairs={{0,2},{2,0},{1,3},{3,1},{4,6},{6,4},{5,7},{7,5},{8,10},{10,8},{9,1... | collective-permute-start | bytes 3145736 | tf_op jit(solution)/shard_map/ppermute | solution.py:35
  77.5 32.0 %collective-permute-start.16 = (bf16[512,1152]{1,0:T(8,128)(2,1)S(1)}, bf16[512,1152]{1,0:T(8,128)(2,1)}, u32[]{:S(2)}, u32[]{:S(2)}) collective-permute-start(bf16[512,1152]{1,0:T(8,128)(2,1)S(1)} %pack.1.refs_0_), channel_id=1, source_target_pairs={{0,8},{4,12},{8,0},{12,4},{1,9},{5,13},{9,1},{13,5},{2,10},{6,14},... | collective-permute-start | bytes 3538952 | tf_op jit(solution)/shard_map/ppermute | solution.py:35
  79.1 30.4 %collective-permute-start.15 = (bf16[512,1152]{1,0:T(8,128)(2,1)S(1)}, bf16[512,1152]{1,0:T(8,128)(2,1)}, u32[]{:S(2)}, u32[]{:S(2)}) collective-permute-start(bf16[512,1152]{1,0:T(8,128)(2,1)S(1)} %pack.1.refs_0_), channel_id=1, source_target_pairs={{0,4},{4,0},{8,12},{12,8},{1,5},{5,1},{9,13},{13,9},{2,6},{6,2},{1... | collective-permute-start | bytes 3538952 | tf_op jit(solution)/shard_map/ppermute | solution.py:35
  109.5 55.4 %collective-permute-start.18 = (bf16[512,1024]{1,0:T(8,128)(2,1)S(1)}, bf16[512,1024]{1,0:T(8,128)(2,1)S(1)}, u32[]{:S(2)}, u32[]{:S(2)}) collective-permute-start(bf16[512,1024]{1,0:T(8,128)(2,1)S(1)} %copy-done.23), channel_id=1, source_target_pairs={{0,8},{4,12},{8,0},{12,4},{1,9},{5,13},{9,1},{13,5},{2,10},{6,14},... | collective-permute-start | bytes 3145736 | tf_op jit(solution)/shard_map/ppermute | solution.py:35
  112.3 35.1 %collective-permute-start.20 = (bf16[256,1152]{1,0:T(8,128)(2,1)S(1)}, bf16[256,1152]{1,0:T(8,128)(2,1)S(1)}, u32[]{:S(2)}, u32[]{:S(2)}) collective-permute-start(bf16[256,1152]{1,0:T(8,128)(2,1)S(1)} %slice.63), channel_id=1, source_target_pairs={{0,8},{4,12},{8,0},{12,4},{1,9},{5,13},{9,1},{13,5},{2,10},{6,14},... | collective-permute-start | bytes 1769480 | tf_op jit(solution)/shard_map/ppermute | solution.py:35
  113.9 33.5 %collective-permute-start.19 = (bf16[256,1152]{1,0:T(8,128)(2,1)S(1)}, bf16[256,1152]{1,0:T(8,128)(2,1)}, u32[]{:S(2)}, u32[]{:S(2)}) collective-permute-start(bf16[256,1152]{1,0:T(8,128)(2,1)S(1)} %slice.62), channel_id=1, source_target_pairs={{0,4},{4,0},{8,12},{12,8},{1,5},{5,1},{9,13},{13,9},{2,6},{6,2},{1... | collective-permute-start | bytes 1769480 | tf_op jit(solution)/shard_map/ppermute | solution.py:35
  114.5 45.4 %collective-permute-start.21 = (bf16[256,1024]{1,0:T(8,128)(2,1)S(1)}, bf16[256,1024]{1,0:T(8,128)(2,1)S(1)}, u32[]{:S(2)}, u32[]{:S(2)}) collective-permute-start(bf16[256,1024]{1,0:T(8,128)(2,1)S(1)} %relay.3), channel_id=1, source_target_pairs={{0,16},{16,0},{1,17},{17,1},{2,18},{18,2},{3,19},{19,3},{4,20},{20... | collective-permute-start | bytes 1572872 | tf_op jit(solution)/shard_map/ppermute | solution.py:35
  114.8 50.2 %collective-permute-start.17 = (bf16[512,1024]{1,0:T(8,128)(2,1)S(1)}, bf16[512,1024]{1,0:T(8,128)(2,1)}, u32[]{:S(2)}, u32[]{:S(2)}) collective-permute-start(bf16[512,1024]{1,0:T(8,128)(2,1)S(1)} %copy-done.23), channel_id=1, source_target_pairs={{0,4},{4,0},{8,12},{12,8},{1,5},{5,1},{9,13},{13,9},{2,6},{6,2},{1... | collective-permute-start | bytes 3145736 | tf_op jit(solution)/shard_map/ppermute | solution.py:35
  168.5 28.2 %collective-permute-start.31 = (bf16[256,1152]{1,0:T(8,128)(2,1)}, bf16[256,1152]{1,0:T(8,128)(2,1)S(1)}, u32[]{:S(2)}, u32[]{:S(2)}) collective-permute-start(bf16[256,1152]{1,0:T(8,128)(2,1)} %relay.4), channel_id=1, source_target_pairs={{0,16},{16,0},{1,17},{17,1},{2,18},{18,2},{3,19},{19,3},{4,20},{20... | collective-permute-start | bytes 1769480 | tf_op jit(solution)/shard_map/ppermute | solution.py:35
  175.7 23.4 %collective-permute-start.35 = (bf16[256,1152]{1,0:T(8,128)(2,1)}, bf16[256,1152]{1,0:T(8,128)(2,1)S(1)}, u32[]{:S(2)}, u32[]{:S(2)}) collective-permute-start(bf16[256,1152]{1,0:T(8,128)(2,1)} %get-tuple-element.134), channel_id=1, source_target_pairs={{0,2},{2,0},{1,3},{3,1},{4,6},{6,4},{5,7},{7,5},{8,10},{10,8},{9,1... | collective-permute-start | bytes 1769480 | tf_op jit(solution)/shard_map/ppermute | solution.py:35
  180.4 21.4 %collective-permute-start.33 = (bf16[256,1024]{1,0:T(8,128)(2,1)}, bf16[256,1024]{1,0:T(8,128)(2,1)}, u32[]{:S(2)}, u32[]{:S(2)}) collective-permute-start(bf16[256,1024]{1,0:T(8,128)(2,1)} %get-tuple-element.132), channel_id=1, source_target_pairs={{0,2},{2,0},{1,3},{3,1},{4,6},{6,4},{5,7},{7,5},{8,10},{10,8},{9,1... | collective-permute-start | bytes 1572872 | tf_op jit(solution)/shard_map/ppermute | solution.py:35
  196.8 24.8 %collective-permute-start.30 = (bf16[256,1024]{1,0:T(8,128)(2,1)}, bf16[256,1024]{1,0:T(8,128)(2,1)}, u32[]{:S(2)}, u32[]{:S(2)}) collective-permute-start(bf16[256,1024]{1,0:T(8,128)(2,1)} %get-tuple-element.128), channel_id=1, source_target_pairs={{0,2},{2,0},{1,3},{3,1},{4,6},{6,4},{5,7},{7,5},{8,10},{10,8},{9,1... | collective-permute-start | bytes 1572872 | tf_op jit(solution)/shard_map/ppermute | solution.py:35
  196.8 26.8 %collective-permute-start.32 = (bf16[256,1024]{1,0:T(8,128)(2,1)}, bf16[256,1024]{1,0:T(8,128)(2,1)}, u32[]{:S(2)}, u32[]{:S(2)}) collective-permute-start(bf16[256,1024]{1,0:T(8,128)(2,1)} %relay.5), channel_id=1, source_target_pairs={{0,16},{16,0},{1,17},{17,1},{2,18},{18,2},{3,19},{19,3},{4,20},{20... | collective-permute-start | bytes 1572872 | tf_op jit(solution)/shard_map/ppermute | solution.py:35
  (63 other events, 573.6 us)

commit v5 on v4

--- a/solution.py
+++ b/solution.py
@@ -102,19 +102,36 @@
     )(swag_coef, mean_part, dev_part)
 
 
-def sampled(mean_part, dev_part, swag_coef):
-    factor = (2.0 * (dev_part.shape[0] - 1)) ** (-0.5)
-    accum = mean_part.astype(F32)
-    for member in range(dev_part.shape[0]):
-        accum = accum + factor * swag_coef[member] * dev_part[member].astype(F32)
-    return accum.astype(BF16)
-
-
-def pack_kernel(bc_ref, dt_ref, out_ref):
-    width, heads = bc_ref.shape[1], dt_ref.shape[1]
-    out_ref[:, :width] = bc_ref[...]
-    out_ref[:, width:] = jnp.zeros((out_ref.shape[0], LANES), BF16)
-    out_ref[:, width : width + heads] = dt_ref[...]
+def sample_pair_kernel(count, coef_ref, mean_ref, devs_ref, dt_ref, out_ref):
+    factor = (2.0 * (count - 1)) ** (-0.5)
+    accum = mean_ref[...].astype(F32)
+    for member in range(count):
+        accum = accum + factor * coef_ref[member] * devs_ref[member].astype(F32)
+    width, heads = mean_ref.shape[2], dt_ref.shape[1]
+    for k in range(2):
+        out_ref[:, k * width : (k + 1) * width] = accum[:, k, :].astype(BF16)
+    out_ref[:, 2 * width :] = jnp.zeros((out_ref.shape[0], LANES), BF16)
+    out_ref[:, 2 * width : 2 * width + heads] = dt_ref[...]
+
+
+def sampled_pair(mean_part, dev_part, dt_part, swag_coef):
+    rows, _, width = mean_part.shape
+    count = dev_part.shape[0]
+    tile = rows // 8
+    return call(
+        functools.partial(sample_pair_kernel, count),
+        "sample_pair",
+        jax.ShapeDtypeStruct((rows, 2 * width + LANES), BF16),
+        moved=4 * (count + 2) * rows * width,
+        grid=(8,),
+        in_specs=[
+            SMEM,
+            pl.BlockSpec((tile, 2, width), lambda i: (i, 0, 0)),
+            pl.BlockSpec((count, tile, 2, width), lambda i: (0, i, 0, 0)),
+            pl.BlockSpec((tile, dt_part.shape[1]), lambda i: (i, 0)),
+        ],
+        out_specs=pl.BlockSpec((tile, 2 * width + LANES), lambda i: (i, 0)),
+    )(swag_coef, mean_part, dev_part, dt_part)
 
 
 def sent_straight(weight):
@@ -420,22 +437,12 @@
         in_specs=[SMEM, VMEM],
         out_specs=[VMEM] * 3,
     )(at, tokens)
-    proj_mean = after(proj_mean, own)
+    proj_mean, bc_mean = after((proj_mean, bc_mean), own)
     far_sent = swapped(far_sent, "fsdp")
     far_kept = swapped(after(far_kept, far_sent), "fsdp")
-    bc_mean = after(bc_mean, far_sent)
 
     weight_early = sampled_cols(proj_mean, proj_devs, swag_coef, 0, early_groups * width)
-    weight_bc = sampled(bc_mean, bc_devs, swag_coef).reshape(rows_k, width_bc)
-    weight_bc = call(
-        pack_kernel,
-        "pack",
-        jax.ShapeDtypeStruct((rows_k, width_bc + LANES), BF16),
-        moved=4 * weight_bc.size,
-        vmem=12,
-        in_specs=[VMEM] * 2,
-        out_specs=VMEM,
-    )(weight_bc, dt_weight)
+    weight_bc = sampled_pair(bc_mean, bc_devs, dt_weight, swag_coef)
     weight_late = None
     if late:
         weight_late = sampled_cols(proj_mean, proj_devs, swag_coef, early_groups // len(late), len(late) * width)
@@ -448,31 +455,52 @@
         back = relayed(kept, swapped(first, "core"), swapped(second, "core"), heads_here, with_steps)
         return (kept, swapped(after(sent, back), "core")), back
 
+    specs_of = lambda width: [pl.BlockSpec((1, tok_count, width), lambda i: (1, 0, i))] + [
+        pl.BlockSpec((tok_count, width), lambda i: (0, i)),
+        pl.BlockSpec((tok_count, width), lambda i: (0, i)),
+        pl.BlockSpec((RIM, width), lambda i: (0, i)),
+    ]
+    whole_of = lambda *shape: pl.BlockSpec(shape, lambda i: (0,) * len(shape))
+    by_group = (groups_here, tok_count, per_group)
+    by_head = (heads_here, tok_count)
+    by_decay = (groups_here, 1, per_group)
+    state_proj = lambda part: call(
+        functools.partial(state_proj_kernel, heads_here),
+        "state_proj",
+        (jax.ShapeDtypeStruct((tok_count, width_bc), BF16),)
+        + tuple(jax.ShapeDtypeStruct(a, F32) for a in (by_group, by_group, by_head, by_head, by_decay)),
+        moved=10 * tok_count * width_bc,
+        grid=(1,),
+        in_specs=specs_of(width_bc + LANES) + [whole_of(CONV, width_bc)] + [whole_of(1, heads_here)] * 2,
+        out_specs=[whole_of(*a) for a in ((tok_count, width_bc), by_group, by_group, by_head, by_head, by_decay)],
+        scratch_shapes=[pltpu.VMEM((tok_count + 8, width_bc), F32)],
+    )(*part, rows_before(*part), conv_bc.reshape(CONV, width_bc), dt_bias[None], decay_rate[None])
     if plane and two_shares:
-        early = [weight_early, *sent_straight(weight_early)]
-        early += sent_on(corner_parts(early[1:], 1))
+        bc = [weight_bc, *sent_straight(weight_bc)]
+        bc += sent_on(corner_parts(bc[1:], 1))
         own_t = swapped(own, "tp")
-        far_sent = after(far_sent, own_t)
+        far_sent = after(far_sent, (own_t, weight_early, weight_late))
         sent_t = swapped(far_sent, "tp")
         got, got_t = swapped(far_sent, "core"), swapped(sent_t, "core")
-        far_kept = after(far_kept, (got_t, weight_bc, weight_late))
+        far_kept = after(far_kept, got_t)
         own, own_t = after((own, own_t), far_kept)
         own_c, own_tc = swapped(own, "core"), swapped(own_t, "core")
         kept_t = swapped(far_kept, "tp")
-        weight_bc = after(weight_bc, (early[3:], far_kept))
-        bc = [weight_bc, *sent_straight(weight_bc)]
+        weight_early = after(weight_early, (bc[3:], far_kept))
+        early = [weight_early, *sent_straight(weight_early)]
         rows = token_rows(at, far_kept, kept_t, got, got_t, own, own_t, own_c, own_tc)
-        part, back = partial_sums(rows, early, False)
-        bc += sent_on(corner_parts(after(bc[1:], back), 1))
-        got = swapped(back, "fsdp")
-        weight_late = after(weight_late, (back, bc[1:3]))
-        part_bc, back_bc = partial_sums(rows, bc, True, got)
-        got_bc = swapped(after(back_bc, got), "fsdp")
+        part_bc, back_bc = partial_sums(rows, bc, True)
+        early += sent_on(corner_parts(after(early[1:], back_bc), 1))
+        got_bc = swapped(back_bc, "fsdp")
+        weight_late = after(weight_late, (back_bc, early[1:3]))
+        part, back = partial_sums(rows, early, False, got_bc)
+        got = swapped(after(back, got_bc), "fsdp")
         straight = sent_straight(weight_late)
-        corners = sent_on(after(corner_parts(straight, 2), back_bc))
-        part_late, back_late = partial_sums(rows, after([weight_late, *straight, *corners], back_bc), False)
-        got_late = swapped(after(back_late, got_bc), "fsdp")
-        got_bc = after(got_bc, back_late)
+        seen = state_proj(after(part_bc + (got_bc,), back))
+        corners = sent_on(after(corner_parts(straight, 2), back))
+        part_late, back_late = partial_sums(rows, after([weight_late, *straight, *corners], seen), False)
+        got_late = swapped(after(back_late, got), "fsdp")
+        got = after(got, back_late)
     else:
         whole = lambda a, axis: lax.all_gather(a, axis, axis=0, tiled=True)
         ranges = [far_kept, swapped(far_sent, "core"), own[:share], swapped(own[share:], "core")]
@@ -483,31 +511,12 @@
         if late:
             part_late, back_late = partial_sums(rows, [whole(weight_late, "chip")], False)
             got_late = swapped(back_late, "fsdp")
+        seen = state_proj(part_bc + (got_bc,))
+    conv_out, cum_g, steps_g, cum_t, steps_t, decay = seen
     parts = [part + (got,)]
     if late:
         parts.append(part_late + (got_late,))
-    part_bc += (got_bc,)
-
-    specs_of = lambda width: [pl.BlockSpec((1, tok_count, width), lambda i: (1, 0, i))] + [
-        pl.BlockSpec((tok_count, width), lambda i: (0, i)),
-        pl.BlockSpec((tok_count, width), lambda i: (0, i)),
-        pl.BlockSpec((RIM, width), lambda i: (0, i)),
-    ]
-    whole_of = lambda *shape: pl.BlockSpec(shape, lambda i: (0,) * len(shape))
-    by_group = (groups_here, tok_count, per_group)
-    by_head = (heads_here, tok_count)
-    by_decay = (groups_here, 1, per_group)
-    conv_out, cum_g, steps_g, cum_t, steps_t, decay = call(
-        functools.partial(state_proj_kernel, heads_here),
-        "state_proj",
-        (jax.ShapeDtypeStruct((tok_count, width_bc), BF16),)
-        + tuple(jax.ShapeDtypeStruct(a, F32) for a in (by_group, by_group, by_head, by_head, by_decay)),
-        moved=10 * tok_count * width_bc,
-        grid=(1,),
-        in_specs=specs_of(width_bc + LANES) + [whole_of(CONV, width_bc)] + [whole_of(1, heads_here)] * 2,
-        out_specs=[whole_of(*a) for a in ((tok_count, width_bc), by_group, by_group, by_head, by_head, by_decay)],
-        scratch_shapes=[pltpu.VMEM((tok_count + 8, width_bc), F32)],
-    )(*part_bc, rows_before(*part_bc), conv_bc.reshape(CONV, width_bc), dt_bias[None], decay_rate[None])
+
     skip = skip_gain.reshape(by_decay)
     levels = count.bit_length() - 1
     seq_place = (2 * lax.axis_index("chip") + lax.axis_index("core")).astype(jnp.int32).reshape(1)

time: 263 us -> 275 us (1.046)
  waiting for transfers between devices: 115 us -> 123 us
  Pallas kernels: 67.9 us -> 74.2 us
  other arithmetic: 5.35 us -> 0 us
    ppermute x41, waiting for transfers between devices: 114 us -> 122 us  [swapped(): lax.ppermute(part, axis, [(i, i ^ by) for i in range(lax.axis_size(axis))])]
    pallas_call x1, Pallas kernels: 0.1 us -> 7.79 us  [sampled_pair(): call(functools.partial(sample_pair_kernel, count), 'sample_pair', jax.Sha...]
    convert_element_type x1 -> x0, other arithmetic: 5.35 us -> none  [sampled(): return accum.astype(BF16)]
    ppermute x41, starting transfers between devices: 43.9 us -> 47.7 us  [swapped(): lax.ppermute(part, axis, [(i, i ^ by) for i in range(lax.axis_size(axis))])]
    slice x6, local copies, waits for them, and re-layouts: 3.73 us -> 6.93 us  [corner_parts(): cut = lambda a, i: a[i * rows:(i + 1) * rows]]
    unnamed x89 -> x88, local copies, waits for them, and re-layouts: 14.9 us -> 14.7 us
  transfers between devices with their start and end apart: 44 -> 44, of which waited for: 22 -> 23; matrix products, arithmetic and copies ran while one was open for 4% -> 3% of each run, Pallas kernels for 22% -> 23%
where the time goes in v5:
time: 275 us; the launch traced here: 273 us
  waiting for transfers between devices  123 us (45%)
  Pallas kernels  74.2 us (27%)
  starting transfers between devices  52.7 us (19%)
  local copies, waits for them, and re-layouts  22.8 us (8%)
    ppermute x41, waiting for transfers between devices, swapped(): lax.ppermute(part, axis, [(i, i ^ by) for i in range(lax.axis_size(axis))])  122 us
    ppermute x41, starting transfers between devices, swapped(): lax.ppermute(part, axis, [(i, i ^ by) for i in range(lax.axis_size(axis))])  47.7 us
    pallas_call x3, Pallas kernels, multiplied(): call(functools.partial(multiply_kernel, heads, with_steps, len(weights)),...  29.3 us
    unnamed x88, local copies, waits for them, and re-layouts  14.7 us
    pallas_call x2, Pallas kernels, body(): call(mix_kernel, 'mix', (jax.ShapeDtypeStruct((tok_count, groups * width)...  10.1 us
    pallas_call x2, Pallas kernels, sampled_cols(): call(functools.partial(sample_kernel, count), 'sample', jax.ShapeDtypeStr...  9.29 us
    pallas_call x1, Pallas kernels, sampled_pair(): call(functools.partial(sample_pair_kernel, count), 'sample_pair', jax.Sha...  7.79 us
    slice x6, local copies, waits for them, and re-layouts, corner_parts(): cut = lambda a, i: a[i * rows:(i + 1) * rows]  6.93 us
  transfers between devices with their start and end apart: 44, of which 23 were waited for; matrix products, arithmetic and copies ran while one was open for 3% of the time, Pallas kernels for 23%

profile of v5, /device:TPU:0, one launch (start us, length us, event | category | flops | bytes accessed | tf_op | source)
XLA Modules:
  0.0 273.4 jit_solution(12154277524568982611)
XLA Ops:
  0.6 3.1 %cut_tokens.1 = (bf16[128,2048]{1,0:T(8,128)(2,1)}, bf16[128,2048]{1,0:T(8,128)(2,1)}, bf16[256,2048]{1,0:T(8,128)(2,1)}) custom-call(s32[7]{0:T(128)} %stack.31.at_ref, bf16[128,8192]{1,0:T(8,128)(2,1)} %tokens_ref.1), custom_call_target="tpu_custom_call" | custom-call | bytes 83886 | tf_op jit(solution)/shard_map/cut_tokens/pallas_call | solution.py:432
  3.7 3.0 %collective-permute-start.2 = (bf16[256,2048]{1,0:T(8,128)(2,1)}, bf16[256,2048]{1,0:T(8,128)(2,1)S(1)}, u32[]{:S(2)}, u32[]{:S(2)}) collective-permute-start(bf16[256,2048]{1,0:T(8,128)(2,1)} %get-tuple-element.97.refs_4_), channel_id=1, source_target_pairs={{0,1},{1,0},{2,3},{3,2},{4,5},{5,4},{6,7},{7,6},{8,9},{9,8},{10,11... | collective-permute-start | bytes 3145736 | tf_op jit(solution)/shard_map/ppermute | solution.py:35
  10.1 7.8 %sample_pair.1.refs_0_ = bf16[512,1152]{1,0:T(8,128)(2,1)} custom-call(f32[4]{0:T(128)} %coef_ref.5, bf16[512,2,512]{2,1,0:T(2,128)(2,1)} %mean_ref.2, bf16[4,512,2,512]{3,2,1,0:T(2,128)(2,1)} %devs_ref.5, bf16[512,32]{1,0:T(8,128)(2,1)} %copy.14.dt_ref), custom_call_target="tpu_custom_call" | custom-call | bytes 125829 | tf_op jit(solution)/shard_map/sample_pair/pallas_call | solution.py:121
  20.9 4.6 %sample.3.refs_0_ = bf16[512,1024]{1,0:T(8,128)(2,1)} custom-call(f32[4]{0:T(128)} %coef_ref.5, bf16[512,2048]{1,0:T(8,128)(2,1)} %mean_ref.1, bf16[4,512,2048]{2,1,0:T(8,128)(2,1)} %devs_ref.4), custom_call_target="tpu_custom_call" | custom-call | bytes 125829 | tf_op jit(solution)/shard_map/sample/pallas_call | solution.py:90
  25.5 4.7 %sample.2.refs_0_ = bf16[512,1024]{1,0:T(8,128)(2,1)} custom-call(f32[4]{0:T(128)} %coef_ref.5, bf16[512,2048]{1,0:T(8,128)(2,1)} %mean_ref.1, bf16[4,512,2048]{2,1,0:T(8,128)(2,1)} %devs_ref.4), custom_call_target="tpu_custom_call" | custom-call | bytes 125829 | tf_op jit(solution)/shard_map/sample/pallas_call | solution.py:90
  30.2 10.5 %collective-permute-done = bf16[128,2048]{1,0:T(8,128)(2,1)S(1)} collective-permute-done((bf16[128,2048]{1,0:T(8,128)(2,1)}, bf16[128,2048]{1,0:T(8,128)(2,1)S(1)}, u32[]{:S(2)}, u32[]{:S(2)}) %collective-permute-start) | collective-permute-done | bytes 524320 | tf_op jit(solution)/shard_map/ppermute | solution.py:35
  41.3 2.8 %collective-permute-start.3 = (bf16[128,2048]{1,0:T(8,128)(2,1)S(1)}, bf16[128,2048]{1,0:T(8,128)(2,1)S(1)}, u32[]{:S(2)}, u32[]{:S(2)}) collective-permute-start(bf16[128,2048]{1,0:T(8,128)(2,1)S(1)} %collective-permute-done), channel_id=1, source_target_pairs={{0,1},{1,0},{2,3},{3,2},{4,5},{5,4},{6,7},{7,6},{8,9},{9,8},{10,11... | collective-permute-start | bytes 1572872 | tf_op jit(solution)/shard_map/ppermute | solution.py:35
  45.7 19.5 %collective-permute-done.3 = bf16[128,2048]{1,0:T(8,128)(2,1)S(1)} collective-permute-done((bf16[128,2048]{1,0:T(8,128)(2,1)S(1)}, bf16[128,2048]{1,0:T(8,128)(2,1)S(1)}, u32[]{:S(2)}, u32[]{:S(2)}) %collective-permute-start.3) | collective-permute-done | bytes 524320 | tf_op jit(solution)/shard_map/ppermute | solution.py:35
  71.2 10.9 %collective-permute-done.11.refs_3_ = bf16[256,1152]{1,0:T(8,128)(2,1)S(1)} collective-permute-done((bf16[256,1152]{1,0:T(8,128)(2,1)S(1)}, bf16[256,1152]{1,0:T(8,128)(2,1)S(1)}, u32[]{:S(2)}, u32[]{:S(2)}) %collective-permute-start.11) | collective-permute-done | bytes 589856 | tf_op jit(solution)/shard_map/ppermute | solution.py:35
  86.6 12.7 %collective-permute-done.5.refs_1_ = bf16[128,2048]{1,0:T(8,128)(2,1)S(1)} collective-permute-done((bf16[128,2048]{1,0:T(8,128)(2,1)S(1)}, bf16[128,2048]{1,0:T(8,128)(2,1)S(1)}, u32[]{:S(2)}, u32[]{:S(2)}) %collective-permute-start.5) | collective-permute-done | bytes 524320 | tf_op jit(solution)/shard_map/ppermute | solution.py:35
  102.1 11.6 %multiply.3 = (bf16[128,1152]{1,0:T(8,128)(2,1)}, bf16[128,1152]{1,0:T(8,128)(2,1)}, bf16[256,1152]{1,0:T(8,128)(2,1)}, f32[2,256,1152]{2,1,0:T(8,128)}) custom-call(bf16[1024,2048]{1,0:T(8,128)(2,1)} %copy-done, bf16[512,1152]{1,0:T(8,128)(2,1)} %sample_pair.1.refs_0_, bf16[512,1152]{1,0:T(8,128)(2,1)} %collective-permute-done.9.refs_1_, ...), custom_call_target="tpu_custom_call" | custom-call | flops 96636768 | bytes 249036 | tf_op jit(solution)/shard_map/multiply/pallas_call | solution.py:182
  127.0 27.6 %collective-permute-done.20.refs_4_ = bf16[256,1024]{1,0:T(8,128)(2,1)} collective-permute-done((bf16[256,1024]{1,0:T(8,128)(2,1)S(1)}, bf16[256,1024]{1,0:T(8,128)(2,1)}, u32[]{:S(2)}, u32[]{:S(2)}) %collective-permute-start.20) | collective-permute-done | bytes 524320 | tf_op jit(solution)/shard_map/ppermute | solution.py:35
  154.6 3.0 %collective-permute-done.19.refs_3_ = bf16[256,1024]{1,0:T(8,128)(2,1)} collective-permute-done((bf16[256,1024]{1,0:T(8,128)(2,1)S(1)}, bf16[256,1024]{1,0:T(8,128)(2,1)}, u32[]{:S(2)}, u32[]{:S(2)}) %collective-permute-start.19) | collective-permute-done | bytes 524320 | tf_op jit(solution)/shard_map/ppermute | solution.py:35
  157.6 8.8 %multiply.4 = (bf16[128,1024]{1,0:T(8,128)(2,1)}, bf16[128,1024]{1,0:T(8,128)(2,1)}, bf16[256,1024]{1,0:T(8,128)(2,1)}, f32[2,256,1024]{2,1,0:T(8,128)}) custom-call(bf16[1024,2048]{1,0:T(8,128)(2,1)} %copy-done, bf16[512,1024]{1,0:T(8,128)(2,1)} %sample.2.refs_0_, bf16[512,1024]{1,0:T(8,128)(2,1)} %collective-permute-done.15.refs_1_, ...), custom_call_target="tpu_custom_call" | custom-call | flops 85899344 | bytes 230686 | tf_op jit(solution)/shard_map/multiply/pallas_call | solution.py:182
  183.5 4.6 %state_proj.1 = (bf16[256,1024]{1,0:T(8,128)(2,1)}, f32[4,256,8]{2,1,0:T(8,128)}, f32[4,256,8]{2,1,0:T(8,128)}, f32[32,256]{1,0:T(8,128)}, f32[32,256]{1,0:T(8,128)}, /*index=5*/f32[4,1,8]{2,1,0:T(1,128)}) custom-call(f32[2,256,1152]{2,1,0:T(8,128)} %get-tuple-element.120.kept_ref.kept, bf16[256,1152]{1,0:T(8,128)(2,1)} %copy-done.10, ...), custom_call_target="tpu_custom_call" | custom-call | bytes 52428 | tf_op jit(solution)/shard_map/state_proj/pallas_call | solution.py:467
  188.1 3.7 %collective-permute-done.27.refs_6_ = bf16[128,1024]{1,0:T(8,128)(2,1)S(1)} collective-permute-done((bf16[128,1024]{1,0:T(8,128)(2,1)S(1)}, bf16[128,1024]{1,0:T(8,128)(2,1)S(1)}, u32[]{:S(2)}, u32[]{:S(2)}) %collective-permute-start.27) | collective-permute-done | bytes 262176 | tf_op jit(solution)/shard_map/ppermute | solution.py:35
  192.5 8.9 %multiply.5 = (bf16[128,1024]{1,0:T(8,128)(2,1)}, bf16[128,1024]{1,0:T(8,128)(2,1)}, bf16[256,1024]{1,0:T(8,128)(2,1)}, f32[2,256,1024]{2,1,0:T(8,128)}) custom-call(bf16[1024,2048]{1,0:T(8,128)(2,1)} %copy-done, bf16[512,1024]{1,0:T(8,128)(2,1)} %sample.3.refs_0_, bf16[512,1024]{1,0:T(8,128)(2,1)} %collective-permute-done.17.refs_1_, ...), custom_call_target="tpu_custom_call" | custom-call | flops 85899344 | bytes 230686 | tf_op jit(solution)/shard_map/multiply/pallas_call | solution.py:182
  211.4 5.1 %mix.2 = (f32[256,1024]{1,0:T(8,128)}, f32[1,128,1024]{2,1,0:T(8,128)}, f32[128,1024]{1,0:T(8,128)}, f32[8,1024]{1,0:T(8,128)}, bf16[144,1024]{1,0:T(8,128)(2,1)}) custom-call(f32[2,256,1024]{2,1,0:T(8,128)} %get-tuple-element.109.kept_ref.kept, bf16[256,1024]{1,0:T(8,128)(2,1)} %copy-done.12, bf16[256,1024]{1,0:T(8,128)(2,1)} %copy-done.11, ...), custom_call_target="tpu_custom_call" | custom-call | flops 5368709 | bytes 73400 | tf_op jit(solution)/shard_map/mix/pallas_call | solution.py:538
  221.6 12.0 %collective-permute-done.34.got_f = bf16[256,1024]{1,0:T(8,128)(2,1)} collective-permute-done((bf16[256,1024]{1,0:T(8,128)(2,1)}, bf16[256,1024]{1,0:T(8,128)(2,1)}, u32[]{:S(2)}, u32[]{:S(2)}) %collective-permute-start.34) | collective-permute-done | bytes 524320 | tf_op jit(solution)/shard_map/ppermute | solution.py:35
  237.1 5.1 %mix.3 = (f32[256,1024]{1,0:T(8,128)}, f32[1,128,1024]{2,1,0:T(8,128)}, f32[128,1024]{1,0:T(8,128)}, f32[8,1024]{1,0:T(8,128)}, bf16[144,1024]{1,0:T(8,128)(2,1)}) custom-call(f32[2,256,1024]{2,1,0:T(8,128)} %get-tuple-element.152.kept_ref.kept, bf16[256,1024]{1,0:T(8,128)(2,1)} %copy-done.13, bf16[256,1024]{1,0:T(8,128)(2,1)} %collective-permute-done.34.got_f, ...), custom_call_target="tpu_custom_call" | custom-call | flops 5368709 | bytes 73400 | tf_op jit(solution)/shard_map/mix/pallas_call | solution.py:538
  250.4 3.9 %collective-permute-done.42.other = bf16[144,1024]{1,0:T(8,128)(2,1)S(1)} collective-permute-done((bf16[144,1024]{1,0:T(8,128)(2,1)S(1)}, bf16[144,1024]{1,0:T(8,128)(2,1)S(1)}, u32[]{:S(2)}, u32[]{:S(2)}) %collective-permute-start.42) | collective-permute-done | bytes 294944 | tf_op jit(solution)/shard_map/ppermute | solution.py:35
  255.4 3.6 %collective-permute-start.43 = (bf16[144,1024]{1,0:T(8,128)(2,1)S(1)}, bf16[144,1024]{1,0:T(8,128)(2,1)S(1)}, u32[]{:S(2)}, u32[]{:S(2)}) collective-permute-start(bf16[144,1024]{1,0:T(8,128)(2,1)S(1)} %get-tuple-element.174), channel_id=1, source_target_pairs={{0,8},{2,10},{4,12},{6,14},{8,0},{10,2},{12,4},{14,6},{1,9},{3,11}... | collective-permute-start | bytes 884744 | tf_op jit(solution)/shard_map/ppermute | solution.py:35
  261.4 3.4 %collective-permute-start.41 = (bf16[144,1024]{1,0:T(8,128)(2,1)S(1)}, bf16[144,1024]{1,0:T(8,128)(2,1)S(1)}, u32[]{:S(2)}, u32[]{:S(2)}) collective-permute-start(bf16[144,1024]{1,0:T(8,128)(2,1)S(1)} %get-tuple-element.166), channel_id=1, source_target_pairs={{0,8},{2,10},{4,12},{6,14},{8,0},{10,2},{12,4},{14,6},{1,9},{3,11}... | collective-permute-start | bytes 884744 | tf_op jit(solution)/shard_map/ppermute | solution.py:35
  267.1 4.5 %collective-permute-done.41.other = bf16[144,1024]{1,0:T(8,128)(2,1)S(1)} collective-permute-done((bf16[144,1024]{1,0:T(8,128)(2,1)S(1)}, bf16[144,1024]{1,0:T(8,128)(2,1)S(1)}, u32[]{:S(2)}, u32[]{:S(2)}) %collective-permute-start.41) | collective-permute-done | bytes 294944 | tf_op jit(solution)/shard_map/ppermute | solution.py:35
  (183 shorter events, 87.8 us)
Async XLA Ops:
  3.7 37.6 %collective-permute-start.2 = (bf16[256,2048]{1,0:T(8,128)(2,1)}, bf16[256,2048]{1,0:T(8,128)(2,1)S(1)}, u32[]{:S(2)}, u32[]{:S(2)}) collective-permute-start(bf16[256,2048]{1,0:T(8,128)(2,1)} %get-tuple-element.97.refs_4_), channel_id=1, source_target_pairs={{0,1},{1,0},{2,3},{3,2},{4,5},{5,4},{6,7},{7,6},{8,9},{9,8},{10,11... | collective-permute-start | bytes 3145736 | tf_op jit(solution)/shard_map/ppermute | solution.py:35
  6.7 34.0 %collective-permute-start = (bf16[128,2048]{1,0:T(8,128)(2,1)}, bf16[128,2048]{1,0:T(8,128)(2,1)S(1)}, u32[]{:S(2)}, u32[]{:S(2)}) collective-permute-start(bf16[128,2048]{1,0:T(8,128)(2,1)} %get-tuple-element.91), channel_id=1, source_target_pairs={{0,16},{16,0},{1,17},{17,1},{2,18},{18,2},{3,19},{19,3},{4,20},{20... | collective-permute-start | bytes 1572872 | tf_op jit(solution)/shard_map/ppermute | solution.py:35
  17.8 47.3 %collective-permute-start.10 = (bf16[512,1152]{1,0:T(8,128)(2,1)}, bf16[512,1152]{1,0:T(8,128)(2,1)}, u32[]{:S(2)}, u32[]{:S(2)}) collective-permute-start(bf16[512,1152]{1,0:T(8,128)(2,1)} %sample_pair.1.refs_0_), channel_id=1, source_target_pairs={{0,8},{4,12},{8,0},{12,4},{1,9},{5,13},{9,1},{13,5},{2,10},{6,14},... | collective-permute-start | bytes 3538952 | tf_op jit(solution)/shard_map/ppermute | solution.py:35
  19.4 48.5 %collective-permute-start.9 = (bf16[512,1152]{1,0:T(8,128)(2,1)}, bf16[512,1152]{1,0:T(8,128)(2,1)}, u32[]{:S(2)}, u32[]{:S(2)}) collective-permute-start(bf16[512,1152]{1,0:T(8,128)(2,1)} %sample_pair.1.refs_0_), channel_id=1, source_target_pairs={{0,4},{4,0},{8,12},{12,8},{1,5},{5,1},{9,13},{13,9},{2,6},{6,2},{1... | collective-permute-start | bytes 3538952 | tf_op jit(solution)/shard_map/ppermute | solution.py:35
  41.3 23.9 %collective-permute-start.3 = (bf16[128,2048]{1,0:T(8,128)(2,1)S(1)}, bf16[128,2048]{1,0:T(8,128)(2,1)S(1)}, u32[]{:S(2)}, u32[]{:S(2)}) collective-permute-start(bf16[128,2048]{1,0:T(8,128)(2,1)S(1)} %collective-permute-done), channel_id=1, source_target_pairs={{0,1},{1,0},{2,3},{3,2},{4,5},{5,4},{6,7},{7,6},{8,9},{9,8},{10,11... | collective-permute-start | bytes 1572872 | tf_op jit(solution)/shard_map/ppermute | solution.py:35
  44.1 26.5 %collective-permute-start.1 = (bf16[128,2048]{1,0:T(8,128)(2,1)S(1)}, bf16[128,2048]{1,0:T(8,128)(2,1)S(1)}, u32[]{:S(2)}, u32[]{:S(2)}) collective-permute-start(bf16[128,2048]{1,0:T(8,128)(2,1)S(1)} %copy-done.42), channel_id=1, source_target_pairs={{0,16},{16,0},{1,17},{17,1},{2,18},{18,2},{3,19},{19,3},{4,20},{20... | collective-permute-start | bytes 1572872 | tf_op jit(solution)/shard_map/ppermute | solution.py:35
  66.3 15.8 %collective-permute-start.11 = (bf16[256,1152]{1,0:T(8,128)(2,1)S(1)}, bf16[256,1152]{1,0:T(8,128)(2,1)S(1)}, u32[]{:S(2)}, u32[]{:S(2)}) collective-permute-start(bf16[256,1152]{1,0:T(8,128)(2,1)S(1)} %slice.32), channel_id=1, source_target_pairs={{0,4},{4,0},{8,12},{12,8},{1,5},{5,1},{9,13},{13,9},{2,6},{6,2},{1... | collective-permute-start | bytes 1769480 | tf_op jit(solution)/shard_map/ppermute | solution.py:35
  69.0 15.5 %collective-permute-start.12 = (bf16[256,1152]{1,0:T(8,128)(2,1)S(1)}, bf16[256,1152]{1,0:T(8,128)(2,1)S(1)}, u32[]{:S(2)}, u32[]{:S(2)}) collective-permute-start(bf16[256,1152]{1,0:T(8,128)(2,1)S(1)} %slice.33), channel_id=1, source_target_pairs={{0,8},{4,12},{8,0},{12,4},{1,9},{5,13},{9,1},{13,5},{2,10},{6,14},... | collective-permute-start | bytes 1769480 | tf_op jit(solution)/shard_map/ppermute | solution.py:35
  70.6 16.0 %collective-permute-start.6 = (bf16[128,2048]{1,0:T(8,128)(2,1)S(1)}, bf16[128,2048]{1,0:T(8,128)(2,1)S(1)}, u32[]{:S(2)}, u32[]{:S(2)}) collective-permute-start(bf16[128,2048]{1,0:T(8,128)(2,1)S(1)} %collective-permute-done), channel_id=1, source_target_pairs={{0,2},{2,0},{1,3},{3,1},{4,6},{6,4},{5,7},{7,5},{8,10},{10,8},{9,1... | collective-permute-start | bytes 1572872 | tf_op jit(solution)/shard_map/ppermute | solution.py:35
  70.6 28.7 %collective-permute-start.7 = (bf16[256,2048]{1,0:T(8,128)(2,1)S(1)}, bf16[256,2048]{1,0:T(8,128)(2,1)S(1)}, u32[]{:S(2)}, u32[]{:S(2)}) collective-permute-start(bf16[256,2048]{1,0:T(8,128)(2,1)S(1)} %copy-done.16), channel_id=1, source_target_pairs={{0,2},{2,0},{1,3},{3,1},{4,6},{6,4},{5,7},{7,5},{8,10},{10,8},{9,1... | collective-permute-start | bytes 3145736 | tf_op jit(solution)/shard_map/ppermute | solution.py:35
  71.1 28.1 %collective-permute-start.8 = (bf16[256,2048]{1,0:T(8,128)(2,1)S(1)}, bf16[256,2048]{1,0:T(8,128)(2,1)S(1)}, u32[]{:S(2)}, u32[]{:S(2)}) collective-permute-start(bf16[256,2048]{1,0:T(8,128)(2,1)S(1)} %collective-permute-done.2.refs_5_), channel_id=1, source_target_pairs={{0,2},{2,0},{1,3},{3,1},{4,6},{6,4},{5,7},{7,5},{8,10},{10,8},{9,1... | collective-permute-start | bytes 3145736 | tf_op jit(solution)/shard_map/ppermute | solution.py:35
  84.5 33.5 %collective-permute-start.16 = (bf16[512,1024]{1,0:T(8,128)(2,1)S(1)}, bf16[512,1024]{1,0:T(8,128)(2,1)}, u32[]{:S(2)}, u32[]{:S(2)}) collective-permute-start(bf16[512,1024]{1,0:T(8,128)(2,1)S(1)} %copy-done.27), channel_id=1, source_target_pairs={{0,8},{4,12},{8,0},{12,4},{1,9},{5,13},{9,1},{13,5},{2,10},{6,14},... | collective-permute-start | bytes 3145736 | tf_op jit(solution)/shard_map/ppermute | solution.py:35
  86.0 31.9 %collective-permute-start.15 = (bf16[512,1024]{1,0:T(8,128)(2,1)S(1)}, bf16[512,1024]{1,0:T(8,128)(2,1)}, u32[]{:S(2)}, u32[]{:S(2)}) collective-permute-start(bf16[512,1024]{1,0:T(8,128)(2,1)S(1)} %copy-done.27), channel_id=1, source_target_pairs={{0,4},{4,0},{8,12},{12,8},{1,5},{5,1},{9,13},{13,9},{2,6},{6,2},{1... | collective-permute-start | bytes 3145736 | tf_op jit(solution)/shard_map/ppermute | solution.py:35
  86.6 12.7 %collective-permute-start.5 = (bf16[128,2048]{1,0:T(8,128)(2,1)S(1)}, bf16[128,2048]{1,0:T(8,128)(2,1)S(1)}, u32[]{:S(2)}, u32[]{:S(2)}) collective-permute-start(bf16[128,2048]{1,0:T(8,128)(2,1)S(1)} %collective-permute-done.1.refs_0_), channel_id=1, source_target_pairs={{0,1},{1,0},{2,3},{3,2},{4,5},{5,4},{6,7},{7,6},{8,9},{9,8},{10,11... | collective-permute-start | bytes 1572872 | tf_op jit(solution)/shard_map/ppermute | solution.py:35
  118.0 53.1 %collective-permute-start.18 = (bf16[512,1024]{1,0:T(8,128)(2,1)S(1)}, bf16[512,1024]{1,0:T(8,128)(2,1)S(1)}, u32[]{:S(2)}, u32[]{:S(2)}) collective-permute-start(bf16[512,1024]{1,0:T(8,128)(2,1)S(1)} %copy-done.26), channel_id=1, source_target_pairs={{0,8},{4,12},{8,0},{12,4},{1,9},{5,13},{9,1},{13,5},{2,10},{6,14},... | collective-permute-start | bytes 3145736 | tf_op jit(solution)/shard_map/ppermute | solution.py:35
  118.9 47.5 %collective-permute-start.21 = (bf16[256,1152]{1,0:T(8,128)(2,1)S(1)}, bf16[256,1152]{1,0:T(8,128)(2,1)S(1)}, u32[]{:S(2)}, u32[]{:S(2)}) collective-permute-start(bf16[256,1152]{1,0:T(8,128)(2,1)S(1)} %relay.3), channel_id=1, source_target_pairs={{0,16},{16,0},{1,17},{17,1},{2,18},{18,2},{3,19},{19,3},{4,20},{20... | collective-permute-start | bytes 1769480 | tf_op jit(solution)/shard_map/ppermute | solution.py:35
  121.6 50.3 %collective-permute-start.17 = (bf16[512,1024]{1,0:T(8,128)(2,1)S(1)}, bf16[512,1024]{1,0:T(8,128)(2,1)}, u32[]{:S(2)}, u32[]{:S(2)}) collective-permute-start(bf16[512,1024]{1,0:T(8,128)(2,1)S(1)} %copy-done.26), channel_id=1, source_target_pairs={{0,4},{4,0},{8,12},{12,8},{1,5},{5,1},{9,13},{13,9},{2,6},{6,2},{1... | collective-permute-start | bytes 3145736 | tf_op jit(solution)/shard_map/ppermute | solution.py:35
  124.9 29.7 %collective-permute-start.20 = (bf16[256,1024]{1,0:T(8,128)(2,1)S(1)}, bf16[256,1024]{1,0:T(8,128)(2,1)}, u32[]{:S(2)}, u32[]{:S(2)}) collective-permute-start(bf16[256,1024]{1,0:T(8,128)(2,1)S(1)} %slice.31), channel_id=1, source_target_pairs={{0,8},{4,12},{8,0},{12,4},{1,9},{5,13},{9,1},{13,5},{2,10},{6,14},... | collective-permute-start | bytes 1572872 | tf_op jit(solution)/shard_map/ppermute | solution.py:35
  126.5 31.1 %collective-permute-start.19 = (bf16[256,1024]{1,0:T(8,128)(2,1)S(1)}, bf16[256,1024]{1,0:T(8,128)(2,1)}, u32[]{:S(2)}, u32[]{:S(2)}) collective-permute-start(bf16[256,1024]{1,0:T(8,128)(2,1)S(1)} %slice.30), channel_id=1, source_target_pairs={{0,4},{4,0},{8,12},{12,8},{1,5},{5,1},{9,13},{13,9},{2,6},{6,2},{1... | collective-permute-start | bytes 1572872 | tf_op jit(solution)/shard_map/ppermute | solution.py:35
  178.9 12.9 %collective-permute-start.27 = (bf16[128,1024]{1,0:T(8,128)(2,1)S(1)}, bf16[128,1024]{1,0:T(8,128)(2,1)S(1)}, u32[]{:S(2)}, u32[]{:S(2)}) collective-permute-start(bf16[128,1024]{1,0:T(8,128)(2,1)S(1)} %get-tuple-element.117), channel_id=1, source_target_pairs={{0,8},{4,12},{8,0},{12,4},{1,9},{5,13},{9,1},{13,5},{2,10},{6,14},... | collective-permute-start | bytes 786440 | tf_op jit(solution)/shard_map/ppermute | solution.py:35
  179.8 27.0 %collective-permute-start.33 = (bf16[256,1024]{1,0:T(8,128)(2,1)}, bf16[256,1024]{1,0:T(8,128)(2,1)S(1)}, u32[]{:S(2)}, u32[]{:S(2)}) collective-permute-start(bf16[256,1024]{1,0:T(8,128)(2,1)} %relay.4), channel_id=1, source_target_pairs={{0,16},{16,0},{1,17},{17,1},{2,18},{18,2},{3,19},{19,3},{4,20},{20... | collective-permute-start | bytes 1572872 | tf_op jit(solution)/shard_map/ppermute | solution.py:35
  182.8 24.6 %collective-permute-start.35 = (bf16[256,1024]{1,0:T(8,128)(2,1)}, bf16[256,1024]{1,0:T(8,128)(2,1)S(1)}, u32[]{:S(2)}, u32[]{:S(2)}) collective-permute-start(bf16[256,1024]{1,0:T(8,128)(2,1)} %get-tuple-element.146), channel_id=1, source_target_pairs={{0,2},{2,0},{1,3},{3,1},{4,6},{6,4},{5,7},{7,5},{8,10},{10,8},{9,1... | collective-permute-start | bytes 1572872 | tf_op jit(solution)/shard_map/ppermute | solution.py:35
  206.8 14.8 %collective-permute-start.32 = (bf16[256,1024]{1,0:T(8,128)(2,1)}, bf16[256,1024]{1,0:T(8,128)(2,1)S(1)}, u32[]{:S(2)}, u32[]{:S(2)}) collective-permute-start(bf16[256,1024]{1,0:T(8,128)(2,1)} %get-tuple-element.142), channel_id=1, source_target_pairs={{0,2},{2,0},{1,3},{3,1},{4,6},{6,4},{5,7},{7,5},{8,10},{10,8},{9,1... | collective-permute-start | bytes 1572872 | tf_op jit(solution)/shard_map/ppermute | solution.py:35
  207.1 26.4 %collective-permute-start.34 = (bf16[256,1024]{1,0:T(8,128)(2,1)}, bf16[256,1024]{1,0:T(8,128)(2,1)}, u32[]{:S(2)}, u32[]{:S(2)}) collective-permute-start(bf16[256,1024]{1,0:T(8,128)(2,1)} %relay.5), channel_id=1, source_target_pairs={{0,16},{16,0},{1,17},{17,1},{2,18},{18,2},{3,19},{19,3},{4,20},{20... | collective-permute-start | bytes 1572872 | tf_op jit(solution)/shard_map/ppermute | solution.py:35
  (63 other events, 630.8 us)

commit v6 on v5

--- a/solution.py
+++ b/solution.py
@@ -13,6 +13,7 @@
 SPAN = 128
 LANES = 128
 RIM = 16
+FAR_PARTS = 4
 SEQ = ("chip", "core")
 F32 = jnp.float32
 BF16 = jnp.bfloat16
@@ -35,21 +36,15 @@
     return lax.ppermute(part, axis, [(i, i ^ by) for i in range(lax.axis_size(axis))])
 
 
-def cut_kernel(chips, at_ref, tokens_ref, far_sent, far_kept, own_ref):
-    depth = far_kept.shape[1] // chips
+def cut_kernel(chips, at_ref, tokens_ref, far_ref, own_ref):
+    depth = far_ref.shape[1] // chips
     rows = tokens_ref.shape[0]
     f_at, c_at = at_ref[0], at_ref[1]
-    for i in range(chips):
-        cols = slice(i * depth, (i + 1) * depth)
-
-        def taken(f, c):
-            start = pl.multiple_of(((f * chips + at_ref[3 + i]) * 2 + c) * depth, depth)
-            return tokens_ref[:, pl.ds(start, depth)]
-
-        far_sent[:, cols] = taken(1 - f_at, 1 - c_at)
-        far_kept[:, cols] = taken(1 - f_at, c_at)
-        own_ref[:rows, cols] = taken(f_at, c_at)
-        own_ref[rows:, cols] = taken(f_at, 1 - c_at)
+    for out, f in ((far_ref, 1 - f_at), (own_ref, f_at)):
+        for k, c in enumerate((c_at, 1 - c_at)):
+            for i in range(chips):
+                start = pl.multiple_of(((f * chips + at_ref[3 + i]) * 2 + c) * depth, depth)
+                out[k * rows : (k + 1) * rows, i * depth : (i + 1) * depth] = tokens_ref[:, pl.ds(start, depth)]
 
 
 def stack_kernel(at_ref, *refs):
@@ -60,8 +55,8 @@
         rows_ref[pl.ds(pl.multiple_of((k + 1 - at_ref[2]) * count, count), count), :] = pieces[k + 1][...]
 
 
-def token_rows(at, kept, kept_t, got, got_t, own, own_t, own_c, own_tc):
-    count, depth = kept.shape
+def token_rows(at, far, far_t, far_c, far_tc, own, own_t, own_c, own_tc):
+    count, depth = far.shape[0] // 2, far.shape[1]
     low = pl.BlockSpec((count, depth), lambda i: (0, 0))
     high = pl.BlockSpec((count, depth), lambda i: (1, 0))
     return call(
@@ -71,9 +66,9 @@
         moved=32 * count * depth,
         vmem=40,
         grid=(1,),
-        in_specs=[SMEM] + [low] * 6 + [high] * 2,
+        in_specs=[SMEM] + [low, low, high, high] * 2,
         out_specs=pl.BlockSpec((8 * count, depth), lambda i: (0, 0)),
-    )(at, kept, kept_t, got, got_t, own, own_t, own_c, own_tc)
+    )(at, far, far_t, far_c, far_tc, own, own_t, own_c, own_tc)
 
 
 def sample_kernel(count, coef_ref, mean_ref, devs_ref, out_ref):
@@ -159,13 +154,14 @@
 
 
 def multiply_kernel(heads, with_steps, pieces, rows_ref, *refs):
-    weights, (first_ref, second_ref, sent_ref, kept_ref) = refs[:pieces], refs[pieces:]
+    weights, far_refs, (sent_ref, far_ref, own_ref) = refs[:pieces], refs[pieces:-3], refs[-3:]
     joined = jnp.concatenate([weight[...] for weight in weights], axis=0)
     total = jnp.dot(rows_ref[...], joined, preferred_element_type=F32)
     half = total.shape[0] // 4
-    kept_ref[0] = total[:half]
-    kept_ref[1] = total[2 * half : 3 * half]
-    for out, first in ((first_ref, half), (second_ref, half + half // 2), (sent_ref, 3 * half)):
+    far_ref[...] = total[:half]
+    own_ref[...] = total[2 * half : 3 * half]
+    parts = [(out, half + i * out.shape[0]) for i, out in enumerate(far_refs)]
+    for out, first in parts + [(sent_ref, 3 * half)]:
         sent = total[first : first + out.shape[0]]
         out[...] = sent.astype(BF16)
         if with_steps:
@@ -182,21 +178,21 @@
     return call(
         functools.partial(multiply_kernel, heads, with_steps, len(weights)),
         "multiply",
-        (sent(half // 2), sent(half // 2), sent(half), jax.ShapeDtypeStruct((2, half, width), F32)),
+        (sent(half // FAR_PARTS),) * FAR_PARTS + (sent(half),) + (jax.ShapeDtypeStruct((half, width), F32),) * 2,
         flops=2 * rows.size * width,
         moved=2 * rows.size + 2 * rows.shape[1] * width + 12 * half * width,
         grid=(width // tile,),
         in_specs=[pl.BlockSpec(rows.shape, lambda i: (0, 0))]
         + [pl.BlockSpec((w.shape[0], tile), lambda i: (0, i)) for w in weights],
-        out_specs=[pl.BlockSpec((count, tile), lambda i: (0, i)) for count in (half // 2, half // 2, half)]
-        + [pl.BlockSpec((2, half, tile), lambda i: (0, 0, i))],
+        out_specs=[pl.BlockSpec((count, tile), lambda i: (0, i)) for count in [half // FAR_PARTS] * FAR_PARTS + [half] * 3],
     )(rows, *weights)
 
 
-def relay_kernel(heads, with_steps, kept_ref, first_ref, second_ref, out_ref):
-    half = first_ref.shape[0]
-    for got_ref, rows in ((first_ref, slice(0, half)), (second_ref, slice(half, 2 * half))):
-        kept, got = kept_ref[0, rows, :], got_ref[...].astype(F32)
+def relay_kernel(heads, with_steps, kept_ref, *refs):
+    out_ref, count = refs[-1], refs[0].shape[0]
+    for i, got_ref in enumerate(refs[:-1]):
+        rows = slice(i * count, (i + 1) * count)
+        kept, got = kept_ref[rows, :], got_ref[...].astype(F32)
         out_ref[rows, :] = (kept + got).astype(BF16)
         if with_steps:
             wide = kept[:, -LANES:] + decoded(got[:, -LANES:], heads)
@@ -204,9 +200,9 @@
             out_ref[rows, -LANES:] = coded(jnp.where(lane < heads, wide, 0.0), heads).astype(BF16)
 
 
-def relayed(kept, first, second, heads, with_steps):
-    rows, width = kept.shape[1:]
-    half = pl.BlockSpec((rows // 2, width), lambda i: (0, 0))
+def relayed(kept, got, heads, with_steps):
+    rows, width = kept.shape
+    part = pl.BlockSpec((rows // len(got), width), lambda i: (0, 0))
     return call(
         functools.partial(relay_kernel, heads, with_steps),
         "relay",
@@ -214,13 +210,13 @@
         moved=8 * rows * width,
         vmem=12,
         grid=(1,),
-        in_specs=[pl.BlockSpec((1, rows, width), lambda i: (0, 0, 0)), half, half],
+        in_specs=[pl.BlockSpec((rows, width), lambda i: (0, 0))] + [part] * len(got),
         out_specs=pl.BlockSpec((rows, width), lambda i: (0, 0)),
-    )(kept, first, second)
+    )(kept, *got)
 
 
 def rim_kernel(kept, got_c, got_f, rim_ref):
-    rim_ref[...] = (kept[0] + got_c[...].astype(F32) + got_f[...].astype(F32)).astype(BF16)
+    rim_ref[...] = (kept[...] + got_c[...].astype(F32) + got_f[...].astype(F32)).astype(BF16)
 
 
 def rows_before(kept, got_c, got_f):
@@ -233,7 +229,7 @@
         moved=10 * RIM * width,
         vmem=12,
         grid=(1,),
-        in_specs=[pl.BlockSpec((1, RIM, width), lambda i: (1, at, 0))] + [pl.BlockSpec((RIM, width), lambda i: (at, 0))] * 2,
+        in_specs=[pl.BlockSpec((RIM, width), lambda i: (at, 0))] * 3,
         out_specs=pl.BlockSpec((RIM, width), lambda i: (0, 0)),
     )(kept, got_c, got_f)
     return lax.ppermute(rim, SEQ, [(i, i + 1) for i in range(lax.axis_size(SEQ) - 1)])
@@ -241,7 +237,7 @@
 
 def convolved(width, kept, got_c, got_f, rim, taps, padded):
     count = padded.shape[0] - 8
-    proj = kept[0, :, :width] + got_c[:, :width].astype(F32) + got_f[:, :width].astype(F32)
+    proj = kept[:, :width] + got_c[:, :width].astype(F32) + got_f[:, :width].astype(F32)
     padded[8:, :] = proj.astype(BF16).astype(F32)
     padded[:8, :] = rim[:, :width].astype(F32)[RIM - 8 :]
     first = 8 - (CONV - 1)
@@ -256,7 +252,7 @@
 ):
     count, width = out_ref.shape
     out_ref[...] = convolved(width, kept, got_c, got_f, rim, taps, padded)
-    logits = kept[0, :, width:] + decoded(got_c[:, width:].astype(F32), heads) + decoded(got_f[:, width:].astype(F32), heads)
+    logits = kept[:, width:] + decoded(got_c[:, width:].astype(F32), heads) + decoded(got_f[:, width:].astype(F32), heads)
     steps = jax.nn.softplus(logits[:, :heads] + bias[...])
     row = lax.broadcasted_iota(jnp.int32, (SPAN, SPAN), 0)
     col = lax.broadcasted_iota(jnp.int32, (SPAN, SPAN), 1)
@@ -428,21 +424,21 @@
     place = lax.axis_index("chip") if plane else 0
     at = jnp.stack([lax.axis_index(a) for a in ("fsdp", "core", "tp")] + [place ^ i for i in range(chips)]).astype(jnp.int32)
     share, depth = tokens.shape[0], chips * rows_k
-    cut = lambda rows: jax.ShapeDtypeStruct((rows, depth), BF16)
-    far_sent, far_kept, own = call(
+    weight_bc = sampled_pair(bc_mean, bc_devs, dt_weight, swag_coef)
+    tokens = after(tokens, weight_bc)
+    cut = jax.ShapeDtypeStruct((2 * share, depth), BF16)
+    far, own = call(
         functools.partial(cut_kernel, chips),
         "cut_tokens",
-        (cut(share), cut(share), cut(2 * share)),
+        (cut,) * 2,
         moved=4 * tokens.size,
         in_specs=[SMEM, VMEM],
-        out_specs=[VMEM] * 3,
+        out_specs=[VMEM] * 2,
     )(at, tokens)
-    proj_mean, bc_mean = after((proj_mean, bc_mean), own)
-    far_sent = swapped(far_sent, "fsdp")
-    far_kept = swapped(after(far_kept, far_sent), "fsdp")
+    proj_mean = after(proj_mean, own)
+    far = swapped(far, "fsdp")
 
     weight_early = sampled_cols(proj_mean, proj_devs, swag_coef, 0, early_groups * width)
-    weight_bc = sampled_pair(bc_mean, bc_devs, dt_weight, swag_coef)
     weight_late = None
     if late:
         weight_late = sampled_cols(proj_mean, proj_devs, swag_coef, early_groups // len(late), len(late) * width)
@@ -450,14 +446,12 @@
     blocks = tok_count // SPAN
 
     def partial_sums(rows, pieces, with_steps, earlier=()):
-        first, second, sent, kept = multiplied(rows, pieces, heads_here, with_steps)
-        first, second = after((first, second), earlier)
-        back = relayed(kept, swapped(first, "core"), swapped(second, "core"), heads_here, with_steps)
+        *far_sent, sent, far_kept, kept = multiplied(rows, pieces, heads_here, with_steps)
+        far_sent = after(far_sent, earlier)
+        back = relayed(far_kept, [swapped(a, "core") for a in far_sent], heads_here, with_steps)
         return (kept, swapped(after(sent, back), "core")), back
 
-    specs_of = lambda width: [pl.BlockSpec((1, tok_count, width), lambda i: (1, 0, i))] + [
-        pl.BlockSpec((tok_count, width), lambda i: (0, i)),
-        pl.BlockSpec((tok_count, width), lambda i: (0, i)),
+    specs_of = lambda width: [pl.BlockSpec((tok_count, width), lambda i: (0, i))] * 3 + [
         pl.BlockSpec((RIM, width), lambda i: (0, i)),
     ]
     whole_of = lambda *shape: pl.BlockSpec(shape, lambda i: (0,) * len(shape))
@@ -479,31 +473,30 @@
         bc = [weight_bc, *sent_straight(weight_bc)]
         bc += sent_on(corner_parts(bc[1:], 1))
         own_t = swapped(own, "tp")
-        far_sent = after(far_sent, (own_t, weight_early, weight_late))
-        sent_t = swapped(far_sent, "tp")
-        got, got_t = swapped(far_sent, "core"), swapped(sent_t, "core")
-        far_kept = after(far_kept, got_t)
-        own, own_t = after((own, own_t), far_kept)
+        weight_early = after(weight_early, bc[3:])
+        early = [weight_early, *sent_straight(weight_early)]
+        far = after(far, (own_t, bc[3:], weight_late))
+        far_t = swapped(far, "tp")
+        own, own_t = after((own, own_t), far)
         own_c, own_tc = swapped(own, "core"), swapped(own_t, "core")
-        kept_t = swapped(far_kept, "tp")
-        weight_early = after(weight_early, (bc[3:], far_kept))
-        early = [weight_early, *sent_straight(weight_early)]
-        rows = token_rows(at, far_kept, kept_t, got, got_t, own, own_t, own_c, own_tc)
+        halves = corner_parts(early[1:], 1)
+        far_c, far_tc = swapped(far, "core"), swapped(after(far_t, halves), "core")
+        rows = token_rows(at, far, far_t, far_c, far_tc, own, own_t, own_c, own_tc)
         part_bc, back_bc = partial_sums(rows, bc, True)
-        early += sent_on(corner_parts(after(early[1:], back_bc), 1))
+        early += sent_on(halves)
         got_bc = swapped(back_bc, "fsdp")
-        weight_late = after(weight_late, (back_bc, early[1:3]))
+        weight_late = after(weight_late, (back_bc, early[3:]))
         part, back = partial_sums(rows, early, False, got_bc)
         got = swapped(after(back, got_bc), "fsdp")
         straight = sent_straight(weight_late)
-        seen = state_proj(after(part_bc + (got_bc,), back))
         corners = sent_on(after(corner_parts(straight, 2), back))
-        part_late, back_late = partial_sums(rows, after([weight_late, *straight, *corners], seen), False)
+        part_late, back_late = partial_sums(rows, after([weight_late, *straight, *corners], back), False)
+        seen = state_proj(after(part_bc + (got_bc,), back_late))
         got_late = swapped(after(back_late, got), "fsdp")
         got = after(got, back_late)
     else:
         whole = lambda a, axis: lax.all_gather(a, axis, axis=0, tiled=True)
-        ranges = [far_kept, swapped(far_sent, "core"), own[:share], swapped(own[share:], "core")]
+        ranges = [r for a in (far, own) for r in (a[:share], swapped(a[share:], "core"))]
         rows = jnp.concatenate([whole(r, "tp") for r in ranges], axis=0)
         part, back = partial_sums(rows, [whole(weight_early, "chip")], False)
         part_bc, back_bc = partial_sums(rows, [whole(weight_bc, "chip")], True)

time: 275 us -> 246 us (0.89)
  waiting for transfers between devices: 123 us -> 100 us
  starting transfers between devices: 52.7 us -> 48 us
    ppermute x41 -> x45, waiting for transfers between devices: 122 us -> 99.3 us  [swapped(): lax.ppermute(part, axis, [(i, i ^ by) for i in range(lax.axis_size(axis))])]
    ppermute x41 -> x45, starting transfers between devices: 47.7 us -> 41.6 us  [swapped(): lax.ppermute(part, axis, [(i, i ^ by) for i in range(lax.axis_size(axis))])]
    unnamed x88 -> x76, local copies, waits for them, and re-layouts: 14.7 us -> 14.1 us
  transfers between devices with their start and end apart: 44 -> 48, of which waited for: 23 -> 30; matrix products, arithmetic and copies ran while one was open for 3% -> 3% of each run, Pallas kernels for 23% -> 24%
where the time goes in v6:
time: 246 us; the launch traced here: 245 us
  waiting for transfers between devices  100 us (41%)
  Pallas kernels  75.1 us (31%)
  starting transfers between devices  48 us (20%)
  local copies, waits for them, and re-layouts  21.5 us (9%)
    ppermute x45, waiting for transfers between devices, swapped(): lax.ppermute(part, axis, [(i, i ^ by) for i in range(lax.axis_size(axis))])  99.3 us
    ppermute x45, starting transfers between devices, swapped(): lax.ppermute(part, axis, [(i, i ^ by) for i in range(lax.axis_size(axis))])  41.6 us
    pallas_call x3, Pallas kernels, multiplied(): call(functools.partial(multiply_kernel, heads, with_steps, len(weights)),...  29.5 us
    unnamed x76, local copies, waits for them, and re-layouts  14.1 us
    pallas_call x2, Pallas kernels, body(): call(mix_kernel, 'mix', (jax.ShapeDtypeStruct((tok_count, groups * width)...  10 us
    pallas_call x2, Pallas kernels, sampled_cols(): call(functools.partial(sample_kernel, count), 'sample', jax.ShapeDtypeStr...  9.31 us
    pallas_call x1, Pallas kernels, sampled_pair(): call(functools.partial(sample_pair_kernel, count), 'sample_pair', jax.Sha...  7.76 us
    ppermute x3, starting transfers between devices, rows_before(): lax.ppermute(rim, SEQ, [(i, i + 1) for i in range(lax.axis_size(SEQ) - 1)])  6.46 us
  transfers between devices with their start and end apart: 48, of which 30 were waited for; matrix products, arithmetic and copies ran while one was open for 3% of the time, Pallas kernels for 24%

profile of v6, /device:TPU:0, one launch (start us, length us, event | category | flops | bytes accessed | tf_op | source)
XLA Modules:
  0.0 245.1 jit_solution(6026495401874430704)
XLA Ops:
  1.5 7.8 %sample_pair.1.refs_0_ = bf16[512,1152]{1,0:T(8,128)(2,1)} custom-call(f32[4]{0:T(128)} %coef_ref.5, bf16[512,2,512]{2,1,0:T(2,128)(2,1)} %mean_ref.1, bf16[4,512,2,512]{3,2,1,0:T(2,128)(2,1)} %devs_ref.3, bf16[512,32]{1,0:T(8,128)(2,1)} %copy.14.dt_ref), custom_call_target="tpu_custom_call" | custom-call | bytes 125829 | tf_op jit(solution)/shard_map/sample_pair/pallas_call | solution.py:116
  14.4 3.1 %cut_tokens.1 = (bf16[256,2048]{1,0:T(8,128)(2,1)}, bf16[256,2048]{1,0:T(8,128)(2,1)}) custom-call(s32[7]{0:T(128)} %stack.31.at_ref, bf16[128,8192]{1,0:T(8,128)(2,1)} %tokens_ref), custom_call_target="tpu_custom_call" | custom-call | bytes 83886 | tf_op jit(solution)/shard_map/cut_tokens/pallas_call | solution.py:430
  21.6 16.8 %collective-permute-done.2.refs_2_ = bf16[512,1152]{1,0:T(8,128)(2,1)S(1)} collective-permute-done((bf16[512,1152]{1,0:T(8,128)(2,1)}, bf16[512,1152]{1,0:T(8,128)(2,1)S(1)}, u32[]{:S(2)}, u32[]{:S(2)}) %collective-permute-start.2) | collective-permute-done | bytes 1179680 | tf_op jit(solution)/shard_map/ppermute | solution.py:36
  44.5 4.6 %sample.2.refs_0_ = bf16[512,1024]{1,0:T(8,128)(2,1)} custom-call(f32[4]{0:T(128)} %coef_ref.5, bf16[512,2048]{1,0:T(8,128)(2,1)} %mean_ref.3, bf16[4,512,2048]{2,1,0:T(8,128)(2,1)} %devs_ref.5), custom_call_target="tpu_custom_call" | custom-call | bytes 125829 | tf_op jit(solution)/shard_map/sample/pallas_call | solution.py:85
  49.1 4.7 %sample.3.refs_0_ = bf16[512,1024]{1,0:T(8,128)(2,1)} custom-call(f32[4]{0:T(128)} %coef_ref.5, bf16[512,2048]{1,0:T(8,128)(2,1)} %mean_ref.3, bf16[4,512,2048]{2,1,0:T(8,128)(2,1)} %devs_ref.5), custom_call_target="tpu_custom_call" | custom-call | bytes 125829 | tf_op jit(solution)/shard_map/sample/pallas_call | solution.py:85
  54.2 3.2 %collective-permute-done.5.refs_4_ = bf16[256,1152]{1,0:T(8,128)(2,1)} collective-permute-done((bf16[256,1152]{1,0:T(8,128)(2,1)}, bf16[256,1152]{1,0:T(8,128)(2,1)}, u32[]{:S(2)}, u32[]{:S(2)}) %collective-permute-start.5) | collective-permute-done | bytes 589856 | tf_op jit(solution)/shard_map/ppermute | solution.py:36
  59.4 6.1 %collective-permute-done.refs_0_ = bf16[256,2048]{1,0:T(8,128)(2,1)S(1)} collective-permute-done((bf16[256,2048]{1,0:T(8,128)(2,1)}, bf16[256,2048]{1,0:T(8,128)(2,1)S(1)}, u32[]{:S(2)}, u32[]{:S(2)}) %collective-permute-start) | collective-permute-done | bytes 1048608 | tf_op jit(solution)/shard_map/ppermute | solution.py:36
  67.6 12.9 %collective-permute-done.8.refs_2_ = bf16[512,1024]{1,0:T(8,128)(2,1)S(1)} collective-permute-done((bf16[512,1024]{1,0:T(8,128)(2,1)}, bf16[512,1024]{1,0:T(8,128)(2,1)S(1)}, u32[]{:S(2)}, u32[]{:S(2)}) %collective-permute-start.8) | collective-permute-done | bytes 1048608 | tf_op jit(solution)/shard_map/ppermute | solution.py:36
  82.6 6.8 %collective-permute-done.6.refs_1_ = bf16[256,2048]{1,0:T(8,128)(2,1)S(1)} collective-permute-done((bf16[256,2048]{1,0:T(8,128)(2,1)S(1)}, bf16[256,2048]{1,0:T(8,128)(2,1)S(1)}, u32[]{:S(2)}, u32[]{:S(2)}) %collective-permute-start.6) | collective-permute-done | bytes 1048608 | tf_op jit(solution)/shard_map/ppermute | solution.py:36
  95.0 11.8 %multiply.3 = (bf16[64,1152]{1,0:T(8,128)(2,1)}, bf16[64,1152]{1,0:T(8,128)(2,1)}, bf16[64,1152]{1,0:T(8,128)(2,1)}, bf16[64,1152]{1,0:T(8,128)(2,1)}, bf16[256,...) custom-call(bf16[1024,2048]{1,0:T(8,128)(2,1)} %copy-done, bf16[512,1152]{1,0:T(8,128)(2,1)} %sample_pair.1.refs_0_, ...), custom_call_target="tpu_custom_call" | custom-call | flops 96636768 | bytes 249036 | tf_op jit(solution)/shard_map/multiply/pallas_call | solution.py:178
  112.2 3.3 %collective-permute-start.21 = (bf16[256,1152]{1,0:T(8,128)(2,1)S(1)}, bf16[256,1152]{1,0:T(8,128)(2,1)S(1)}, u32[]{:S(2)}, u32[]{:S(2)}) collective-permute-start(bf16[256,1152]{1,0:T(8,128)(2,1)S(1)} %relay.3), channel_id=1, source_target_pairs={{0,16},{16,0},{1,17},{17,1},{2,18},{18,2},{3,19},{19,3},{4,20},{20... | collective-permute-start | bytes 1769480 | tf_op jit(solution)/shard_map/ppermute | solution.py:36
  116.4 8.8 %multiply.4 = (bf16[64,1024]{1,0:T(8,128)(2,1)}, bf16[64,1024]{1,0:T(8,128)(2,1)}, bf16[64,1024]{1,0:T(8,128)(2,1)}, bf16[64,1024]{1,0:T(8,128)(2,1)}, bf16[256,...) custom-call(bf16[1024,2048]{1,0:T(8,128)(2,1)} %copy-done, bf16[512,1024]{1,0:T(8,128)(2,1)} %sample.3.refs_0_, ...), custom_call_target="tpu_custom_call" | custom-call | flops 85899344 | bytes 230686 | tf_op jit(solution)/shard_map/multiply/pallas_call | solution.py:178
  125.2 16.2 %collective-permute-done.21.got_f = bf16[256,1152]{1,0:T(8,128)(2,1)S(1)} collective-permute-done((bf16[256,1152]{1,0:T(8,128)(2,1)S(1)}, bf16[256,1152]{1,0:T(8,128)(2,1)S(1)}, u32[]{:S(2)}, u32[]{:S(2)}) %collective-permute-start.21) | collective-permute-done | bytes 589856 | tf_op jit(solution)/shard_map/ppermute | solution.py:36
  152.3 5.1 %collective-permute-done.26.refs_3_ = bf16[128,1024]{1,0:T(8,128)(2,1)S(1)} collective-permute-done((bf16[128,1024]{1,0:T(8,128)(2,1)S(1)}, bf16[128,1024]{1,0:T(8,128)(2,1)S(1)}, u32[]{:S(2)}, u32[]{:S(2)}) %collective-permute-start.26) | collective-permute-done | bytes 262176 | tf_op jit(solution)/shard_map/ppermute | solution.py:36
  157.4 4.8 %collective-permute-done.27.refs_4_ = bf16[128,1024]{1,0:T(8,128)(2,1)S(1)} collective-permute-done((bf16[128,1024]{1,0:T(8,128)(2,1)S(1)}, bf16[128,1024]{1,0:T(8,128)(2,1)S(1)}, u32[]{:S(2)}, u32[]{:S(2)}) %collective-permute-start.27) | collective-permute-done | bytes 262176 | tf_op jit(solution)/shard_map/ppermute | solution.py:36
  164.4 8.9 %multiply.5 = (bf16[64,1024]{1,0:T(8,128)(2,1)}, bf16[64,1024]{1,0:T(8,128)(2,1)}, bf16[64,1024]{1,0:T(8,128)(2,1)}, bf16[64,1024]{1,0:T(8,128)(2,1)}, bf16[256,...) custom-call(bf16[1024,2048]{1,0:T(8,128)(2,1)} %copy-done, bf16[512,1024]{1,0:T(8,128)(2,1)} %sample.2.refs_0_, ...), custom_call_target="tpu_custom_call" | custom-call | flops 85899344 | bytes 230686 | tf_op jit(solution)/shard_map/multiply/pallas_call | solution.py:178
  187.1 4.6 %state_proj.1 = (bf16[256,1024]{1,0:T(8,128)(2,1)}, f32[4,256,8]{2,1,0:T(8,128)}, f32[4,256,8]{2,1,0:T(8,128)}, f32[32,256]{1,0:T(8,128)}, f32[32,256]{1,0:T(8,128)}, /*index=5*/f32[4,1,8]{2,1,0:T(1,128)}) custom-call(f32[256,1152]{1,0:T(8,128)} %get-tuple-element.161.kept, bf16[256,1152]{1,0:T(8,128)(2,1)} %copy-done.7, bf16[256,1152]{1,0:T(8,128)(2,1)} %copy-done.6, ...), custom_call_target="tpu_custom_call" | custom-call | bytes 52428 | tf_op jit(solution)/shard_map/state_proj/pallas_call | solution.py:461
  192.3 5.0 %mix.2 = (f32[256,1024]{1,0:T(8,128)}, f32[1,128,1024]{2,1,0:T(8,128)}, f32[128,1024]{1,0:T(8,128)}, f32[8,1024]{1,0:T(8,128)}, bf16[144,1024]{1,0:T(8,128)(2,1)}) custom-call(f32[256,1024]{1,0:T(8,128)} %get-tuple-element.154.kept, bf16[256,1024]{1,0:T(8,128)(2,1)} %collective-permute-done.37.got_c, bf16[256,1024]{1,0:T(8,128)(2,1)} %copy-done.8, ...), custom_call_target="tpu_custom_call" | custom-call | flops 5368709 | bytes 73400 | tf_op jit(solution)/shard_map/mix/pallas_call | solution.py:531
  201.4 4.2 %collective-permute-done.36.got_f = bf16[256,1024]{1,0:T(8,128)(2,1)} collective-permute-done((bf16[256,1024]{1,0:T(8,128)(2,1)}, bf16[256,1024]{1,0:T(8,128)(2,1)}, u32[]{:S(2)}, u32[]{:S(2)}) %collective-permute-start.36) | collective-permute-done | bytes 524320 | tf_op jit(solution)/shard_map/ppermute | solution.py:36
  209.1 5.0 %mix.3 = (f32[256,1024]{1,0:T(8,128)}, f32[1,128,1024]{2,1,0:T(8,128)}, f32[128,1024]{1,0:T(8,128)}, f32[8,1024]{1,0:T(8,128)}, bf16[144,1024]{1,0:T(8,128)(2,1)}) custom-call(f32[256,1024]{1,0:T(8,128)} %get-tuple-element.174.kept, bf16[256,1024]{1,0:T(8,128)(2,1)} %collective-permute-done.34.got_c, bf16[256,1024]{1,0:T(8,128)(2,1)} %collective-permute-done.36.got_f, ...), custom_call_target="tpu_custom_call" | custom-call | flops 5368709 | bytes 73400 | tf_op jit(solution)/shard_map/mix/pallas_call | solution.py:531
  222.2 3.9 %collective-permute-done.46.other = bf16[144,1024]{1,0:T(8,128)(2,1)S(1)} collective-permute-done((bf16[144,1024]{1,0:T(8,128)(2,1)S(1)}, bf16[144,1024]{1,0:T(8,128)(2,1)S(1)}, u32[]{:S(2)}, u32[]{:S(2)}) %collective-permute-start.46) | collective-permute-done | bytes 294944 | tf_op jit(solution)/shard_map/ppermute | solution.py:36
  227.2 3.4 %collective-permute-start.47 = (bf16[144,1024]{1,0:T(8,128)(2,1)S(1)}, bf16[144,1024]{1,0:T(8,128)(2,1)S(1)}, u32[]{:S(2)}, u32[]{:S(2)}) collective-permute-start(bf16[144,1024]{1,0:T(8,128)(2,1)S(1)} %get-tuple-element.196), channel_id=1, source_target_pairs={{0,8},{2,10},{4,12},{6,14},{8,0},{10,2},{12,4},{14,6},{1,9},{3,11}... | collective-permute-start | bytes 884744 | tf_op jit(solution)/shard_map/ppermute | solution.py:36
  233.2 3.3 %collective-permute-start.45 = (bf16[144,1024]{1,0:T(8,128)(2,1)S(1)}, bf16[144,1024]{1,0:T(8,128)(2,1)S(1)}, u32[]{:S(2)}, u32[]{:S(2)}) collective-permute-start(bf16[144,1024]{1,0:T(8,128)(2,1)S(1)} %get-tuple-element.188), channel_id=1, source_target_pairs={{0,8},{2,10},{4,12},{6,14},{8,0},{10,2},{12,4},{14,6},{1,9},{3,11}... | collective-permute-start | bytes 884744 | tf_op jit(solution)/shard_map/ppermute | solution.py:36
  238.8 4.5 %collective-permute-done.45.other = bf16[144,1024]{1,0:T(8,128)(2,1)S(1)} collective-permute-done((bf16[144,1024]{1,0:T(8,128)(2,1)S(1)}, bf16[144,1024]{1,0:T(8,128)(2,1)S(1)}, u32[]{:S(2)}, u32[]{:S(2)}) %collective-permute-start.45) | collective-permute-done | bytes 294944 | tf_op jit(solution)/shard_map/ppermute | solution.py:36
  (179 shorter events, 85.9 us)
Async XLA Ops:
  9.3 29.1 %collective-permute-start.2 = (bf16[512,1152]{1,0:T(8,128)(2,1)}, bf16[512,1152]{1,0:T(8,128)(2,1)S(1)}, u32[]{:S(2)}, u32[]{:S(2)}) collective-permute-start(bf16[512,1152]{1,0:T(8,128)(2,1)} %sample_pair.1.refs_0_), channel_id=1, source_target_pairs={{0,8},{4,12},{8,0},{12,4},{1,9},{5,13},{9,1},{13,5},{2,10},{6,14},... | collective-permute-start | bytes 3538952 | tf_op jit(solution)/shard_map/ppermute | solution.py:36
  12.2 28.8 %collective-permute-start.4 = (bf16[512,1152]{1,0:T(8,128)(2,1)}, bf16[512,1152]{1,0:T(8,128)(2,1)}, u32[]{:S(2)}, u32[]{:S(2)}) collective-permute-start(bf16[512,1152]{1,0:T(8,128)(2,1)} %sample_pair.1.refs_0_), channel_id=1, source_target_pairs={{0,4},{4,0},{8,12},{12,8},{1,5},{5,1},{9,13},{13,9},{2,6},{6,2},{1... | collective-permute-start | bytes 3538952 | tf_op jit(solution)/shard_map/ppermute | solution.py:36
  17.4 48.0 %collective-permute-start = (bf16[256,2048]{1,0:T(8,128)(2,1)}, bf16[256,2048]{1,0:T(8,128)(2,1)S(1)}, u32[]{:S(2)}, u32[]{:S(2)}) collective-permute-start(bf16[256,2048]{1,0:T(8,128)(2,1)} %get-tuple-element.102), channel_id=1, source_target_pairs={{0,16},{16,0},{1,17},{17,1},{2,18},{18,2},{3,19},{19,3},{4,20},{20... | collective-permute-start | bytes 3145736 | tf_op jit(solution)/shard_map/ppermute | solution.py:36
  20.0 45.6 %collective-permute-start.1 = (bf16[256,2048]{1,0:T(8,128)(2,1)}, bf16[256,2048]{1,0:T(8,128)(2,1)S(1)}, u32[]{:S(2)}, u32[]{:S(2)}) collective-permute-start(bf16[256,2048]{1,0:T(8,128)(2,1)} %get-tuple-element.108.refs_4_), channel_id=1, source_target_pairs={{0,1},{1,0},{2,3},{3,2},{4,5},{5,4},{6,7},{7,6},{8,9},{9,8},{10,11... | collective-permute-start | bytes 3145736 | tf_op jit(solution)/shard_map/ppermute | solution.py:36
  39.3 14.8 %collective-permute-start.3 = (bf16[256,1152]{1,0:T(8,128)(2,1)}, bf16[256,1152]{1,0:T(8,128)(2,1)S(1)}, u32[]{:S(2)}, u32[]{:S(2)}) collective-permute-start(bf16[256,1152]{1,0:T(8,128)(2,1)} %slice.32), channel_id=1, source_target_pairs={{0,4},{4,0},{8,12},{12,8},{1,5},{5,1},{9,13},{13,9},{2,6},{6,2},{1... | collective-permute-start | bytes 1769480 | tf_op jit(solution)/shard_map/ppermute | solution.py:36
  43.0 14.3 %collective-permute-start.5 = (bf16[256,1152]{1,0:T(8,128)(2,1)}, bf16[256,1152]{1,0:T(8,128)(2,1)}, u32[]{:S(2)}, u32[]{:S(2)}) collective-permute-start(bf16[256,1152]{1,0:T(8,128)(2,1)} %slice.33), channel_id=1, source_target_pairs={{0,8},{4,12},{8,0},{12,4},{1,9},{5,13},{9,1},{13,5},{2,10},{6,14},... | collective-permute-start | bytes 1769480 | tf_op jit(solution)/shard_map/ppermute | solution.py:36
  57.3 23.1 %collective-permute-start.8 = (bf16[512,1024]{1,0:T(8,128)(2,1)}, bf16[512,1024]{1,0:T(8,128)(2,1)S(1)}, u32[]{:S(2)}, u32[]{:S(2)}) collective-permute-start(bf16[512,1024]{1,0:T(8,128)(2,1)} %sample.3.refs_0_), channel_id=1, source_target_pairs={{0,8},{4,12},{8,0},{12,4},{1,9},{5,13},{9,1},{13,5},{2,10},{6,14},... | collective-permute-start | bytes 3145736 | tf_op jit(solution)/shard_map/ppermute | solution.py:36
  58.8 22.9 %collective-permute-start.9 = (bf16[512,1024]{1,0:T(8,128)(2,1)}, bf16[512,1024]{1,0:T(8,128)(2,1)S(1)}, u32[]{:S(2)}, u32[]{:S(2)}) collective-permute-start(bf16[512,1024]{1,0:T(8,128)(2,1)} %sample.3.refs_0_), channel_id=1, source_target_pairs={{0,4},{4,0},{8,12},{12,8},{1,5},{5,1},{9,13},{13,9},{2,6},{6,2},{1... | collective-permute-start | bytes 3145736 | tf_op jit(solution)/shard_map/ppermute | solution.py:36
  65.7 23.8 %collective-permute-start.6 = (bf16[256,2048]{1,0:T(8,128)(2,1)S(1)}, bf16[256,2048]{1,0:T(8,128)(2,1)S(1)}, u32[]{:S(2)}, u32[]{:S(2)}) collective-permute-start(bf16[256,2048]{1,0:T(8,128)(2,1)S(1)} %collective-permute-done.refs_0_), channel_id=1, source_target_pairs={{0,1},{1,0},{2,3},{3,2},{4,5},{5,4},{6,7},{7,6},{8,9},{9,8},{10,11... | collective-permute-start | bytes 3145736 | tf_op jit(solution)/shard_map/ppermute | solution.py:36
  67.1 22.9 %collective-permute-start.7 = (bf16[256,2048]{1,0:T(8,128)(2,1)S(1)}, bf16[256,2048]{1,0:T(8,128)(2,1)S(1)}, u32[]{:S(2)}, u32[]{:S(2)}) collective-permute-start(bf16[256,2048]{1,0:T(8,128)(2,1)S(1)} %collective-permute-done.refs_0_), channel_id=1, source_target_pairs={{0,2},{2,0},{1,3},{3,1},{4,6},{6,4},{5,7},{7,5},{8,10},{10,8},{9,1... | collective-permute-start | bytes 3145736 | tf_op jit(solution)/shard_map/ppermute | solution.py:36
  67.1 23.4 %collective-permute-start.11 = (bf16[256,2048]{1,0:T(8,128)(2,1)S(1)}, bf16[256,2048]{1,0:T(8,128)(2,1)S(1)}, u32[]{:S(2)}, u32[]{:S(2)}) collective-permute-start(bf16[256,2048]{1,0:T(8,128)(2,1)S(1)} %copy-done.11), channel_id=1, source_target_pairs={{0,2},{2,0},{1,3},{3,1},{4,6},{6,4},{5,7},{7,5},{8,10},{10,8},{9,1... | collective-permute-start | bytes 3145736 | tf_op jit(solution)/shard_map/ppermute | solution.py:36
  89.5 22.1 %collective-permute-start.17 = (bf16[256,1024]{1,0:T(8,128)(2,1)}, bf16[256,1024]{1,0:T(8,128)(2,1)}, u32[]{:S(2)}, u32[]{:S(2)}) collective-permute-start(bf16[256,1024]{1,0:T(8,128)(2,1)} %slice.34), channel_id=1, source_target_pairs={{0,4},{4,0},{8,12},{12,8},{1,5},{5,1},{9,13},{13,9},{2,6},{6,2},{1... | collective-permute-start | bytes 1572872 | tf_op jit(solution)/shard_map/ppermute | solution.py:36
  90.0 21.5 %collective-permute-start.18 = (bf16[256,1024]{1,0:T(8,128)(2,1)}, bf16[256,1024]{1,0:T(8,128)(2,1)}, u32[]{:S(2)}, u32[]{:S(2)}) collective-permute-start(bf16[256,1024]{1,0:T(8,128)(2,1)} %slice.35), channel_id=1, source_target_pairs={{0,8},{4,12},{8,0},{12,4},{1,9},{5,13},{9,1},{13,5},{2,10},{6,14},... | collective-permute-start | bytes 1572872 | tf_op jit(solution)/shard_map/ppermute | solution.py:36
  111.6 35.1 %collective-permute-start.20 = (bf16[512,1024]{1,0:T(8,128)(2,1)S(1)}, bf16[512,1024]{1,0:T(8,128)(2,1)S(1)}, u32[]{:S(2)}, u32[]{:S(2)}) collective-permute-start(bf16[512,1024]{1,0:T(8,128)(2,1)S(1)} %copy-done.22), channel_id=1, source_target_pairs={{0,8},{4,12},{8,0},{12,4},{1,9},{5,13},{9,1},{13,5},{2,10},{6,14},... | collective-permute-start | bytes 3145736 | tf_op jit(solution)/shard_map/ppermute | solution.py:36
  112.2 29.3 %collective-permute-start.21 = (bf16[256,1152]{1,0:T(8,128)(2,1)S(1)}, bf16[256,1152]{1,0:T(8,128)(2,1)S(1)}, u32[]{:S(2)}, u32[]{:S(2)}) collective-permute-start(bf16[256,1152]{1,0:T(8,128)(2,1)S(1)} %relay.3), channel_id=1, source_target_pairs={{0,16},{16,0},{1,17},{17,1},{2,18},{18,2},{3,19},{19,3},{4,20},{20... | collective-permute-start | bytes 1769480 | tf_op jit(solution)/shard_map/ppermute | solution.py:36
  115.4 31.3 %collective-permute-start.19 = (bf16[512,1024]{1,0:T(8,128)(2,1)S(1)}, bf16[512,1024]{1,0:T(8,128)(2,1)}, u32[]{:S(2)}, u32[]{:S(2)}) collective-permute-start(bf16[512,1024]{1,0:T(8,128)(2,1)S(1)} %copy-done.22), channel_id=1, source_target_pairs={{0,4},{4,0},{8,12},{12,8},{1,5},{5,1},{9,13},{13,9},{2,6},{6,2},{1... | collective-permute-start | bytes 3145736 | tf_op jit(solution)/shard_map/ppermute | solution.py:36
  149.2 13.1 %collective-permute-start.27 = (bf16[128,1024]{1,0:T(8,128)(2,1)S(1)}, bf16[128,1024]{1,0:T(8,128)(2,1)S(1)}, u32[]{:S(2)}, u32[]{:S(2)}) collective-permute-start(bf16[128,1024]{1,0:T(8,128)(2,1)S(1)} %get-tuple-element.130), channel_id=1, source_target_pairs={{0,4},{4,0},{8,12},{12,8},{1,5},{5,1},{9,13},{13,9},{2,6},{6,2},{1... | collective-permute-start | bytes 786440 | tf_op jit(solution)/shard_map/ppermute | solution.py:36
  150.3 12.0 %collective-permute-start.28 = (bf16[128,1024]{1,0:T(8,128)(2,1)S(1)}, bf16[128,1024]{1,0:T(8,128)(2,1)S(1)}, u32[]{:S(2)}, u32[]{:S(2)}) collective-permute-start(bf16[128,1024]{1,0:T(8,128)(2,1)S(1)} %get-tuple-element.131), channel_id=1, source_target_pairs={{0,8},{4,12},{8,0},{12,4},{1,9},{5,13},{9,1},{13,5},{2,10},{6,14},... | collective-permute-start | bytes 786440 | tf_op jit(solution)/shard_map/ppermute | solution.py:36
  151.8 11.9 %collective-permute-start.29 = (bf16[128,1024]{1,0:T(8,128)(2,1)S(1)}, bf16[128,1024]{1,0:T(8,128)(2,1)S(1)}, u32[]{:S(2)}, u32[]{:S(2)}) collective-permute-start(bf16[128,1024]{1,0:T(8,128)(2,1)S(1)} %get-tuple-element.132), channel_id=1, source_target_pairs={{0,8},{4,12},{8,0},{12,4},{1,9},{5,13},{9,1},{13,5},{2,10},{6,14},... | collective-permute-start | bytes 786440 | tf_op jit(solution)/shard_map/ppermute | solution.py:36
  152.3 26.8 %collective-permute-start.35 = (bf16[256,1024]{1,0:T(8,128)(2,1)}, bf16[256,1024]{1,0:T(8,128)(2,1)S(1)}, u32[]{:S(2)}, u32[]{:S(2)}) collective-permute-start(bf16[256,1024]{1,0:T(8,128)(2,1)} %relay.4), channel_id=1, source_target_pairs={{0,16},{16,0},{1,17},{17,1},{2,18},{18,2},{3,19},{19,3},{4,20},{20... | collective-permute-start | bytes 1572872 | tf_op jit(solution)/shard_map/ppermute | solution.py:36
  157.4 21.7 %collective-permute-start.39 = (bf16[256,1152]{1,0:T(8,128)(2,1)}, bf16[256,1152]{1,0:T(8,128)(2,1)S(1)}, u32[]{:S(2)}, u32[]{:S(2)}) collective-permute-start(bf16[256,1152]{1,0:T(8,128)(2,1)} %get-tuple-element.160), channel_id=1, source_target_pairs={{0,2},{2,0},{1,3},{3,1},{4,6},{6,4},{5,7},{7,5},{8,10},{10,8},{9,1... | collective-permute-start | bytes 1769480 | tf_op jit(solution)/shard_map/ppermute | solution.py:36
  162.2 19.2 %collective-permute-start.37 = (bf16[256,1024]{1,0:T(8,128)(2,1)}, bf16[256,1024]{1,0:T(8,128)(2,1)}, u32[]{:S(2)}, u32[]{:S(2)}) collective-permute-start(bf16[256,1024]{1,0:T(8,128)(2,1)} %get-tuple-element.156), channel_id=1, source_target_pairs={{0,2},{2,0},{1,3},{3,1},{4,6},{6,4},{5,7},{7,5},{8,10},{10,8},{9,1... | collective-permute-start | bytes 1572872 | tf_op jit(solution)/shard_map/ppermute | solution.py:36
  178.8 22.6 %collective-permute-start.34 = (bf16[256,1024]{1,0:T(8,128)(2,1)}, bf16[256,1024]{1,0:T(8,128)(2,1)}, u32[]{:S(2)}, u32[]{:S(2)}) collective-permute-start(bf16[256,1024]{1,0:T(8,128)(2,1)} %get-tuple-element.151), channel_id=1, source_target_pairs={{0,2},{2,0},{1,3},{3,1},{4,6},{6,4},{5,7},{7,5},{8,10},{10,8},{9,1... | collective-permute-start | bytes 1572872 | tf_op jit(solution)/shard_map/ppermute | solution.py:36
  179.1 26.5 %collective-permute-start.36 = (bf16[256,1024]{1,0:T(8,128)(2,1)}, bf16[256,1024]{1,0:T(8,128)(2,1)}, u32[]{:S(2)}, u32[]{:S(2)}) collective-permute-start(bf16[256,1024]{1,0:T(8,128)(2,1)} %relay.5), channel_id=1, source_target_pairs={{0,16},{16,0},{1,17},{17,1},{2,18},{18,2},{3,19},{19,3},{4,20},{20... | collective-permute-start | bytes 1572872 | tf_op jit(solution)/shard_map/ppermute | solution.py:36
  (61 other events, 458.4 us)

commit v7 on v6

--- a/solution.py
+++ b/solution.py
@@ -13,7 +13,7 @@
 SPAN = 128
 LANES = 128
 RIM = 16
-FAR_PARTS = 4
+FAR_PARTS = 2
 SEQ = ("chip", "core")
 F32 = jnp.float32
 BF16 = jnp.bfloat16
@@ -153,38 +153,42 @@
     return part + pltpu.roll(part, LANES - heads, 1)
 
 
-def multiply_kernel(heads, with_steps, pieces, rows_ref, *refs):
-    weights, far_refs, (sent_ref, far_ref, own_ref) = refs[:pieces], refs[pieces:-3], refs[-3:]
+def multiply_kernel(heads, with_steps, pieces, plan, rows_ref, *refs):
+    weights, outs = refs[:pieces], refs[pieces:]
     joined = jnp.concatenate([weight[...] for weight in weights], axis=0)
     total = jnp.dot(rows_ref[...], joined, preferred_element_type=F32)
-    half = total.shape[0] // 4
-    far_ref[...] = total[:half]
-    own_ref[...] = total[2 * half : 3 * half]
-    parts = [(out, half + i * out.shape[0]) for i, out in enumerate(far_refs)]
-    for out, first in parts + [(sent_ref, 3 * half)]:
-        sent = total[first : first + out.shape[0]]
-        out[...] = sent.astype(BF16)
-        if with_steps:
+    for out, (first, sent) in zip(outs, plan):
+        part = total[first : first + out.shape[0]]
+        out[...] = part.astype(out.dtype)
+        if with_steps and sent:
             @pl.when(pl.program_id(0) == pl.num_programs(0) - 1)
             def _():
-                out[:, -LANES:] = coded(sent[:, -LANES:], heads).astype(BF16)
-
-
-def multiplied(rows, weights, heads, with_steps):
+                out[:, -LANES:] = coded(part[:, -LANES:], heads).astype(BF16)
+
+
+def multiplied(rows, weights, heads, with_steps, document=None):
     width = weights[0].shape[1]
     tile = next(t for t in (512, 384, 128) if width % t == 0)
     half = rows.shape[0] // 4
-    sent = lambda count: jax.ShapeDtypeStruct((count, width), BF16)
+    part = half // FAR_PARTS
+    plan, shapes = [], []
+    count = rows.shape[0] if document is None else 2 * half
+    if document != 1:
+        plan += [(half + i * part, True) for i in range(FAR_PARTS)] + [(0, False)]
+        shapes += [(part, BF16)] * FAR_PARTS + [(half, F32)]
+    if document != 0:
+        plan += [(count - half, True), (count - 2 * half, False)]
+        shapes += [(half, BF16), (half, F32)]
     return call(
-        functools.partial(multiply_kernel, heads, with_steps, len(weights)),
+        functools.partial(multiply_kernel, heads, with_steps, len(weights), plan),
         "multiply",
-        (sent(half // FAR_PARTS),) * FAR_PARTS + (sent(half),) + (jax.ShapeDtypeStruct((half, width), F32),) * 2,
-        flops=2 * rows.size * width,
+        tuple(jax.ShapeDtypeStruct((r, width), dtype) for r, dtype in shapes),
+        flops=2 * count * rows.shape[1] * width,
         moved=2 * rows.size + 2 * rows.shape[1] * width + 12 * half * width,
         grid=(width // tile,),
-        in_specs=[pl.BlockSpec(rows.shape, lambda i: (0, 0))]
+        in_specs=[pl.BlockSpec((count, rows.shape[1]), lambda i: (document or 0, 0))]
         + [pl.BlockSpec((w.shape[0], tile), lambda i: (0, i)) for w in weights],
-        out_specs=[pl.BlockSpec((count, tile), lambda i: (0, i)) for count in [half // FAR_PARTS] * FAR_PARTS + [half] * 3],
+        out_specs=[pl.BlockSpec((r, tile), lambda i: (0, i)) for r, _ in shapes],
     )(rows, *weights)
 
 
@@ -445,10 +449,10 @@
     tok_count = share * lax.axis_size("tp")
     blocks = tok_count // SPAN
 
-    def partial_sums(rows, pieces, with_steps, earlier=()):
-        *far_sent, sent, far_kept, kept = multiplied(rows, pieces, heads_here, with_steps)
-        far_sent = after(far_sent, earlier)
-        back = relayed(far_kept, [swapped(a, "core") for a in far_sent], heads_here, with_steps)
+    def partial_sums(rows, pieces, with_steps, before_send=(), before_relay=()):
+        *far_sent, far_kept, sent, kept = multiplied(rows, pieces, heads_here, with_steps)
+        far_got = [swapped(a, "core") for a in after(far_sent, before_send)]
+        back = relayed(far_kept, after(far_got, before_relay), heads_here, with_steps)
         return (kept, swapped(after(sent, back), "core")), back
 
     specs_of = lambda width: [pl.BlockSpec((tok_count, width), lambda i: (0, i))] * 3 + [
@@ -486,12 +490,12 @@
         early += sent_on(halves)
         got_bc = swapped(back_bc, "fsdp")
         weight_late = after(weight_late, (back_bc, early[3:]))
-        part, back = partial_sums(rows, early, False, got_bc)
+        part, back = partial_sums(rows, early, False, before_relay=got_bc)
         got = swapped(after(back, got_bc), "fsdp")
         straight = sent_straight(weight_late)
-        corners = sent_on(after(corner_parts(straight, 2), back))
-        part_late, back_late = partial_sums(rows, after([weight_late, *straight, *corners], back), False)
-        seen = state_proj(after(part_bc + (got_bc,), back_late))
+        corners = sent_on(corner_parts(straight, 1))
+        seen = state_proj(after(part_bc + (got_bc,), back))
+        part_late, back_late = partial_sums(rows, [weight_late, *straight, *corners], False, before_send=seen)
         got_late = swapped(after(back_late, got), "fsdp")
         got = after(got, back_late)
     else:
@@ -517,7 +521,7 @@
     result = None
     for first, groups, part in zip((0, early_groups), (early_groups, len(late)), parts):
         if first:
-            part = after(part, first_total)
+            part = after(part, first_sent)
         part = part + (rows_before(*part),)
         grid = (groups,)
         cols = lambda rows: pl.BlockSpec((rows, width), lambda i: (0, i))
@@ -545,13 +549,12 @@
             out_specs=[cols(tok_count), early_spec, cols(N), cols(8), cols(N + RIM)],
             scratch_shapes=[pltpu.VMEM((tok_count + 8, width), F32)],
         )(*part, conv_proj, conv_out, conv_out, cum_g, steps_g, cum_t, steps_t, skip, decay)
-        before = ()
-        first_total = None
+        before, first_sent = (), None
         for level in range(levels - 1):
             other = swapped(sent, SEQ, 1 << level)
             total, decays, sent, fresh = combined(level, seq_place, total, decays, other, before, groups)
             before = (fresh,)
-            first_total = total if first_total is None else first_total
+            first_sent = first_sent if level else sent
         other = swapped(sent, SEQ, 1 << (levels - 1))
         operands = [seq_place, y, conv_out, cum_g, early, decays, *before, other]
         specs = [SMEM, cols(tok_count), reads, heads_g, early_spec, cols(8), cols(N), cols(N + RIM)]

time: 246 us -> 238 us (0.967)
  waiting for transfers between devices: 100 us -> 87.3 us
  starting transfers between devices: 48 us -> 53.9 us
    ppermute x45 -> x37, waiting for transfers between devices: 99.3 us -> 86.2 us  [swapped(): lax.ppermute(part, axis, [(i, i ^ by) for i in range(lax.axis_size(axis))])]
    ppermute x45 -> x37, starting transfers between devices: 41.6 us -> 48.2 us  [swapped(): lax.ppermute(part, axis, [(i, i ^ by) for i in range(lax.axis_size(axis))])]
  transfers between devices with their start and end apart: 48 -> 40, of which waited for: 30 -> 24; matrix products, arithmetic and copies ran while one was open for 3% -> 4% of each run, Pallas kernels for 24% -> 25%
where the time goes in v7:
time: 238 us; the launch traced here: 237 us
  waiting for transfers between devices  87.3 us (37%)
  Pallas kernels  72.7 us (31%)
  starting transfers between devices  53.9 us (23%)
  local copies, waits for them, and re-layouts  22.6 us (9%)
    ppermute x37, waiting for transfers between devices, swapped(): lax.ppermute(part, axis, [(i, i ^ by) for i in range(lax.axis_size(axis))])  86.2 us
    ppermute x37, starting transfers between devices, swapped(): lax.ppermute(part, axis, [(i, i ^ by) for i in range(lax.axis_size(axis))])  48.2 us
    pallas_call x3, Pallas kernels, multiplied(): call(functools.partial(multiply_kernel, heads, with_steps, len(weights),...  29.5 us
    unnamed x76, local copies, waits for them, and re-layouts  12.9 us
    pallas_call x2, Pallas kernels, body(): call(mix_kernel, 'mix', (jax.ShapeDtypeStruct((tok_count, groups * width)...  10 us
    pallas_call x2, Pallas kernels, sampled_cols(): call(functools.partial(sample_kernel, count), 'sample', jax.ShapeDtypeStr...  9.33 us
    slice x6, local copies, waits for them, and re-layouts, corner_parts(): cut = lambda a, i: a[i * rows:(i + 1) * rows]  8.39 us
    pallas_call x1, Pallas kernels, sampled_pair(): call(functools.partial(sample_pair_kernel, count), 'sample_pair', jax.Sha...  7.75 us
  transfers between devices with their start and end apart: 40, of which 24 were waited for; matrix products, arithmetic and copies ran while one was open for 4% of the time, Pallas kernels for 25%

profile of v7, /device:TPU:0, one launch (start us, length us, event | category | flops | bytes accessed | tf_op | source)
XLA Modules:
  0.0 236.8 jit_solution(14178207552089179846)
XLA Ops:
  1.5 7.8 %sample_pair.1.refs_0_ = bf16[512,1152]{1,0:T(8,128)(2,1)} custom-call(f32[4]{0:T(128)} %coef_ref.5, bf16[512,2,512]{2,1,0:T(2,128)(2,1)} %mean_ref.1, bf16[4,512,2,512]{3,2,1,0:T(2,128)(2,1)} %devs_ref.3, bf16[512,32]{1,0:T(8,128)(2,1)} %copy.14.dt_ref), custom_call_target="tpu_custom_call" | custom-call | bytes 125829 | tf_op jit(solution)/shard_map/sample_pair/pallas_call | solution.py:116
  14.4 3.1 %cut_tokens.1 = (bf16[256,2048]{1,0:T(8,128)(2,1)}, bf16[256,2048]{1,0:T(8,128)(2,1)}) custom-call(s32[7]{0:T(128)} %stack.31.at_ref, bf16[128,8192]{1,0:T(8,128)(2,1)} %tokens_ref), custom_call_target="tpu_custom_call" | custom-call | bytes 83886 | tf_op jit(solution)/shard_map/cut_tokens/pallas_call | solution.py:434
  21.6 16.8 %collective-permute-done.2.refs_2_ = bf16[512,1152]{1,0:T(8,128)(2,1)S(1)} collective-permute-done((bf16[512,1152]{1,0:T(8,128)(2,1)}, bf16[512,1152]{1,0:T(8,128)(2,1)S(1)}, u32[]{:S(2)}, u32[]{:S(2)}) %collective-permute-start.2) | collective-permute-done | bytes 1179680 | tf_op jit(solution)/shard_map/ppermute | solution.py:36
  44.5 4.6 %sample.2.refs_0_ = bf16[512,1024]{1,0:T(8,128)(2,1)} custom-call(f32[4]{0:T(128)} %coef_ref.5, bf16[512,2048]{1,0:T(8,128)(2,1)} %mean_ref.3, bf16[4,512,2048]{2,1,0:T(8,128)(2,1)} %devs_ref.5), custom_call_target="tpu_custom_call" | custom-call | bytes 125829 | tf_op jit(solution)/shard_map/sample/pallas_call | solution.py:85
  49.1 4.7 %sample.3.refs_0_ = bf16[512,1024]{1,0:T(8,128)(2,1)} custom-call(f32[4]{0:T(128)} %coef_ref.5, bf16[512,2048]{1,0:T(8,128)(2,1)} %mean_ref.3, bf16[4,512,2048]{2,1,0:T(8,128)(2,1)} %devs_ref.5), custom_call_target="tpu_custom_call" | custom-call | bytes 125829 | tf_op jit(solution)/shard_map/sample/pallas_call | solution.py:85
  54.2 3.1 %collective-permute-done.5.refs_4_ = bf16[256,1152]{1,0:T(8,128)(2,1)} collective-permute-done((bf16[256,1152]{1,0:T(8,128)(2,1)}, bf16[256,1152]{1,0:T(8,128)(2,1)}, u32[]{:S(2)}, u32[]{:S(2)}) %collective-permute-start.5) | collective-permute-done | bytes 589856 | tf_op jit(solution)/shard_map/ppermute | solution.py:36
  59.4 6.1 %collective-permute-done.refs_0_ = bf16[256,2048]{1,0:T(8,128)(2,1)S(1)} collective-permute-done((bf16[256,2048]{1,0:T(8,128)(2,1)}, bf16[256,2048]{1,0:T(8,128)(2,1)S(1)}, u32[]{:S(2)}, u32[]{:S(2)}) %collective-permute-start) | collective-permute-done | bytes 1048608 | tf_op jit(solution)/shard_map/ppermute | solution.py:36
  67.6 12.8 %collective-permute-done.8.refs_2_ = bf16[512,1024]{1,0:T(8,128)(2,1)S(1)} collective-permute-done((bf16[512,1024]{1,0:T(8,128)(2,1)}, bf16[512,1024]{1,0:T(8,128)(2,1)S(1)}, u32[]{:S(2)}, u32[]{:S(2)}) %collective-permute-start.8) | collective-permute-done | bytes 1048608 | tf_op jit(solution)/shard_map/ppermute | solution.py:36
  82.6 6.9 %collective-permute-done.6.refs_1_ = bf16[256,2048]{1,0:T(8,128)(2,1)S(1)} collective-permute-done((bf16[256,2048]{1,0:T(8,128)(2,1)S(1)}, bf16[256,2048]{1,0:T(8,128)(2,1)S(1)}, u32[]{:S(2)}, u32[]{:S(2)}) %collective-permute-start.6) | collective-permute-done | bytes 1048608 | tf_op jit(solution)/shard_map/ppermute | solution.py:36
  95.0 11.8 %multiply.3 = (bf16[128,1152]{1,0:T(8,128)(2,1)}, bf16[128,1152]{1,0:T(8,128)(2,1)}, f32[256,1152]{1,0:T(8,128)}, bf16[256,1152]{1,0:T(8,128)(2,1)}, f32[256,1152]{1,0:T(8,128)}) custom-call(bf16[1024,2048]{1,0:T(8,128)(2,1)} %copy-done, bf16[512,1152]{1,0:T(8,128)(2,1)} %sample_pair.1.refs_0_, bf16[512,1152]{1,0:T(8,128)(2,1)} %collective-permute-done.4.refs_1_, ...), custom_call_target="tpu_custom_call" | custom-call | flops 96636768 | bytes 249036 | tf_op jit(solution)/shard_map/multiply/pallas_call | solution.py:182
  112.3 3.3 %collective-permute-start.22 = (bf16[256,1152]{1,0:T(8,128)(2,1)S(1)}, bf16[256,1152]{1,0:T(8,128)(2,1)S(1)}, u32[]{:S(2)}, u32[]{:S(2)}) collective-permute-start(bf16[256,1152]{1,0:T(8,128)(2,1)S(1)} %relay.3), channel_id=1, source_target_pairs={{0,16},{16,0},{1,17},{17,1},{2,18},{18,2},{3,19},{19,3},{4,20},{20... | collective-permute-start | bytes 1769480 | tf_op jit(solution)/shard_map/ppermute | solution.py:36
  115.5 8.9 %multiply.5 = (bf16[128,1024]{1,0:T(8,128)(2,1)}, bf16[128,1024]{1,0:T(8,128)(2,1)}, f32[256,1024]{1,0:T(8,128)}, bf16[256,1024]{1,0:T(8,128)(2,1)}, f32[256,1024]{1,0:T(8,128)}) custom-call(bf16[1024,2048]{1,0:T(8,128)(2,1)} %copy-done, bf16[512,1024]{1,0:T(8,128)(2,1)} %sample.3.refs_0_, bf16[512,1024]{1,0:T(8,128)(2,1)} %copy-done.28, ...), custom_call_target="tpu_custom_call" | custom-call | flops 85899344 | bytes 230686 | tf_op jit(solution)/shard_map/multiply/pallas_call | solution.py:182
  125.0 11.1 %collective-permute-done.18.refs_2_ = bf16[512,1024]{1,0:T(8,128)(2,1)} collective-permute-done((bf16[512,1024]{1,0:T(8,128)(2,1)S(1)}, bf16[512,1024]{1,0:T(8,128)(2,1)}, u32[]{:S(2)}, u32[]{:S(2)}) %collective-permute-start.18) | collective-permute-done | bytes 1048608 | tf_op jit(solution)/shard_map/ppermute | solution.py:36
  143.0 3.3 %collective-permute-start.29 = (bf16[256,1024]{1,0:T(8,128)(2,1)S(1)}, bf16[256,1024]{1,0:T(8,128)(2,1)S(1)}, u32[]{:S(2)}, u32[]{:S(2)}) collective-permute-start(bf16[256,1024]{1,0:T(8,128)(2,1)S(1)} %relay.4), channel_id=1, source_target_pairs={{0,16},{16,0},{1,17},{17,1},{2,18},{18,2},{3,19},{19,3},{4,20},{20... | collective-permute-start | bytes 1572872 | tf_op jit(solution)/shard_map/ppermute | solution.py:36
  150.2 4.6 %state_proj.1 = (bf16[256,1024]{1,0:T(8,128)(2,1)}, f32[4,256,8]{2,1,0:T(8,128)}, f32[4,256,8]{2,1,0:T(8,128)}, f32[32,256]{1,0:T(8,128)}, f32[32,256]{1,0:T(8,128)}, /*index=5*/f32[4,1,8]{2,1,0:T(1,128)}) custom-call(f32[256,1152]{1,0:T(8,128)} %get-tuple-element.116.kept, bf16[256,1152]{1,0:T(8,128)(2,1)} %copy-done.7, bf16[256,1152]{1,0:T(8,128)(2,1)} %copy-done.6, ...), custom_call_target="tpu_custom_call" | custom-call | bytes 52428 | tf_op jit(solution)/shard_map/state_proj/pallas_call | solution.py:465
  155.6 8.8 %multiply.4 = (bf16[128,1024]{1,0:T(8,128)(2,1)}, bf16[128,1024]{1,0:T(8,128)(2,1)}, f32[256,1024]{1,0:T(8,128)}, bf16[256,1024]{1,0:T(8,128)(2,1)}, f32[256,1024]{1,0:T(8,128)}) custom-call(bf16[1024,2048]{1,0:T(8,128)(2,1)} %copy-done, bf16[512,1024]{1,0:T(8,128)(2,1)} %sample.2.refs_0_, bf16[512,1024]{1,0:T(8,128)(2,1)} %collective-permute-done.17.refs_1_, ...), custom_call_target="tpu_custom_call" | custom-call | flops 85899344 | bytes 230686 | tf_op jit(solution)/shard_map/multiply/pallas_call | solution.py:182
  174.2 5.0 %mix.2 = (f32[256,1024]{1,0:T(8,128)}, f32[1,128,1024]{2,1,0:T(8,128)}, f32[128,1024]{1,0:T(8,128)}, f32[8,1024]{1,0:T(8,128)}, bf16[144,1024]{1,0:T(8,128)(2,1)}) custom-call(f32[256,1024]{1,0:T(8,128)} %get-tuple-element.132.kept, bf16[256,1024]{1,0:T(8,128)(2,1)} %copy-done.9, bf16[256,1024]{1,0:T(8,128)(2,1)} %copy-done.8, bf16[16,1024]{1,0:T(8,128)(2,1)} %copy-done.33, ...), custom_call_target="tpu_custom_call" | custom-call | flops 5368709 | bytes 73400 | tf_op jit(solution)/shard_map/mix/pallas_call | solution.py:535
  185.8 10.1 %collective-permute-done.30.got_f = bf16[256,1024]{1,0:T(8,128)(2,1)S(1)} collective-permute-done((bf16[256,1024]{1,0:T(8,128)(2,1)}, bf16[256,1024]{1,0:T(8,128)(2,1)S(1)}, u32[]{:S(2)}, u32[]{:S(2)}) %collective-permute-start.30) | collective-permute-done | bytes 524320 | tf_op jit(solution)/shard_map/ppermute | solution.py:36
  198.7 5.0 %mix.3 = (f32[256,1024]{1,0:T(8,128)}, f32[1,128,1024]{2,1,0:T(8,128)}, f32[128,1024]{1,0:T(8,128)}, f32[8,1024]{1,0:T(8,128)}, bf16[144,1024]{1,0:T(8,128)(2,1)}) custom-call(f32[256,1024]{1,0:T(8,128)} %get-tuple-element.140.kept, bf16[256,1024]{1,0:T(8,128)(2,1)} %copy-done.10, bf16[256,1024]{1,0:T(8,128)(2,1)} %copy-done.11, ...), custom_call_target="tpu_custom_call" | custom-call | flops 5368709 | bytes 73400 | tf_op jit(solution)/shard_map/mix/pallas_call | solution.py:535
  203.8 3.5 %collective-permute-start.35 = (bf16[144,1024]{1,0:T(8,128)(2,1)}, bf16[144,1024]{1,0:T(8,128)(2,1)S(1)}, u32[]{:S(2)}, u32[]{:S(2)}) collective-permute-start(bf16[144,1024]{1,0:T(8,128)(2,1)} %get-tuple-element.147), channel_id=1, source_target_pairs={{0,2},{2,0},{4,6},{6,4},{8,10},{10,8},{12,14},{14,12},{1,3},{3,1},... | collective-permute-start | bytes 884744 | tf_op jit(solution)/shard_map/ppermute | solution.py:36
  213.5 4.1 %collective-permute-done.38.other = bf16[144,1024]{1,0:T(8,128)(2,1)S(1)} collective-permute-done((bf16[144,1024]{1,0:T(8,128)(2,1)S(1)}, bf16[144,1024]{1,0:T(8,128)(2,1)S(1)}, u32[]{:S(2)}, u32[]{:S(2)}) %collective-permute-start.38) | collective-permute-done | bytes 294944 | tf_op jit(solution)/shard_map/ppermute | solution.py:36
  218.6 3.7 %collective-permute-start.39 = (bf16[144,1024]{1,0:T(8,128)(2,1)S(1)}, bf16[144,1024]{1,0:T(8,128)(2,1)S(1)}, u32[]{:S(2)}, u32[]{:S(2)}) collective-permute-start(bf16[144,1024]{1,0:T(8,128)(2,1)S(1)} %get-tuple-element.162), channel_id=1, source_target_pairs={{0,8},{2,10},{4,12},{6,14},{8,0},{10,2},{12,4},{14,6},{1,9},{3,11}... | collective-permute-start | bytes 884744 | tf_op jit(solution)/shard_map/ppermute | solution.py:36
  224.5 3.7 %collective-permute-start.37 = (bf16[144,1024]{1,0:T(8,128)(2,1)S(1)}, bf16[144,1024]{1,0:T(8,128)(2,1)S(1)}, u32[]{:S(2)}, u32[]{:S(2)}) collective-permute-start(bf16[144,1024]{1,0:T(8,128)(2,1)S(1)} %get-tuple-element.154), channel_id=1, source_target_pairs={{0,8},{2,10},{4,12},{6,14},{8,0},{10,2},{12,4},{14,6},{1,9},{3,11}... | collective-permute-start | bytes 884744 | tf_op jit(solution)/shard_map/ppermute | solution.py:36
  230.6 4.5 %collective-permute-done.37.other = bf16[144,1024]{1,0:T(8,128)(2,1)S(1)} collective-permute-done((bf16[144,1024]{1,0:T(8,128)(2,1)S(1)}, bf16[144,1024]{1,0:T(8,128)(2,1)S(1)}, u32[]{:S(2)}, u32[]{:S(2)}) %collective-permute-start.37) | collective-permute-done | bytes 294944 | tf_op jit(solution)/shard_map/ppermute | solution.py:36
  (163 shorter events, 79.1 us)
Async XLA Ops:
  9.3 29.1 %collective-permute-start.2 = (bf16[512,1152]{1,0:T(8,128)(2,1)}, bf16[512,1152]{1,0:T(8,128)(2,1)S(1)}, u32[]{:S(2)}, u32[]{:S(2)}) collective-permute-start(bf16[512,1152]{1,0:T(8,128)(2,1)} %sample_pair.1.refs_0_), channel_id=1, source_target_pairs={{0,8},{4,12},{8,0},{12,4},{1,9},{5,13},{9,1},{13,5},{2,10},{6,14},... | collective-permute-start | bytes 3538952 | tf_op jit(solution)/shard_map/ppermute | solution.py:36
  12.2 28.8 %collective-permute-start.4 = (bf16[512,1152]{1,0:T(8,128)(2,1)}, bf16[512,1152]{1,0:T(8,128)(2,1)}, u32[]{:S(2)}, u32[]{:S(2)}) collective-permute-start(bf16[512,1152]{1,0:T(8,128)(2,1)} %sample_pair.1.refs_0_), channel_id=1, source_target_pairs={{0,4},{4,0},{8,12},{12,8},{1,5},{5,1},{9,13},{13,9},{2,6},{6,2},{1... | collective-permute-start | bytes 3538952 | tf_op jit(solution)/shard_map/ppermute | solution.py:36
  17.5 48.0 %collective-permute-start = (bf16[256,2048]{1,0:T(8,128)(2,1)}, bf16[256,2048]{1,0:T(8,128)(2,1)S(1)}, u32[]{:S(2)}, u32[]{:S(2)}) collective-permute-start(bf16[256,2048]{1,0:T(8,128)(2,1)} %get-tuple-element.85), channel_id=1, source_target_pairs={{0,16},{16,0},{1,17},{17,1},{2,18},{18,2},{3,19},{19,3},{4,20},{20... | collective-permute-start | bytes 3145736 | tf_op jit(solution)/shard_map/ppermute | solution.py:36
  20.1 45.6 %collective-permute-start.1 = (bf16[256,2048]{1,0:T(8,128)(2,1)}, bf16[256,2048]{1,0:T(8,128)(2,1)S(1)}, u32[]{:S(2)}, u32[]{:S(2)}) collective-permute-start(bf16[256,2048]{1,0:T(8,128)(2,1)} %get-tuple-element.91.refs_4_), channel_id=1, source_target_pairs={{0,1},{1,0},{2,3},{3,2},{4,5},{5,4},{6,7},{7,6},{8,9},{9,8},{10,11... | collective-permute-start | bytes 3145736 | tf_op jit(solution)/shard_map/ppermute | solution.py:36
  39.3 14.8 %collective-permute-start.3 = (bf16[256,1152]{1,0:T(8,128)(2,1)}, bf16[256,1152]{1,0:T(8,128)(2,1)S(1)}, u32[]{:S(2)}, u32[]{:S(2)}) collective-permute-start(bf16[256,1152]{1,0:T(8,128)(2,1)} %slice.24), channel_id=1, source_target_pairs={{0,4},{4,0},{8,12},{12,8},{1,5},{5,1},{9,13},{13,9},{2,6},{6,2},{1... | collective-permute-start | bytes 1769480 | tf_op jit(solution)/shard_map/ppermute | solution.py:36
  43.0 14.3 %collective-permute-start.5 = (bf16[256,1152]{1,0:T(8,128)(2,1)}, bf16[256,1152]{1,0:T(8,128)(2,1)}, u32[]{:S(2)}, u32[]{:S(2)}) collective-permute-start(bf16[256,1152]{1,0:T(8,128)(2,1)} %slice.25), channel_id=1, source_target_pairs={{0,8},{4,12},{8,0},{12,4},{1,9},{5,13},{9,1},{13,5},{2,10},{6,14},... | collective-permute-start | bytes 1769480 | tf_op jit(solution)/shard_map/ppermute | solution.py:36
  57.3 23.1 %collective-permute-start.8 = (bf16[512,1024]{1,0:T(8,128)(2,1)}, bf16[512,1024]{1,0:T(8,128)(2,1)S(1)}, u32[]{:S(2)}, u32[]{:S(2)}) collective-permute-start(bf16[512,1024]{1,0:T(8,128)(2,1)} %sample.3.refs_0_), channel_id=1, source_target_pairs={{0,8},{4,12},{8,0},{12,4},{1,9},{5,13},{9,1},{13,5},{2,10},{6,14},... | collective-permute-start | bytes 3145736 | tf_op jit(solution)/shard_map/ppermute | solution.py:36
  58.8 22.9 %collective-permute-start.9 = (bf16[512,1024]{1,0:T(8,128)(2,1)}, bf16[512,1024]{1,0:T(8,128)(2,1)S(1)}, u32[]{:S(2)}, u32[]{:S(2)}) collective-permute-start(bf16[512,1024]{1,0:T(8,128)(2,1)} %sample.3.refs_0_), channel_id=1, source_target_pairs={{0,4},{4,0},{8,12},{12,8},{1,5},{5,1},{9,13},{13,9},{2,6},{6,2},{1... | collective-permute-start | bytes 3145736 | tf_op jit(solution)/shard_map/ppermute | solution.py:36
  65.7 23.8 %collective-permute-start.6 = (bf16[256,2048]{1,0:T(8,128)(2,1)S(1)}, bf16[256,2048]{1,0:T(8,128)(2,1)S(1)}, u32[]{:S(2)}, u32[]{:S(2)}) collective-permute-start(bf16[256,2048]{1,0:T(8,128)(2,1)S(1)} %collective-permute-done.refs_0_), channel_id=1, source_target_pairs={{0,1},{1,0},{2,3},{3,2},{4,5},{5,4},{6,7},{7,6},{8,9},{9,8},{10,11... | collective-permute-start | bytes 3145736 | tf_op jit(solution)/shard_map/ppermute | solution.py:36
  67.1 22.9 %collective-permute-start.7 = (bf16[256,2048]{1,0:T(8,128)(2,1)S(1)}, bf16[256,2048]{1,0:T(8,128)(2,1)S(1)}, u32[]{:S(2)}, u32[]{:S(2)}) collective-permute-start(bf16[256,2048]{1,0:T(8,128)(2,1)S(1)} %collective-permute-done.refs_0_), channel_id=1, source_target_pairs={{0,2},{2,0},{1,3},{3,1},{4,6},{6,4},{5,7},{7,5},{8,10},{10,8},{9,1... | collective-permute-start | bytes 3145736 | tf_op jit(solution)/shard_map/ppermute | solution.py:36
  67.1 23.4 %collective-permute-start.11 = (bf16[256,2048]{1,0:T(8,128)(2,1)S(1)}, bf16[256,2048]{1,0:T(8,128)(2,1)S(1)}, u32[]{:S(2)}, u32[]{:S(2)}) collective-permute-start(bf16[256,2048]{1,0:T(8,128)(2,1)S(1)} %copy-done.14), channel_id=1, source_target_pairs={{0,2},{2,0},{1,3},{3,1},{4,6},{6,4},{5,7},{7,5},{8,10},{10,8},{9,1... | collective-permute-start | bytes 3145736 | tf_op jit(solution)/shard_map/ppermute | solution.py:36
  89.5 21.2 %collective-permute-start.15 = (bf16[256,1024]{1,0:T(8,128)(2,1)}, bf16[256,1024]{1,0:T(8,128)(2,1)}, u32[]{:S(2)}, u32[]{:S(2)}) collective-permute-start(bf16[256,1024]{1,0:T(8,128)(2,1)} %slice.26), channel_id=1, source_target_pairs={{0,4},{4,0},{8,12},{12,8},{1,5},{5,1},{9,13},{13,9},{2,6},{6,2},{1... | collective-permute-start | bytes 1572872 | tf_op jit(solution)/shard_map/ppermute | solution.py:36
  90.0 20.7 %collective-permute-start.16 = (bf16[256,1024]{1,0:T(8,128)(2,1)}, bf16[256,1024]{1,0:T(8,128)(2,1)}, u32[]{:S(2)}, u32[]{:S(2)}) collective-permute-start(bf16[256,1024]{1,0:T(8,128)(2,1)} %slice.27), channel_id=1, source_target_pairs={{0,8},{4,12},{8,0},{12,4},{1,9},{5,13},{9,1},{13,5},{2,10},{6,14},... | collective-permute-start | bytes 1572872 | tf_op jit(solution)/shard_map/ppermute | solution.py:36
  110.8 25.4 %collective-permute-start.18 = (bf16[512,1024]{1,0:T(8,128)(2,1)S(1)}, bf16[512,1024]{1,0:T(8,128)(2,1)}, u32[]{:S(2)}, u32[]{:S(2)}) collective-permute-start(bf16[512,1024]{1,0:T(8,128)(2,1)S(1)} %copy-done.25), channel_id=1, source_target_pairs={{0,8},{4,12},{8,0},{12,4},{1,9},{5,13},{9,1},{13,5},{2,10},{6,14},... | collective-permute-start | bytes 3145736 | tf_op jit(solution)/shard_map/ppermute | solution.py:36
  111.3 27.2 %collective-permute-start.17 = (bf16[512,1024]{1,0:T(8,128)(2,1)S(1)}, bf16[512,1024]{1,0:T(8,128)(2,1)}, u32[]{:S(2)}, u32[]{:S(2)}) collective-permute-start(bf16[512,1024]{1,0:T(8,128)(2,1)S(1)} %copy-done.25), channel_id=1, source_target_pairs={{0,4},{4,0},{8,12},{12,8},{1,5},{5,1},{9,13},{13,9},{2,6},{6,2},{1... | collective-permute-start | bytes 3145736 | tf_op jit(solution)/shard_map/ppermute | solution.py:36
  112.3 30.6 %collective-permute-start.22 = (bf16[256,1152]{1,0:T(8,128)(2,1)S(1)}, bf16[256,1152]{1,0:T(8,128)(2,1)S(1)}, u32[]{:S(2)}, u32[]{:S(2)}) collective-permute-start(bf16[256,1152]{1,0:T(8,128)(2,1)S(1)} %relay.3), channel_id=1, source_target_pairs={{0,16},{16,0},{1,17},{17,1},{2,18},{18,2},{3,19},{19,3},{4,20},{20... | collective-permute-start | bytes 1769480 | tf_op jit(solution)/shard_map/ppermute | solution.py:36
  124.4 16.9 %collective-permute-start.23 = (bf16[128,1024]{1,0:T(8,128)(2,1)}, bf16[128,1024]{1,0:T(8,128)(2,1)S(1)}, u32[]{:S(2)}, u32[]{:S(2)}) collective-permute-start(bf16[128,1024]{1,0:T(8,128)(2,1)} %get-tuple-element.112), channel_id=1, source_target_pairs={{0,2},{2,0},{1,3},{3,1},{4,6},{6,4},{5,7},{7,5},{8,10},{10,8},{9,1... | collective-permute-start | bytes 786440 | tf_op jit(solution)/shard_map/ppermute | solution.py:36
  124.5 21.8 %collective-permute-start.21 = (bf16[256,1152]{1,0:T(8,128)(2,1)}, bf16[256,1152]{1,0:T(8,128)(2,1)S(1)}, u32[]{:S(2)}, u32[]{:S(2)}) collective-permute-start(bf16[256,1152]{1,0:T(8,128)(2,1)} %get-tuple-element.108), channel_id=1, source_target_pairs={{0,2},{2,0},{1,3},{3,1},{4,6},{6,4},{5,7},{7,5},{8,10},{10,8},{9,1... | collective-permute-start | bytes 1769480 | tf_op jit(solution)/shard_map/ppermute | solution.py:36
  138.0 16.8 %collective-permute-start.19 = (bf16[256,1024]{1,0:T(8,128)(2,1)}, bf16[256,1024]{1,0:T(8,128)(2,1)S(1)}, u32[]{:S(2)}, u32[]{:S(2)}) collective-permute-start(bf16[256,1024]{1,0:T(8,128)(2,1)} %slice.28), channel_id=1, source_target_pairs={{0,4},{4,0},{8,12},{12,8},{1,5},{5,1},{9,13},{13,9},{2,6},{6,2},{1... | collective-permute-start | bytes 1572872 | tf_op jit(solution)/shard_map/ppermute | solution.py:36
  140.4 14.5 %collective-permute-start.20 = (bf16[256,1024]{1,0:T(8,128)(2,1)}, bf16[256,1024]{1,0:T(8,128)(2,1)}, u32[]{:S(2)}, u32[]{:S(2)}) collective-permute-start(bf16[256,1024]{1,0:T(8,128)(2,1)} %slice.29), channel_id=1, source_target_pairs={{0,8},{4,12},{8,0},{12,4},{1,9},{5,13},{9,1},{13,5},{2,10},{6,14},... | collective-permute-start | bytes 1572872 | tf_op jit(solution)/shard_map/ppermute | solution.py:36
  143.0 26.8 %collective-permute-start.29 = (bf16[256,1024]{1,0:T(8,128)(2,1)S(1)}, bf16[256,1024]{1,0:T(8,128)(2,1)S(1)}, u32[]{:S(2)}, u32[]{:S(2)}) collective-permute-start(bf16[256,1024]{1,0:T(8,128)(2,1)S(1)} %relay.4), channel_id=1, source_target_pairs={{0,16},{16,0},{1,17},{17,1},{2,18},{18,2},{3,19},{19,3},{4,20},{20... | collective-permute-start | bytes 1572872 | tf_op jit(solution)/shard_map/ppermute | solution.py:36
  146.3 24.7 %collective-permute-start.31 = (bf16[256,1024]{1,0:T(8,128)(2,1)}, bf16[256,1024]{1,0:T(8,128)(2,1)S(1)}, u32[]{:S(2)}, u32[]{:S(2)}) collective-permute-start(bf16[256,1024]{1,0:T(8,128)(2,1)} %get-tuple-element.134), channel_id=1, source_target_pairs={{0,2},{2,0},{1,3},{3,1},{4,6},{6,4},{5,7},{7,5},{8,10},{10,8},{9,1... | collective-permute-start | bytes 1572872 | tf_op jit(solution)/shard_map/ppermute | solution.py:36
  169.3 16.5 %collective-permute-start.28 = (bf16[256,1024]{1,0:T(8,128)(2,1)}, bf16[256,1024]{1,0:T(8,128)(2,1)S(1)}, u32[]{:S(2)}, u32[]{:S(2)}) collective-permute-start(bf16[256,1024]{1,0:T(8,128)(2,1)} %get-tuple-element.129), channel_id=1, source_target_pairs={{0,2},{2,0},{1,3},{3,1},{4,6},{6,4},{5,7},{7,5},{8,10},{10,8},{9,1... | collective-permute-start | bytes 1572872 | tf_op jit(solution)/shard_map/ppermute | solution.py:36
  169.8 26.2 %collective-permute-start.30 = (bf16[256,1024]{1,0:T(8,128)(2,1)}, bf16[256,1024]{1,0:T(8,128)(2,1)S(1)}, u32[]{:S(2)}, u32[]{:S(2)}) collective-permute-start(bf16[256,1024]{1,0:T(8,128)(2,1)} %relay.5), channel_id=1, source_target_pairs={{0,16},{16,0},{1,17},{17,1},{2,18},{18,2},{3,19},{19,3},{4,20},{20... | collective-permute-start | bytes 1572872 | tf_op jit(solution)/shard_map/ppermute | solution.py:36
  (53 other events, 458.3 us)

commit v8 on v7

--- a/solution.py
+++ b/solution.py
@@ -64,7 +64,6 @@
         "stack_rows",
         jax.ShapeDtypeStruct((8 * count, depth), BF16),
         moved=32 * count * depth,
-        vmem=40,
         grid=(1,),
         in_specs=[SMEM] + [low, low, high, high] * 2,
         out_specs=pl.BlockSpec((8 * count, depth), lambda i: (0, 0)),
@@ -102,31 +101,33 @@
     accum = mean_ref[...].astype(F32)
     for member in range(count):
         accum = accum + factor * coef_ref[member] * devs_ref[member].astype(F32)
-    width, heads = mean_ref.shape[2], dt_ref.shape[1]
+    width, heads = mean_ref.shape[2], dt_ref.shape[0]
     for k in range(2):
         out_ref[:, k * width : (k + 1) * width] = accum[:, k, :].astype(BF16)
     out_ref[:, 2 * width :] = jnp.zeros((out_ref.shape[0], LANES), BF16)
-    out_ref[:, 2 * width : 2 * width + heads] = dt_ref[...]
+    rows = out_ref.shape[0]
+    steps = dt_ref[:, pl.ds(pl.multiple_of(pl.program_id(0) * rows, rows), rows)]
+    out_ref[:, 2 * width : 2 * width + heads] = jnp.transpose(steps.astype(F32)).astype(BF16)
 
 
 def sampled_pair(mean_part, dev_part, dt_part, swag_coef):
     rows, _, width = mean_part.shape
     count = dev_part.shape[0]
-    tile = rows // 8
+    tile = min(rows, LANES)
     return call(
         functools.partial(sample_pair_kernel, count),
         "sample_pair",
         jax.ShapeDtypeStruct((rows, 2 * width + LANES), BF16),
         moved=4 * (count + 2) * rows * width,
-        grid=(8,),
+        grid=(rows // tile,),
         in_specs=[
             SMEM,
             pl.BlockSpec((tile, 2, width), lambda i: (i, 0, 0)),
             pl.BlockSpec((count, tile, 2, width), lambda i: (0, i, 0, 0)),
-            pl.BlockSpec((tile, dt_part.shape[1]), lambda i: (i, 0)),
+            pl.BlockSpec((dt_part.shape[1], rows), lambda i: (0, 0)),
         ],
         out_specs=pl.BlockSpec((tile, 2 * width + LANES), lambda i: (i, 0)),
-    )(swag_coef, mean_part, dev_part, dt_part)
+    )(swag_coef, mean_part, dev_part, dt_part.T)
 
 
 def sent_straight(weight):
@@ -333,39 +334,48 @@
     wide = over_channels(decay[0])
     decays_ref[0:1, :] = wide
     decays_ref[1:2, :] = jnp.ones_like(wide)
-    pack_state(sent_ref, state, wide)
-
-
-def pack_state(sent_ref, state, decay):
-    sent_ref[:N, :] = state.astype(BF16)
+    pack_state([sent_ref], state, wide)
+
+
+def pack_state(sent_refs, state, decay):
     high = decay.astype(BF16).astype(F32)
     row = lax.broadcasted_iota(jnp.int32, (RIM, decay.shape[1]), 0)
-    sent_ref[N:, :] = jnp.where(row == 0, high, jnp.where(row == 1, decay - high, 0.0)).astype(BF16)
-
-
-def unpack_state(got_ref):
-    rows = got_ref[N:, :].astype(F32)
-    return got_ref[:N, :].astype(F32), rows[0:1, :] + rows[1:2, :]
-
-
-def combine_kernel(level, place_ref, total, decays, other, *refs):
-    before, (total_ref, decays_ref, sent_ref, before_ref) = refs[:-4], refs[-4:]
+    tail = jnp.where(row == 0, high, jnp.where(row == 1, decay - high, 0.0)).astype(BF16)
+    state = state.astype(BF16)
+    at = 0
+    for sent_ref in sent_refs[:-1]:
+        sent_ref[...] = state[at : at + sent_ref.shape[0]]
+        at += sent_ref.shape[0]
+    sent_refs[-1][: N - at, :] = state[at:]
+    sent_refs[-1][N - at :, :] = tail
+
+
+def unpack_state(got_refs):
+    rows = jnp.concatenate([ref[...] for ref in got_refs], axis=0).astype(F32)
+    return rows[:N], rows[N : N + 1, :] + rows[N + 1 : N + 2, :]
+
+
+def combine_kernel(level, got, has_before, place_ref, total, decays, *refs):
+    other, refs = refs[:got], refs[got:]
+    if has_before:
+        before, refs = refs[0][...], refs[1:]
+    total_ref, decays_ref, before_ref, *sent_refs = refs
     come, decay = unpack_state(other)
     whole, part = decays[0:1, :], decays[1:2, :]
     upper = (place_ref[0] >> level) & 1 == 1
     fresh = jnp.where(upper, part, 0.0) * come
-    before_ref[...] = before[0][...] + fresh if before else fresh
+    before_ref[...] = before + fresh if has_before else fresh
     joint = jnp.where(upper, 1.0, decay) * total[...] + jnp.where(upper, whole, 1.0) * come
     total_ref[...] = joint
     decays_ref[0:1, :] = whole * decay
     decays_ref[1:2, :] = jnp.where(upper, decay * part, part)
-    pack_state(sent_ref, joint, whole * decay)
+    pack_state(sent_refs, joint, whole * decay)
 
 
 def read_kernel(level, place_ref, y, reads, cum_g, early, decays, before, other, *refs):
     out_ref = refs[-1]
     upper = (place_ref[0] >> level) & 1 == 1
-    state = before[...] + jnp.where(upper, decays[1:2, :], 0.0) * unpack_state(other)[0]
+    state = before[...] + jnp.where(upper, decays[1:2, :], 0.0) * unpack_state([other])[0]
     cum = cum_g[0]
     for at in range(0, out_ref.shape[0], SPAN):
         span = slice(at, at + SPAN)
@@ -376,21 +386,22 @@
             state = over_channels(jnp.exp(cum_b[SPAN - 1 : SPAN, :])) * state + early[at // SPAN]
 
 
-def combined(level, place, total, decays, other, before, groups):
+def combined(level, place, total, decays, other, before, groups, cut):
     width = total.shape[1] // groups
     block = lambda rows: pl.BlockSpec((rows, width), lambda i: (0, i))
     shape = lambda rows, dtype: jax.ShapeDtypeStruct((rows, total.shape[1]), dtype)
-    return call(
-        functools.partial(combine_kernel, level),
+    total, decays, before, *sent = call(
+        functools.partial(combine_kernel, level, len(other), bool(before)),
         "combine",
-        (shape(N, F32), shape(8, F32), shape(N + RIM, BF16), shape(N, F32)),
+        (shape(N, F32), shape(8, F32), shape(N, F32)) + tuple(shape(rows, BF16) for rows in cut),
         flops=6 * total.size,
         moved=20 * total.size,
         vmem=12,
         grid=(groups,),
-        in_specs=[SMEM, block(N), block(8), block(N + RIM)] + [block(N)] * len(before),
-        out_specs=[block(N), block(8), block(N + RIM), block(N)],
-    )(place, total, decays, other, *before)
+        in_specs=[SMEM, block(N), block(8)] + [block(a.shape[0]) for a in other] + [block(N)] * len(before),
+        out_specs=[block(N), block(8), block(N)] + [block(rows) for rows in cut],
+    )(place, total, decays, *other, *before)
+    return total, decays, before, sent
 
 
 def body(
@@ -520,9 +531,9 @@
 
     result = None
     for first, groups, part in zip((0, early_groups), (early_groups, len(late)), parts):
+        part = part + (rows_before(*part),)
         if first:
-            part = after(part, first_sent)
-        part = part + (rows_before(*part),)
+            part = after(part, sent)
         grid = (groups,)
         cols = lambda rows: pl.BlockSpec((rows, width), lambda i: (0, i))
         cols_all = lambda rows: pl.BlockSpec((rows, width), lambda i: (0, first + i))
@@ -549,13 +560,13 @@
             out_specs=[cols(tok_count), early_spec, cols(N), cols(8), cols(N + RIM)],
             scratch_shapes=[pltpu.VMEM((tok_count + 8, width), F32)],
         )(*part, conv_proj, conv_out, conv_out, cum_g, steps_g, cum_t, steps_t, skip, decay)
-        before, first_sent = (), None
+        before, sent = (), [sent]
         for level in range(levels - 1):
-            other = swapped(sent, SEQ, 1 << level)
-            total, decays, sent, fresh = combined(level, seq_place, total, decays, other, before, groups)
+            other = [swapped(a, SEQ, 1 << level) for a in sent]
+            cut = (N // 2, N // 2 + RIM) if not first and level + 2 < levels else (N + RIM,)
+            total, decays, fresh, sent = combined(level, seq_place, total, decays, other, before, groups, cut)
             before = (fresh,)
-            first_sent = first_sent if level else sent
-        other = swapped(sent, SEQ, 1 << (levels - 1))
+        (other,) = [swapped(a, SEQ, 1 << (levels - 1)) for a in sent]
         operands = [seq_place, y, conv_out, cum_g, early, decays, *before, other]
         specs = [SMEM, cols(tok_count), reads, heads_g, early_spec, cols(8), cols(N), cols(N + RIM)]
         alias = {}

time: 238 us -> 236 us (level)
  waiting for transfers between devices: 87.3 us -> 81.8 us
  Pallas kernels: 72.7 us -> 75.9 us
    ppermute x37 -> x38, waiting for transfers between devices: 86.2 us -> 81.6 us  [swapped(): lax.ppermute(part, axis, [(i, i ^ by) for i in range(lax.axis_size(axis))])]
    pallas_call x1, Pallas kernels: 0.82 us -> 4.47 us  [token_rows(): call(stack_kernel, 'stack_rows', jax.ShapeDtypeStruct((8 * count, depth),...]
    ppermute x37 -> x38, starting transfers between devices: 48.2 us -> 50.6 us  [swapped(): lax.ppermute(part, axis, [(i, i ^ by) for i in range(lax.axis_size(axis))])]
    unnamed x76 -> x79, local copies, waits for them, and re-layouts: 12.9 us -> 12.9 us
  transfers between devices with their start and end apart: 40 -> 41, of which waited for: 24 -> 21; matrix products, arithmetic and copies ran while one was open for 4% -> 4% of each run, Pallas kernels for 25% -> 26%
where the time goes in v8:
time: 236 us; the launch traced here: 235 us
  waiting for transfers between devices  81.8 us (35%)
  Pallas kernels  75.9 us (32%)
  starting transfers between devices  56.2 us (24%)
  local copies, waits for them, and re-layouts  20.7 us (9%)
    ppermute x38, waiting for transfers between devices, swapped(): lax.ppermute(part, axis, [(i, i ^ by) for i in range(lax.axis_size(axis))])  81.6 us
    ppermute x38, starting transfers between devices, swapped(): lax.ppermute(part, axis, [(i, i ^ by) for i in range(lax.axis_size(axis))])  50.6 us
    pallas_call x3, Pallas kernels, multiplied(): call(functools.partial(multiply_kernel, heads, with_steps, len(weights),...  29.5 us
    unnamed x79, local copies, waits for them, and re-layouts  12.9 us
    pallas_call x2, Pallas kernels, body(): call(mix_kernel, 'mix', (jax.ShapeDtypeStruct((tok_count, groups * width)...  10 us
    pallas_call x2, Pallas kernels, sampled_cols(): call(functools.partial(sample_kernel, count), 'sample', jax.ShapeDtypeStr...  9.31 us
    pallas_call x1, Pallas kernels, sampled_pair(): call(functools.partial(sample_pair_kernel, count), 'sample_pair', jax.Sha...  7.24 us
    slice x6, local copies, waits for them, and re-layouts, corner_parts(): cut = lambda a, i: a[i * rows:(i + 1) * rows]  6.5 us
  transfers between devices with their start and end apart: 41, of which 21 were waited for; matrix products, arithmetic and copies ran while one was open for 4% of the time, Pallas kernels for 26%

profile of v8, /device:TPU:0, one launch (start us, length us, event | category | flops | bytes accessed | tf_op | source)
XLA Modules:
  0.0 235.0 jit_solution(360136644506192356)
XLA Ops:
  0.0 7.2 %sample_pair.1.refs_0_ = bf16[512,1152]{1,0:T(8,128)(2,1)} custom-call(f32[4]{0:T(128)} %coef_ref.5, bf16[512,2,512]{2,1,0:T(2,128)(2,1)} %mean_ref.1, bf16[4,512,2,512]{3,2,1,0:T(2,128)(2,1)} %devs_ref.3, bf16[32,512]{1,0:T(8,128)(2,1)} %bitcast.15), custom_call_target="tpu_custom_call" | custom-call | bytes 125829 | tf_op jit(solution)/shard_map/sample_pair/pallas_call | solution.py:117
  12.4 3.1 %cut_tokens.1 = (bf16[256,2048]{1,0:T(8,128)(2,1)}, bf16[256,2048]{1,0:T(8,128)(2,1)}) custom-call(s32[7]{0:T(128)} %stack.31.at_ref, bf16[128,8192]{1,0:T(8,128)(2,1)} %tokens_ref), custom_call_target="tpu_custom_call" | custom-call | bytes 83886 | tf_op jit(solution)/shard_map/cut_tokens/pallas_call | solution.py:445
  19.6 16.8 %collective-permute-done.2.refs_2_ = bf16[512,1152]{1,0:T(8,128)(2,1)S(1)} collective-permute-done((bf16[512,1152]{1,0:T(8,128)(2,1)}, bf16[512,1152]{1,0:T(8,128)(2,1)S(1)}, u32[]{:S(2)}, u32[]{:S(2)}) %collective-permute-start.2) | collective-permute-done | bytes 1179680 | tf_op jit(solution)/shard_map/ppermute | solution.py:36
  41.4 4.6 %sample.2.refs_0_ = bf16[512,1024]{1,0:T(8,128)(2,1)} custom-call(f32[4]{0:T(128)} %coef_ref.5, bf16[512,2048]{1,0:T(8,128)(2,1)} %mean_ref.3, bf16[4,512,2048]{2,1,0:T(8,128)(2,1)} %devs_ref.5), custom_call_target="tpu_custom_call" | custom-call | bytes 125829 | tf_op jit(solution)/shard_map/sample/pallas_call | solution.py:84
  46.1 4.7 %sample.3.refs_0_ = bf16[512,1024]{1,0:T(8,128)(2,1)} custom-call(f32[4]{0:T(128)} %coef_ref.5, bf16[512,2048]{1,0:T(8,128)(2,1)} %mean_ref.3, bf16[4,512,2048]{2,1,0:T(8,128)(2,1)} %devs_ref.5), custom_call_target="tpu_custom_call" | custom-call | bytes 125829 | tf_op jit(solution)/shard_map/sample/pallas_call | solution.py:84
  56.3 7.2 %collective-permute-done.refs_0_ = bf16[256,2048]{1,0:T(8,128)(2,1)} collective-permute-done((bf16[256,2048]{1,0:T(8,128)(2,1)}, bf16[256,2048]{1,0:T(8,128)(2,1)}, u32[]{:S(2)}, u32[]{:S(2)}) %collective-permute-start) | collective-permute-done | bytes 1048608 | tf_op jit(solution)/shard_map/ppermute | solution.py:36
  65.7 11.7 %collective-permute-done.8.refs_2_ = bf16[512,1024]{1,0:T(8,128)(2,1)S(1)} collective-permute-done((bf16[512,1024]{1,0:T(8,128)(2,1)}, bf16[512,1024]{1,0:T(8,128)(2,1)S(1)}, u32[]{:S(2)}, u32[]{:S(2)}) %collective-permute-start.8) | collective-permute-done | bytes 1048608 | tf_op jit(solution)/shard_map/ppermute | solution.py:36
  80.5 7.2 %collective-permute-done.6.refs_1_ = bf16[256,2048]{1,0:T(8,128)(2,1)S(1)} collective-permute-done((bf16[256,2048]{1,0:T(8,128)(2,1)}, bf16[256,2048]{1,0:T(8,128)(2,1)S(1)}, u32[]{:S(2)}, u32[]{:S(2)}) %collective-permute-start.6) | collective-permute-done | bytes 1048608 | tf_op jit(solution)/shard_map/ppermute | solution.py:36
  91.3 4.5 %stack_rows.1.rows_ref = bf16[1024,2048]{1,0:T(8,128)(2,1)} custom-call(s32[7]{0:T(128)} %stack.31.at_ref, bf16[256,2048]{1,0:T(8,128)(2,1)} %collective-permute-done.refs_0_, bf16[256,2048]{1,0:T(8,128)(2,1)} %copy-done.28, bf16[256,2048]{1,0:T(8,128)(2,1)} %copy-done.29, bf16[256,2048]{1,0:T(8,128)(2,1)} %collective-permute-done.10.refs_3_, ...), custom_call_target="tpu_custom_call" | custom-call | bytes 167772 | tf_op jit(solution)/shard_map/stack_rows/pallas_call | solution.py:62
  95.7 11.8 %multiply.3 = (bf16[128,1152]{1,0:T(8,128)(2,1)}, bf16[128,1152]{1,0:T(8,128)(2,1)}, f32[256,1152]{1,0:T(8,128)}, bf16[256,1152]{1,0:T(8,128)(2,1)}, f32[256,1152]{1,0:T(8,128)}) custom-call(bf16[1024,2048]{1,0:T(8,128)(2,1)} %stack_rows.1.rows_ref, bf16[512,1152]{1,0:T(8,128)(2,1)} %sample_pair.1.refs_0_, bf16[512,1152]{1,0:T(8,128)(2,1)} %copy-done.24, ...), custom_call_target="tpu_custom_call" | custom-call | flops 96636768 | bytes 249036 | tf_op jit(solution)/shard_map/multiply/pallas_call | solution.py:183
  114.0 3.4 %collective-permute-start.22 = (bf16[256,1152]{1,0:T(8,128)(2,1)S(1)}, bf16[256,1152]{1,0:T(8,128)(2,1)S(1)}, u32[]{:S(2)}, u32[]{:S(2)}) collective-permute-start(bf16[256,1152]{1,0:T(8,128)(2,1)S(1)} %relay.3), channel_id=1, source_target_pairs={{0,16},{16,0},{1,17},{17,1},{2,18},{18,2},{3,19},{19,3},{4,20},{20... | collective-permute-start | bytes 1769480 | tf_op jit(solution)/shard_map/ppermute | solution.py:36
  117.4 8.8 %multiply.5 = (bf16[128,1024]{1,0:T(8,128)(2,1)}, bf16[128,1024]{1,0:T(8,128)(2,1)}, f32[256,1024]{1,0:T(8,128)}, bf16[256,1024]{1,0:T(8,128)(2,1)}, f32[256,1024]{1,0:T(8,128)}) custom-call(bf16[1024,2048]{1,0:T(8,128)(2,1)} %stack_rows.1.rows_ref, bf16[512,1024]{1,0:T(8,128)(2,1)} %sample.3.refs_0_, bf16[512,1024]{1,0:T(8,128)(2,1)} %copy-done.26, ...), custom_call_target="tpu_custom_call" | custom-call | flops 85899344 | bytes 230686 | tf_op jit(solution)/shard_map/multiply/pallas_call | solution.py:183
  126.8 10.1 %collective-permute-done.18.refs_2_ = bf16[512,1024]{1,0:T(8,128)(2,1)} collective-permute-done((bf16[512,1024]{1,0:T(8,128)(2,1)S(1)}, bf16[512,1024]{1,0:T(8,128)(2,1)}, u32[]{:S(2)}, u32[]{:S(2)}) %collective-permute-start.18) | collective-permute-done | bytes 1048608 | tf_op jit(solution)/shard_map/ppermute | solution.py:36
  144.0 3.4 %collective-permute-start.29 = (bf16[256,1024]{1,0:T(8,128)(2,1)S(1)}, bf16[256,1024]{1,0:T(8,128)(2,1)S(1)}, u32[]{:S(2)}, u32[]{:S(2)}) collective-permute-start(bf16[256,1024]{1,0:T(8,128)(2,1)S(1)} %relay.4), channel_id=1, source_target_pairs={{0,16},{16,0},{1,17},{17,1},{2,18},{18,2},{3,19},{19,3},{4,20},{20... | collective-permute-start | bytes 1572872 | tf_op jit(solution)/shard_map/ppermute | solution.py:36
  151.3 4.6 %state_proj.1 = (bf16[256,1024]{1,0:T(8,128)(2,1)}, f32[4,256,8]{2,1,0:T(8,128)}, f32[4,256,8]{2,1,0:T(8,128)}, f32[32,256]{1,0:T(8,128)}, f32[32,256]{1,0:T(8,128)}, /*index=5*/f32[4,1,8]{2,1,0:T(1,128)}) custom-call(f32[256,1152]{1,0:T(8,128)} %get-tuple-element.118.kept, bf16[256,1152]{1,0:T(8,128)(2,1)} %copy-done.6, bf16[256,1152]{1,0:T(8,128)(2,1)} %copy-done.5, ...), custom_call_target="tpu_custom_call" | custom-call | bytes 52428 | tf_op jit(solution)/shard_map/state_proj/pallas_call | solution.py:476
  156.7 8.8 %multiply.4 = (bf16[128,1024]{1,0:T(8,128)(2,1)}, bf16[128,1024]{1,0:T(8,128)(2,1)}, f32[256,1024]{1,0:T(8,128)}, bf16[256,1024]{1,0:T(8,128)(2,1)}, f32[256,1024]{1,0:T(8,128)}) custom-call(bf16[1024,2048]{1,0:T(8,128)(2,1)} %stack_rows.1.rows_ref, bf16[512,1024]{1,0:T(8,128)(2,1)} %sample.2.refs_0_, bf16[512,1024]{1,0:T(8,128)(2,1)} %collective-permute-done.17.refs_1_, ...), custom_call_target="tpu_custom_call" | custom-call | flops 85899344 | bytes 230686 | tf_op jit(solution)/shard_map/multiply/pallas_call | solution.py:183
  176.3 5.0 %mix.2 = (f32[256,1024]{1,0:T(8,128)}, f32[1,128,1024]{2,1,0:T(8,128)}, f32[128,1024]{1,0:T(8,128)}, f32[8,1024]{1,0:T(8,128)}, bf16[144,1024]{1,0:T(8,128)(2,1)}) custom-call(f32[256,1024]{1,0:T(8,128)} %get-tuple-element.134.kept, bf16[256,1024]{1,0:T(8,128)(2,1)} %copy-done.10, bf16[256,1024]{1,0:T(8,128)(2,1)} %copy-done.8, bf16[16,1024]{1,0:T(8,128)(2,1)} %copy-done.35, ...), custom_call_target="tpu_custom_call" | custom-call | flops 5368709 | bytes 73400 | tf_op jit(solution)/shard_map/mix/pallas_call | solution.py:546
  181.3 3.0 %collective-permute-start.34 = (bf16[144,1024]{1,0:T(8,128)(2,1)}, bf16[144,1024]{1,0:T(8,128)(2,1)S(1)}, u32[]{:S(2)}, u32[]{:S(2)}) collective-permute-start(bf16[144,1024]{1,0:T(8,128)(2,1)} %get-tuple-element.140), channel_id=1, source_target_pairs={{0,2},{2,0},{4,6},{6,4},{8,10},{10,8},{12,14},{14,12},{1,3},{3,1},... | collective-permute-start | bytes 884744 | tf_op jit(solution)/shard_map/ppermute | solution.py:36
  190.6 6.3 %collective-permute-done.30.got_f = bf16[256,1024]{1,0:T(8,128)(2,1)S(1)} collective-permute-done((bf16[256,1024]{1,0:T(8,128)(2,1)}, bf16[256,1024]{1,0:T(8,128)(2,1)S(1)}, u32[]{:S(2)}, u32[]{:S(2)}) %collective-permute-start.30) | collective-permute-done | bytes 524320 | tf_op jit(solution)/shard_map/ppermute | solution.py:36
  199.9 5.0 %mix.3 = (f32[256,1024]{1,0:T(8,128)}, f32[1,128,1024]{2,1,0:T(8,128)}, f32[128,1024]{1,0:T(8,128)}, f32[8,1024]{1,0:T(8,128)}, bf16[144,1024]{1,0:T(8,128)(2,1)}) custom-call(f32[256,1024]{1,0:T(8,128)} %get-tuple-element.147.kept, bf16[256,1024]{1,0:T(8,128)(2,1)} %copy-done.7, bf16[256,1024]{1,0:T(8,128)(2,1)} %copy-done.9, bf16[16,1024]{1,0:T(8,128)(2,1)} %copy-done.34, ...), custom_call_target="tpu_custom_call" | custom-call | flops 5368709 | bytes 73400 | tf_op jit(solution)/shard_map/mix/pallas_call | solution.py:546
  204.9 3.5 %collective-permute-start.37 = (bf16[144,1024]{1,0:T(8,128)(2,1)}, bf16[144,1024]{1,0:T(8,128)(2,1)S(1)}, u32[]{:S(2)}, u32[]{:S(2)}) collective-permute-start(bf16[144,1024]{1,0:T(8,128)(2,1)} %get-tuple-element.155), channel_id=1, source_target_pairs={{0,2},{2,0},{4,6},{6,4},{8,10},{10,8},{12,14},{14,12},{1,3},{3,1},... | collective-permute-start | bytes 884744 | tf_op jit(solution)/shard_map/ppermute | solution.py:36
  216.7 5.5 %collective-permute-done.38.refs_0_ = bf16[144,1024]{1,0:T(8,128)(2,1)S(1)} collective-permute-done((bf16[144,1024]{1,0:T(8,128)(2,1)S(1)}, bf16[144,1024]{1,0:T(8,128)(2,1)S(1)}, u32[]{:S(2)}, u32[]{:S(2)}) %collective-permute-start.38) | collective-permute-done | bytes 294944 | tf_op jit(solution)/shard_map/ppermute | solution.py:36
  223.3 3.5 %collective-permute-start.39 = (bf16[144,1024]{1,0:T(8,128)(2,1)S(1)}, bf16[144,1024]{1,0:T(8,128)(2,1)S(1)}, u32[]{:S(2)}, u32[]{:S(2)}) collective-permute-start(bf16[144,1024]{1,0:T(8,128)(2,1)S(1)} %get-tuple-element.162), channel_id=1, source_target_pairs={{0,8},{2,10},{4,12},{6,14},{8,0},{10,2},{12,4},{14,6},{1,9},{3,11}... | collective-permute-start | bytes 884744 | tf_op jit(solution)/shard_map/ppermute | solution.py:36
  228.6 4.6 %collective-permute-done.39.other = bf16[144,1024]{1,0:T(8,128)(2,1)S(1)} collective-permute-done((bf16[144,1024]{1,0:T(8,128)(2,1)S(1)}, bf16[144,1024]{1,0:T(8,128)(2,1)S(1)}, u32[]{:S(2)}, u32[]{:S(2)}) %collective-permute-start.39) | collective-permute-done | bytes 294944 | tf_op jit(solution)/shard_map/ppermute | solution.py:36
  (168 shorter events, 80.2 us)
Async XLA Ops:
  7.2 29.1 %collective-permute-start.2 = (bf16[512,1152]{1,0:T(8,128)(2,1)}, bf16[512,1152]{1,0:T(8,128)(2,1)S(1)}, u32[]{:S(2)}, u32[]{:S(2)}) collective-permute-start(bf16[512,1152]{1,0:T(8,128)(2,1)} %sample_pair.1.refs_0_), channel_id=1, source_target_pairs={{0,8},{4,12},{8,0},{12,4},{1,9},{5,13},{9,1},{13,5},{2,10},{6,14},... | collective-permute-start | bytes 3538952 | tf_op jit(solution)/shard_map/ppermute | solution.py:36
  10.2 28.8 %collective-permute-start.4 = (bf16[512,1152]{1,0:T(8,128)(2,1)}, bf16[512,1152]{1,0:T(8,128)(2,1)S(1)}, u32[]{:S(2)}, u32[]{:S(2)}) collective-permute-start(bf16[512,1152]{1,0:T(8,128)(2,1)} %sample_pair.1.refs_0_), channel_id=1, source_target_pairs={{0,4},{4,0},{8,12},{12,8},{1,5},{5,1},{9,13},{13,9},{2,6},{6,2},{1... | collective-permute-start | bytes 3538952 | tf_op jit(solution)/shard_map/ppermute | solution.py:36
  15.4 48.1 %collective-permute-start = (bf16[256,2048]{1,0:T(8,128)(2,1)}, bf16[256,2048]{1,0:T(8,128)(2,1)}, u32[]{:S(2)}, u32[]{:S(2)}) collective-permute-start(bf16[256,2048]{1,0:T(8,128)(2,1)} %get-tuple-element.87), channel_id=1, source_target_pairs={{0,16},{16,0},{1,17},{17,1},{2,18},{18,2},{3,19},{19,3},{4,20},{20... | collective-permute-start | bytes 3145736 | tf_op jit(solution)/shard_map/ppermute | solution.py:36
  18.0 45.7 %collective-permute-start.1 = (bf16[256,2048]{1,0:T(8,128)(2,1)}, bf16[256,2048]{1,0:T(8,128)(2,1)}, u32[]{:S(2)}, u32[]{:S(2)}) collective-permute-start(bf16[256,2048]{1,0:T(8,128)(2,1)} %get-tuple-element.93.refs_4_), channel_id=1, source_target_pairs={{0,1},{1,0},{2,3},{3,2},{4,5},{5,4},{6,7},{7,6},{8,9},{9,8},{10,11... | collective-permute-start | bytes 3145736 | tf_op jit(solution)/shard_map/ppermute | solution.py:36
  37.3 14.9 %collective-permute-start.3 = (bf16[256,1152]{1,0:T(8,128)(2,1)}, bf16[256,1152]{1,0:T(8,128)(2,1)}, u32[]{:S(2)}, u32[]{:S(2)}) collective-permute-start(bf16[256,1152]{1,0:T(8,128)(2,1)} %slice.24), channel_id=1, source_target_pairs={{0,4},{4,0},{8,12},{12,8},{1,5},{5,1},{9,13},{13,9},{2,6},{6,2},{1... | collective-permute-start | bytes 1769480 | tf_op jit(solution)/shard_map/ppermute | solution.py:36
  39.9 14.3 %collective-permute-start.5 = (bf16[256,1152]{1,0:T(8,128)(2,1)}, bf16[256,1152]{1,0:T(8,128)(2,1)}, u32[]{:S(2)}, u32[]{:S(2)}) collective-permute-start(bf16[256,1152]{1,0:T(8,128)(2,1)} %slice.25), channel_id=1, source_target_pairs={{0,8},{4,12},{8,0},{12,4},{1,9},{5,13},{9,1},{13,5},{2,10},{6,14},... | collective-permute-start | bytes 1769480 | tf_op jit(solution)/shard_map/ppermute | solution.py:36
  54.3 23.1 %collective-permute-start.8 = (bf16[512,1024]{1,0:T(8,128)(2,1)}, bf16[512,1024]{1,0:T(8,128)(2,1)S(1)}, u32[]{:S(2)}, u32[]{:S(2)}) collective-permute-start(bf16[512,1024]{1,0:T(8,128)(2,1)} %sample.3.refs_0_), channel_id=1, source_target_pairs={{0,8},{4,12},{8,0},{12,4},{1,9},{5,13},{9,1},{13,5},{2,10},{6,14},... | collective-permute-start | bytes 3145736 | tf_op jit(solution)/shard_map/ppermute | solution.py:36
  55.8 22.9 %collective-permute-start.9 = (bf16[512,1024]{1,0:T(8,128)(2,1)}, bf16[512,1024]{1,0:T(8,128)(2,1)S(1)}, u32[]{:S(2)}, u32[]{:S(2)}) collective-permute-start(bf16[512,1024]{1,0:T(8,128)(2,1)} %sample.3.refs_0_), channel_id=1, source_target_pairs={{0,4},{4,0},{8,12},{12,8},{1,5},{5,1},{9,13},{13,9},{2,6},{6,2},{1... | collective-permute-start | bytes 3145736 | tf_op jit(solution)/shard_map/ppermute | solution.py:36
  63.7 24.0 %collective-permute-start.6 = (bf16[256,2048]{1,0:T(8,128)(2,1)}, bf16[256,2048]{1,0:T(8,128)(2,1)S(1)}, u32[]{:S(2)}, u32[]{:S(2)}) collective-permute-start(bf16[256,2048]{1,0:T(8,128)(2,1)} %collective-permute-done.refs_0_), channel_id=1, source_target_pairs={{0,1},{1,0},{2,3},{3,2},{4,5},{5,4},{6,7},{7,6},{8,9},{9,8},{10,11... | collective-permute-start | bytes 3145736 | tf_op jit(solution)/shard_map/ppermute | solution.py:36
  65.2 23.1 %collective-permute-start.7 = (bf16[256,2048]{1,0:T(8,128)(2,1)}, bf16[256,2048]{1,0:T(8,128)(2,1)S(1)}, u32[]{:S(2)}, u32[]{:S(2)}) collective-permute-start(bf16[256,2048]{1,0:T(8,128)(2,1)} %collective-permute-done.refs_0_), channel_id=1, source_target_pairs={{0,2},{2,0},{1,3},{3,1},{4,6},{6,4},{5,7},{7,5},{8,10},{10,8},{9,1... | collective-permute-start | bytes 3145736 | tf_op jit(solution)/shard_map/ppermute | solution.py:36
  65.2 23.5 %collective-permute-start.11 = (bf16[256,2048]{1,0:T(8,128)(2,1)S(1)}, bf16[256,2048]{1,0:T(8,128)(2,1)S(1)}, u32[]{:S(2)}, u32[]{:S(2)}) collective-permute-start(bf16[256,2048]{1,0:T(8,128)(2,1)S(1)} %copy-done.27), channel_id=1, source_target_pairs={{0,2},{2,0},{1,3},{3,1},{4,6},{6,4},{5,7},{7,5},{8,10},{10,8},{9,1... | collective-permute-start | bytes 3145736 | tf_op jit(solution)/shard_map/ppermute | solution.py:36
  87.7 23.7 %collective-permute-start.15 = (bf16[256,1024]{1,0:T(8,128)(2,1)}, bf16[256,1024]{1,0:T(8,128)(2,1)}, u32[]{:S(2)}, u32[]{:S(2)}) collective-permute-start(bf16[256,1024]{1,0:T(8,128)(2,1)} %slice.26), channel_id=1, source_target_pairs={{0,4},{4,0},{8,12},{12,8},{1,5},{5,1},{9,13},{13,9},{2,6},{6,2},{1... | collective-permute-start | bytes 1572872 | tf_op jit(solution)/shard_map/ppermute | solution.py:36
  88.3 23.2 %collective-permute-start.16 = (bf16[256,1024]{1,0:T(8,128)(2,1)}, bf16[256,1024]{1,0:T(8,128)(2,1)}, u32[]{:S(2)}, u32[]{:S(2)}) collective-permute-start(bf16[256,1024]{1,0:T(8,128)(2,1)} %slice.27), channel_id=1, source_target_pairs={{0,8},{4,12},{8,0},{12,4},{1,9},{5,13},{9,1},{13,5},{2,10},{6,14},... | collective-permute-start | bytes 1572872 | tf_op jit(solution)/shard_map/ppermute | solution.py:36
  111.4 25.5 %collective-permute-start.18 = (bf16[512,1024]{1,0:T(8,128)(2,1)S(1)}, bf16[512,1024]{1,0:T(8,128)(2,1)}, u32[]{:S(2)}, u32[]{:S(2)}) collective-permute-start(bf16[512,1024]{1,0:T(8,128)(2,1)S(1)} %copy-done.22), channel_id=1, source_target_pairs={{0,8},{4,12},{8,0},{12,4},{1,9},{5,13},{9,1},{13,5},{2,10},{6,14},... | collective-permute-start | bytes 3145736 | tf_op jit(solution)/shard_map/ppermute | solution.py:36
  112.5 27.7 %collective-permute-start.17 = (bf16[512,1024]{1,0:T(8,128)(2,1)S(1)}, bf16[512,1024]{1,0:T(8,128)(2,1)}, u32[]{:S(2)}, u32[]{:S(2)}) collective-permute-start(bf16[512,1024]{1,0:T(8,128)(2,1)S(1)} %copy-done.22), channel_id=1, source_target_pairs={{0,4},{4,0},{8,12},{12,8},{1,5},{5,1},{9,13},{13,9},{2,6},{6,2},{1... | collective-permute-start | bytes 3145736 | tf_op jit(solution)/shard_map/ppermute | solution.py:36
  114.0 29.9 %collective-permute-start.22 = (bf16[256,1152]{1,0:T(8,128)(2,1)S(1)}, bf16[256,1152]{1,0:T(8,128)(2,1)S(1)}, u32[]{:S(2)}, u32[]{:S(2)}) collective-permute-start(bf16[256,1152]{1,0:T(8,128)(2,1)S(1)} %relay.3), channel_id=1, source_target_pairs={{0,16},{16,0},{1,17},{17,1},{2,18},{18,2},{3,19},{19,3},{4,20},{20... | collective-permute-start | bytes 1769480 | tf_op jit(solution)/shard_map/ppermute | solution.py:36
  126.2 16.1 %collective-permute-start.23 = (bf16[128,1024]{1,0:T(8,128)(2,1)}, bf16[128,1024]{1,0:T(8,128)(2,1)S(1)}, u32[]{:S(2)}, u32[]{:S(2)}) collective-permute-start(bf16[128,1024]{1,0:T(8,128)(2,1)} %get-tuple-element.114), channel_id=1, source_target_pairs={{0,2},{2,0},{1,3},{3,1},{4,6},{6,4},{5,7},{7,5},{8,10},{10,8},{9,1... | collective-permute-start | bytes 786440 | tf_op jit(solution)/shard_map/ppermute | solution.py:36
  126.3 21.1 %collective-permute-start.21 = (bf16[256,1152]{1,0:T(8,128)(2,1)}, bf16[256,1152]{1,0:T(8,128)(2,1)S(1)}, u32[]{:S(2)}, u32[]{:S(2)}) collective-permute-start(bf16[256,1152]{1,0:T(8,128)(2,1)} %get-tuple-element.110), channel_id=1, source_target_pairs={{0,2},{2,0},{1,3},{3,1},{4,6},{6,4},{5,7},{7,5},{8,10},{10,8},{9,1... | collective-permute-start | bytes 1769480 | tf_op jit(solution)/shard_map/ppermute | solution.py:36
  138.8 17.2 %collective-permute-start.19 = (bf16[256,1024]{1,0:T(8,128)(2,1)}, bf16[256,1024]{1,0:T(8,128)(2,1)}, u32[]{:S(2)}, u32[]{:S(2)}) collective-permute-start(bf16[256,1024]{1,0:T(8,128)(2,1)} %slice.28), channel_id=1, source_target_pairs={{0,4},{4,0},{8,12},{12,8},{1,5},{5,1},{9,13},{13,9},{2,6},{6,2},{1... | collective-permute-start | bytes 1572872 | tf_op jit(solution)/shard_map/ppermute | solution.py:36
  141.3 14.6 %collective-permute-start.20 = (bf16[256,1024]{1,0:T(8,128)(2,1)S(1)}, bf16[256,1024]{1,0:T(8,128)(2,1)S(1)}, u32[]{:S(2)}, u32[]{:S(2)}) collective-permute-start(bf16[256,1024]{1,0:T(8,128)(2,1)S(1)} %slice.29), channel_id=1, source_target_pairs={{0,8},{4,12},{8,0},{12,4},{1,9},{5,13},{9,1},{13,5},{2,10},{6,14},... | collective-permute-start | bytes 1572872 | tf_op jit(solution)/shard_map/ppermute | solution.py:36
  144.0 26.9 %collective-permute-start.29 = (bf16[256,1024]{1,0:T(8,128)(2,1)S(1)}, bf16[256,1024]{1,0:T(8,128)(2,1)S(1)}, u32[]{:S(2)}, u32[]{:S(2)}) collective-permute-start(bf16[256,1024]{1,0:T(8,128)(2,1)S(1)} %relay.4), channel_id=1, source_target_pairs={{0,16},{16,0},{1,17},{17,1},{2,18},{18,2},{3,19},{19,3},{4,20},{20... | collective-permute-start | bytes 1572872 | tf_op jit(solution)/shard_map/ppermute | solution.py:36
  147.4 25.6 %collective-permute-start.32 = (bf16[256,1024]{1,0:T(8,128)(2,1)}, bf16[256,1024]{1,0:T(8,128)(2,1)S(1)}, u32[]{:S(2)}, u32[]{:S(2)}) collective-permute-start(bf16[256,1024]{1,0:T(8,128)(2,1)} %get-tuple-element.136), channel_id=1, source_target_pairs={{0,2},{2,0},{1,3},{3,1},{4,6},{6,4},{5,7},{7,5},{8,10},{10,8},{9,1... | collective-permute-start | bytes 1572872 | tf_op jit(solution)/shard_map/ppermute | solution.py:36
  170.2 20.4 %collective-permute-start.28 = (bf16[256,1024]{1,0:T(8,128)(2,1)}, bf16[256,1024]{1,0:T(8,128)(2,1)S(1)}, u32[]{:S(2)}, u32[]{:S(2)}) collective-permute-start(bf16[256,1024]{1,0:T(8,128)(2,1)} %get-tuple-element.131), channel_id=1, source_target_pairs={{0,2},{2,0},{1,3},{3,1},{4,6},{6,4},{5,7},{7,5},{8,10},{10,8},{9,1... | collective-permute-start | bytes 1572872 | tf_op jit(solution)/shard_map/ppermute | solution.py:36
  170.9 26.0 %collective-permute-start.30 = (bf16[256,1024]{1,0:T(8,128)(2,1)}, bf16[256,1024]{1,0:T(8,128)(2,1)S(1)}, u32[]{:S(2)}, u32[]{:S(2)}) collective-permute-start(bf16[256,1024]{1,0:T(8,128)(2,1)} %relay.5), channel_id=1, source_target_pairs={{0,16},{16,0},{1,17},{17,1},{2,18},{18,2},{3,19},{19,3},{4,20},{20... | collective-permute-start | bytes 1572872 | tf_op jit(solution)/shard_map/ppermute | solution.py:36
  (56 other events, 403.9 us)

commit v9 on v8

--- a/solution.py
+++ b/solution.py
@@ -47,27 +47,11 @@
                 out[k * rows : (k + 1) * rows, i * depth : (i + 1) * depth] = tokens_ref[:, pl.ds(start, depth)]
 
 
-def stack_kernel(at_ref, *refs):
-    pieces, rows_ref = refs[:-1], refs[-1]
+def stack_rows(at_ref, pieces, rows_ref):
     count = pieces[0].shape[0]
     for k in range(0, len(pieces), 2):
         rows_ref[pl.ds(pl.multiple_of((k + at_ref[2]) * count, count), count), :] = pieces[k][...]
         rows_ref[pl.ds(pl.multiple_of((k + 1 - at_ref[2]) * count, count), count), :] = pieces[k + 1][...]
-
-
-def token_rows(at, far, far_t, far_c, far_tc, own, own_t, own_c, own_tc):
-    count, depth = far.shape[0] // 2, far.shape[1]
-    low = pl.BlockSpec((count, depth), lambda i: (0, 0))
-    high = pl.BlockSpec((count, depth), lambda i: (1, 0))
-    return call(
-        stack_kernel,
-        "stack_rows",
-        jax.ShapeDtypeStruct((8 * count, depth), BF16),
-        moved=32 * count * depth,
-        grid=(1,),
-        in_specs=[SMEM] + [low, low, high, high] * 2,
-        out_specs=pl.BlockSpec((8 * count, depth), lambda i: (0, 0)),
-    )(at, far, far_t, far_c, far_tc, own, own_t, own_c, own_tc)
 
 
 def sample_kernel(count, coef_ref, mean_ref, devs_ref, out_ref):
@@ -98,12 +82,12 @@
 
 def sample_pair_kernel(count, coef_ref, mean_ref, devs_ref, dt_ref, out_ref):
     factor = (2.0 * (count - 1)) ** (-0.5)
-    accum = mean_ref[...].astype(F32)
-    for member in range(count):
-        accum = accum + factor * coef_ref[member] * devs_ref[member].astype(F32)
     width, heads = mean_ref.shape[2], dt_ref.shape[0]
     for k in range(2):
-        out_ref[:, k * width : (k + 1) * width] = accum[:, k, :].astype(BF16)
+        accum = mean_ref[:, k, :].astype(F32)
+        for member in range(count):
+            accum = accum + factor * coef_ref[member] * devs_ref[member, :, k, :].astype(F32)
+        out_ref[:, k * width : (k + 1) * width] = accum.astype(BF16)
     out_ref[:, 2 * width :] = jnp.zeros((out_ref.shape[0], LANES), BF16)
     rows = out_ref.shape[0]
     steps = dt_ref[:, pl.ds(pl.multiple_of(pl.program_id(0) * rows, rows), rows)]
@@ -154,8 +138,16 @@
     return part + pltpu.roll(part, LANES - heads, 1)
 
 
-def multiply_kernel(heads, with_steps, pieces, plan, rows_ref, *refs):
-    weights, outs = refs[:pieces], refs[pieces:]
+def multiply_kernel(heads, with_steps, shares, pieces, plan, at_ref, *refs):
+    shares, weights, outs, rows_ref = refs[:shares], refs[shares : shares + pieces], refs[shares + pieces : -1], refs[-1]
+
+    @pl.when(pl.program_id(0) == 0)
+    def _():
+        if len(shares) == 1:
+            rows_ref[...] = shares[0][...]
+        else:
+            stack_rows(at_ref, shares, rows_ref)
+
     joined = jnp.concatenate([weight[...] for weight in weights], axis=0)
     total = jnp.dot(rows_ref[...], joined, preferred_element_type=F32)
     for out, (first, sent) in zip(outs, plan):
@@ -167,30 +159,35 @@
                 out[:, -LANES:] = coded(part[:, -LANES:], heads).astype(BF16)
 
 
-def multiplied(rows, weights, heads, with_steps, document=None):
+def multiplied(at, rows, weights, heads, with_steps):
     width = weights[0].shape[1]
     tile = next(t for t in (512, 384, 128) if width % t == 0)
-    half = rows.shape[0] // 4
+    depth = rows[0].shape[1]
+    if len(rows) == 1:
+        count = rows[0].shape[0]
+        row_specs = [pl.BlockSpec(rows[0].shape, lambda i: (0, 0))]
+    else:
+        share = rows[0].shape[0] // 2
+        count = len(rows) * share
+        low = pl.BlockSpec((share, depth), lambda i: (0, 0))
+        high = pl.BlockSpec((share, depth), lambda i: (1, 0))
+        row_specs = [low, low, high, high] * 2
+    half = count // 4
     part = half // FAR_PARTS
-    plan, shapes = [], []
-    count = rows.shape[0] if document is None else 2 * half
-    if document != 1:
-        plan += [(half + i * part, True) for i in range(FAR_PARTS)] + [(0, False)]
-        shapes += [(part, BF16)] * FAR_PARTS + [(half, F32)]
-    if document != 0:
-        plan += [(count - half, True), (count - 2 * half, False)]
-        shapes += [(half, BF16), (half, F32)]
+    plan = [(half + i * part, True) for i in range(FAR_PARTS)] + [(0, False), (3 * half, True), (2 * half, False)]
+    shapes = [(part, BF16)] * FAR_PARTS + [(half, F32), (half, BF16), (half, F32)]
     return call(
-        functools.partial(multiply_kernel, heads, with_steps, len(weights), plan),
+        functools.partial(multiply_kernel, heads, with_steps, len(rows), len(weights), plan),
         "multiply",
         tuple(jax.ShapeDtypeStruct((r, width), dtype) for r, dtype in shapes),
-        flops=2 * count * rows.shape[1] * width,
-        moved=2 * rows.size + 2 * rows.shape[1] * width + 12 * half * width,
+        flops=2 * count * depth * width,
+        moved=2 * count * depth + 2 * depth * width + 12 * half * width,
+        vmem=34,
         grid=(width // tile,),
-        in_specs=[pl.BlockSpec((count, rows.shape[1]), lambda i: (document or 0, 0))]
-        + [pl.BlockSpec((w.shape[0], tile), lambda i: (0, i)) for w in weights],
+        in_specs=[SMEM] + row_specs + [pl.BlockSpec((w.shape[0], tile), lambda i: (0, i)) for w in weights],
         out_specs=[pl.BlockSpec((r, tile), lambda i: (0, i)) for r, _ in shapes],
-    )(rows, *weights)
+        scratch_shapes=[pltpu.VMEM((count, depth), BF16)],
+    )(at, *rows, *weights)
 
 
 def relay_kernel(heads, with_steps, kept_ref, *refs):
@@ -461,7 +458,7 @@
     blocks = tok_count // SPAN
 
     def partial_sums(rows, pieces, with_steps, before_send=(), before_relay=()):
-        *far_sent, far_kept, sent, kept = multiplied(rows, pieces, heads_here, with_steps)
+        *far_sent, far_kept, sent, kept = multiplied(at, rows, pieces, heads_here, with_steps)
         far_got = [swapped(a, "core") for a in after(far_sent, before_send)]
         back = relayed(far_kept, after(far_got, before_relay), heads_here, with_steps)
         return (kept, swapped(after(sent, back), "core")), back
@@ -479,6 +476,7 @@
         (jax.ShapeDtypeStruct((tok_count, width_bc), BF16),)
         + tuple(jax.ShapeDtypeStruct(a, F32) for a in (by_group, by_group, by_head, by_head, by_decay)),
         moved=10 * tok_count * width_bc,
+        vmem=30,
         grid=(1,),
         in_specs=specs_of(width_bc + LANES) + [whole_of(CONV, width_bc)] + [whole_of(1, heads_here)] * 2,
         out_specs=[whole_of(*a) for a in ((tok_count, width_bc), by_group, by_group, by_head, by_head, by_decay)],
@@ -496,7 +494,7 @@
         own_c, own_tc = swapped(own, "core"), swapped(own_t, "core")
         halves = corner_parts(early[1:], 1)
         far_c, far_tc = swapped(far, "core"), swapped(after(far_t, halves), "core")
-        rows = token_rows(at, far, far_t, far_c, far_tc, own, own_t, own_c, own_tc)
+        rows = (far, far_t, far_c, far_tc, own, own_t, own_c, own_tc)
         part_bc, back_bc = partial_sums(rows, bc, True)
         early += sent_on(halves)
         got_bc = swapped(back_bc, "fsdp")
@@ -512,7 +510,7 @@
     else:
         whole = lambda a, axis: lax.all_gather(a, axis, axis=0, tiled=True)
         ranges = [r for a in (far, own) for r in (a[:share], swapped(a[share:], "core"))]
-        rows = jnp.concatenate([whole(r, "tp") for r in ranges], axis=0)
+        rows = (jnp.concatenate([whole(r, "tp") for r in ranges], axis=0),)
         part, back = partial_sums(rows, [whole(weight_early, "chip")], False)
         part_bc, back_bc = partial_sums(rows, [whole(weight_bc, "chip")], True)
         got, got_bc = swapped(back, "fsdp"), swapped(back_bc, "fsdp")
@@ -555,6 +553,7 @@
             ),
             flops=8 * tok_count * N * width * groups,
             moved=14 * tok_count * width * groups,
+            vmem=24,
             grid=grid,
             in_specs=specs_of(width) + [cols_all(CONV), keys, reads, heads_g, heads_g, heads_t, heads_t, heads_1, heads_1],
             out_specs=[cols(tok_count), early_spec, cols(N), cols(8), cols(N + RIM)],

time: 236 us -> 218 us (0.924)
  waiting for transfers between devices: 81.8 us -> 100 us
  starting transfers between devices: 56.2 us -> 39.6 us
  Pallas kernels: 75.9 us -> 61 us
  local copies, waits for them, and re-layouts: 20.7 us -> 16 us
    ppermute x38, waiting for transfers between devices: 81.6 us -> 98.9 us  [swapped(): lax.ppermute(part, axis, [(i, i ^ by) for i in range(lax.axis_size(axis))])]
    ppermute x38, starting transfers between devices: 50.6 us -> 33.4 us  [swapped(): lax.ppermute(part, axis, [(i, i ^ by) for i in range(lax.axis_size(axis))])]
    pallas_call x4 -> x3, Pallas kernels: 34 us -> 21.9 us  [multiplied(): call(functools.partial(multiply_kernel, heads, with_steps, len(rows), len...]
    slice x6, local copies, waits for them, and re-layouts: 6.5 us -> 3.02 us  [corner_parts(): cut = lambda a, i: a[i * rows:(i + 1) * rows]]
    pallas_call x2, Pallas kernels: 10 us -> 7.5 us  [body(): call(mix_kernel, 'mix', (jax.ShapeDtypeStruct((tok_count, groups * width)...]
    pallas_call x1, Pallas kernels: 4.61 us -> 2.23 us  [body(): call(functools.partial(state_proj_kernel, heads_here), 'state_proj', (jax...]
    unnamed x79 -> x65, local copies, waits for them, and re-layouts: 12.9 us -> 12.2 us
  transfers between devices with their start and end apart: 41 -> 41, of which waited for: 21 -> 26; matrix products, arithmetic and copies ran while one was open for 4% -> 2% of each run, Pallas kernels for 26% -> 21%
where the time goes in v9:
time: 218 us; the launch traced here: 217 us
  waiting for transfers between devices  100 us (46%)
  Pallas kernels  61 us (28%)
  starting transfers between devices  39.6 us (18%)
  local copies, waits for them, and re-layouts  16 us (7%)
    ppermute x38, waiting for transfers between devices, swapped(): lax.ppermute(part, axis, [(i, i ^ by) for i in range(lax.axis_size(axis))])  98.9 us
    ppermute x38, starting transfers between devices, swapped(): lax.ppermute(part, axis, [(i, i ^ by) for i in range(lax.axis_size(axis))])  33.4 us
    pallas_call x3, Pallas kernels, multiplied(): call(functools.partial(multiply_kernel, heads, with_steps, len(rows), len...  21.9 us
    unnamed x65, local copies, waits for them, and re-layouts  12.2 us
    pallas_call x2, Pallas kernels, sampled_cols(): call(functools.partial(sample_kernel, count), 'sample', jax.ShapeDtypeStr...  9.33 us
    pallas_call x1, Pallas kernels, sampled_pair(): call(functools.partial(sample_pair_kernel, count), 'sample_pair', jax.Sha...  8.54 us
    pallas_call x2, Pallas kernels, body(): call(mix_kernel, 'mix', (jax.ShapeDtypeStruct((tok_count, groups * width)...  7.5 us
    ppermute x3, starting transfers between devices, rows_before(): lax.ppermute(rim, SEQ, [(i, i + 1) for i in range(lax.axis_size(SEQ) - 1)])  6.11 us
  transfers between devices with their start and end apart: 41, of which 26 were waited for; matrix products, arithmetic and copies ran while one was open for 2% of the time, Pallas kernels for 21%

profile of v9, /device:TPU:0, one launch (start us, length us, event | category | flops | bytes accessed | tf_op | source)
XLA Modules:
  0.0 217.2 jit_solution(636587894045005242)
XLA Ops:
  0.0 8.5 %sample_pair.1.refs_8_ = bf16[512,1152]{1,0:T(8,128)(2,1)} custom-call(f32[4]{0:T(128)} %coef_ref.5, bf16[512,2,512]{2,1,0:T(2,128)(2,1)} %mean_ref.1, bf16[4,512,2,512]{3,2,1,0:T(2,128)(2,1)} %devs_ref.3, bf16[32,512]{1,0:T(8,128)(2,1)} %bitcast.19), custom_call_target="tpu_custom_call" | custom-call | bytes 125829 | tf_op jit(solution)/shard_map/sample_pair/pallas_call | solution.py:101
  8.5 3.0 %collective-permute-start.2 = (bf16[512,1152]{1,0:T(8,128)(2,1)}, bf16[512,1152]{1,0:T(8,128)(2,1)S(1)}, u32[]{:S(2)}, u32[]{:S(2)}) collective-permute-start(bf16[512,1152]{1,0:T(8,128)(2,1)} %sample_pair.1.refs_8_), channel_id=1, source_target_pairs={{0,8},{4,12},{8,0},{12,4},{1,9},{5,13},{9,1},{13,5},{2,10},{6,14},... | collective-permute-start | bytes 3538952 | tf_op jit(solution)/shard_map/ppermute | solution.py:36
  13.7 3.1 %cut_tokens.1 = (bf16[256,2048]{1,0:T(8,128)(2,1)}, bf16[256,2048]{1,0:T(8,128)(2,1)}) custom-call(s32[7]{0:T(128)} %stack.31.at_ref, bf16[128,8192]{1,0:T(8,128)(2,1)} %tokens_ref), custom_call_target="tpu_custom_call" | custom-call | bytes 83886 | tf_op jit(solution)/shard_map/cut_tokens/pallas_call | solution.py:442
  18.3 2.6 %collective-permute-start = (bf16[256,2048]{1,0:T(8,128)(2,1)}, bf16[256,2048]{1,0:T(8,128)(2,1)S(1)}, u32[]{:S(2)}, u32[]{:S(2)}) collective-permute-start(bf16[256,2048]{1,0:T(8,128)(2,1)} %get-tuple-element.87), channel_id=1, source_target_pairs={{0,16},{16,0},{1,17},{17,1},{2,18},{18,2},{3,19},{19,3},{4,20},{20... | collective-permute-start | bytes 3145736 | tf_op jit(solution)/shard_map/ppermute | solution.py:36
  20.9 16.8 %collective-permute-done.2.refs_10_ = bf16[512,1152]{1,0:T(8,128)(2,1)S(1)} collective-permute-done((bf16[512,1152]{1,0:T(8,128)(2,1)}, bf16[512,1152]{1,0:T(8,128)(2,1)S(1)}, u32[]{:S(2)}, u32[]{:S(2)}) %collective-permute-start.2) | collective-permute-done | bytes 1179680 | tf_op jit(solution)/shard_map/ppermute | solution.py:36
  43.8 4.6 %sample.2.refs_8_ = bf16[512,1024]{1,0:T(8,128)(2,1)} custom-call(f32[4]{0:T(128)} %coef_ref.5, bf16[512,2048]{1,0:T(8,128)(2,1)} %mean_ref.3, bf16[4,512,2048]{2,1,0:T(8,128)(2,1)} %devs_ref.5), custom_call_target="tpu_custom_call" | custom-call | bytes 125829 | tf_op jit(solution)/shard_map/sample/pallas_call | solution.py:68
  48.4 4.7 %sample.3.refs_8_ = bf16[512,1024]{1,0:T(8,128)(2,1)} custom-call(f32[4]{0:T(128)} %coef_ref.5, bf16[512,2048]{1,0:T(8,128)(2,1)} %mean_ref.3, bf16[4,512,2048]{2,1,0:T(8,128)(2,1)} %devs_ref.5), custom_call_target="tpu_custom_call" | custom-call | bytes 125829 | tf_op jit(solution)/shard_map/sample/pallas_call | solution.py:68
  53.6 3.1 %collective-permute-done.5.refs_12_ = bf16[256,1152]{1,0:T(8,128)(2,1)} collective-permute-done((bf16[256,1152]{1,0:T(8,128)(2,1)}, bf16[256,1152]{1,0:T(8,128)(2,1)}, u32[]{:S(2)}, u32[]{:S(2)}) %collective-permute-start.5) | collective-permute-done | bytes 589856 | tf_op jit(solution)/shard_map/ppermute | solution.py:36
  58.7 5.0 %collective-permute-done.1.refs_5_ = bf16[256,2048]{1,0:T(8,128)(2,1)S(1)} collective-permute-done((bf16[256,2048]{1,0:T(8,128)(2,1)}, bf16[256,2048]{1,0:T(8,128)(2,1)S(1)}, u32[]{:S(2)}, u32[]{:S(2)}) %collective-permute-start.1) | collective-permute-done | bytes 1048608 | tf_op jit(solution)/shard_map/ppermute | solution.py:36
  67.0 12.8 %collective-permute-done.8.refs_10_ = bf16[512,1024]{1,0:T(8,128)(2,1)S(1)} collective-permute-done((bf16[512,1024]{1,0:T(8,128)(2,1)}, bf16[512,1024]{1,0:T(8,128)(2,1)S(1)}, u32[]{:S(2)}, u32[]{:S(2)}) %collective-permute-start.8) | collective-permute-done | bytes 1048608 | tf_op jit(solution)/shard_map/ppermute | solution.py:36
  81.0 7.1 %collective-permute-done.6.refs_1_ = bf16[256,2048]{1,0:T(8,128)(2,1)S(1)} collective-permute-done((bf16[256,2048]{1,0:T(8,128)(2,1)S(1)}, bf16[256,2048]{1,0:T(8,128)(2,1)S(1)}, u32[]{:S(2)}, u32[]{:S(2)}) %collective-permute-start.6) | collective-permute-done | bytes 1048608 | tf_op jit(solution)/shard_map/ppermute | solution.py:36
  92.1 9.5 %multiply.3 = (bf16[128,1152]{1,0:T(8,128)(2,1)S(1)}, bf16[128,1152]{1,0:T(8,128)(2,1)S(1)}, f32[256,1152]{1,0:T(8,128)S(1)}, bf16[256,1152]{1,0:T(8,128)(2,1)S(1)}, f32[256,1152]{1,0:T(8,128)S(1)}) custom-call(s32[7]{0:T(128)S(1)} %copy-done.27, bf16[256,2048]{1,0:T(8,128)(2,1)S(1)} %collective-permute-done.refs_0_, ...), custom_call_target="tpu_custom_call" | custom-call | flops 96636768 | bytes 249036 | tf_op jit(solution)/shard_map/multiply/pallas_call | solution.py:179
  107.8 5.9 %multiply.5 = (bf16[128,1024]{1,0:T(8,128)(2,1)S(1)}, bf16[128,1024]{1,0:T(8,128)(2,1)S(1)}, f32[256,1024]{1,0:T(8,128)S(1)}, bf16[256,1024]{1,0:T(8,128)(2,1)S(1)}, f32[256,1024]{1,0:T(8,128)S(1)}) custom-call(s32[7]{0:T(128)S(1)} %copy-done.27, bf16[256,2048]{1,0:T(8,128)(2,1)S(1)} %collective-permute-done.refs_0_, ...), custom_call_target="tpu_custom_call" | custom-call | flops 85899344 | bytes 230686 | tf_op jit(solution)/shard_map/multiply/pallas_call | solution.py:179
  114.3 15.7 %collective-permute-done.18.refs_10_ = bf16[512,1024]{1,0:T(8,128)(2,1)S(1)} collective-permute-done((bf16[512,1024]{1,0:T(8,128)(2,1)S(1)}, bf16[512,1024]{1,0:T(8,128)(2,1)S(1)}, u32[]{:S(2)}, u32[]{:S(2)}) %collective-permute-start.18) | collective-permute-done | bytes 1048608 | tf_op jit(solution)/shard_map/ppermute | solution.py:36
  135.2 2.6 %collective-permute-start.25 = (bf16[16,1152]{1,0:T(8,128)(2,1)S(1)}, bf16[16,1152]{1,0:T(8,128)(2,1)S(1)}, u32[]{:S(2)}, u32[]{:S(2)}) collective-permute-start(bf16[16,1152]{1,0:T(8,128)(2,1)S(1)} %rim.3), channel_id=1, source_target_pairs={{0,2},{2,4},{4,6},{6,8},{8,10},{10,12},{12,14},{1,3},{3,5},{5,7},{... | collective-permute-start | bytes 110600 | tf_op jit(solution)/shard_map/ppermute | solution.py:237
  143.7 6.6 %multiply.4 = (bf16[128,1024]{1,0:T(8,128)(2,1)S(1)}, bf16[128,1024]{1,0:T(8,128)(2,1)S(1)}, f32[256,1024]{1,0:T(8,128)S(1)}, bf16[256,1024]{1,0:T(8,128)(2,1)}, f32[256,1024]{1,0:T(8,128)S(1)}) custom-call(s32[7]{0:T(128)S(1)} %copy-done.27, bf16[256,2048]{1,0:T(8,128)(2,1)S(1)} %copy-done.2, bf16[256,2048]{1,0:T(8,128)(2,1)S(1)} %collective-permute-done.6.refs_1_, ...), custom_call_target="tpu_custom_call" | custom-call | flops 85899344 | bytes 230686 | tf_op jit(solution)/shard_map/multiply/pallas_call | solution.py:179
  153.1 6.6 %collective-permute-done.29.got_f = bf16[256,1024]{1,0:T(8,128)(2,1)S(1)} collective-permute-done((bf16[256,1024]{1,0:T(8,128)(2,1)S(1)}, bf16[256,1024]{1,0:T(8,128)(2,1)S(1)}, u32[]{:S(2)}, u32[]{:S(2)}) %collective-permute-start.29) | collective-permute-done | bytes 524320 | tf_op jit(solution)/shard_map/ppermute | solution.py:36
  167.1 3.7 %mix.2 = (f32[256,1024]{1,0:T(8,128)S(1)}, f32[1,128,1024]{2,1,0:T(8,128)S(1)}, f32[128,1024]{1,0:T(8,128)S(1)}, f32[8,1024]{1,0:T(8,128)S(1)}, bf16[144,1024]{1,0:T(8,128)(2,1)}) custom-call(f32[256,1024]{1,0:T(8,128)S(1)} %copy-done.7, bf16[256,1024]{1,0:T(8,128)(2,1)S(1)} %copy-done.17, bf16[256,1024]{1,0:T(8,128)(2,1)S(1)} %copy-done.15, ...), custom_call_target="tpu_custom_call" | custom-call | flops 5368709 | bytes 73400 | tf_op jit(solution)/shard_map/mix/pallas_call | solution.py:544
  178.6 2.6 %collective-permute-start.36 = (bf16[80,1024]{1,0:T(8,128)(2,1)S(1)}, bf16[80,1024]{1,0:T(8,128)(2,1)S(1)}, u32[]{:S(2)}, u32[]{:S(2)}) collective-permute-start(bf16[80,1024]{1,0:T(8,128)(2,1)S(1)} %get-tuple-element.144), channel_id=1, source_target_pairs={{0,4},{2,6},{4,0},{6,2},{8,12},{10,14},{12,8},{14,10},{1,5},{3,7},... | collective-permute-start | bytes 491528 | tf_op jit(solution)/shard_map/ppermute | solution.py:36
  181.3 3.5 %collective-permute-done.30.got_f = bf16[256,1024]{1,0:T(8,128)(2,1)S(1)} collective-permute-done((bf16[256,1024]{1,0:T(8,128)(2,1)}, bf16[256,1024]{1,0:T(8,128)(2,1)S(1)}, u32[]{:S(2)}, u32[]{:S(2)}) %collective-permute-start.30) | collective-permute-done | bytes 524320 | tf_op jit(solution)/shard_map/ppermute | solution.py:36
  189.5 3.8 %mix.3 = (f32[256,1024]{1,0:T(8,128)S(1)}, f32[1,128,1024]{2,1,0:T(8,128)S(1)}, f32[128,1024]{1,0:T(8,128)S(1)}, f32[8,1024]{1,0:T(8,128)S(1)}, bf16[144,1024]{1,0:T(8,128)(2,1)S(1)}) custom-call(f32[256,1024]{1,0:T(8,128)S(1)} %copy-done.9, bf16[256,1024]{1,0:T(8,128)(2,1)} %collective-permute-done.28.got_c, ...), custom_call_target="tpu_custom_call" | custom-call | flops 5368709 | bytes 73400 | tf_op jit(solution)/shard_map/mix/pallas_call | solution.py:544
  199.5 5.8 %collective-permute-done.38.refs_0_ = bf16[144,1024]{1,0:T(8,128)(2,1)S(1)} collective-permute-done((bf16[144,1024]{1,0:T(8,128)(2,1)S(1)}, bf16[144,1024]{1,0:T(8,128)(2,1)S(1)}, u32[]{:S(2)}, u32[]{:S(2)}) %collective-permute-start.38) | collective-permute-done | bytes 294944 | tf_op jit(solution)/shard_map/ppermute | solution.py:36
  206.2 2.7 %collective-permute-start.39 = (bf16[144,1024]{1,0:T(8,128)(2,1)S(1)}, bf16[144,1024]{1,0:T(8,128)(2,1)S(1)}, u32[]{:S(2)}, u32[]{:S(2)}) collective-permute-start(bf16[144,1024]{1,0:T(8,128)(2,1)S(1)} %get-tuple-element.162), channel_id=1, source_target_pairs={{0,8},{2,10},{4,12},{6,14},{8,0},{10,2},{12,4},{14,6},{1,9},{3,11}... | collective-permute-start | bytes 884744 | tf_op jit(solution)/shard_map/ppermute | solution.py:36
  210.7 4.7 %collective-permute-done.39.other = bf16[144,1024]{1,0:T(8,128)(2,1)S(1)} collective-permute-done((bf16[144,1024]{1,0:T(8,128)(2,1)S(1)}, bf16[144,1024]{1,0:T(8,128)(2,1)S(1)}, u32[]{:S(2)}, u32[]{:S(2)}) %collective-permute-start.39) | collective-permute-done | bytes 294944 | tf_op jit(solution)/shard_map/ppermute | solution.py:36
  (153 shorter events, 71.9 us)
Async XLA Ops:
  8.5 29.1 %collective-permute-start.2 = (bf16[512,1152]{1,0:T(8,128)(2,1)}, bf16[512,1152]{1,0:T(8,128)(2,1)S(1)}, u32[]{:S(2)}, u32[]{:S(2)}) collective-permute-start(bf16[512,1152]{1,0:T(8,128)(2,1)} %sample_pair.1.refs_8_), channel_id=1, source_target_pairs={{0,8},{4,12},{8,0},{12,4},{1,9},{5,13},{9,1},{13,5},{2,10},{6,14},... | collective-permute-start | bytes 3538952 | tf_op jit(solution)/shard_map/ppermute | solution.py:36
  11.5 28.8 %collective-permute-start.4 = (bf16[512,1152]{1,0:T(8,128)(2,1)}, bf16[512,1152]{1,0:T(8,128)(2,1)}, u32[]{:S(2)}, u32[]{:S(2)}) collective-permute-start(bf16[512,1152]{1,0:T(8,128)(2,1)} %sample_pair.1.refs_8_), channel_id=1, source_target_pairs={{0,4},{4,0},{8,12},{12,8},{1,5},{5,1},{9,13},{13,9},{2,6},{6,2},{1... | collective-permute-start | bytes 3538952 | tf_op jit(solution)/shard_map/ppermute | solution.py:36
  16.7 46.9 %collective-permute-start.1 = (bf16[256,2048]{1,0:T(8,128)(2,1)}, bf16[256,2048]{1,0:T(8,128)(2,1)S(1)}, u32[]{:S(2)}, u32[]{:S(2)}) collective-permute-start(bf16[256,2048]{1,0:T(8,128)(2,1)} %get-tuple-element.93.refs_4_), channel_id=1, source_target_pairs={{0,1},{1,0},{2,3},{3,2},{4,5},{5,4},{6,7},{7,6},{8,9},{9,8},{10,11... | collective-permute-start | bytes 3145736 | tf_op jit(solution)/shard_map/ppermute | solution.py:36
  18.3 47.8 %collective-permute-start = (bf16[256,2048]{1,0:T(8,128)(2,1)}, bf16[256,2048]{1,0:T(8,128)(2,1)S(1)}, u32[]{:S(2)}, u32[]{:S(2)}) collective-permute-start(bf16[256,2048]{1,0:T(8,128)(2,1)} %get-tuple-element.87), channel_id=1, source_target_pairs={{0,16},{16,0},{1,17},{17,1},{2,18},{18,2},{3,19},{19,3},{4,20},{20... | collective-permute-start | bytes 3145736 | tf_op jit(solution)/shard_map/ppermute | solution.py:36
  38.6 14.9 %collective-permute-start.3 = (bf16[256,1152]{1,0:T(8,128)(2,1)}, bf16[256,1152]{1,0:T(8,128)(2,1)}, u32[]{:S(2)}, u32[]{:S(2)}) collective-permute-start(bf16[256,1152]{1,0:T(8,128)(2,1)} %slice.24), channel_id=1, source_target_pairs={{0,4},{4,0},{8,12},{12,8},{1,5},{5,1},{9,13},{13,9},{2,6},{6,2},{1... | collective-permute-start | bytes 1769480 | tf_op jit(solution)/shard_map/ppermute | solution.py:36
  42.3 14.3 %collective-permute-start.5 = (bf16[256,1152]{1,0:T(8,128)(2,1)}, bf16[256,1152]{1,0:T(8,128)(2,1)}, u32[]{:S(2)}, u32[]{:S(2)}) collective-permute-start(bf16[256,1152]{1,0:T(8,128)(2,1)} %slice.25), channel_id=1, source_target_pairs={{0,8},{4,12},{8,0},{12,4},{1,9},{5,13},{9,1},{13,5},{2,10},{6,14},... | collective-permute-start | bytes 1769480 | tf_op jit(solution)/shard_map/ppermute | solution.py:36
  56.6 23.1 %collective-permute-start.8 = (bf16[512,1024]{1,0:T(8,128)(2,1)}, bf16[512,1024]{1,0:T(8,128)(2,1)S(1)}, u32[]{:S(2)}, u32[]{:S(2)}) collective-permute-start(bf16[512,1024]{1,0:T(8,128)(2,1)} %sample.3.refs_8_), channel_id=1, source_target_pairs={{0,8},{4,12},{8,0},{12,4},{1,9},{5,13},{9,1},{13,5},{2,10},{6,14},... | collective-permute-start | bytes 3145736 | tf_op jit(solution)/shard_map/ppermute | solution.py:36
  58.1 22.9 %collective-permute-start.9 = (bf16[512,1024]{1,0:T(8,128)(2,1)}, bf16[512,1024]{1,0:T(8,128)(2,1)S(1)}, u32[]{:S(2)}, u32[]{:S(2)}) collective-permute-start(bf16[512,1024]{1,0:T(8,128)(2,1)} %sample.3.refs_8_), channel_id=1, source_target_pairs={{0,4},{4,0},{8,12},{12,8},{1,5},{5,1},{9,13},{13,9},{2,6},{6,2},{1... | collective-permute-start | bytes 3145736 | tf_op jit(solution)/shard_map/ppermute | solution.py:36
  66.1 22.1 %collective-permute-start.6 = (bf16[256,2048]{1,0:T(8,128)(2,1)S(1)}, bf16[256,2048]{1,0:T(8,128)(2,1)S(1)}, u32[]{:S(2)}, u32[]{:S(2)}) collective-permute-start(bf16[256,2048]{1,0:T(8,128)(2,1)S(1)} %collective-permute-done.refs_0_), channel_id=1, source_target_pairs={{0,1},{1,0},{2,3},{3,2},{4,5},{5,4},{6,7},{7,6},{8,9},{9,8},{10,11... | collective-permute-start | bytes 3145736 | tf_op jit(solution)/shard_map/ppermute | solution.py:36
  66.5 22.3 %collective-permute-start.11 = (bf16[256,2048]{1,0:T(8,128)(2,1)S(1)}, bf16[256,2048]{1,0:T(8,128)(2,1)S(1)}, u32[]{:S(2)}, u32[]{:S(2)}) collective-permute-start(bf16[256,2048]{1,0:T(8,128)(2,1)S(1)} %copy-done), channel_id=1, source_target_pairs={{0,2},{2,0},{1,3},{3,1},{4,6},{6,4},{5,7},{7,5},{8,10},{10,8},{9,1... | collective-permute-start | bytes 3145736 | tf_op jit(solution)/shard_map/ppermute | solution.py:36
  66.5 22.8 %collective-permute-start.7 = (bf16[256,2048]{1,0:T(8,128)(2,1)S(1)}, bf16[256,2048]{1,0:T(8,128)(2,1)S(1)}, u32[]{:S(2)}, u32[]{:S(2)}) collective-permute-start(bf16[256,2048]{1,0:T(8,128)(2,1)S(1)} %collective-permute-done.refs_0_), channel_id=1, source_target_pairs={{0,2},{2,0},{1,3},{3,1},{4,6},{6,4},{5,7},{7,5},{8,10},{10,8},{9,1... | collective-permute-start | bytes 3145736 | tf_op jit(solution)/shard_map/ppermute | solution.py:36
  88.2 15.8 %collective-permute-start.15 = (bf16[256,1024]{1,0:T(8,128)(2,1)S(1)}, bf16[256,1024]{1,0:T(8,128)(2,1)S(1)}, u32[]{:S(2)}, u32[]{:S(2)}) collective-permute-start(bf16[256,1024]{1,0:T(8,128)(2,1)S(1)} %slice.26), channel_id=1, source_target_pairs={{0,4},{4,0},{8,12},{12,8},{1,5},{5,1},{9,13},{13,9},{2,6},{6,2},{1... | collective-permute-start | bytes 1572872 | tf_op jit(solution)/shard_map/ppermute | solution.py:36
  88.7 15.3 %collective-permute-start.16 = (bf16[256,1024]{1,0:T(8,128)(2,1)S(1)}, bf16[256,1024]{1,0:T(8,128)(2,1)S(1)}, u32[]{:S(2)}, u32[]{:S(2)}) collective-permute-start(bf16[256,1024]{1,0:T(8,128)(2,1)S(1)} %slice.27), channel_id=1, source_target_pairs={{0,8},{4,12},{8,0},{12,4},{1,9},{5,13},{9,1},{13,5},{2,10},{6,14},... | collective-permute-start | bytes 1572872 | tf_op jit(solution)/shard_map/ppermute | solution.py:36
  104.9 25.2 %collective-permute-start.18 = (bf16[512,1024]{1,0:T(8,128)(2,1)S(1)}, bf16[512,1024]{1,0:T(8,128)(2,1)S(1)}, u32[]{:S(2)}, u32[]{:S(2)}) collective-permute-start(bf16[512,1024]{1,0:T(8,128)(2,1)S(1)} %copy-done.4), channel_id=1, source_target_pairs={{0,8},{4,12},{8,0},{12,4},{1,9},{5,13},{9,1},{13,5},{2,10},{6,14},... | collective-permute-start | bytes 3145736 | tf_op jit(solution)/shard_map/ppermute | solution.py:36
  105.4 25.3 %collective-permute-start.17 = (bf16[512,1024]{1,0:T(8,128)(2,1)S(1)}, bf16[512,1024]{1,0:T(8,128)(2,1)S(1)}, u32[]{:S(2)}, u32[]{:S(2)}) collective-permute-start(bf16[512,1024]{1,0:T(8,128)(2,1)S(1)} %copy-done.4), channel_id=1, source_target_pairs={{0,4},{4,0},{8,12},{12,8},{1,5},{5,1},{9,13},{13,9},{2,6},{6,2},{1... | collective-permute-start | bytes 3145736 | tf_op jit(solution)/shard_map/ppermute | solution.py:36
  106.3 28.3 %collective-permute-start.22 = (bf16[256,1152]{1,0:T(8,128)(2,1)S(1)}, bf16[256,1152]{1,0:T(8,128)(2,1)S(1)}, u32[]{:S(2)}, u32[]{:S(2)}) collective-permute-start(bf16[256,1152]{1,0:T(8,128)(2,1)S(1)} %relay.3), channel_id=1, source_target_pairs={{0,16},{16,0},{1,17},{17,1},{2,18},{18,2},{3,19},{19,3},{4,20},{20... | collective-permute-start | bytes 1769480 | tf_op jit(solution)/shard_map/ppermute | solution.py:36
  113.8 18.2 %collective-permute-start.23 = (bf16[128,1024]{1,0:T(8,128)(2,1)S(1)}, bf16[128,1024]{1,0:T(8,128)(2,1)S(1)}, u32[]{:S(2)}, u32[]{:S(2)}) collective-permute-start(bf16[128,1024]{1,0:T(8,128)(2,1)S(1)} %get-tuple-element.114), channel_id=1, source_target_pairs={{0,2},{2,0},{1,3},{3,1},{4,6},{6,4},{5,7},{7,5},{8,10},{10,8},{9,1... | collective-permute-start | bytes 786440 | tf_op jit(solution)/shard_map/ppermute | solution.py:36
  113.8 21.3 %collective-permute-start.21 = (bf16[256,1152]{1,0:T(8,128)(2,1)S(1)}, bf16[256,1152]{1,0:T(8,128)(2,1)S(1)}, u32[]{:S(2)}, u32[]{:S(2)}) collective-permute-start(bf16[256,1152]{1,0:T(8,128)(2,1)S(1)} %get-tuple-element.110), channel_id=1, source_target_pairs={{0,2},{2,0},{1,3},{3,1},{4,6},{6,4},{5,7},{7,5},{8,10},{10,8},{9,1... | collective-permute-start | bytes 1769480 | tf_op jit(solution)/shard_map/ppermute | solution.py:36
  130.1 13.6 %collective-permute-start.19 = (bf16[256,1024]{1,0:T(8,128)(2,1)S(1)}, bf16[256,1024]{1,0:T(8,128)(2,1)S(1)}, u32[]{:S(2)}, u32[]{:S(2)}) collective-permute-start(bf16[256,1024]{1,0:T(8,128)(2,1)S(1)} %slice.28), channel_id=1, source_target_pairs={{0,4},{4,0},{8,12},{12,8},{1,5},{5,1},{9,13},{13,9},{2,6},{6,2},{1... | collective-permute-start | bytes 1572872 | tf_op jit(solution)/shard_map/ppermute | solution.py:36
  130.8 13.0 %collective-permute-start.20 = (bf16[256,1024]{1,0:T(8,128)(2,1)S(1)}, bf16[256,1024]{1,0:T(8,128)(2,1)S(1)}, u32[]{:S(2)}, u32[]{:S(2)}) collective-permute-start(bf16[256,1024]{1,0:T(8,128)(2,1)S(1)} %slice.29), channel_id=1, source_target_pairs={{0,8},{4,12},{8,0},{12,4},{1,9},{5,13},{9,1},{13,5},{2,10},{6,14},... | collective-permute-start | bytes 1572872 | tf_op jit(solution)/shard_map/ppermute | solution.py:36
  134.8 25.0 %collective-permute-start.29 = (bf16[256,1024]{1,0:T(8,128)(2,1)S(1)}, bf16[256,1024]{1,0:T(8,128)(2,1)S(1)}, u32[]{:S(2)}, u32[]{:S(2)}) collective-permute-start(bf16[256,1024]{1,0:T(8,128)(2,1)S(1)} %relay.4), channel_id=1, source_target_pairs={{0,16},{16,0},{1,17},{17,1},{2,18},{18,2},{3,19},{19,3},{4,20},{20... | collective-permute-start | bytes 1572872 | tf_op jit(solution)/shard_map/ppermute | solution.py:36
  135.1 24.6 %collective-permute-start.32 = (bf16[256,1024]{1,0:T(8,128)(2,1)S(1)}, bf16[256,1024]{1,0:T(8,128)(2,1)S(1)}, u32[]{:S(2)}, u32[]{:S(2)}) collective-permute-start(bf16[256,1024]{1,0:T(8,128)(2,1)S(1)} %get-tuple-element.136), channel_id=1, source_target_pairs={{0,2},{2,0},{1,3},{3,1},{4,6},{6,4},{5,7},{7,5},{8,10},{10,8},{9,1... | collective-permute-start | bytes 1572872 | tf_op jit(solution)/shard_map/ppermute | solution.py:36
  159.7 25.1 %collective-permute-start.30 = (bf16[256,1024]{1,0:T(8,128)(2,1)}, bf16[256,1024]{1,0:T(8,128)(2,1)S(1)}, u32[]{:S(2)}, u32[]{:S(2)}) collective-permute-start(bf16[256,1024]{1,0:T(8,128)(2,1)} %relay.5), channel_id=1, source_target_pairs={{0,16},{16,0},{1,17},{17,1},{2,18},{18,2},{3,19},{19,3},{4,20},{20... | collective-permute-start | bytes 1572872 | tf_op jit(solution)/shard_map/ppermute | solution.py:36
  159.7 25.1 %collective-permute-start.28 = (bf16[256,1024]{1,0:T(8,128)(2,1)}, bf16[256,1024]{1,0:T(8,128)(2,1)}, u32[]{:S(2)}, u32[]{:S(2)}) collective-permute-start(bf16[256,1024]{1,0:T(8,128)(2,1)} %get-tuple-element.131), channel_id=1, source_target_pairs={{0,2},{2,0},{1,3},{3,1},{4,6},{6,4},{5,7},{7,5},{8,10},{10,8},{9,1... | collective-permute-start | bytes 1572872 | tf_op jit(solution)/shard_map/ppermute | solution.py:36
  (49 other events, 389.6 us)

commit v10 on v9

--- a/solution.py
+++ b/solution.py
@@ -70,6 +70,7 @@
         "sample",
         jax.ShapeDtypeStruct((rows, width), BF16),
         moved=2 * (count + 2) * rows * width,
+        vmem=24,
         grid=(4,),
         in_specs=[
             SMEM,
@@ -82,12 +83,12 @@
 
 def sample_pair_kernel(count, coef_ref, mean_ref, devs_ref, dt_ref, out_ref):
     factor = (2.0 * (count - 1)) ** (-0.5)
+    accum = mean_ref[...].astype(F32)
+    for member in range(count):
+        accum = accum + factor * coef_ref[member] * devs_ref[member].astype(F32)
     width, heads = mean_ref.shape[2], dt_ref.shape[0]
     for k in range(2):
-        accum = mean_ref[:, k, :].astype(F32)
-        for member in range(count):
-            accum = accum + factor * coef_ref[member] * devs_ref[member, :, k, :].astype(F32)
-        out_ref[:, k * width : (k + 1) * width] = accum.astype(BF16)
+        out_ref[:, k * width : (k + 1) * width] = accum[:, k, :].astype(BF16)
     out_ref[:, 2 * width :] = jnp.zeros((out_ref.shape[0], LANES), BF16)
     rows = out_ref.shape[0]
     steps = dt_ref[:, pl.ds(pl.multiple_of(pl.program_id(0) * rows, rows), rows)]
@@ -444,6 +445,7 @@
         "cut_tokens",
         (cut,) * 2,
         moved=4 * tokens.size,
+        vmem=24,
         in_specs=[SMEM, VMEM],
         out_specs=[VMEM] * 2,
     )(at, tokens)

time: 218 us -> 214 us (0.982)
  Pallas kernels: 61 us -> 51.4 us
  waiting for transfers between devices: 100 us -> 105 us
  starting transfers between devices: 39.6 us -> 42 us
    pallas_call x2, Pallas kernels: 9.33 us -> 3.67 us  [sampled_cols(): call(functools.partial(sample_kernel, count), 'sample', jax.ShapeDtypeStr...]
    ppermute x38, waiting for transfers between devices: 98.9 us -> 103 us  [swapped(): lax.ppermute(part, axis, [(i, i ^ by) for i in range(lax.axis_size(axis))])]
    slice x6, local copies, waits for them, and re-layouts: 3.02 us -> 0.23 us  [corner_parts(): cut = lambda a, i: a[i * rows:(i + 1) * rows]]
    pallas_call x1, Pallas kernels: 3.08 us -> 0.69 us  [body(): call(functools.partial(cut_kernel, chips), 'cut_tokens', (cut,) * 2, move...]
    unnamed x65 -> x47, local copies, waits for them, and re-layouts: 12.2 us -> 14.2 us
  transfers between devices with their start and end apart: 41 -> 41, of which waited for: 26 -> 29; matrix products, arithmetic and copies ran while one was open for 2% -> 0% of each run, Pallas kernels for 21% -> 18%
where the time goes in v10:
time: 214 us; the launch traced here: 213 us
  waiting for transfers between devices  105 us (49%)
  Pallas kernels  51.4 us (24%)
  starting transfers between devices  42 us (20%)
  local copies, waits for them, and re-layouts  14.6 us (7%)
    ppermute x38, waiting for transfers between devices, swapped(): lax.ppermute(part, axis, [(i, i ^ by) for i in range(lax.axis_size(axis))])  103 us
    ppermute x38, starting transfers between devices, swapped(): lax.ppermute(part, axis, [(i, i ^ by) for i in range(lax.axis_size(axis))])  35.6 us
    pallas_call x3, Pallas kernels, multiplied(): call(functools.partial(multiply_kernel, heads, with_steps, len(rows), len...  21.5 us
    unnamed x47, local copies, waits for them, and re-layouts  14.2 us
    pallas_call x2, Pallas kernels, body(): call(mix_kernel, 'mix', (jax.ShapeDtypeStruct((tok_count, groups * width)...  7.62 us
    pallas_call x1, Pallas kernels, sampled_pair(): call(functools.partial(sample_pair_kernel, count), 'sample_pair', jax.Sha...  7.26 us
    ppermute x3, starting transfers between devices, rows_before(): lax.ppermute(rim, SEQ, [(i, i + 1) for i in range(lax.axis_size(SEQ) - 1)])  6.4 us
  transfers between devices with their start and end apart: 41, of which 29 were waited for; matrix products, arithmetic and copies ran while one was open for 0% of the time, Pallas kernels for 18%

profile of v10, /device:TPU:0, one launch (start us, length us, event | category | flops | bytes accessed | tf_op | source)
XLA Modules:
  0.0 212.9 jit_solution(15026697700728258789)
XLA Ops:
  0.0 7.3 %sample_pair.1.refs_8_ = bf16[512,1152]{1,0:T(8,128)(2,1)} custom-call(f32[4]{0:T(128)} %coef_ref.5, bf16[512,2,512]{2,1,0:T(2,128)(2,1)} %mean_ref.1, bf16[4,512,2,512]{3,2,1,0:T(2,128)(2,1)} %devs_ref.3, bf16[32,512]{1,0:T(8,128)(2,1)} %bitcast.19), custom_call_target="tpu_custom_call" | custom-call | bytes 125829 | tf_op jit(solution)/shard_map/sample_pair/pallas_call | solution.py:102
  7.3 3.0 %collective-permute-start.2 = (bf16[512,1152]{1,0:T(8,128)(2,1)}, bf16[512,1152]{1,0:T(8,128)(2,1)S(1)}, u32[]{:S(2)}, u32[]{:S(2)}) collective-permute-start(bf16[512,1152]{1,0:T(8,128)(2,1)} %sample_pair.1.refs_8_), channel_id=1, source_target_pairs={{0,8},{4,12},{8,0},{12,4},{1,9},{5,13},{9,1},{13,5},{2,10},{6,14},... | collective-permute-start | bytes 3538952 | tf_op jit(solution)/shard_map/ppermute | solution.py:36
  15.7 2.6 %collective-permute-start = (bf16[256,2048]{1,0:T(8,128)(2,1)S(1)}, bf16[256,2048]{1,0:T(8,128)(2,1)S(1)}, u32[]{:S(2)}, u32[]{:S(2)}) collective-permute-start(bf16[256,2048]{1,0:T(8,128)(2,1)S(1)} %get-tuple-element.87), channel_id=1, source_target_pairs={{0,16},{16,0},{1,17},{17,1},{2,18},{18,2},{3,19},{19,3},{4,20},{20... | collective-permute-start | bytes 3145736 | tf_op jit(solution)/shard_map/ppermute | solution.py:36
  18.3 18.1 %collective-permute-done.2.refs_10_ = bf16[512,1152]{1,0:T(8,128)(2,1)S(1)} collective-permute-done((bf16[512,1152]{1,0:T(8,128)(2,1)}, bf16[512,1152]{1,0:T(8,128)(2,1)S(1)}, u32[]{:S(2)}, u32[]{:S(2)}) %collective-permute-start.2) | collective-permute-done | bytes 1179680 | tf_op jit(solution)/shard_map/ppermute | solution.py:36
  39.9 3.4 %copy-done = bf16[4,512,2048]{2,1,0:T(8,128)(2,1)S(1)} copy-done((bf16[4,512,2048]{2,1,0:T(8,128)(2,1)S(1)}, bf16[4,512,2048]{2,1,0:T(8,128)(2,1)}, u32[]{:S(2)}) %copy-start) | copy-done | bytes 8388632
  47.0 4.1 %collective-permute-done.3.refs_11_ = bf16[256,1152]{1,0:T(8,128)(2,1)S(1)} collective-permute-done((bf16[256,1152]{1,0:T(8,128)(2,1)S(1)}, bf16[256,1152]{1,0:T(8,128)(2,1)S(1)}, u32[]{:S(2)}, u32[]{:S(2)}) %collective-permute-start.3) | collective-permute-done | bytes 589856 | tf_op jit(solution)/shard_map/ppermute | solution.py:36
  54.3 6.5 %collective-permute-done.1.refs_5_ = bf16[256,2048]{1,0:T(8,128)(2,1)S(1)} collective-permute-done((bf16[256,2048]{1,0:T(8,128)(2,1)S(1)}, bf16[256,2048]{1,0:T(8,128)(2,1)S(1)}, u32[]{:S(2)}, u32[]{:S(2)}) %collective-permute-start.1) | collective-permute-done | bytes 1048608 | tf_op jit(solution)/shard_map/ppermute | solution.py:36
  60.9 2.5 %collective-permute-done.refs_0_ = bf16[256,2048]{1,0:T(8,128)(2,1)S(1)} collective-permute-done((bf16[256,2048]{1,0:T(8,128)(2,1)S(1)}, bf16[256,2048]{1,0:T(8,128)(2,1)S(1)}, u32[]{:S(2)}, u32[]{:S(2)}) %collective-permute-start) | collective-permute-done | bytes 1048608 | tf_op jit(solution)/shard_map/ppermute | solution.py:36
  64.2 10.9 %collective-permute-done.8.refs_10_ = bf16[512,1024]{1,0:T(8,128)(2,1)S(1)} collective-permute-done((bf16[512,1024]{1,0:T(8,128)(2,1)S(1)}, bf16[512,1024]{1,0:T(8,128)(2,1)S(1)}, u32[]{:S(2)}, u32[]{:S(2)}) %collective-permute-start.8) | collective-permute-done | bytes 1048608 | tf_op jit(solution)/shard_map/ppermute | solution.py:36
  76.4 9.0 %collective-permute-done.6.refs_1_ = bf16[256,2048]{1,0:T(8,128)(2,1)S(1)} collective-permute-done((bf16[256,2048]{1,0:T(8,128)(2,1)S(1)}, bf16[256,2048]{1,0:T(8,128)(2,1)S(1)}, u32[]{:S(2)}, u32[]{:S(2)}) %collective-permute-start.6) | collective-permute-done | bytes 1048608 | tf_op jit(solution)/shard_map/ppermute | solution.py:36
  88.1 9.1 %multiply.3 = (bf16[128,1152]{1,0:T(8,128)(2,1)S(1)}, bf16[128,1152]{1,0:T(8,128)(2,1)S(1)}, f32[256,1152]{1,0:T(8,128)S(1)}, bf16[256,1152]{1,0:T(8,128)(2,1)S(1)}, f32[256,1152]{1,0:T(8,128)S(1)}) custom-call(s32[7]{0:T(128)S(1)} %stack.31.at_ref, bf16[256,2048]{1,0:T(8,128)(2,1)S(1)} %collective-permute-done.refs_0_, ...), custom_call_target="tpu_custom_call" | custom-call | flops 96636768 | bytes 249036 | tf_op jit(solution)/shard_map/multiply/pallas_call | solution.py:180
  103.5 5.9 %multiply.5 = (bf16[128,1024]{1,0:T(8,128)(2,1)S(1)}, bf16[128,1024]{1,0:T(8,128)(2,1)S(1)}, f32[256,1024]{1,0:T(8,128)S(1)}, bf16[256,1024]{1,0:T(8,128)(2,1)S(1)}, f32[256,1024]{1,0:T(8,128)S(1)}) custom-call(s32[7]{0:T(128)S(1)} %stack.31.at_ref, bf16[256,2048]{1,0:T(8,128)(2,1)S(1)} %collective-permute-done.refs_0_, ...), custom_call_target="tpu_custom_call" | custom-call | flops 85899344 | bytes 230686 | tf_op jit(solution)/shard_map/multiply/pallas_call | solution.py:180
  110.0 14.8 %collective-permute-done.18.refs_10_ = bf16[512,1024]{1,0:T(8,128)(2,1)S(1)} collective-permute-done((bf16[512,1024]{1,0:T(8,128)(2,1)S(1)}, bf16[512,1024]{1,0:T(8,128)(2,1)S(1)}, u32[]{:S(2)}, u32[]{:S(2)}) %collective-permute-start.18) | collective-permute-done | bytes 1048608 | tf_op jit(solution)/shard_map/ppermute | solution.py:36
  130.0 2.6 %collective-permute-start.25 = (bf16[16,1152]{1,0:T(8,128)(2,1)S(1)}, bf16[16,1152]{1,0:T(8,128)(2,1)S(1)}, u32[]{:S(2)}, u32[]{:S(2)}) collective-permute-start(bf16[16,1152]{1,0:T(8,128)(2,1)S(1)} %rim.3), channel_id=1, source_target_pairs={{0,2},{2,4},{4,6},{6,8},{8,10},{10,12},{12,14},{1,3},{3,5},{5,7},{... | collective-permute-start | bytes 110600 | tf_op jit(solution)/shard_map/ppermute | solution.py:238
  138.2 6.5 %multiply.4 = (bf16[128,1024]{1,0:T(8,128)(2,1)S(1)}, bf16[128,1024]{1,0:T(8,128)(2,1)S(1)}, f32[256,1024]{1,0:T(8,128)S(1)}, bf16[256,1024]{1,0:T(8,128)(2,1)}, f32[256,1024]{1,0:T(8,128)S(1)}) custom-call(s32[7]{0:T(128)S(1)} %stack.31.at_ref, bf16[256,2048]{1,0:T(8,128)(2,1)S(1)} %collective-permute-done.refs_0_, ...), custom_call_target="tpu_custom_call" | custom-call | flops 85899344 | bytes 230686 | tf_op jit(solution)/shard_map/multiply/pallas_call | solution.py:180
  147.5 7.1 %collective-permute-done.29.got_f = bf16[256,1024]{1,0:T(8,128)(2,1)S(1)} collective-permute-done((bf16[256,1024]{1,0:T(8,128)(2,1)S(1)}, bf16[256,1024]{1,0:T(8,128)(2,1)S(1)}, u32[]{:S(2)}, u32[]{:S(2)}) %collective-permute-start.29) | collective-permute-done | bytes 524320 | tf_op jit(solution)/shard_map/ppermute | solution.py:36
  162.6 3.7 %mix.2 = (f32[256,1024]{1,0:T(8,128)S(1)}, f32[1,128,1024]{2,1,0:T(8,128)S(1)}, f32[128,1024]{1,0:T(8,128)S(1)}, f32[8,1024]{1,0:T(8,128)S(1)}, bf16[144,1024]{1,0:T(8,128)(2,1)}) custom-call(f32[256,1024]{1,0:T(8,128)S(1)} %get-tuple-element.134.kept, bf16[256,1024]{1,0:T(8,128)(2,1)S(1)} %copy-done.10, bf16[256,1024]{1,0:T(8,128)(2,1)S(1)} %copy-done.8, ...), custom_call_target="tpu_custom_call" | custom-call | flops 5368709 | bytes 73400 | tf_op jit(solution)/shard_map/mix/pallas_call | solution.py:546
  172.5 2.6 %collective-permute-start.36 = (bf16[80,1024]{1,0:T(8,128)(2,1)S(1)}, bf16[80,1024]{1,0:T(8,128)(2,1)S(1)}, u32[]{:S(2)}, u32[]{:S(2)}) collective-permute-start(bf16[80,1024]{1,0:T(8,128)(2,1)S(1)} %get-tuple-element.144), channel_id=1, source_target_pairs={{0,4},{2,6},{4,0},{6,2},{8,12},{10,14},{12,8},{14,10},{1,5},{3,7},... | collective-permute-start | bytes 491528 | tf_op jit(solution)/shard_map/ppermute | solution.py:36
  175.2 4.8 %collective-permute-done.30.got_f = bf16[256,1024]{1,0:T(8,128)(2,1)} collective-permute-done((bf16[256,1024]{1,0:T(8,128)(2,1)}, bf16[256,1024]{1,0:T(8,128)(2,1)}, u32[]{:S(2)}, u32[]{:S(2)}) %collective-permute-start.30) | collective-permute-done | bytes 524320 | tf_op jit(solution)/shard_map/ppermute | solution.py:36
  183.5 3.9 %mix.3 = (f32[256,1024]{1,0:T(8,128)S(1)}, f32[1,128,1024]{2,1,0:T(8,128)S(1)}, f32[128,1024]{1,0:T(8,128)S(1)}, f32[8,1024]{1,0:T(8,128)S(1)}, bf16[144,1024]{1,0:T(8,128)(2,1)S(1)}) custom-call(f32[256,1024]{1,0:T(8,128)S(1)} %get-tuple-element.147.kept, bf16[256,1024]{1,0:T(8,128)(2,1)} %collective-permute-done.28.got_c, ...), custom_call_target="tpu_custom_call" | custom-call | flops 5368709 | bytes 73400 | tf_op jit(solution)/shard_map/mix/pallas_call | solution.py:546
  190.4 2.6 %collective-permute-start.38 = (bf16[144,1024]{1,0:T(8,128)(2,1)S(1)}, bf16[144,1024]{1,0:T(8,128)(2,1)S(1)}, u32[]{:S(2)}, u32[]{:S(2)}) collective-permute-start(bf16[144,1024]{1,0:T(8,128)(2,1)S(1)} %get-tuple-element.158), channel_id=1, source_target_pairs={{0,4},{2,6},{4,0},{6,2},{8,12},{10,14},{12,8},{14,10},{1,5},{3,7},... | collective-permute-start | bytes 884744 | tf_op jit(solution)/shard_map/ppermute | solution.py:36
  194.6 5.6 %collective-permute-done.38.refs_0_ = bf16[144,1024]{1,0:T(8,128)(2,1)S(1)} collective-permute-done((bf16[144,1024]{1,0:T(8,128)(2,1)S(1)}, bf16[144,1024]{1,0:T(8,128)(2,1)S(1)}, u32[]{:S(2)}, u32[]{:S(2)}) %collective-permute-start.38) | collective-permute-done | bytes 294944 | tf_op jit(solution)/shard_map/ppermute | solution.py:36
  201.3 3.3 %collective-permute-start.39 = (bf16[144,1024]{1,0:T(8,128)(2,1)S(1)}, bf16[144,1024]{1,0:T(8,128)(2,1)S(1)}, u32[]{:S(2)}, u32[]{:S(2)}) collective-permute-start(bf16[144,1024]{1,0:T(8,128)(2,1)S(1)} %get-tuple-element.162), channel_id=1, source_target_pairs={{0,8},{2,10},{4,12},{6,14},{8,0},{10,2},{12,4},{14,6},{1,9},{3,11}... | collective-permute-start | bytes 884744 | tf_op jit(solution)/shard_map/ppermute | solution.py:36
  206.4 4.7 %collective-permute-done.39.other = bf16[144,1024]{1,0:T(8,128)(2,1)S(1)} collective-permute-done((bf16[144,1024]{1,0:T(8,128)(2,1)S(1)}, bf16[144,1024]{1,0:T(8,128)(2,1)S(1)}, u32[]{:S(2)}, u32[]{:S(2)}) %collective-permute-start.39) | collective-permute-done | bytes 294944 | tf_op jit(solution)/shard_map/ppermute | solution.py:36
  (135 shorter events, 68.0 us)
Async XLA Ops:
  7.3 29.1 %collective-permute-start.2 = (bf16[512,1152]{1,0:T(8,128)(2,1)}, bf16[512,1152]{1,0:T(8,128)(2,1)S(1)}, u32[]{:S(2)}, u32[]{:S(2)}) collective-permute-start(bf16[512,1152]{1,0:T(8,128)(2,1)} %sample_pair.1.refs_8_), channel_id=1, source_target_pairs={{0,8},{4,12},{8,0},{12,4},{1,9},{5,13},{9,1},{13,5},{2,10},{6,14},... | collective-permute-start | bytes 3538952 | tf_op jit(solution)/shard_map/ppermute | solution.py:36
  10.2 28.0 %collective-permute-start.4 = (bf16[512,1152]{1,0:T(8,128)(2,1)}, bf16[512,1152]{1,0:T(8,128)(2,1)S(1)}, u32[]{:S(2)}, u32[]{:S(2)}) collective-permute-start(bf16[512,1152]{1,0:T(8,128)(2,1)} %sample_pair.1.refs_8_), channel_id=1, source_target_pairs={{0,4},{4,0},{8,12},{12,8},{1,5},{5,1},{9,13},{13,9},{2,6},{6,2},{1... | collective-permute-start | bytes 3538952 | tf_op jit(solution)/shard_map/ppermute | solution.py:36
  14.1 46.8 %collective-permute-start.1 = (bf16[256,2048]{1,0:T(8,128)(2,1)S(1)}, bf16[256,2048]{1,0:T(8,128)(2,1)S(1)}, u32[]{:S(2)}, u32[]{:S(2)}) collective-permute-start(bf16[256,2048]{1,0:T(8,128)(2,1)S(1)} %get-tuple-element.93.refs_4_), channel_id=1, source_target_pairs={{0,1},{1,0},{2,3},{3,2},{4,5},{5,4},{6,7},{7,6},{8,9},{9,8},{10,11... | collective-permute-start | bytes 3145736 | tf_op jit(solution)/shard_map/ppermute | solution.py:36
  15.7 47.6 %collective-permute-start = (bf16[256,2048]{1,0:T(8,128)(2,1)S(1)}, bf16[256,2048]{1,0:T(8,128)(2,1)S(1)}, u32[]{:S(2)}, u32[]{:S(2)}) collective-permute-start(bf16[256,2048]{1,0:T(8,128)(2,1)S(1)} %get-tuple-element.87), channel_id=1, source_target_pairs={{0,16},{16,0},{1,17},{17,1},{2,18},{18,2},{3,19},{19,3},{4,20},{20... | collective-permute-start | bytes 3145736 | tf_op jit(solution)/shard_map/ppermute | solution.py:36
  36.5 14.6 %collective-permute-start.3 = (bf16[256,1152]{1,0:T(8,128)(2,1)S(1)}, bf16[256,1152]{1,0:T(8,128)(2,1)S(1)}, u32[]{:S(2)}, u32[]{:S(2)}) collective-permute-start(bf16[256,1152]{1,0:T(8,128)(2,1)S(1)} %slice.24), channel_id=1, source_target_pairs={{0,4},{4,0},{8,12},{12,8},{1,5},{5,1},{9,13},{13,9},{2,6},{6,2},{1... | collective-permute-start | bytes 1769480 | tf_op jit(solution)/shard_map/ppermute | solution.py:36
  38.3 14.0 %collective-permute-start.5 = (bf16[256,1152]{1,0:T(8,128)(2,1)S(1)}, bf16[256,1152]{1,0:T(8,128)(2,1)S(1)}, u32[]{:S(2)}, u32[]{:S(2)}) collective-permute-start(bf16[256,1152]{1,0:T(8,128)(2,1)S(1)} %slice.25), channel_id=1, source_target_pairs={{0,8},{4,12},{8,0},{12,4},{1,9},{5,13},{9,1},{13,5},{2,10},{6,14},... | collective-permute-start | bytes 1769480 | tf_op jit(solution)/shard_map/ppermute | solution.py:36
  52.3 22.8 %collective-permute-start.8 = (bf16[512,1024]{1,0:T(8,128)(2,1)S(1)}, bf16[512,1024]{1,0:T(8,128)(2,1)S(1)}, u32[]{:S(2)}, u32[]{:S(2)}) collective-permute-start(bf16[512,1024]{1,0:T(8,128)(2,1)S(1)} %sample.3.refs_8_), channel_id=1, source_target_pairs={{0,8},{4,12},{8,0},{12,4},{1,9},{5,13},{9,1},{13,5},{2,10},{6,14},... | collective-permute-start | bytes 3145736 | tf_op jit(solution)/shard_map/ppermute | solution.py:36
  53.8 22.5 %collective-permute-start.9 = (bf16[512,1024]{1,0:T(8,128)(2,1)S(1)}, bf16[512,1024]{1,0:T(8,128)(2,1)S(1)}, u32[]{:S(2)}, u32[]{:S(2)}) collective-permute-start(bf16[512,1024]{1,0:T(8,128)(2,1)S(1)} %sample.3.refs_8_), channel_id=1, source_target_pairs={{0,4},{4,0},{8,12},{12,8},{1,5},{5,1},{9,13},{13,9},{2,6},{6,2},{1... | collective-permute-start | bytes 3145736 | tf_op jit(solution)/shard_map/ppermute | solution.py:36
  63.3 22.1 %collective-permute-start.6 = (bf16[256,2048]{1,0:T(8,128)(2,1)S(1)}, bf16[256,2048]{1,0:T(8,128)(2,1)S(1)}, u32[]{:S(2)}, u32[]{:S(2)}) collective-permute-start(bf16[256,2048]{1,0:T(8,128)(2,1)S(1)} %collective-permute-done.refs_0_), channel_id=1, source_target_pairs={{0,1},{1,0},{2,3},{3,2},{4,5},{5,4},{6,7},{7,6},{8,9},{9,8},{10,11... | collective-permute-start | bytes 3145736 | tf_op jit(solution)/shard_map/ppermute | solution.py:36
  63.7 22.3 %collective-permute-start.11 = (bf16[256,2048]{1,0:T(8,128)(2,1)S(1)}, bf16[256,2048]{1,0:T(8,128)(2,1)S(1)}, u32[]{:S(2)}, u32[]{:S(2)}) collective-permute-start(bf16[256,2048]{1,0:T(8,128)(2,1)S(1)} %get-tuple-element.93.refs_4_), channel_id=1, source_target_pairs={{0,2},{2,0},{1,3},{3,1},{4,6},{6,4},{5,7},{7,5},{8,10},{10,8},{9,1... | collective-permute-start | bytes 3145736 | tf_op jit(solution)/shard_map/ppermute | solution.py:36
  63.7 22.8 %collective-permute-start.7 = (bf16[256,2048]{1,0:T(8,128)(2,1)S(1)}, bf16[256,2048]{1,0:T(8,128)(2,1)S(1)}, u32[]{:S(2)}, u32[]{:S(2)}) collective-permute-start(bf16[256,2048]{1,0:T(8,128)(2,1)S(1)} %collective-permute-done.refs_0_), channel_id=1, source_target_pairs={{0,2},{2,0},{1,3},{3,1},{4,6},{6,4},{5,7},{7,5},{8,10},{10,8},{9,1... | collective-permute-start | bytes 3145736 | tf_op jit(solution)/shard_map/ppermute | solution.py:36
  85.4 14.3 %collective-permute-start.15 = (bf16[256,1024]{1,0:T(8,128)(2,1)S(1)}, bf16[256,1024]{1,0:T(8,128)(2,1)S(1)}, u32[]{:S(2)}, u32[]{:S(2)}) collective-permute-start(bf16[256,1024]{1,0:T(8,128)(2,1)S(1)} %slice.26), channel_id=1, source_target_pairs={{0,4},{4,0},{8,12},{12,8},{1,5},{5,1},{9,13},{13,9},{2,6},{6,2},{1... | collective-permute-start | bytes 1572872 | tf_op jit(solution)/shard_map/ppermute | solution.py:36
  85.9 14.1 %collective-permute-start.16 = (bf16[256,1024]{1,0:T(8,128)(2,1)S(1)}, bf16[256,1024]{1,0:T(8,128)(2,1)S(1)}, u32[]{:S(2)}, u32[]{:S(2)}) collective-permute-start(bf16[256,1024]{1,0:T(8,128)(2,1)S(1)} %slice.27), channel_id=1, source_target_pairs={{0,8},{4,12},{8,0},{12,4},{1,9},{5,13},{9,1},{13,5},{2,10},{6,14},... | collective-permute-start | bytes 1572872 | tf_op jit(solution)/shard_map/ppermute | solution.py:36
  100.0 24.8 %collective-permute-start.18 = (bf16[512,1024]{1,0:T(8,128)(2,1)S(1)}, bf16[512,1024]{1,0:T(8,128)(2,1)S(1)}, u32[]{:S(2)}, u32[]{:S(2)}) collective-permute-start(bf16[512,1024]{1,0:T(8,128)(2,1)S(1)} %sample.2.refs_8_), channel_id=1, source_target_pairs={{0,8},{4,12},{8,0},{12,4},{1,9},{5,13},{9,1},{13,5},{2,10},{6,14},... | collective-permute-start | bytes 3145736 | tf_op jit(solution)/shard_map/ppermute | solution.py:36
  100.5 25.6 %collective-permute-start.17 = (bf16[512,1024]{1,0:T(8,128)(2,1)S(1)}, bf16[512,1024]{1,0:T(8,128)(2,1)S(1)}, u32[]{:S(2)}, u32[]{:S(2)}) collective-permute-start(bf16[512,1024]{1,0:T(8,128)(2,1)S(1)} %sample.2.refs_8_), channel_id=1, source_target_pairs={{0,4},{4,0},{8,12},{12,8},{1,5},{5,1},{9,13},{13,9},{2,6},{6,2},{1... | collective-permute-start | bytes 3145736 | tf_op jit(solution)/shard_map/ppermute | solution.py:36
  102.0 27.6 %collective-permute-start.22 = (bf16[256,1152]{1,0:T(8,128)(2,1)S(1)}, bf16[256,1152]{1,0:T(8,128)(2,1)S(1)}, u32[]{:S(2)}, u32[]{:S(2)}) collective-permute-start(bf16[256,1152]{1,0:T(8,128)(2,1)S(1)} %relay.3), channel_id=1, source_target_pairs={{0,16},{16,0},{1,17},{17,1},{2,18},{18,2},{3,19},{19,3},{4,20},{20... | collective-permute-start | bytes 1769480 | tf_op jit(solution)/shard_map/ppermute | solution.py:36
  109.4 17.3 %collective-permute-start.23 = (bf16[128,1024]{1,0:T(8,128)(2,1)S(1)}, bf16[128,1024]{1,0:T(8,128)(2,1)S(1)}, u32[]{:S(2)}, u32[]{:S(2)}) collective-permute-start(bf16[128,1024]{1,0:T(8,128)(2,1)S(1)} %get-tuple-element.114), channel_id=1, source_target_pairs={{0,2},{2,0},{1,3},{3,1},{4,6},{6,4},{5,7},{7,5},{8,10},{10,8},{9,1... | collective-permute-start | bytes 786440 | tf_op jit(solution)/shard_map/ppermute | solution.py:36
  109.5 20.4 %collective-permute-start.21 = (bf16[256,1152]{1,0:T(8,128)(2,1)S(1)}, bf16[256,1152]{1,0:T(8,128)(2,1)S(1)}, u32[]{:S(2)}, u32[]{:S(2)}) collective-permute-start(bf16[256,1152]{1,0:T(8,128)(2,1)S(1)} %get-tuple-element.110), channel_id=1, source_target_pairs={{0,2},{2,0},{1,3},{3,1},{4,6},{6,4},{5,7},{7,5},{8,10},{10,8},{9,1... | collective-permute-start | bytes 1769480 | tf_op jit(solution)/shard_map/ppermute | solution.py:36
  124.9 13.2 %collective-permute-start.19 = (bf16[256,1024]{1,0:T(8,128)(2,1)S(1)}, bf16[256,1024]{1,0:T(8,128)(2,1)S(1)}, u32[]{:S(2)}, u32[]{:S(2)}) collective-permute-start(bf16[256,1024]{1,0:T(8,128)(2,1)S(1)} %slice.28), channel_id=1, source_target_pairs={{0,4},{4,0},{8,12},{12,8},{1,5},{5,1},{9,13},{13,9},{2,6},{6,2},{1... | collective-permute-start | bytes 1572872 | tf_op jit(solution)/shard_map/ppermute | solution.py:36
  126.1 12.1 %collective-permute-start.20 = (bf16[256,1024]{1,0:T(8,128)(2,1)S(1)}, bf16[256,1024]{1,0:T(8,128)(2,1)S(1)}, u32[]{:S(2)}, u32[]{:S(2)}) collective-permute-start(bf16[256,1024]{1,0:T(8,128)(2,1)S(1)} %slice.29), channel_id=1, source_target_pairs={{0,8},{4,12},{8,0},{12,4},{1,9},{5,13},{9,1},{13,5},{2,10},{6,14},... | collective-permute-start | bytes 1572872 | tf_op jit(solution)/shard_map/ppermute | solution.py:36
  129.7 24.9 %collective-permute-start.29 = (bf16[256,1024]{1,0:T(8,128)(2,1)S(1)}, bf16[256,1024]{1,0:T(8,128)(2,1)S(1)}, u32[]{:S(2)}, u32[]{:S(2)}) collective-permute-start(bf16[256,1024]{1,0:T(8,128)(2,1)S(1)} %relay.4), channel_id=1, source_target_pairs={{0,16},{16,0},{1,17},{17,1},{2,18},{18,2},{3,19},{19,3},{4,20},{20... | collective-permute-start | bytes 1572872 | tf_op jit(solution)/shard_map/ppermute | solution.py:36
  129.9 24.8 %collective-permute-start.32 = (bf16[256,1024]{1,0:T(8,128)(2,1)S(1)}, bf16[256,1024]{1,0:T(8,128)(2,1)S(1)}, u32[]{:S(2)}, u32[]{:S(2)}) collective-permute-start(bf16[256,1024]{1,0:T(8,128)(2,1)S(1)} %get-tuple-element.136), channel_id=1, source_target_pairs={{0,2},{2,0},{1,3},{3,1},{4,6},{6,4},{5,7},{7,5},{8,10},{10,8},{9,1... | collective-permute-start | bytes 1572872 | tf_op jit(solution)/shard_map/ppermute | solution.py:36
  154.7 25.3 %collective-permute-start.30 = (bf16[256,1024]{1,0:T(8,128)(2,1)}, bf16[256,1024]{1,0:T(8,128)(2,1)}, u32[]{:S(2)}, u32[]{:S(2)}) collective-permute-start(bf16[256,1024]{1,0:T(8,128)(2,1)} %relay.5), channel_id=1, source_target_pairs={{0,16},{16,0},{1,17},{17,1},{2,18},{18,2},{3,19},{19,3},{4,20},{20... | collective-permute-start | bytes 1572872 | tf_op jit(solution)/shard_map/ppermute | solution.py:36
  154.7 25.3 %collective-permute-start.28 = (bf16[256,1024]{1,0:T(8,128)(2,1)}, bf16[256,1024]{1,0:T(8,128)(2,1)}, u32[]{:S(2)}, u32[]{:S(2)}) collective-permute-start(bf16[256,1024]{1,0:T(8,128)(2,1)} %get-tuple-element.131), channel_id=1, source_target_pairs={{0,2},{2,0},{1,3},{3,1},{4,6},{6,4},{5,7},{7,5},{8,10},{10,8},{9,1... | collective-permute-start | bytes 1572872 | tf_op jit(solution)/shard_map/ppermute | solution.py:36
  (40 other events, 258.2 us)

commit v11 on v10

--- a/solution.py
+++ b/solution.py
@@ -370,18 +370,44 @@
     pack_state(sent_refs, joint, whole * decay)
 
 
-def read_kernel(level, place_ref, y, reads, cum_g, early, decays, before, other, *refs):
+def pair_kernel(place_ref, total, decays, other, total_ref, decays_ref, sent_ref, before_ref, part_ref):
+    come, decay = unpack_state([other])
+    whole = decays[0:1, :]
+    upper = place_ref[0] & 1 == 1
+    before_ref[...] = jnp.where(upper, come, 0.0)
+    part_ref[0:1, :] = jnp.where(upper, decay, 1.0)
+    joint = jnp.where(upper, 1.0, decay) * total[...] + jnp.where(upper, whole, 1.0) * come
+    half = joint.shape[1] // 2
+    picked = lambda a: jnp.where(upper, a[:, half:], a[:, :half])
+    joint, whole = picked(joint), picked(whole * decay)
+    total_ref[...] = joint
+    decays_ref[0:1, :] = whole
+    decays_ref[1:2, :] = jnp.ones_like(whole)
+    pack_state([sent_ref], joint, whole)
+
+
+def settle_kernel(level, has_before, place_ref, decays, other, *refs):
+    upper = (place_ref[0] >> level) & 1 == 1
+    state = jnp.where(upper, decays[1:2, :], 0.0) * unpack_state([other])[0]
+    refs[-1][...] = (refs[0][...] + state if has_before else state).astype(BF16)
+
+
+def read_kernel(place_ref, y, reads, cum_g, early, part, before, mine, theirs, *refs):
     out_ref = refs[-1]
-    upper = (place_ref[0] >> level) & 1 == 1
-    state = before[...] + jnp.where(upper, decays[1:2, :], 0.0) * unpack_state([other])[0]
-    cum = cum_g[0]
-    for at in range(0, out_ref.shape[0], SPAN):
-        span = slice(at, at + SPAN)
-        cum_b = cum[span, :]
-        seen = jnp.dot(reads[span, :], state.astype(BF16), preferred_element_type=F32)
-        out_ref[span, :] = (y[span, :] + over_channels(jnp.exp(cum_b)) * seen).astype(BF16)
-        if at + SPAN < out_ref.shape[0]:
-            state = over_channels(jnp.exp(cum_b[SPAN - 1 : SPAN, :])) * state + early[at // SPAN]
+    upper = place_ref[0] & 1 == 1
+    mine, theirs = mine[...].astype(F32), theirs[...].astype(F32)
+    chip = jnp.concatenate([jnp.where(upper, theirs, mine), jnp.where(upper, mine, theirs)], axis=1)
+    whole = before[...] + part[0:1, :] * chip
+    width = whole.shape[1] // cum_g.shape[0]
+    for g in range(cum_g.shape[0]):
+        chans, state = slice(g * width, (g + 1) * width), whole[:, g * width : (g + 1) * width]
+        for at in range(0, out_ref.shape[0], SPAN):
+            span = slice(at, at + SPAN)
+            cum_b = cum_g[g, span, :]
+            seen = jnp.dot(reads[span, g * N : (g + 1) * N], state.astype(BF16), preferred_element_type=F32)
+            out_ref[span, chans] = (y[span, chans] + over_channels(jnp.exp(cum_b)) * seen).astype(BF16)
+            if at + SPAN < out_ref.shape[0]:
+                state = over_channels(jnp.exp(cum_b[SPAN - 1 : SPAN, :])) * state + early[at // SPAN, :, chans]
 
 
 def combined(level, place, total, decays, other, before, groups, cut):
@@ -561,30 +587,59 @@
             out_specs=[cols(tok_count), early_spec, cols(N), cols(8), cols(N + RIM)],
             scratch_shapes=[pltpu.VMEM((tok_count + 8, width), F32)],
         )(*part, conv_proj, conv_out, conv_out, cum_g, steps_g, cum_t, steps_t, skip, decay)
+        wide = groups * width
+        shape = lambda rows, cols, dtype=F32: jax.ShapeDtypeStruct((rows, cols), dtype)
+        total, decays, sent, core_before, core_part = call(
+            pair_kernel,
+            "pair",
+            (shape(N, wide // 2), shape(8, wide // 2), shape(N + RIM, wide // 2, BF16), shape(N, wide), shape(8, wide)),
+            moved=20 * N * wide,
+            vmem=12,
+            in_specs=[SMEM] + [VMEM] * 3,
+            out_specs=[VMEM] * 5,
+        )(seq_place, total, decays, swapped(sent, SEQ, 1))
         before, sent = (), [sent]
-        for level in range(levels - 1):
+        for level in range(1, levels - 1):
             other = [swapped(a, SEQ, 1 << level) for a in sent]
-            cut = (N // 2, N // 2 + RIM) if not first and level + 2 < levels else (N + RIM,)
-            total, decays, fresh, sent = combined(level, seq_place, total, decays, other, before, groups, cut)
+            total, decays, fresh, sent = combined(level, seq_place, total, decays, other, before, 1, (N + RIM,))
             before = (fresh,)
-        (other,) = [swapped(a, SEQ, 1 << (levels - 1)) for a in sent]
-        operands = [seq_place, y, conv_out, cum_g, early, decays, *before, other]
-        specs = [SMEM, cols(tok_count), reads, heads_g, early_spec, cols(8), cols(N), cols(N + RIM)]
+        mine = call(
+            functools.partial(settle_kernel, levels - 1, bool(before)),
+            "settle",
+            shape(N, wide // 2, BF16),
+            moved=6 * N * wide,
+            vmem=12,
+            in_specs=[SMEM] + [VMEM] * (2 + len(before)),
+            out_specs=VMEM,
+        )(seq_place, decays, swapped(sent[0], SEQ, 1 << (levels - 1)), *before)
+        operands = [seq_place, y, conv_out, cum_g, early, core_part, core_before, mine, swapped(mine, "core")]
+        at_block = first // groups
+        specs = [
+            SMEM,
+            whole_of(tok_count, wide),
+            pl.BlockSpec((tok_count, groups * N), lambda i: (0, groups_here // groups + at_block)),
+            pl.BlockSpec((groups, tok_count, per_group), lambda i: (at_block, 0, 0)),
+            whole_of(blocks - 1, N, wide),
+            whole_of(8, wide),
+            whole_of(N, wide),
+            whole_of(N, wide // 2),
+            whole_of(N, wide // 2),
+        ]
         alias = {}
         if result is not None:
             operands.append(result)
             specs.append(pl.BlockSpec(memory_space=pl.ANY))
             alias = {len(operands) - 1: 0}
         result = call(
-            functools.partial(read_kernel, levels - 1),
+            read_kernel,
             "read_out",
             jax.ShapeDtypeStruct((tok_count, heads_here * P_SIZE), BF16),
             flops=2 * tok_count * N * width * groups,
             moved=10 * tok_count * width * groups,
             vmem=12,
-            grid=grid,
+            grid=(1,),
             in_specs=specs,
-            out_specs=cols_all(tok_count),
+            out_specs=pl.BlockSpec((tok_count, wide), lambda i: (0, at_block)),
             input_output_aliases=alias,
         )(*operands)
     return result

time: 214 us -> 208 us (0.972)
  waiting for transfers between devices: 105 us -> 100 us
    ppermute x38 -> x39, waiting for transfers between devices: 103 us -> 98.6 us  [swapped(): lax.ppermute(part, axis, [(i, i ^ by) for i in range(lax.axis_size(axis))])]
    ppermute x38 -> x39, starting transfers between devices: 35.6 us -> 36.1 us  [swapped(): lax.ppermute(part, axis, [(i, i ^ by) for i in range(lax.axis_size(axis))])]
  transfers between devices with their start and end apart: 41 -> 42, of which waited for: 29 -> 29; matrix products, arithmetic and copies ran while one was open for 0% -> 0% of each run, Pallas kernels for 18% -> 18%
where the time goes in v11:
time: 208 us
  waiting for transfers between devices  100 us (48%)
  Pallas kernels  50.2 us (24%)
  starting transfers between devices  42.3 us (20%)
  local copies, waits for them, and re-layouts  14.5 us (7%)
    ppermute x39, waiting for transfers between devices, swapped(): lax.ppermute(part, axis, [(i, i ^ by) for i in range(lax.axis_size(axis))])  98.6 us
    ppermute x39, starting transfers between devices, swapped(): lax.ppermute(part, axis, [(i, i ^ by) for i in range(lax.axis_size(axis))])  36.1 us
    pallas_call x3, Pallas kernels, multiplied(): call(functools.partial(multiply_kernel, heads, with_steps, len(rows), len...  21.5 us
    unnamed x47, local copies, waits for them, and re-layouts  14.1 us
    pallas_call x2, Pallas kernels, body(): call(mix_kernel, 'mix', (jax.ShapeDtypeStruct((tok_count, groups * width)...  7.61 us
    pallas_call x1, Pallas kernels, sampled_pair(): call(functools.partial(sample_pair_kernel, count), 'sample_pair', jax.Sha...  7.27 us
    ppermute x3, starting transfers between devices, rows_before(): lax.ppermute(rim, SEQ, [(i, i + 1) for i in range(lax.axis_size(SEQ) - 1)])  6.26 us
  transfers between devices with their start and end apart: 42, of which 29 were waited for; matrix products, arithmetic and copies ran while one was open for 0% of the time, Pallas kernels for 18%

profile of v11, /device:TPU:0, one launch (start us, length us, event | category | flops | bytes accessed | tf_op | source)
XLA Modules:
  0.0 207.5 jit_solution(13284061139888590598)
XLA Ops:
  0.0 7.3 %sample_pair.1.refs_8_ = bf16[512,1152]{1,0:T(8,128)(2,1)} custom-call(f32[4]{0:T(128)} %coef_ref.5, bf16[512,2,512]{2,1,0:T(2,128)(2,1)} %mean_ref.1, bf16[4,512,2,512]{3,2,1,0:T(2,128)(2,1)} %devs_ref.3, bf16[32,512]{1,0:T(8,128)(2,1)} %bitcast.19), custom_call_target="tpu_custom_call" | custom-call | bytes 125829 | tf_op jit(solution)/shard_map/sample_pair/pallas_call | solution.py:102
  7.3 3.0 %collective-permute-start.2 = (bf16[512,1152]{1,0:T(8,128)(2,1)}, bf16[512,1152]{1,0:T(8,128)(2,1)S(1)}, u32[]{:S(2)}, u32[]{:S(2)}) collective-permute-start(bf16[512,1152]{1,0:T(8,128)(2,1)} %sample_pair.1.refs_8_), channel_id=1, source_target_pairs={{0,8},{4,12},{8,0},{12,4},{1,9},{5,13},{9,1},{13,5},{2,10},{6,14},... | collective-permute-start | bytes 3538952 | tf_op jit(solution)/shard_map/ppermute | solution.py:36
  15.8 2.6 %collective-permute-start = (bf16[256,2048]{1,0:T(8,128)(2,1)S(1)}, bf16[256,2048]{1,0:T(8,128)(2,1)S(1)}, u32[]{:S(2)}, u32[]{:S(2)}) collective-permute-start(bf16[256,2048]{1,0:T(8,128)(2,1)S(1)} %get-tuple-element.88), channel_id=1, source_target_pairs={{0,16},{16,0},{1,17},{17,1},{2,18},{18,2},{3,19},{19,3},{4,20},{20... | collective-permute-start | bytes 3145736 | tf_op jit(solution)/shard_map/ppermute | solution.py:36
  18.3 18.1 %collective-permute-done.2.refs_10_ = bf16[512,1152]{1,0:T(8,128)(2,1)S(1)} collective-permute-done((bf16[512,1152]{1,0:T(8,128)(2,1)}, bf16[512,1152]{1,0:T(8,128)(2,1)S(1)}, u32[]{:S(2)}, u32[]{:S(2)}) %collective-permute-start.2) | collective-permute-done | bytes 1179680 | tf_op jit(solution)/shard_map/ppermute | solution.py:36
  39.9 3.4 %copy-done = bf16[4,512,2048]{2,1,0:T(8,128)(2,1)S(1)} copy-done((bf16[4,512,2048]{2,1,0:T(8,128)(2,1)S(1)}, bf16[4,512,2048]{2,1,0:T(8,128)(2,1)}, u32[]{:S(2)}) %copy-start) | copy-done | bytes 8388632
  47.0 4.1 %collective-permute-done.3.refs_11_ = bf16[256,1152]{1,0:T(8,128)(2,1)S(1)} collective-permute-done((bf16[256,1152]{1,0:T(8,128)(2,1)S(1)}, bf16[256,1152]{1,0:T(8,128)(2,1)S(1)}, u32[]{:S(2)}, u32[]{:S(2)}) %collective-permute-start.3) | collective-permute-done | bytes 589856 | tf_op jit(solution)/shard_map/ppermute | solution.py:36
  54.3 6.5 %collective-permute-done.1.refs_5_ = bf16[256,2048]{1,0:T(8,128)(2,1)S(1)} collective-permute-done((bf16[256,2048]{1,0:T(8,128)(2,1)S(1)}, bf16[256,2048]{1,0:T(8,128)(2,1)S(1)}, u32[]{:S(2)}, u32[]{:S(2)}) %collective-permute-start.1) | collective-permute-done | bytes 1048608 | tf_op jit(solution)/shard_map/ppermute | solution.py:36
  60.9 2.5 %collective-permute-done.refs_0_ = bf16[256,2048]{1,0:T(8,128)(2,1)S(1)} collective-permute-done((bf16[256,2048]{1,0:T(8,128)(2,1)S(1)}, bf16[256,2048]{1,0:T(8,128)(2,1)S(1)}, u32[]{:S(2)}, u32[]{:S(2)}) %collective-permute-start) | collective-permute-done | bytes 1048608 | tf_op jit(solution)/shard_map/ppermute | solution.py:36
  64.2 10.9 %collective-permute-done.8.refs_10_ = bf16[512,1024]{1,0:T(8,128)(2,1)S(1)} collective-permute-done((bf16[512,1024]{1,0:T(8,128)(2,1)S(1)}, bf16[512,1024]{1,0:T(8,128)(2,1)S(1)}, u32[]{:S(2)}, u32[]{:S(2)}) %collective-permute-start.8) | collective-permute-done | bytes 1048608 | tf_op jit(solution)/shard_map/ppermute | solution.py:36
  76.4 9.0 %collective-permute-done.6.refs_1_ = bf16[256,2048]{1,0:T(8,128)(2,1)S(1)} collective-permute-done((bf16[256,2048]{1,0:T(8,128)(2,1)S(1)}, bf16[256,2048]{1,0:T(8,128)(2,1)S(1)}, u32[]{:S(2)}, u32[]{:S(2)}) %collective-permute-start.6) | collective-permute-done | bytes 1048608 | tf_op jit(solution)/shard_map/ppermute | solution.py:36
  88.1 9.1 %multiply.3 = (bf16[128,1152]{1,0:T(8,128)(2,1)S(1)}, bf16[128,1152]{1,0:T(8,128)(2,1)S(1)}, f32[256,1152]{1,0:T(8,128)S(1)}, bf16[256,1152]{1,0:T(8,128)(2,1)S(1)}, f32[256,1152]{1,0:T(8,128)S(1)}) custom-call(s32[7]{0:T(128)S(1)} %stack.31.at_ref, bf16[256,2048]{1,0:T(8,128)(2,1)S(1)} %collective-permute-done.refs_0_, ...), custom_call_target="tpu_custom_call" | custom-call | flops 96636768 | bytes 249036 | tf_op jit(solution)/shard_map/multiply/pallas_call | solution.py:180
  103.5 5.9 %multiply.5 = (bf16[128,1024]{1,0:T(8,128)(2,1)S(1)}, bf16[128,1024]{1,0:T(8,128)(2,1)S(1)}, f32[256,1024]{1,0:T(8,128)S(1)}, bf16[256,1024]{1,0:T(8,128)(2,1)S(1)}, f32[256,1024]{1,0:T(8,128)S(1)}) custom-call(s32[7]{0:T(128)S(1)} %stack.31.at_ref, bf16[256,2048]{1,0:T(8,128)(2,1)S(1)} %collective-permute-done.refs_0_, ...), custom_call_target="tpu_custom_call" | custom-call | flops 85899344 | bytes 230686 | tf_op jit(solution)/shard_map/multiply/pallas_call | solution.py:180
  110.0 14.8 %collective-permute-done.18.refs_10_ = bf16[512,1024]{1,0:T(8,128)(2,1)S(1)} collective-permute-done((bf16[512,1024]{1,0:T(8,128)(2,1)S(1)}, bf16[512,1024]{1,0:T(8,128)(2,1)S(1)}, u32[]{:S(2)}, u32[]{:S(2)}) %collective-permute-start.18) | collective-permute-done | bytes 1048608 | tf_op jit(solution)/shard_map/ppermute | solution.py:36
  130.0 2.6 %collective-permute-start.25 = (bf16[16,1152]{1,0:T(8,128)(2,1)S(1)}, bf16[16,1152]{1,0:T(8,128)(2,1)S(1)}, u32[]{:S(2)}, u32[]{:S(2)}) collective-permute-start(bf16[16,1152]{1,0:T(8,128)(2,1)S(1)} %rim.3), channel_id=1, source_target_pairs={{0,2},{2,4},{4,6},{6,8},{8,10},{10,12},{12,14},{1,3},{3,5},{5,7},{... | collective-permute-start | bytes 110600 | tf_op jit(solution)/shard_map/ppermute | solution.py:238
  138.2 6.5 %multiply.4 = (bf16[128,1024]{1,0:T(8,128)(2,1)S(1)}, bf16[128,1024]{1,0:T(8,128)(2,1)S(1)}, f32[256,1024]{1,0:T(8,128)S(1)}, bf16[256,1024]{1,0:T(8,128)(2,1)}, f32[256,1024]{1,0:T(8,128)S(1)}) custom-call(s32[7]{0:T(128)S(1)} %stack.31.at_ref, bf16[256,2048]{1,0:T(8,128)(2,1)S(1)} %collective-permute-done.refs_0_, ...), custom_call_target="tpu_custom_call" | custom-call | flops 85899344 | bytes 230686 | tf_op jit(solution)/shard_map/multiply/pallas_call | solution.py:180
  147.6 7.1 %collective-permute-done.29.got_f = bf16[256,1024]{1,0:T(8,128)(2,1)S(1)} collective-permute-done((bf16[256,1024]{1,0:T(8,128)(2,1)S(1)}, bf16[256,1024]{1,0:T(8,128)(2,1)S(1)}, u32[]{:S(2)}, u32[]{:S(2)}) %collective-permute-start.29) | collective-permute-done | bytes 524320 | tf_op jit(solution)/shard_map/ppermute | solution.py:36
  162.7 3.7 %mix.2 = (f32[256,1024]{1,0:T(8,128)S(1)}, f32[1,128,1024]{2,1,0:T(8,128)S(1)}, f32[128,1024]{1,0:T(8,128)S(1)}, f32[8,1024]{1,0:T(8,128)S(1)}, bf16[144,1024]{1,0:T(8,128)(2,1)}) custom-call(f32[256,1024]{1,0:T(8,128)S(1)} %get-tuple-element.135.kept, bf16[256,1024]{1,0:T(8,128)(2,1)S(1)} %copy-done.10, bf16[256,1024]{1,0:T(8,128)(2,1)S(1)} %copy-done.8, ...), custom_call_target="tpu_custom_call" | custom-call | flops 5368709 | bytes 73400 | tf_op jit(solution)/shard_map/mix/pallas_call | solution.py:572
  172.3 2.6 %collective-permute-start.35 = (bf16[144,512]{1,0:T(8,128)(2,1)S(1)}, bf16[144,512]{1,0:T(8,128)(2,1)S(1)}, u32[]{:S(2)}, u32[]{:S(2)}) collective-permute-start(bf16[144,512]{1,0:T(8,128)(2,1)S(1)} %get-tuple-element.144), channel_id=1, source_target_pairs={{0,4},{2,6},{4,0},{6,2},{8,12},{10,14},{12,8},{14,10},{1,5},{3,7},... | collective-permute-start | bytes 442376 | tf_op jit(solution)/shard_map/ppermute | solution.py:36
  174.9 5.0 %collective-permute-done.30.got_f = bf16[256,1024]{1,0:T(8,128)(2,1)} collective-permute-done((bf16[256,1024]{1,0:T(8,128)(2,1)}, bf16[256,1024]{1,0:T(8,128)(2,1)}, u32[]{:S(2)}, u32[]{:S(2)}) %collective-permute-start.30) | collective-permute-done | bytes 524320 | tf_op jit(solution)/shard_map/ppermute | solution.py:36
  183.0 3.9 %mix.3 = (f32[256,1024]{1,0:T(8,128)S(1)}, f32[1,128,1024]{2,1,0:T(8,128)S(1)}, f32[128,1024]{1,0:T(8,128)S(1)}, f32[8,1024]{1,0:T(8,128)S(1)}, bf16[144,1024]{1,0:T(8,128)(2,1)S(1)}) custom-call(f32[256,1024]{1,0:T(8,128)S(1)} %get-tuple-element.146.kept, bf16[256,1024]{1,0:T(8,128)(2,1)} %collective-permute-done.28.got_c, ...), custom_call_target="tpu_custom_call" | custom-call | flops 5368709 | bytes 73400 | tf_op jit(solution)/shard_map/mix/pallas_call | solution.py:572
  190.0 2.6 %collective-permute-start.37 = (bf16[144,512]{1,0:T(8,128)(2,1)S(1)}, bf16[144,512]{1,0:T(8,128)(2,1)S(1)}, u32[]{:S(2)}, u32[]{:S(2)}) collective-permute-start(bf16[144,512]{1,0:T(8,128)(2,1)S(1)} %get-tuple-element.159), channel_id=1, source_target_pairs={{0,4},{2,6},{4,0},{6,2},{8,12},{10,14},{12,8},{14,10},{1,5},{3,7},... | collective-permute-start | bytes 442376 | tf_op jit(solution)/shard_map/ppermute | solution.py:36
  194.3 2.5 %collective-permute-done.37.refs_0_ = bf16[144,512]{1,0:T(8,128)(2,1)S(1)} collective-permute-done((bf16[144,512]{1,0:T(8,128)(2,1)S(1)}, bf16[144,512]{1,0:T(8,128)(2,1)S(1)}, u32[]{:S(2)}, u32[]{:S(2)}) %collective-permute-start.37) | collective-permute-done | bytes 147488 | tf_op jit(solution)/shard_map/ppermute | solution.py:36
  197.6 3.3 %collective-permute-start.38 = (bf16[144,512]{1,0:T(8,128)(2,1)S(1)}, bf16[144,512]{1,0:T(8,128)(2,1)S(1)}, u32[]{:S(2)}, u32[]{:S(2)}) collective-permute-start(bf16[144,512]{1,0:T(8,128)(2,1)S(1)} %get-tuple-element.161), channel_id=1, source_target_pairs={{0,8},{2,10},{4,12},{6,14},{8,0},{10,2},{12,4},{14,6},{1,9},{3,11}... | collective-permute-start | bytes 442376 | tf_op jit(solution)/shard_map/ppermute | solution.py:36
  201.0 3.2 %collective-permute-done.38.other = bf16[144,512]{1,0:T(8,128)(2,1)S(1)} collective-permute-done((bf16[144,512]{1,0:T(8,128)(2,1)S(1)}, bf16[144,512]{1,0:T(8,128)(2,1)S(1)}, u32[]{:S(2)}, u32[]{:S(2)}) %collective-permute-start.38) | collective-permute-done | bytes 147488 | tf_op jit(solution)/shard_map/ppermute | solution.py:36
  (139 shorter events, 66.9 us)
Async XLA Ops:
  7.3 29.1 %collective-permute-start.2 = (bf16[512,1152]{1,0:T(8,128)(2,1)}, bf16[512,1152]{1,0:T(8,128)(2,1)S(1)}, u32[]{:S(2)}, u32[]{:S(2)}) collective-permute-start(bf16[512,1152]{1,0:T(8,128)(2,1)} %sample_pair.1.refs_8_), channel_id=1, source_target_pairs={{0,8},{4,12},{8,0},{12,4},{1,9},{5,13},{9,1},{13,5},{2,10},{6,14},... | collective-permute-start | bytes 3538952 | tf_op jit(solution)/shard_map/ppermute | solution.py:36
  10.2 28.0 %collective-permute-start.4 = (bf16[512,1152]{1,0:T(8,128)(2,1)}, bf16[512,1152]{1,0:T(8,128)(2,1)S(1)}, u32[]{:S(2)}, u32[]{:S(2)}) collective-permute-start(bf16[512,1152]{1,0:T(8,128)(2,1)} %sample_pair.1.refs_8_), channel_id=1, source_target_pairs={{0,4},{4,0},{8,12},{12,8},{1,5},{5,1},{9,13},{13,9},{2,6},{6,2},{1... | collective-permute-start | bytes 3538952 | tf_op jit(solution)/shard_map/ppermute | solution.py:36
  14.1 46.8 %collective-permute-start.1 = (bf16[256,2048]{1,0:T(8,128)(2,1)S(1)}, bf16[256,2048]{1,0:T(8,128)(2,1)S(1)}, u32[]{:S(2)}, u32[]{:S(2)}) collective-permute-start(bf16[256,2048]{1,0:T(8,128)(2,1)S(1)} %get-tuple-element.94.refs_4_), channel_id=1, source_target_pairs={{0,1},{1,0},{2,3},{3,2},{4,5},{5,4},{6,7},{7,6},{8,9},{9,8},{10,11... | collective-permute-start | bytes 3145736 | tf_op jit(solution)/shard_map/ppermute | solution.py:36
  15.8 47.6 %collective-permute-start = (bf16[256,2048]{1,0:T(8,128)(2,1)S(1)}, bf16[256,2048]{1,0:T(8,128)(2,1)S(1)}, u32[]{:S(2)}, u32[]{:S(2)}) collective-permute-start(bf16[256,2048]{1,0:T(8,128)(2,1)S(1)} %get-tuple-element.88), channel_id=1, source_target_pairs={{0,16},{16,0},{1,17},{17,1},{2,18},{18,2},{3,19},{19,3},{4,20},{20... | collective-permute-start | bytes 3145736 | tf_op jit(solution)/shard_map/ppermute | solution.py:36
  36.5 14.6 %collective-permute-start.3 = (bf16[256,1152]{1,0:T(8,128)(2,1)S(1)}, bf16[256,1152]{1,0:T(8,128)(2,1)S(1)}, u32[]{:S(2)}, u32[]{:S(2)}) collective-permute-start(bf16[256,1152]{1,0:T(8,128)(2,1)S(1)} %slice.24), channel_id=1, source_target_pairs={{0,4},{4,0},{8,12},{12,8},{1,5},{5,1},{9,13},{13,9},{2,6},{6,2},{1... | collective-permute-start | bytes 1769480 | tf_op jit(solution)/shard_map/ppermute | solution.py:36
  38.3 14.0 %collective-permute-start.5 = (bf16[256,1152]{1,0:T(8,128)(2,1)S(1)}, bf16[256,1152]{1,0:T(8,128)(2,1)S(1)}, u32[]{:S(2)}, u32[]{:S(2)}) collective-permute-start(bf16[256,1152]{1,0:T(8,128)(2,1)S(1)} %slice.25), channel_id=1, source_target_pairs={{0,8},{4,12},{8,0},{12,4},{1,9},{5,13},{9,1},{13,5},{2,10},{6,14},... | collective-permute-start | bytes 1769480 | tf_op jit(solution)/shard_map/ppermute | solution.py:36
  52.3 22.8 %collective-permute-start.8 = (bf16[512,1024]{1,0:T(8,128)(2,1)S(1)}, bf16[512,1024]{1,0:T(8,128)(2,1)S(1)}, u32[]{:S(2)}, u32[]{:S(2)}) collective-permute-start(bf16[512,1024]{1,0:T(8,128)(2,1)S(1)} %sample.3.refs_8_), channel_id=1, source_target_pairs={{0,8},{4,12},{8,0},{12,4},{1,9},{5,13},{9,1},{13,5},{2,10},{6,14},... | collective-permute-start | bytes 3145736 | tf_op jit(solution)/shard_map/ppermute | solution.py:36
  53.8 22.5 %collective-permute-start.9 = (bf16[512,1024]{1,0:T(8,128)(2,1)S(1)}, bf16[512,1024]{1,0:T(8,128)(2,1)S(1)}, u32[]{:S(2)}, u32[]{:S(2)}) collective-permute-start(bf16[512,1024]{1,0:T(8,128)(2,1)S(1)} %sample.3.refs_8_), channel_id=1, source_target_pairs={{0,4},{4,0},{8,12},{12,8},{1,5},{5,1},{9,13},{13,9},{2,6},{6,2},{1... | collective-permute-start | bytes 3145736 | tf_op jit(solution)/shard_map/ppermute | solution.py:36
  63.3 22.1 %collective-permute-start.6 = (bf16[256,2048]{1,0:T(8,128)(2,1)S(1)}, bf16[256,2048]{1,0:T(8,128)(2,1)S(1)}, u32[]{:S(2)}, u32[]{:S(2)}) collective-permute-start(bf16[256,2048]{1,0:T(8,128)(2,1)S(1)} %collective-permute-done.refs_0_), channel_id=1, source_target_pairs={{0,1},{1,0},{2,3},{3,2},{4,5},{5,4},{6,7},{7,6},{8,9},{9,8},{10,11... | collective-permute-start | bytes 3145736 | tf_op jit(solution)/shard_map/ppermute | solution.py:36
  63.7 22.3 %collective-permute-start.11 = (bf16[256,2048]{1,0:T(8,128)(2,1)S(1)}, bf16[256,2048]{1,0:T(8,128)(2,1)S(1)}, u32[]{:S(2)}, u32[]{:S(2)}) collective-permute-start(bf16[256,2048]{1,0:T(8,128)(2,1)S(1)} %get-tuple-element.94.refs_4_), channel_id=1, source_target_pairs={{0,2},{2,0},{1,3},{3,1},{4,6},{6,4},{5,7},{7,5},{8,10},{10,8},{9,1... | collective-permute-start | bytes 3145736 | tf_op jit(solution)/shard_map/ppermute | solution.py:36
  63.7 22.8 %collective-permute-start.7 = (bf16[256,2048]{1,0:T(8,128)(2,1)S(1)}, bf16[256,2048]{1,0:T(8,128)(2,1)S(1)}, u32[]{:S(2)}, u32[]{:S(2)}) collective-permute-start(bf16[256,2048]{1,0:T(8,128)(2,1)S(1)} %collective-permute-done.refs_0_), channel_id=1, source_target_pairs={{0,2},{2,0},{1,3},{3,1},{4,6},{6,4},{5,7},{7,5},{8,10},{10,8},{9,1... | collective-permute-start | bytes 3145736 | tf_op jit(solution)/shard_map/ppermute | solution.py:36
  85.4 14.3 %collective-permute-start.15 = (bf16[256,1024]{1,0:T(8,128)(2,1)S(1)}, bf16[256,1024]{1,0:T(8,128)(2,1)S(1)}, u32[]{:S(2)}, u32[]{:S(2)}) collective-permute-start(bf16[256,1024]{1,0:T(8,128)(2,1)S(1)} %slice.26), channel_id=1, source_target_pairs={{0,4},{4,0},{8,12},{12,8},{1,5},{5,1},{9,13},{13,9},{2,6},{6,2},{1... | collective-permute-start | bytes 1572872 | tf_op jit(solution)/shard_map/ppermute | solution.py:36
  86.0 14.1 %collective-permute-start.16 = (bf16[256,1024]{1,0:T(8,128)(2,1)S(1)}, bf16[256,1024]{1,0:T(8,128)(2,1)S(1)}, u32[]{:S(2)}, u32[]{:S(2)}) collective-permute-start(bf16[256,1024]{1,0:T(8,128)(2,1)S(1)} %slice.27), channel_id=1, source_target_pairs={{0,8},{4,12},{8,0},{12,4},{1,9},{5,13},{9,1},{13,5},{2,10},{6,14},... | collective-permute-start | bytes 1572872 | tf_op jit(solution)/shard_map/ppermute | solution.py:36
  100.0 24.8 %collective-permute-start.18 = (bf16[512,1024]{1,0:T(8,128)(2,1)S(1)}, bf16[512,1024]{1,0:T(8,128)(2,1)S(1)}, u32[]{:S(2)}, u32[]{:S(2)}) collective-permute-start(bf16[512,1024]{1,0:T(8,128)(2,1)S(1)} %sample.2.refs_8_), channel_id=1, source_target_pairs={{0,8},{4,12},{8,0},{12,4},{1,9},{5,13},{9,1},{13,5},{2,10},{6,14},... | collective-permute-start | bytes 3145736 | tf_op jit(solution)/shard_map/ppermute | solution.py:36
  100.5 25.6 %collective-permute-start.17 = (bf16[512,1024]{1,0:T(8,128)(2,1)S(1)}, bf16[512,1024]{1,0:T(8,128)(2,1)S(1)}, u32[]{:S(2)}, u32[]{:S(2)}) collective-permute-start(bf16[512,1024]{1,0:T(8,128)(2,1)S(1)} %sample.2.refs_8_), channel_id=1, source_target_pairs={{0,4},{4,0},{8,12},{12,8},{1,5},{5,1},{9,13},{13,9},{2,6},{6,2},{1... | collective-permute-start | bytes 3145736 | tf_op jit(solution)/shard_map/ppermute | solution.py:36
  102.0 27.6 %collective-permute-start.22 = (bf16[256,1152]{1,0:T(8,128)(2,1)S(1)}, bf16[256,1152]{1,0:T(8,128)(2,1)S(1)}, u32[]{:S(2)}, u32[]{:S(2)}) collective-permute-start(bf16[256,1152]{1,0:T(8,128)(2,1)S(1)} %relay.3), channel_id=1, source_target_pairs={{0,16},{16,0},{1,17},{17,1},{2,18},{18,2},{3,19},{19,3},{4,20},{20... | collective-permute-start | bytes 1769480 | tf_op jit(solution)/shard_map/ppermute | solution.py:36
  109.4 17.3 %collective-permute-start.23 = (bf16[128,1024]{1,0:T(8,128)(2,1)S(1)}, bf16[128,1024]{1,0:T(8,128)(2,1)S(1)}, u32[]{:S(2)}, u32[]{:S(2)}) collective-permute-start(bf16[128,1024]{1,0:T(8,128)(2,1)S(1)} %get-tuple-element.115), channel_id=1, source_target_pairs={{0,2},{2,0},{1,3},{3,1},{4,6},{6,4},{5,7},{7,5},{8,10},{10,8},{9,1... | collective-permute-start | bytes 786440 | tf_op jit(solution)/shard_map/ppermute | solution.py:36
  109.5 20.4 %collective-permute-start.21 = (bf16[256,1152]{1,0:T(8,128)(2,1)S(1)}, bf16[256,1152]{1,0:T(8,128)(2,1)S(1)}, u32[]{:S(2)}, u32[]{:S(2)}) collective-permute-start(bf16[256,1152]{1,0:T(8,128)(2,1)S(1)} %get-tuple-element.111), channel_id=1, source_target_pairs={{0,2},{2,0},{1,3},{3,1},{4,6},{6,4},{5,7},{7,5},{8,10},{10,8},{9,1... | collective-permute-start | bytes 1769480 | tf_op jit(solution)/shard_map/ppermute | solution.py:36
  124.9 13.2 %collective-permute-start.19 = (bf16[256,1024]{1,0:T(8,128)(2,1)S(1)}, bf16[256,1024]{1,0:T(8,128)(2,1)S(1)}, u32[]{:S(2)}, u32[]{:S(2)}) collective-permute-start(bf16[256,1024]{1,0:T(8,128)(2,1)S(1)} %slice.28), channel_id=1, source_target_pairs={{0,4},{4,0},{8,12},{12,8},{1,5},{5,1},{9,13},{13,9},{2,6},{6,2},{1... | collective-permute-start | bytes 1572872 | tf_op jit(solution)/shard_map/ppermute | solution.py:36
  126.1 12.1 %collective-permute-start.20 = (bf16[256,1024]{1,0:T(8,128)(2,1)S(1)}, bf16[256,1024]{1,0:T(8,128)(2,1)S(1)}, u32[]{:S(2)}, u32[]{:S(2)}) collective-permute-start(bf16[256,1024]{1,0:T(8,128)(2,1)S(1)} %slice.29), channel_id=1, source_target_pairs={{0,8},{4,12},{8,0},{12,4},{1,9},{5,13},{9,1},{13,5},{2,10},{6,14},... | collective-permute-start | bytes 1572872 | tf_op jit(solution)/shard_map/ppermute | solution.py:36
  129.7 24.9 %collective-permute-start.29 = (bf16[256,1024]{1,0:T(8,128)(2,1)S(1)}, bf16[256,1024]{1,0:T(8,128)(2,1)S(1)}, u32[]{:S(2)}, u32[]{:S(2)}) collective-permute-start(bf16[256,1024]{1,0:T(8,128)(2,1)S(1)} %relay.4), channel_id=1, source_target_pairs={{0,16},{16,0},{1,17},{17,1},{2,18},{18,2},{3,19},{19,3},{4,20},{20... | collective-permute-start | bytes 1572872 | tf_op jit(solution)/shard_map/ppermute | solution.py:36
  129.9 24.8 %collective-permute-start.32 = (bf16[256,1024]{1,0:T(8,128)(2,1)S(1)}, bf16[256,1024]{1,0:T(8,128)(2,1)S(1)}, u32[]{:S(2)}, u32[]{:S(2)}) collective-permute-start(bf16[256,1024]{1,0:T(8,128)(2,1)S(1)} %get-tuple-element.137), channel_id=1, source_target_pairs={{0,2},{2,0},{1,3},{3,1},{4,6},{6,4},{5,7},{7,5},{8,10},{10,8},{9,1... | collective-permute-start | bytes 1572872 | tf_op jit(solution)/shard_map/ppermute | solution.py:36
  154.7 25.3 %collective-permute-start.30 = (bf16[256,1024]{1,0:T(8,128)(2,1)}, bf16[256,1024]{1,0:T(8,128)(2,1)}, u32[]{:S(2)}, u32[]{:S(2)}) collective-permute-start(bf16[256,1024]{1,0:T(8,128)(2,1)} %relay.5), channel_id=1, source_target_pairs={{0,16},{16,0},{1,17},{17,1},{2,18},{18,2},{3,19},{19,3},{4,20},{20... | collective-permute-start | bytes 1572872 | tf_op jit(solution)/shard_map/ppermute | solution.py:36
  154.7 25.3 %collective-permute-start.28 = (bf16[256,1024]{1,0:T(8,128)(2,1)}, bf16[256,1024]{1,0:T(8,128)(2,1)}, u32[]{:S(2)}, u32[]{:S(2)}) collective-permute-start(bf16[256,1024]{1,0:T(8,128)(2,1)} %get-tuple-element.132), channel_id=1, source_target_pairs={{0,2},{2,0},{1,3},{3,1},{4,6},{6,4},{5,7},{7,5},{8,10},{10,8},{9,1... | collective-permute-start | bytes 1572872 | tf_op jit(solution)/shard_map/ppermute | solution.py:36
  (41 other events, 240.7 us)

commit v12 on v11

--- a/solution.py
+++ b/solution.py
@@ -83,12 +83,19 @@
 
 def sample_pair_kernel(count, coef_ref, mean_ref, devs_ref, dt_ref, out_ref):
     factor = (2.0 * (count - 1)) ** (-0.5)
-    accum = mean_ref[...].astype(F32)
+    rows, _, width = mean_ref.shape
+    heads = dt_ref.shape[0]
+    flat = lambda a: a.reshape(2 * rows, width).astype(F32)
+    accum = flat(mean_ref[...])
     for member in range(count):
-        accum = accum + factor * coef_ref[member] * devs_ref[member].astype(F32)
-    width, heads = mean_ref.shape[2], dt_ref.shape[0]
+        accum = accum + factor * coef_ref[member] * flat(devs_ref[member])
+    accum = accum.astype(BF16)
+    row = lax.broadcasted_iota(jnp.int32, (rows, 2 * rows), 0)
+    col = lax.broadcasted_iota(jnp.int32, (rows, 2 * rows), 1)
     for k in range(2):
-        out_ref[:, k * width : (k + 1) * width] = accum[:, k, :].astype(BF16)
+        picks = jnp.where(col == 2 * row + k, 1.0, 0.0).astype(BF16)
+        part = jnp.dot(picks, accum, preferred_element_type=F32)
+        out_ref[:, k * width : (k + 1) * width] = part.astype(BF16)
     out_ref[:, 2 * width :] = jnp.zeros((out_ref.shape[0], LANES), BF16)
     rows = out_ref.shape[0]
     steps = dt_ref[:, pl.ds(pl.multiple_of(pl.program_id(0) * rows, rows), rows)]

time: 208 us -> 206 us (level)
  Pallas kernels: 50.2 us -> 48.1 us
    pallas_call x1, Pallas kernels: 7.27 us -> 5.18 us  [sampled_pair(): call(functools.partial(sample_pair_kernel, count), 'sample_pair', jax.Sha...]
where the time goes in v12:
time: 206 us; the launch traced here: 205 us
  waiting for transfers between devices  100 us (49%)
  Pallas kernels  48.1 us (23%)
  starting transfers between devices  42.3 us (21%)
  local copies, waits for them, and re-layouts  14.5 us (7%)
    ppermute x39, waiting for transfers between devices, swapped(): lax.ppermute(part, axis, [(i, i ^ by) for i in range(lax.axis_size(axis))])  98.6 us
    ppermute x39, starting transfers between devices, swapped(): lax.ppermute(part, axis, [(i, i ^ by) for i in range(lax.axis_size(axis))])  36.1 us
    pallas_call x3, Pallas kernels, multiplied(): call(functools.partial(multiply_kernel, heads, with_steps, len(rows), len...  21.5 us
    unnamed x47, local copies, waits for them, and re-layouts  14.1 us
    pallas_call x2, Pallas kernels, body(): call(mix_kernel, 'mix', (jax.ShapeDtypeStruct((tok_count, groups * width)...  7.6 us
    ppermute x3, starting transfers between devices, rows_before(): lax.ppermute(rim, SEQ, [(i, i + 1) for i in range(lax.axis_size(SEQ) - 1)])  6.26 us
    pallas_call x1, Pallas kernels, sampled_pair(): call(functools.partial(sample_pair_kernel, count), 'sample_pair', jax.Sha...  5.18 us
  transfers between devices with their start and end apart: 42, of which 29 were waited for; matrix products, arithmetic and copies ran while one was open for 0% of the time, Pallas kernels for 18%

profile of v12, /device:TPU:0, one launch (start us, length us, event | category | flops | bytes accessed | tf_op | source)
XLA Modules:
  0.0 205.4 jit_solution(7979002204182868095)
XLA Ops:
  0.0 5.2 %sample_pair.1.refs_8_ = bf16[512,1152]{1,0:T(8,128)(2,1)} custom-call(f32[4]{0:T(128)} %coef_ref.5, bf16[512,2,512]{2,1,0:T(2,128)(2,1)} %mean_ref.1, bf16[4,512,2,512]{3,2,1,0:T(2,128)(2,1)} %devs_ref.3, bf16[32,512]{1,0:T(8,128)(2,1)} %bitcast.19), custom_call_target="tpu_custom_call" | custom-call | bytes 125829 | tf_op jit(solution)/shard_map/sample_pair/pallas_call | solution.py:109
  5.2 3.0 %collective-permute-start.2 = (bf16[512,1152]{1,0:T(8,128)(2,1)}, bf16[512,1152]{1,0:T(8,128)(2,1)S(1)}, u32[]{:S(2)}, u32[]{:S(2)}) collective-permute-start(bf16[512,1152]{1,0:T(8,128)(2,1)} %sample_pair.1.refs_8_), channel_id=1, source_target_pairs={{0,8},{4,12},{8,0},{12,4},{1,9},{5,13},{9,1},{13,5},{2,10},{6,14},... | collective-permute-start | bytes 3538952 | tf_op jit(solution)/shard_map/ppermute | solution.py:36
  13.7 2.6 %collective-permute-start = (bf16[256,2048]{1,0:T(8,128)(2,1)S(1)}, bf16[256,2048]{1,0:T(8,128)(2,1)S(1)}, u32[]{:S(2)}, u32[]{:S(2)}) collective-permute-start(bf16[256,2048]{1,0:T(8,128)(2,1)S(1)} %get-tuple-element.88), channel_id=1, source_target_pairs={{0,16},{16,0},{1,17},{17,1},{2,18},{18,2},{3,19},{19,3},{4,20},{20... | collective-permute-start | bytes 3145736 | tf_op jit(solution)/shard_map/ppermute | solution.py:36
  16.3 18.1 %collective-permute-done.2.refs_10_ = bf16[512,1152]{1,0:T(8,128)(2,1)S(1)} collective-permute-done((bf16[512,1152]{1,0:T(8,128)(2,1)}, bf16[512,1152]{1,0:T(8,128)(2,1)S(1)}, u32[]{:S(2)}, u32[]{:S(2)}) %collective-permute-start.2) | collective-permute-done | bytes 1179680 | tf_op jit(solution)/shard_map/ppermute | solution.py:36
  37.8 3.4 %copy-done = bf16[4,512,2048]{2,1,0:T(8,128)(2,1)S(1)} copy-done((bf16[4,512,2048]{2,1,0:T(8,128)(2,1)S(1)}, bf16[4,512,2048]{2,1,0:T(8,128)(2,1)}, u32[]{:S(2)}) %copy-start) | copy-done | bytes 8388632
  44.9 4.1 %collective-permute-done.3.refs_11_ = bf16[256,1152]{1,0:T(8,128)(2,1)S(1)} collective-permute-done((bf16[256,1152]{1,0:T(8,128)(2,1)S(1)}, bf16[256,1152]{1,0:T(8,128)(2,1)S(1)}, u32[]{:S(2)}, u32[]{:S(2)}) %collective-permute-start.3) | collective-permute-done | bytes 589856 | tf_op jit(solution)/shard_map/ppermute | solution.py:36
  52.2 6.5 %collective-permute-done.1.refs_5_ = bf16[256,2048]{1,0:T(8,128)(2,1)S(1)} collective-permute-done((bf16[256,2048]{1,0:T(8,128)(2,1)S(1)}, bf16[256,2048]{1,0:T(8,128)(2,1)S(1)}, u32[]{:S(2)}, u32[]{:S(2)}) %collective-permute-start.1) | collective-permute-done | bytes 1048608 | tf_op jit(solution)/shard_map/ppermute | solution.py:36
  58.8 2.5 %collective-permute-done.refs_0_ = bf16[256,2048]{1,0:T(8,128)(2,1)S(1)} collective-permute-done((bf16[256,2048]{1,0:T(8,128)(2,1)S(1)}, bf16[256,2048]{1,0:T(8,128)(2,1)S(1)}, u32[]{:S(2)}, u32[]{:S(2)}) %collective-permute-start) | collective-permute-done | bytes 1048608 | tf_op jit(solution)/shard_map/ppermute | solution.py:36
  62.1 10.9 %collective-permute-done.8.refs_10_ = bf16[512,1024]{1,0:T(8,128)(2,1)S(1)} collective-permute-done((bf16[512,1024]{1,0:T(8,128)(2,1)S(1)}, bf16[512,1024]{1,0:T(8,128)(2,1)S(1)}, u32[]{:S(2)}, u32[]{:S(2)}) %collective-permute-start.8) | collective-permute-done | bytes 1048608 | tf_op jit(solution)/shard_map/ppermute | solution.py:36
  74.3 9.0 %collective-permute-done.6.refs_1_ = bf16[256,2048]{1,0:T(8,128)(2,1)S(1)} collective-permute-done((bf16[256,2048]{1,0:T(8,128)(2,1)S(1)}, bf16[256,2048]{1,0:T(8,128)(2,1)S(1)}, u32[]{:S(2)}, u32[]{:S(2)}) %collective-permute-start.6) | collective-permute-done | bytes 1048608 | tf_op jit(solution)/shard_map/ppermute | solution.py:36
  86.0 9.1 %multiply.3 = (bf16[128,1152]{1,0:T(8,128)(2,1)S(1)}, bf16[128,1152]{1,0:T(8,128)(2,1)S(1)}, f32[256,1152]{1,0:T(8,128)S(1)}, bf16[256,1152]{1,0:T(8,128)(2,1)S(1)}, f32[256,1152]{1,0:T(8,128)S(1)}) custom-call(s32[7]{0:T(128)S(1)} %stack.31.at_ref, bf16[256,2048]{1,0:T(8,128)(2,1)S(1)} %collective-permute-done.refs_0_, ...), custom_call_target="tpu_custom_call" | custom-call | flops 96636768 | bytes 249036 | tf_op jit(solution)/shard_map/multiply/pallas_call | solution.py:187
  101.4 5.9 %multiply.5 = (bf16[128,1024]{1,0:T(8,128)(2,1)S(1)}, bf16[128,1024]{1,0:T(8,128)(2,1)S(1)}, f32[256,1024]{1,0:T(8,128)S(1)}, bf16[256,1024]{1,0:T(8,128)(2,1)S(1)}, f32[256,1024]{1,0:T(8,128)S(1)}) custom-call(s32[7]{0:T(128)S(1)} %stack.31.at_ref, bf16[256,2048]{1,0:T(8,128)(2,1)S(1)} %collective-permute-done.refs_0_, ...), custom_call_target="tpu_custom_call" | custom-call | flops 85899344 | bytes 230686 | tf_op jit(solution)/shard_map/multiply/pallas_call | solution.py:187
  107.9 14.8 %collective-permute-done.18.refs_10_ = bf16[512,1024]{1,0:T(8,128)(2,1)S(1)} collective-permute-done((bf16[512,1024]{1,0:T(8,128)(2,1)S(1)}, bf16[512,1024]{1,0:T(8,128)(2,1)S(1)}, u32[]{:S(2)}, u32[]{:S(2)}) %collective-permute-start.18) | collective-permute-done | bytes 1048608 | tf_op jit(solution)/shard_map/ppermute | solution.py:36
  127.9 2.6 %collective-permute-start.25 = (bf16[16,1152]{1,0:T(8,128)(2,1)S(1)}, bf16[16,1152]{1,0:T(8,128)(2,1)S(1)}, u32[]{:S(2)}, u32[]{:S(2)}) collective-permute-start(bf16[16,1152]{1,0:T(8,128)(2,1)S(1)} %rim.3), channel_id=1, source_target_pairs={{0,2},{2,4},{4,6},{6,8},{8,10},{10,12},{12,14},{1,3},{3,5},{5,7},{... | collective-permute-start | bytes 110600 | tf_op jit(solution)/shard_map/ppermute | solution.py:245
  136.1 6.5 %multiply.4 = (bf16[128,1024]{1,0:T(8,128)(2,1)S(1)}, bf16[128,1024]{1,0:T(8,128)(2,1)S(1)}, f32[256,1024]{1,0:T(8,128)S(1)}, bf16[256,1024]{1,0:T(8,128)(2,1)}, f32[256,1024]{1,0:T(8,128)S(1)}) custom-call(s32[7]{0:T(128)S(1)} %stack.31.at_ref, bf16[256,2048]{1,0:T(8,128)(2,1)S(1)} %collective-permute-done.refs_0_, ...), custom_call_target="tpu_custom_call" | custom-call | flops 85899344 | bytes 230686 | tf_op jit(solution)/shard_map/multiply/pallas_call | solution.py:187
  145.5 7.1 %collective-permute-done.29.got_f = bf16[256,1024]{1,0:T(8,128)(2,1)S(1)} collective-permute-done((bf16[256,1024]{1,0:T(8,128)(2,1)S(1)}, bf16[256,1024]{1,0:T(8,128)(2,1)S(1)}, u32[]{:S(2)}, u32[]{:S(2)}) %collective-permute-start.29) | collective-permute-done | bytes 524320 | tf_op jit(solution)/shard_map/ppermute | solution.py:36
  160.6 3.7 %mix.2 = (f32[256,1024]{1,0:T(8,128)S(1)}, f32[1,128,1024]{2,1,0:T(8,128)S(1)}, f32[128,1024]{1,0:T(8,128)S(1)}, f32[8,1024]{1,0:T(8,128)S(1)}, bf16[144,1024]{1,0:T(8,128)(2,1)}) custom-call(f32[256,1024]{1,0:T(8,128)S(1)} %get-tuple-element.135.kept, bf16[256,1024]{1,0:T(8,128)(2,1)S(1)} %copy-done.10, bf16[256,1024]{1,0:T(8,128)(2,1)S(1)} %copy-done.8, ...), custom_call_target="tpu_custom_call" | custom-call | flops 5368709 | bytes 73400 | tf_op jit(solution)/shard_map/mix/pallas_call | solution.py:579
  170.2 2.6 %collective-permute-start.35 = (bf16[144,512]{1,0:T(8,128)(2,1)S(1)}, bf16[144,512]{1,0:T(8,128)(2,1)S(1)}, u32[]{:S(2)}, u32[]{:S(2)}) collective-permute-start(bf16[144,512]{1,0:T(8,128)(2,1)S(1)} %get-tuple-element.144), channel_id=1, source_target_pairs={{0,4},{2,6},{4,0},{6,2},{8,12},{10,14},{12,8},{14,10},{1,5},{3,7},... | collective-permute-start | bytes 442376 | tf_op jit(solution)/shard_map/ppermute | solution.py:36
  172.9 5.0 %collective-permute-done.30.got_f = bf16[256,1024]{1,0:T(8,128)(2,1)} collective-permute-done((bf16[256,1024]{1,0:T(8,128)(2,1)}, bf16[256,1024]{1,0:T(8,128)(2,1)}, u32[]{:S(2)}, u32[]{:S(2)}) %collective-permute-start.30) | collective-permute-done | bytes 524320 | tf_op jit(solution)/shard_map/ppermute | solution.py:36
  180.9 3.9 %mix.3 = (f32[256,1024]{1,0:T(8,128)S(1)}, f32[1,128,1024]{2,1,0:T(8,128)S(1)}, f32[128,1024]{1,0:T(8,128)S(1)}, f32[8,1024]{1,0:T(8,128)S(1)}, bf16[144,1024]{1,0:T(8,128)(2,1)S(1)}) custom-call(f32[256,1024]{1,0:T(8,128)S(1)} %get-tuple-element.146.kept, bf16[256,1024]{1,0:T(8,128)(2,1)} %collective-permute-done.28.got_c, ...), custom_call_target="tpu_custom_call" | custom-call | flops 5368709 | bytes 73400 | tf_op jit(solution)/shard_map/mix/pallas_call | solution.py:579
  188.0 2.6 %collective-permute-start.37 = (bf16[144,512]{1,0:T(8,128)(2,1)S(1)}, bf16[144,512]{1,0:T(8,128)(2,1)S(1)}, u32[]{:S(2)}, u32[]{:S(2)}) collective-permute-start(bf16[144,512]{1,0:T(8,128)(2,1)S(1)} %get-tuple-element.159), channel_id=1, source_target_pairs={{0,4},{2,6},{4,0},{6,2},{8,12},{10,14},{12,8},{14,10},{1,5},{3,7},... | collective-permute-start | bytes 442376 | tf_op jit(solution)/shard_map/ppermute | solution.py:36
  192.3 2.5 %collective-permute-done.37.refs_0_ = bf16[144,512]{1,0:T(8,128)(2,1)S(1)} collective-permute-done((bf16[144,512]{1,0:T(8,128)(2,1)S(1)}, bf16[144,512]{1,0:T(8,128)(2,1)S(1)}, u32[]{:S(2)}, u32[]{:S(2)}) %collective-permute-start.37) | collective-permute-done | bytes 147488 | tf_op jit(solution)/shard_map/ppermute | solution.py:36
  195.5 3.3 %collective-permute-start.38 = (bf16[144,512]{1,0:T(8,128)(2,1)S(1)}, bf16[144,512]{1,0:T(8,128)(2,1)S(1)}, u32[]{:S(2)}, u32[]{:S(2)}) collective-permute-start(bf16[144,512]{1,0:T(8,128)(2,1)S(1)} %get-tuple-element.161), channel_id=1, source_target_pairs={{0,8},{2,10},{4,12},{6,14},{8,0},{10,2},{12,4},{14,6},{1,9},{3,11}... | collective-permute-start | bytes 442376 | tf_op jit(solution)/shard_map/ppermute | solution.py:36
  198.9 3.2 %collective-permute-done.38.other = bf16[144,512]{1,0:T(8,128)(2,1)S(1)} collective-permute-done((bf16[144,512]{1,0:T(8,128)(2,1)S(1)}, bf16[144,512]{1,0:T(8,128)(2,1)S(1)}, u32[]{:S(2)}, u32[]{:S(2)}) %collective-permute-start.38) | collective-permute-done | bytes 147488 | tf_op jit(solution)/shard_map/ppermute | solution.py:36
  (139 shorter events, 66.9 us)
Async XLA Ops:
  5.2 29.1 %collective-permute-start.2 = (bf16[512,1152]{1,0:T(8,128)(2,1)}, bf16[512,1152]{1,0:T(8,128)(2,1)S(1)}, u32[]{:S(2)}, u32[]{:S(2)}) collective-permute-start(bf16[512,1152]{1,0:T(8,128)(2,1)} %sample_pair.1.refs_8_), channel_id=1, source_target_pairs={{0,8},{4,12},{8,0},{12,4},{1,9},{5,13},{9,1},{13,5},{2,10},{6,14},... | collective-permute-start | bytes 3538952 | tf_op jit(solution)/shard_map/ppermute | solution.py:36
  8.1 28.0 %collective-permute-start.4 = (bf16[512,1152]{1,0:T(8,128)(2,1)}, bf16[512,1152]{1,0:T(8,128)(2,1)S(1)}, u32[]{:S(2)}, u32[]{:S(2)}) collective-permute-start(bf16[512,1152]{1,0:T(8,128)(2,1)} %sample_pair.1.refs_8_), channel_id=1, source_target_pairs={{0,4},{4,0},{8,12},{12,8},{1,5},{5,1},{9,13},{13,9},{2,6},{6,2},{1... | collective-permute-start | bytes 3538952 | tf_op jit(solution)/shard_map/ppermute | solution.py:36
  12.0 46.8 %collective-permute-start.1 = (bf16[256,2048]{1,0:T(8,128)(2,1)S(1)}, bf16[256,2048]{1,0:T(8,128)(2,1)S(1)}, u32[]{:S(2)}, u32[]{:S(2)}) collective-permute-start(bf16[256,2048]{1,0:T(8,128)(2,1)S(1)} %get-tuple-element.94.refs_4_), channel_id=1, source_target_pairs={{0,1},{1,0},{2,3},{3,2},{4,5},{5,4},{6,7},{7,6},{8,9},{9,8},{10,11... | collective-permute-start | bytes 3145736 | tf_op jit(solution)/shard_map/ppermute | solution.py:36
  13.7 47.6 %collective-permute-start = (bf16[256,2048]{1,0:T(8,128)(2,1)S(1)}, bf16[256,2048]{1,0:T(8,128)(2,1)S(1)}, u32[]{:S(2)}, u32[]{:S(2)}) collective-permute-start(bf16[256,2048]{1,0:T(8,128)(2,1)S(1)} %get-tuple-element.88), channel_id=1, source_target_pairs={{0,16},{16,0},{1,17},{17,1},{2,18},{18,2},{3,19},{19,3},{4,20},{20... | collective-permute-start | bytes 3145736 | tf_op jit(solution)/shard_map/ppermute | solution.py:36
  34.4 14.6 %collective-permute-start.3 = (bf16[256,1152]{1,0:T(8,128)(2,1)S(1)}, bf16[256,1152]{1,0:T(8,128)(2,1)S(1)}, u32[]{:S(2)}, u32[]{:S(2)}) collective-permute-start(bf16[256,1152]{1,0:T(8,128)(2,1)S(1)} %slice.24), channel_id=1, source_target_pairs={{0,4},{4,0},{8,12},{12,8},{1,5},{5,1},{9,13},{13,9},{2,6},{6,2},{1... | collective-permute-start | bytes 1769480 | tf_op jit(solution)/shard_map/ppermute | solution.py:36
  36.2 14.0 %collective-permute-start.5 = (bf16[256,1152]{1,0:T(8,128)(2,1)S(1)}, bf16[256,1152]{1,0:T(8,128)(2,1)S(1)}, u32[]{:S(2)}, u32[]{:S(2)}) collective-permute-start(bf16[256,1152]{1,0:T(8,128)(2,1)S(1)} %slice.25), channel_id=1, source_target_pairs={{0,8},{4,12},{8,0},{12,4},{1,9},{5,13},{9,1},{13,5},{2,10},{6,14},... | collective-permute-start | bytes 1769480 | tf_op jit(solution)/shard_map/ppermute | solution.py:36
  50.2 22.8 %collective-permute-start.8 = (bf16[512,1024]{1,0:T(8,128)(2,1)S(1)}, bf16[512,1024]{1,0:T(8,128)(2,1)S(1)}, u32[]{:S(2)}, u32[]{:S(2)}) collective-permute-start(bf16[512,1024]{1,0:T(8,128)(2,1)S(1)} %sample.3.refs_8_), channel_id=1, source_target_pairs={{0,8},{4,12},{8,0},{12,4},{1,9},{5,13},{9,1},{13,5},{2,10},{6,14},... | collective-permute-start | bytes 3145736 | tf_op jit(solution)/shard_map/ppermute | solution.py:36
  51.7 22.5 %collective-permute-start.9 = (bf16[512,1024]{1,0:T(8,128)(2,1)S(1)}, bf16[512,1024]{1,0:T(8,128)(2,1)S(1)}, u32[]{:S(2)}, u32[]{:S(2)}) collective-permute-start(bf16[512,1024]{1,0:T(8,128)(2,1)S(1)} %sample.3.refs_8_), channel_id=1, source_target_pairs={{0,4},{4,0},{8,12},{12,8},{1,5},{5,1},{9,13},{13,9},{2,6},{6,2},{1... | collective-permute-start | bytes 3145736 | tf_op jit(solution)/shard_map/ppermute | solution.py:36
  61.3 22.1 %collective-permute-start.6 = (bf16[256,2048]{1,0:T(8,128)(2,1)S(1)}, bf16[256,2048]{1,0:T(8,128)(2,1)S(1)}, u32[]{:S(2)}, u32[]{:S(2)}) collective-permute-start(bf16[256,2048]{1,0:T(8,128)(2,1)S(1)} %collective-permute-done.refs_0_), channel_id=1, source_target_pairs={{0,1},{1,0},{2,3},{3,2},{4,5},{5,4},{6,7},{7,6},{8,9},{9,8},{10,11... | collective-permute-start | bytes 3145736 | tf_op jit(solution)/shard_map/ppermute | solution.py:36
  61.6 22.3 %collective-permute-start.11 = (bf16[256,2048]{1,0:T(8,128)(2,1)S(1)}, bf16[256,2048]{1,0:T(8,128)(2,1)S(1)}, u32[]{:S(2)}, u32[]{:S(2)}) collective-permute-start(bf16[256,2048]{1,0:T(8,128)(2,1)S(1)} %get-tuple-element.94.refs_4_), channel_id=1, source_target_pairs={{0,2},{2,0},{1,3},{3,1},{4,6},{6,4},{5,7},{7,5},{8,10},{10,8},{9,1... | collective-permute-start | bytes 3145736 | tf_op jit(solution)/shard_map/ppermute | solution.py:36
  61.6 22.8 %collective-permute-start.7 = (bf16[256,2048]{1,0:T(8,128)(2,1)S(1)}, bf16[256,2048]{1,0:T(8,128)(2,1)S(1)}, u32[]{:S(2)}, u32[]{:S(2)}) collective-permute-start(bf16[256,2048]{1,0:T(8,128)(2,1)S(1)} %collective-permute-done.refs_0_), channel_id=1, source_target_pairs={{0,2},{2,0},{1,3},{3,1},{4,6},{6,4},{5,7},{7,5},{8,10},{10,8},{9,1... | collective-permute-start | bytes 3145736 | tf_op jit(solution)/shard_map/ppermute | solution.py:36
  83.3 14.3 %collective-permute-start.15 = (bf16[256,1024]{1,0:T(8,128)(2,1)S(1)}, bf16[256,1024]{1,0:T(8,128)(2,1)S(1)}, u32[]{:S(2)}, u32[]{:S(2)}) collective-permute-start(bf16[256,1024]{1,0:T(8,128)(2,1)S(1)} %slice.26), channel_id=1, source_target_pairs={{0,4},{4,0},{8,12},{12,8},{1,5},{5,1},{9,13},{13,9},{2,6},{6,2},{1... | collective-permute-start | bytes 1572872 | tf_op jit(solution)/shard_map/ppermute | solution.py:36
  83.9 14.1 %collective-permute-start.16 = (bf16[256,1024]{1,0:T(8,128)(2,1)S(1)}, bf16[256,1024]{1,0:T(8,128)(2,1)S(1)}, u32[]{:S(2)}, u32[]{:S(2)}) collective-permute-start(bf16[256,1024]{1,0:T(8,128)(2,1)S(1)} %slice.27), channel_id=1, source_target_pairs={{0,8},{4,12},{8,0},{12,4},{1,9},{5,13},{9,1},{13,5},{2,10},{6,14},... | collective-permute-start | bytes 1572872 | tf_op jit(solution)/shard_map/ppermute | solution.py:36
  97.9 24.8 %collective-permute-start.18 = (bf16[512,1024]{1,0:T(8,128)(2,1)S(1)}, bf16[512,1024]{1,0:T(8,128)(2,1)S(1)}, u32[]{:S(2)}, u32[]{:S(2)}) collective-permute-start(bf16[512,1024]{1,0:T(8,128)(2,1)S(1)} %sample.2.refs_8_), channel_id=1, source_target_pairs={{0,8},{4,12},{8,0},{12,4},{1,9},{5,13},{9,1},{13,5},{2,10},{6,14},... | collective-permute-start | bytes 3145736 | tf_op jit(solution)/shard_map/ppermute | solution.py:36
  98.4 25.6 %collective-permute-start.17 = (bf16[512,1024]{1,0:T(8,128)(2,1)S(1)}, bf16[512,1024]{1,0:T(8,128)(2,1)S(1)}, u32[]{:S(2)}, u32[]{:S(2)}) collective-permute-start(bf16[512,1024]{1,0:T(8,128)(2,1)S(1)} %sample.2.refs_8_), channel_id=1, source_target_pairs={{0,4},{4,0},{8,12},{12,8},{1,5},{5,1},{9,13},{13,9},{2,6},{6,2},{1... | collective-permute-start | bytes 3145736 | tf_op jit(solution)/shard_map/ppermute | solution.py:36
  99.9 27.6 %collective-permute-start.22 = (bf16[256,1152]{1,0:T(8,128)(2,1)S(1)}, bf16[256,1152]{1,0:T(8,128)(2,1)S(1)}, u32[]{:S(2)}, u32[]{:S(2)}) collective-permute-start(bf16[256,1152]{1,0:T(8,128)(2,1)S(1)} %relay.3), channel_id=1, source_target_pairs={{0,16},{16,0},{1,17},{17,1},{2,18},{18,2},{3,19},{19,3},{4,20},{20... | collective-permute-start | bytes 1769480 | tf_op jit(solution)/shard_map/ppermute | solution.py:36
  107.4 17.3 %collective-permute-start.23 = (bf16[128,1024]{1,0:T(8,128)(2,1)S(1)}, bf16[128,1024]{1,0:T(8,128)(2,1)S(1)}, u32[]{:S(2)}, u32[]{:S(2)}) collective-permute-start(bf16[128,1024]{1,0:T(8,128)(2,1)S(1)} %get-tuple-element.115), channel_id=1, source_target_pairs={{0,2},{2,0},{1,3},{3,1},{4,6},{6,4},{5,7},{7,5},{8,10},{10,8},{9,1... | collective-permute-start | bytes 786440 | tf_op jit(solution)/shard_map/ppermute | solution.py:36
  107.4 20.4 %collective-permute-start.21 = (bf16[256,1152]{1,0:T(8,128)(2,1)S(1)}, bf16[256,1152]{1,0:T(8,128)(2,1)S(1)}, u32[]{:S(2)}, u32[]{:S(2)}) collective-permute-start(bf16[256,1152]{1,0:T(8,128)(2,1)S(1)} %get-tuple-element.111), channel_id=1, source_target_pairs={{0,2},{2,0},{1,3},{3,1},{4,6},{6,4},{5,7},{7,5},{8,10},{10,8},{9,1... | collective-permute-start | bytes 1769480 | tf_op jit(solution)/shard_map/ppermute | solution.py:36
  122.8 13.2 %collective-permute-start.19 = (bf16[256,1024]{1,0:T(8,128)(2,1)S(1)}, bf16[256,1024]{1,0:T(8,128)(2,1)S(1)}, u32[]{:S(2)}, u32[]{:S(2)}) collective-permute-start(bf16[256,1024]{1,0:T(8,128)(2,1)S(1)} %slice.28), channel_id=1, source_target_pairs={{0,4},{4,0},{8,12},{12,8},{1,5},{5,1},{9,13},{13,9},{2,6},{6,2},{1... | collective-permute-start | bytes 1572872 | tf_op jit(solution)/shard_map/ppermute | solution.py:36
  124.0 12.1 %collective-permute-start.20 = (bf16[256,1024]{1,0:T(8,128)(2,1)S(1)}, bf16[256,1024]{1,0:T(8,128)(2,1)S(1)}, u32[]{:S(2)}, u32[]{:S(2)}) collective-permute-start(bf16[256,1024]{1,0:T(8,128)(2,1)S(1)} %slice.29), channel_id=1, source_target_pairs={{0,8},{4,12},{8,0},{12,4},{1,9},{5,13},{9,1},{13,5},{2,10},{6,14},... | collective-permute-start | bytes 1572872 | tf_op jit(solution)/shard_map/ppermute | solution.py:36
  127.7 24.9 %collective-permute-start.29 = (bf16[256,1024]{1,0:T(8,128)(2,1)S(1)}, bf16[256,1024]{1,0:T(8,128)(2,1)S(1)}, u32[]{:S(2)}, u32[]{:S(2)}) collective-permute-start(bf16[256,1024]{1,0:T(8,128)(2,1)S(1)} %relay.4), channel_id=1, source_target_pairs={{0,16},{16,0},{1,17},{17,1},{2,18},{18,2},{3,19},{19,3},{4,20},{20... | collective-permute-start | bytes 1572872 | tf_op jit(solution)/shard_map/ppermute | solution.py:36
  127.8 24.7 %collective-permute-start.32 = (bf16[256,1024]{1,0:T(8,128)(2,1)S(1)}, bf16[256,1024]{1,0:T(8,128)(2,1)S(1)}, u32[]{:S(2)}, u32[]{:S(2)}) collective-permute-start(bf16[256,1024]{1,0:T(8,128)(2,1)S(1)} %get-tuple-element.137), channel_id=1, source_target_pairs={{0,2},{2,0},{1,3},{3,1},{4,6},{6,4},{5,7},{7,5},{8,10},{10,8},{9,1... | collective-permute-start | bytes 1572872 | tf_op jit(solution)/shard_map/ppermute | solution.py:36
  152.6 25.3 %collective-permute-start.30 = (bf16[256,1024]{1,0:T(8,128)(2,1)}, bf16[256,1024]{1,0:T(8,128)(2,1)}, u32[]{:S(2)}, u32[]{:S(2)}) collective-permute-start(bf16[256,1024]{1,0:T(8,128)(2,1)} %relay.5), channel_id=1, source_target_pairs={{0,16},{16,0},{1,17},{17,1},{2,18},{18,2},{3,19},{19,3},{4,20},{20... | collective-permute-start | bytes 1572872 | tf_op jit(solution)/shard_map/ppermute | solution.py:36
  152.6 25.3 %collective-permute-start.28 = (bf16[256,1024]{1,0:T(8,128)(2,1)}, bf16[256,1024]{1,0:T(8,128)(2,1)}, u32[]{:S(2)}, u32[]{:S(2)}) collective-permute-start(bf16[256,1024]{1,0:T(8,128)(2,1)} %get-tuple-element.132), channel_id=1, source_target_pairs={{0,2},{2,0},{1,3},{3,1},{4,6},{6,4},{5,7},{7,5},{8,10},{10,8},{9,1... | collective-permute-start | bytes 1572872 | tf_op jit(solution)/shard_map/ppermute | solution.py:36
  (41 other events, 240.7 us)

commit v13 on v12

--- a/solution.py
+++ b/solution.py
@@ -81,10 +81,38 @@
     )(swag_coef, mean_part, dev_part)
 
 
-def sample_pair_kernel(count, coef_ref, mean_ref, devs_ref, dt_ref, out_ref):
+def sample_steps_kernel(count, coef_ref, mean_ref, devs_ref, dt_ref, out_ref):
+    rows, width = mean_ref.shape
+    heads = dt_ref.shape[0]
+    sample_kernel(count, coef_ref, mean_ref, devs_ref, out_ref.at[:, :width])
+    steps = dt_ref[:, pl.ds(pl.multiple_of(pl.program_id(0) * rows, rows), rows)]
+    out_ref[:, width:] = jnp.zeros((rows, LANES), BF16)
+    out_ref[:, width : width + heads] = jnp.transpose(steps.astype(F32)).astype(BF16)
+
+
+def sampled_steps(mean_part, dev_part, dt_part, swag_coef, width):
+    rows, count = mean_part.shape[0], dev_part.shape[0]
+    tile = min(rows, LANES)
+    return call(
+        functools.partial(sample_steps_kernel, count),
+        "sample_steps",
+        jax.ShapeDtypeStruct((rows, width + LANES), BF16),
+        moved=2 * (count + 2) * rows * width,
+        vmem=24,
+        grid=(rows // tile,),
+        in_specs=[
+            SMEM,
+            pl.BlockSpec((tile, width), lambda i: (i, 0)),
+            pl.BlockSpec((count, tile, width), lambda i: (0, i, 0)),
+            pl.BlockSpec((dt_part.shape[1], rows), lambda i: (0, 0)),
+        ],
+        out_specs=pl.BlockSpec((tile, width + LANES), lambda i: (i, 0)),
+    )(swag_coef, mean_part, dev_part, dt_part.T)
+
+
+def sample_pair_kernel(count, coef_ref, mean_ref, devs_ref, out_ref):
     factor = (2.0 * (count - 1)) ** (-0.5)
     rows, _, width = mean_ref.shape
-    heads = dt_ref.shape[0]
     flat = lambda a: a.reshape(2 * rows, width).astype(F32)
     accum = flat(mean_ref[...])
     for member in range(count):
@@ -96,30 +124,25 @@
         picks = jnp.where(col == 2 * row + k, 1.0, 0.0).astype(BF16)
         part = jnp.dot(picks, accum, preferred_element_type=F32)
         out_ref[:, k * width : (k + 1) * width] = part.astype(BF16)
-    out_ref[:, 2 * width :] = jnp.zeros((out_ref.shape[0], LANES), BF16)
-    rows = out_ref.shape[0]
-    steps = dt_ref[:, pl.ds(pl.multiple_of(pl.program_id(0) * rows, rows), rows)]
-    out_ref[:, 2 * width : 2 * width + heads] = jnp.transpose(steps.astype(F32)).astype(BF16)
-
-
-def sampled_pair(mean_part, dev_part, dt_part, swag_coef):
+
+
+def sampled_pair(mean_part, dev_part, swag_coef):
     rows, _, width = mean_part.shape
     count = dev_part.shape[0]
     tile = min(rows, LANES)
     return call(
         functools.partial(sample_pair_kernel, count),
         "sample_pair",
-        jax.ShapeDtypeStruct((rows, 2 * width + LANES), BF16),
+        jax.ShapeDtypeStruct((rows, 2 * width), BF16),
         moved=4 * (count + 2) * rows * width,
         grid=(rows // tile,),
         in_specs=[
             SMEM,
             pl.BlockSpec((tile, 2, width), lambda i: (i, 0, 0)),
             pl.BlockSpec((count, tile, 2, width), lambda i: (0, i, 0, 0)),
-            pl.BlockSpec((dt_part.shape[1], rows), lambda i: (0, 0)),
         ],
-        out_specs=pl.BlockSpec((tile, 2 * width + LANES), lambda i: (i, 0)),
-    )(swag_coef, mean_part, dev_part, dt_part.T)
+        out_specs=pl.BlockSpec((tile, 2 * width), lambda i: (i, 0)),
+    )(swag_coef, mean_part, dev_part)
 
 
 def sent_straight(weight):
@@ -257,12 +280,13 @@
     return (conv_sum * jax.nn.sigmoid(conv_sum)).astype(BF16)
 
 
-def state_proj_kernel(
-    heads, kept, got_c, got_f, rim, taps, bias, rate, out_ref, cum_ref, steps_ref, cum_t_ref, steps_t_ref, decay_ref, padded
-):
-    count, width = out_ref.shape
-    out_ref[...] = convolved(width, kept, got_c, got_f, rim, taps, padded)
-    logits = kept[:, width:] + decoded(got_c[:, width:].astype(F32), heads) + decoded(got_f[:, width:].astype(F32), heads)
+def state_proj_kernel(kept, got_c, got_f, rim, taps, out_ref, padded):
+    out_ref[...] = convolved(out_ref.shape[1], kept, got_c, got_f, rim, taps, padded)
+
+
+def steps_kernel(heads, kept, got_c, got_f, bias, rate, cum_ref, steps_ref, cum_t_ref, steps_t_ref, decay_ref):
+    count = kept.shape[0]
+    logits = kept[...] + decoded(got_c[...].astype(F32), heads) + decoded(got_f[...].astype(F32), heads)
     steps = jax.nn.softplus(logits[:, :heads] + bias[...])
     row = lax.broadcasted_iota(jnp.int32, (SPAN, SPAN), 0)
     col = lax.broadcasted_iota(jnp.int32, (SPAN, SPAN), 1)
@@ -470,7 +494,7 @@
     place = lax.axis_index("chip") if plane else 0
     at = jnp.stack([lax.axis_index(a) for a in ("fsdp", "core", "tp")] + [place ^ i for i in range(chips)]).astype(jnp.int32)
     share, depth = tokens.shape[0], chips * rows_k
-    weight_bc = sampled_pair(bc_mean, bc_devs, dt_weight, swag_coef)
+    weight_bc = sampled_pair(bc_mean, bc_devs, swag_coef)
     tokens = after(tokens, weight_bc)
     cut = jax.ShapeDtypeStruct((2 * share, depth), BF16)
     far, own = call(
@@ -485,7 +509,7 @@
     proj_mean = after(proj_mean, own)
     far = swapped(far, "fsdp")
 
-    weight_early = sampled_cols(proj_mean, proj_devs, swag_coef, 0, early_groups * width)
+    weight_early = sampled_steps(proj_mean, proj_devs, dt_weight, swag_coef, early_groups * width)
     weight_late = None
     if late:
         weight_late = sampled_cols(proj_mean, proj_devs, swag_coef, early_groups // len(late), len(late) * width)
@@ -506,17 +530,28 @@
     by_head = (heads_here, tok_count)
     by_decay = (groups_here, 1, per_group)
     state_proj = lambda part: call(
-        functools.partial(state_proj_kernel, heads_here),
+        state_proj_kernel,
         "state_proj",
-        (jax.ShapeDtypeStruct((tok_count, width_bc), BF16),)
-        + tuple(jax.ShapeDtypeStruct(a, F32) for a in (by_group, by_group, by_head, by_head, by_decay)),
+        jax.ShapeDtypeStruct((tok_count, width_bc), BF16),
         moved=10 * tok_count * width_bc,
         vmem=30,
         grid=(1,),
-        in_specs=specs_of(width_bc + LANES) + [whole_of(CONV, width_bc)] + [whole_of(1, heads_here)] * 2,
-        out_specs=[whole_of(*a) for a in ((tok_count, width_bc), by_group, by_group, by_head, by_head, by_decay)],
+        in_specs=specs_of(width_bc) + [whole_of(CONV, width_bc)],
+        out_specs=whole_of(tok_count, width_bc),
         scratch_shapes=[pltpu.VMEM((tok_count + 8, width_bc), F32)],
-    )(*part, rows_before(*part), conv_bc.reshape(CONV, width_bc), dt_bias[None], decay_rate[None])
+    )(*part, rows_before(*part), conv_bc.reshape(CONV, width_bc))
+    steps_at = early_groups * width // LANES
+    steps_of = lambda part: call(
+        functools.partial(steps_kernel, heads_here),
+        "steps",
+        tuple(jax.ShapeDtypeStruct(a, F32) for a in (by_group, by_group, by_head, by_head, by_decay)),
+        moved=10 * tok_count * LANES,
+        vmem=12,
+        grid=(1,),
+        in_specs=[pl.BlockSpec((tok_count, LANES), lambda i: (0, steps_at))] * 3 + [whole_of(1, heads_here)] * 2,
+        out_specs=[whole_of(*a) for a in (by_group, by_group, by_head, by_head, by_decay)],
+    )(*part, dt_bias[None], decay_rate[None])
+
     if plane and two_shares:
         bc = [weight_bc, *sent_straight(weight_bc)]
         bc += sent_on(corner_parts(bc[1:], 1))
@@ -530,11 +565,11 @@
         halves = corner_parts(early[1:], 1)
         far_c, far_tc = swapped(far, "core"), swapped(after(far_t, halves), "core")
         rows = (far, far_t, far_c, far_tc, own, own_t, own_c, own_tc)
-        part_bc, back_bc = partial_sums(rows, bc, True)
+        part_bc, back_bc = partial_sums(rows, bc, False)
         early += sent_on(halves)
         got_bc = swapped(back_bc, "fsdp")
         weight_late = after(weight_late, (back_bc, early[3:]))
-        part, back = partial_sums(rows, early, False, before_relay=got_bc)
+        part, back = partial_sums(rows, early, True, before_relay=got_bc)
         got = swapped(after(back, got_bc), "fsdp")
         straight = sent_straight(weight_late)
         corners = sent_on(corner_parts(straight, 1))
@@ -546,15 +581,16 @@
         whole = lambda a, axis: lax.all_gather(a, axis, axis=0, tiled=True)
         ranges = [r for a in (far, own) for r in (a[:share], swapped(a[share:], "core"))]
         rows = (jnp.concatenate([whole(r, "tp") for r in ranges], axis=0),)
-        part, back = partial_sums(rows, [whole(weight_early, "chip")], False)
-        part_bc, back_bc = partial_sums(rows, [whole(weight_bc, "chip")], True)
+        part, back = partial_sums(rows, [whole(weight_early, "chip")], True)
+        part_bc, back_bc = partial_sums(rows, [whole(weight_bc, "chip")], False)
         got, got_bc = swapped(back, "fsdp"), swapped(back_bc, "fsdp")
         if late:
             part_late, back_late = partial_sums(rows, [whole(weight_late, "chip")], False)
             got_late = swapped(back_late, "fsdp")
         seen = state_proj(part_bc + (got_bc,))
-    conv_out, cum_g, steps_g, cum_t, steps_t, decay = seen
+    conv_out = seen
     parts = [part + (got,)]
+    cum_g, steps_g, cum_t, steps_t, decay = steps_of(parts[0])
     if late:
         parts.append(part_late + (got_late,))
 

time: 206 us -> 212 us (1.029)
  waiting for transfers between devices: 100 us -> 104 us
  starting transfers between devices: 42.3 us -> 45.4 us
    ppermute x39, waiting for transfers between devices: 98.6 us -> 103 us  [swapped(): lax.ppermute(part, axis, [(i, i ^ by) for i in range(lax.axis_size(axis))])]
    ppermute x39, starting transfers between devices: 36.1 us -> 38.8 us  [swapped(): lax.ppermute(part, axis, [(i, i ^ by) for i in range(lax.axis_size(axis))])]
    pallas_call x1 -> x3, Pallas kernels: 2.25 us -> 4.75 us  [the longest x1 2.53 us: sampled_steps(): call(functools.partial(sample_steps_kernel, count), 'sample_steps', jax.S...]
    unnamed x47 -> x49, local copies, waits for them, and re-layouts: 14.1 us -> 12 us
  transfers between devices with their start and end apart: 42 -> 42, of which waited for: 29 -> 27; matrix products, arithmetic and copies ran while one was open for 0% -> 0% of each run, Pallas kernels for 18% -> 18%
where the time goes in v13:
time: 212 us; the launch traced here: 211 us
  waiting for transfers between devices  104 us (49%)
  Pallas kernels  49.7 us (23%)
  starting transfers between devices  45.4 us (21%)
  local copies, waits for them, and re-layouts  12.4 us (6%)
    ppermute x39, waiting for transfers between devices, swapped(): lax.ppermute(part, axis, [(i, i ^ by) for i in range(lax.axis_size(axis))])  103 us
    ppermute x39, starting transfers between devices, swapped(): lax.ppermute(part, axis, [(i, i ^ by) for i in range(lax.axis_size(axis))])  38.8 us
    pallas_call x3, Pallas kernels, multiplied(): call(functools.partial(multiply_kernel, heads, with_steps, len(rows), len...  21.5 us
    unnamed x49, local copies, waits for them, and re-layouts  12 us
    pallas_call x2, Pallas kernels, body(): call(mix_kernel, 'mix', (jax.ShapeDtypeStruct((tok_count, groups * width)...  7.82 us
    ppermute x3, starting transfers between devices, rows_before(): lax.ppermute(rim, SEQ, [(i, i + 1) for i in range(lax.axis_size(SEQ) - 1)])  6.62 us
    pallas_call x1, Pallas kernels, sampled_pair(): call(functools.partial(sample_pair_kernel, count), 'sample_pair', jax.Sha...  5.11 us
  transfers between devices with their start and end apart: 42, of which 27 were waited for; matrix products, arithmetic and copies ran while one was open for 0% of the time, Pallas kernels for 18%

profile of v13, /device:TPU:0, one launch (start us, length us, event | category | flops | bytes accessed | tf_op | source)
XLA Modules:
  0.0 211.4 jit_solution(14193809940403680763)
XLA Ops:
  0.0 5.1 %sample_pair.1.refs_8_ = bf16[512,1024]{1,0:T(8,128)(2,1)} custom-call(f32[4]{0:T(128)} %coef_ref.5, bf16[512,2,512]{2,1,0:T(2,128)(2,1)} %mean_ref.1, bf16[4,512,2,512]{3,2,1,0:T(2,128)(2,1)} %devs_ref.3), custom_call_target="tpu_custom_call" | custom-call | bytes 125829 | tf_op jit(solution)/shard_map/sample_pair/pallas_call | solution.py:133
  5.1 2.9 %collective-permute-start.4 = (bf16[512,1024]{1,0:T(8,128)(2,1)}, bf16[512,1024]{1,0:T(8,128)(2,1)S(1)}, u32[]{:S(2)}, u32[]{:S(2)}) collective-permute-start(bf16[512,1024]{1,0:T(8,128)(2,1)} %sample_pair.1.refs_8_), channel_id=1, source_target_pairs={{0,4},{4,0},{8,12},{12,8},{1,5},{5,1},{9,13},{13,9},{2,6},{6,2},{1... | collective-permute-start | bytes 3145736 | tf_op jit(solution)/shard_map/ppermute | solution.py:36
  12.0 2.7 %collective-permute-start = (bf16[256,2048]{1,0:T(8,128)(2,1)S(1)}, bf16[256,2048]{1,0:T(8,128)(2,1)S(1)}, u32[]{:S(2)}, u32[]{:S(2)}) collective-permute-start(bf16[256,2048]{1,0:T(8,128)(2,1)S(1)} %get-tuple-element.87), channel_id=1, source_target_pairs={{0,16},{16,0},{1,17},{17,1},{2,18},{18,2},{3,19},{19,3},{4,20},{20... | collective-permute-start | bytes 3145736 | tf_op jit(solution)/shard_map/ppermute | solution.py:36
  16.2 15.2 %collective-permute-done.4.refs_9_ = bf16[512,1024]{1,0:T(8,128)(2,1)S(1)} collective-permute-done((bf16[512,1024]{1,0:T(8,128)(2,1)}, bf16[512,1024]{1,0:T(8,128)(2,1)S(1)}, u32[]{:S(2)}, u32[]{:S(2)}) %collective-permute-start.4) | collective-permute-done | bytes 1048608 | tf_op jit(solution)/shard_map/ppermute | solution.py:36
  34.9 3.4 %copy-done = bf16[4,512,2048]{2,1,0:T(8,128)(2,1)S(1)} copy-done((bf16[4,512,2048]{2,1,0:T(8,128)(2,1)S(1)}, bf16[4,512,2048]{2,1,0:T(8,128)(2,1)}, u32[]{:S(2)}) %copy-start) | copy-done | bytes 8388632
  40.8 3.8 %collective-permute-done.5.refs_12_ = bf16[256,1024]{1,0:T(8,128)(2,1)S(1)} collective-permute-done((bf16[256,1024]{1,0:T(8,128)(2,1)S(1)}, bf16[256,1024]{1,0:T(8,128)(2,1)S(1)}, u32[]{:S(2)}, u32[]{:S(2)}) %collective-permute-start.5) | collective-permute-done | bytes 524320 | tf_op jit(solution)/shard_map/ppermute | solution.py:36
  49.8 10.1 %collective-permute-done.refs_0_ = bf16[256,2048]{1,0:T(8,128)(2,1)S(1)} collective-permute-done((bf16[256,2048]{1,0:T(8,128)(2,1)S(1)}, bf16[256,2048]{1,0:T(8,128)(2,1)S(1)}, u32[]{:S(2)}, u32[]{:S(2)}) %collective-permute-start) | collective-permute-done | bytes 1048608 | tf_op jit(solution)/shard_map/ppermute | solution.py:36
  62.0 9.5 %collective-permute-done.9.refs_9_ = bf16[512,1152]{1,0:T(8,128)(2,1)S(1)} collective-permute-done((bf16[512,1152]{1,0:T(8,128)(2,1)S(1)}, bf16[512,1152]{1,0:T(8,128)(2,1)S(1)}, u32[]{:S(2)}, u32[]{:S(2)}) %collective-permute-start.9) | collective-permute-done | bytes 1179680 | tf_op jit(solution)/shard_map/ppermute | solution.py:36
  72.8 11.0 %collective-permute-done.6.refs_1_ = bf16[256,2048]{1,0:T(8,128)(2,1)S(1)} collective-permute-done((bf16[256,2048]{1,0:T(8,128)(2,1)S(1)}, bf16[256,2048]{1,0:T(8,128)(2,1)S(1)}, u32[]{:S(2)}, u32[]{:S(2)}) %collective-permute-start.6) | collective-permute-done | bytes 1048608 | tf_op jit(solution)/shard_map/ppermute | solution.py:36
  86.5 5.9 %multiply.3 = (bf16[128,1024]{1,0:T(8,128)(2,1)S(1)}, bf16[128,1024]{1,0:T(8,128)(2,1)S(1)}, f32[256,1024]{1,0:T(8,128)S(1)}, bf16[256,1024]{1,0:T(8,128)(2,1)S(1)}, f32[256,1024]{1,0:T(8,128)S(1)}) custom-call(s32[7]{0:T(128)S(1)} %stack.31.at_ref, bf16[256,2048]{1,0:T(8,128)(2,1)S(1)} %collective-permute-done.refs_0_, ...), custom_call_target="tpu_custom_call" | custom-call | flops 85899344 | bytes 230686 | tf_op jit(solution)/shard_map/multiply/pallas_call | solution.py:210
  94.5 5.0 %collective-permute-done.16.refs_12_ = bf16[256,1152]{1,0:T(8,128)(2,1)S(1)} collective-permute-done((bf16[256,1152]{1,0:T(8,128)(2,1)S(1)}, bf16[256,1152]{1,0:T(8,128)(2,1)S(1)}, u32[]{:S(2)}, u32[]{:S(2)}) %collective-permute-start.16) | collective-permute-done | bytes 589856 | tf_op jit(solution)/shard_map/ppermute | solution.py:36
  101.8 3.3 %collective-permute-start.22 = (bf16[256,1024]{1,0:T(8,128)(2,1)S(1)}, bf16[256,1024]{1,0:T(8,128)(2,1)S(1)}, u32[]{:S(2)}, u32[]{:S(2)}) collective-permute-start(bf16[256,1024]{1,0:T(8,128)(2,1)S(1)} %relay.3), channel_id=1, source_target_pairs={{0,16},{16,0},{1,17},{17,1},{2,18},{18,2},{3,19},{19,3},{4,20},{20... | collective-permute-start | bytes 1572872 | tf_op jit(solution)/shard_map/ppermute | solution.py:36
  105.2 9.1 %multiply.5 = (bf16[128,1152]{1,0:T(8,128)(2,1)S(1)}, bf16[128,1152]{1,0:T(8,128)(2,1)S(1)}, f32[256,1152]{1,0:T(8,128)S(1)}, bf16[256,1152]{1,0:T(8,128)(2,1)S(1)}, f32[256,1152]{1,0:T(8,128)S(1)}) custom-call(s32[7]{0:T(128)S(1)} %stack.31.at_ref, bf16[256,2048]{1,0:T(8,128)(2,1)S(1)} %collective-permute-done.refs_0_, ...), custom_call_target="tpu_custom_call" | custom-call | flops 96636768 | bytes 249036 | tf_op jit(solution)/shard_map/multiply/pallas_call | solution.py:210
  114.8 9.5 %collective-permute-done.18.refs_10_ = bf16[512,1024]{1,0:T(8,128)(2,1)S(1)} collective-permute-done((bf16[512,1024]{1,0:T(8,128)(2,1)S(1)}, bf16[512,1024]{1,0:T(8,128)(2,1)S(1)}, u32[]{:S(2)}, u32[]{:S(2)}) %collective-permute-start.18) | collective-permute-done | bytes 1048608 | tf_op jit(solution)/shard_map/ppermute | solution.py:36
  127.7 2.8 %collective-permute-start.29 = (bf16[256,1152]{1,0:T(8,128)(2,1)S(1)}, bf16[256,1152]{1,0:T(8,128)(2,1)S(1)}, u32[]{:S(2)}, u32[]{:S(2)}) collective-permute-start(bf16[256,1152]{1,0:T(8,128)(2,1)S(1)} %relay.4), channel_id=1, source_target_pairs={{0,16},{16,0},{1,17},{17,1},{2,18},{18,2},{3,19},{19,3},{4,20},{20... | collective-permute-start | bytes 1769480 | tf_op jit(solution)/shard_map/ppermute | solution.py:36
  135.3 3.9 %collective-permute-done.19.refs_11_ = bf16[256,1024]{1,0:T(8,128)(2,1)S(1)} collective-permute-done((bf16[256,1024]{1,0:T(8,128)(2,1)S(1)}, bf16[256,1024]{1,0:T(8,128)(2,1)S(1)}, u32[]{:S(2)}, u32[]{:S(2)}) %collective-permute-start.19) | collective-permute-done | bytes 524320 | tf_op jit(solution)/shard_map/ppermute | solution.py:36
  139.2 6.5 %multiply.4 = (bf16[128,1024]{1,0:T(8,128)(2,1)S(1)}, bf16[128,1024]{1,0:T(8,128)(2,1)S(1)}, f32[256,1024]{1,0:T(8,128)S(1)}, bf16[256,1024]{1,0:T(8,128)(2,1)}, f32[256,1024]{1,0:T(8,128)S(1)}) custom-call(s32[7]{0:T(128)S(1)} %stack.31.at_ref, bf16[256,2048]{1,0:T(8,128)(2,1)S(1)} %collective-permute-done.refs_0_, ...), custom_call_target="tpu_custom_call" | custom-call | flops 85899344 | bytes 230686 | tf_op jit(solution)/shard_map/multiply/pallas_call | solution.py:210
  148.5 7.8 %collective-permute-done.29.got_f = bf16[256,1152]{1,0:T(8,128)(2,1)S(1)} collective-permute-done((bf16[256,1152]{1,0:T(8,128)(2,1)S(1)}, bf16[256,1152]{1,0:T(8,128)(2,1)S(1)}, u32[]{:S(2)}, u32[]{:S(2)}) %collective-permute-start.29) | collective-permute-done | bytes 589856 | tf_op jit(solution)/shard_map/ppermute | solution.py:36
  161.0 3.9 %mix.2 = (f32[256,1024]{1,0:T(8,128)S(1)}, f32[1,128,1024]{2,1,0:T(8,128)S(1)}, f32[128,1024]{1,0:T(8,128)S(1)}, f32[8,1024]{1,0:T(8,128)S(1)}, bf16[144,1024]{1,0:T(8,128)(2,1)}) custom-call(f32[256,1152]{1,0:T(8,128)S(1)} %get-tuple-element.128.kept, bf16[256,1152]{1,0:T(8,128)(2,1)S(1)} %collective-permute-done.32.got_c, ...), custom_call_target="tpu_custom_call" | custom-call | flops 5368709 | bytes 73400 | tf_op jit(solution)/shard_map/mix/pallas_call | solution.py:615
  175.0 8.2 %collective-permute-done.30.got_f = bf16[256,1024]{1,0:T(8,128)(2,1)} collective-permute-done((bf16[256,1024]{1,0:T(8,128)(2,1)}, bf16[256,1024]{1,0:T(8,128)(2,1)}, u32[]{:S(2)}, u32[]{:S(2)}) %collective-permute-start.30) | collective-permute-done | bytes 524320 | tf_op jit(solution)/shard_map/ppermute | solution.py:36
  187.8 3.9 %mix.3 = (f32[256,1024]{1,0:T(8,128)S(1)}, f32[1,128,1024]{2,1,0:T(8,128)S(1)}, f32[128,1024]{1,0:T(8,128)S(1)}, f32[8,1024]{1,0:T(8,128)S(1)}, bf16[144,1024]{1,0:T(8,128)(2,1)S(1)}) custom-call(f32[256,1024]{1,0:T(8,128)S(1)} %copy-done.5, bf16[256,1024]{1,0:T(8,128)(2,1)} %collective-permute-done.28.got_c, ...), custom_call_target="tpu_custom_call" | custom-call | flops 5368709 | bytes 73400 | tf_op jit(solution)/shard_map/mix/pallas_call | solution.py:615
  195.2 2.7 %collective-permute-start.37 = (bf16[144,512]{1,0:T(8,128)(2,1)S(1)}, bf16[144,512]{1,0:T(8,128)(2,1)S(1)}, u32[]{:S(2)}, u32[]{:S(2)}) collective-permute-start(bf16[144,512]{1,0:T(8,128)(2,1)S(1)} %get-tuple-element.157), channel_id=1, source_target_pairs={{0,4},{2,6},{4,0},{6,2},{8,12},{10,14},{12,8},{14,10},{1,5},{3,7},... | collective-permute-start | bytes 442376 | tf_op jit(solution)/shard_map/ppermute | solution.py:36
  198.4 3.5 %collective-permute-done.37.refs_0_ = bf16[144,512]{1,0:T(8,128)(2,1)S(1)} collective-permute-done((bf16[144,512]{1,0:T(8,128)(2,1)S(1)}, bf16[144,512]{1,0:T(8,128)(2,1)S(1)}, u32[]{:S(2)}, u32[]{:S(2)}) %collective-permute-start.37) | collective-permute-done | bytes 147488 | tf_op jit(solution)/shard_map/ppermute | solution.py:36
  204.6 3.5 %collective-permute-done.38.other = bf16[144,512]{1,0:T(8,128)(2,1)S(1)} collective-permute-done((bf16[144,512]{1,0:T(8,128)(2,1)S(1)}, bf16[144,512]{1,0:T(8,128)(2,1)S(1)}, u32[]{:S(2)}, u32[]{:S(2)}) %collective-permute-start.38) | collective-permute-done | bytes 147488 | tf_op jit(solution)/shard_map/ppermute | solution.py:36
  (142 shorter events, 67.6 us)
Async XLA Ops:
  5.1 26.3 %collective-permute-start.4 = (bf16[512,1024]{1,0:T(8,128)(2,1)}, bf16[512,1024]{1,0:T(8,128)(2,1)S(1)}, u32[]{:S(2)}, u32[]{:S(2)}) collective-permute-start(bf16[512,1024]{1,0:T(8,128)(2,1)} %sample_pair.1.refs_8_), channel_id=1, source_target_pairs={{0,4},{4,0},{8,12},{12,8},{1,5},{5,1},{9,13},{13,9},{2,6},{6,2},{1... | collective-permute-start | bytes 3145736 | tf_op jit(solution)/shard_map/ppermute | solution.py:36
  8.0 25.2 %collective-permute-start.2 = (bf16[512,1024]{1,0:T(8,128)(2,1)}, bf16[512,1024]{1,0:T(8,128)(2,1)S(1)}, u32[]{:S(2)}, u32[]{:S(2)}) collective-permute-start(bf16[512,1024]{1,0:T(8,128)(2,1)} %sample_pair.1.refs_8_), channel_id=1, source_target_pairs={{0,8},{4,12},{8,0},{12,4},{1,9},{5,13},{9,1},{13,5},{2,10},{6,14},... | collective-permute-start | bytes 3145736 | tf_op jit(solution)/shard_map/ppermute | solution.py:36
  12.0 47.9 %collective-permute-start = (bf16[256,2048]{1,0:T(8,128)(2,1)S(1)}, bf16[256,2048]{1,0:T(8,128)(2,1)S(1)}, u32[]{:S(2)}, u32[]{:S(2)}) collective-permute-start(bf16[256,2048]{1,0:T(8,128)(2,1)S(1)} %get-tuple-element.87), channel_id=1, source_target_pairs={{0,16},{16,0},{1,17},{17,1},{2,18},{18,2},{3,19},{19,3},{4,20},{20... | collective-permute-start | bytes 3145736 | tf_op jit(solution)/shard_map/ppermute | solution.py:36
  14.6 45.4 %collective-permute-start.1 = (bf16[256,2048]{1,0:T(8,128)(2,1)S(1)}, bf16[256,2048]{1,0:T(8,128)(2,1)S(1)}, u32[]{:S(2)}, u32[]{:S(2)}) collective-permute-start(bf16[256,2048]{1,0:T(8,128)(2,1)S(1)} %get-tuple-element.93.refs_4_), channel_id=1, source_target_pairs={{0,1},{1,0},{2,3},{3,2},{4,5},{5,4},{6,7},{7,6},{8,9},{9,8},{10,11... | collective-permute-start | bytes 3145736 | tf_op jit(solution)/shard_map/ppermute | solution.py:36
  31.5 13.2 %collective-permute-start.5 = (bf16[256,1024]{1,0:T(8,128)(2,1)S(1)}, bf16[256,1024]{1,0:T(8,128)(2,1)S(1)}, u32[]{:S(2)}, u32[]{:S(2)}) collective-permute-start(bf16[256,1024]{1,0:T(8,128)(2,1)S(1)} %slice.25), channel_id=1, source_target_pairs={{0,8},{4,12},{8,0},{12,4},{1,9},{5,13},{9,1},{13,5},{2,10},{6,14},... | collective-permute-start | bytes 1572872 | tf_op jit(solution)/shard_map/ppermute | solution.py:36
  33.3 12.6 %collective-permute-start.3 = (bf16[256,1024]{1,0:T(8,128)(2,1)S(1)}, bf16[256,1024]{1,0:T(8,128)(2,1)S(1)}, u32[]{:S(2)}, u32[]{:S(2)}) collective-permute-start(bf16[256,1024]{1,0:T(8,128)(2,1)S(1)} %slice.24), channel_id=1, source_target_pairs={{0,4},{4,0},{8,12},{12,8},{1,5},{5,1},{9,13},{13,9},{2,6},{6,2},{1... | collective-permute-start | bytes 1572872 | tf_op jit(solution)/shard_map/ppermute | solution.py:36
  45.9 25.6 %collective-permute-start.9 = (bf16[512,1152]{1,0:T(8,128)(2,1)S(1)}, bf16[512,1152]{1,0:T(8,128)(2,1)S(1)}, u32[]{:S(2)}, u32[]{:S(2)}) collective-permute-start(bf16[512,1152]{1,0:T(8,128)(2,1)S(1)} %sample_steps.1.refs_8_), channel_id=1, source_target_pairs={{0,4},{4,0},{8,12},{12,8},{1,5},{5,1},{9,13},{13,9},{2,6},{6,2},{1... | collective-permute-start | bytes 3538952 | tf_op jit(solution)/shard_map/ppermute | solution.py:36
  47.4 25.4 %collective-permute-start.8 = (bf16[512,1152]{1,0:T(8,128)(2,1)S(1)}, bf16[512,1152]{1,0:T(8,128)(2,1)S(1)}, u32[]{:S(2)}, u32[]{:S(2)}) collective-permute-start(bf16[512,1152]{1,0:T(8,128)(2,1)S(1)} %sample_steps.1.refs_8_), channel_id=1, source_target_pairs={{0,8},{4,12},{8,0},{12,4},{1,9},{5,13},{9,1},{13,5},{2,10},{6,14},... | collective-permute-start | bytes 3538952 | tf_op jit(solution)/shard_map/ppermute | solution.py:36
  60.0 23.8 %collective-permute-start.6 = (bf16[256,2048]{1,0:T(8,128)(2,1)S(1)}, bf16[256,2048]{1,0:T(8,128)(2,1)S(1)}, u32[]{:S(2)}, u32[]{:S(2)}) collective-permute-start(bf16[256,2048]{1,0:T(8,128)(2,1)S(1)} %collective-permute-done.refs_0_), channel_id=1, source_target_pairs={{0,1},{1,0},{2,3},{3,2},{4,5},{5,4},{6,7},{7,6},{8,9},{9,8},{10,11... | collective-permute-start | bytes 3145736 | tf_op jit(solution)/shard_map/ppermute | solution.py:36
  61.5 22.8 %collective-permute-start.11 = (bf16[256,2048]{1,0:T(8,128)(2,1)S(1)}, bf16[256,2048]{1,0:T(8,128)(2,1)S(1)}, u32[]{:S(2)}, u32[]{:S(2)}) collective-permute-start(bf16[256,2048]{1,0:T(8,128)(2,1)S(1)} %get-tuple-element.93.refs_4_), channel_id=1, source_target_pairs={{0,2},{2,0},{1,3},{3,1},{4,6},{6,4},{5,7},{7,5},{8,10},{10,8},{9,1... | collective-permute-start | bytes 3145736 | tf_op jit(solution)/shard_map/ppermute | solution.py:36
  61.5 23.3 %collective-permute-start.7 = (bf16[256,2048]{1,0:T(8,128)(2,1)S(1)}, bf16[256,2048]{1,0:T(8,128)(2,1)S(1)}, u32[]{:S(2)}, u32[]{:S(2)}) collective-permute-start(bf16[256,2048]{1,0:T(8,128)(2,1)S(1)} %collective-permute-done.refs_0_), channel_id=1, source_target_pairs={{0,2},{2,0},{1,3},{3,1},{4,6},{6,4},{5,7},{7,5},{8,10},{10,8},{9,1... | collective-permute-start | bytes 3145736 | tf_op jit(solution)/shard_map/ppermute | solution.py:36
  71.5 13.3 %collective-permute-start.12 = (bf16[256,2048]{1,0:T(8,128)(2,1)S(1)}, bf16[256,2048]{1,0:T(8,128)(2,1)S(1)}, u32[]{:S(2)}, u32[]{:S(2)}) collective-permute-start(bf16[256,2048]{1,0:T(8,128)(2,1)S(1)} %collective-permute-done.1.refs_5_), channel_id=1, source_target_pairs={{0,2},{2,0},{1,3},{3,1},{4,6},{6,4},{5,7},{7,5},{8,10},{10,8},{9,1... | collective-permute-start | bytes 3145736 | tf_op jit(solution)/shard_map/ppermute | solution.py:36
  83.8 15.7 %collective-permute-start.16 = (bf16[256,1152]{1,0:T(8,128)(2,1)S(1)}, bf16[256,1152]{1,0:T(8,128)(2,1)S(1)}, u32[]{:S(2)}, u32[]{:S(2)}) collective-permute-start(bf16[256,1152]{1,0:T(8,128)(2,1)S(1)} %slice.27), channel_id=1, source_target_pairs={{0,8},{4,12},{8,0},{12,4},{1,9},{5,13},{9,1},{13,5},{2,10},{6,14},... | collective-permute-start | bytes 1769480 | tf_op jit(solution)/shard_map/ppermute | solution.py:36
  84.3 15.5 %collective-permute-start.15 = (bf16[256,1152]{1,0:T(8,128)(2,1)S(1)}, bf16[256,1152]{1,0:T(8,128)(2,1)S(1)}, u32[]{:S(2)}, u32[]{:S(2)}) collective-permute-start(bf16[256,1152]{1,0:T(8,128)(2,1)S(1)} %slice.26), channel_id=1, source_target_pairs={{0,4},{4,0},{8,12},{12,8},{1,5},{5,1},{9,13},{13,9},{2,6},{6,2},{1... | collective-permute-start | bytes 1769480 | tf_op jit(solution)/shard_map/ppermute | solution.py:36
  99.8 24.6 %collective-permute-start.18 = (bf16[512,1024]{1,0:T(8,128)(2,1)S(1)}, bf16[512,1024]{1,0:T(8,128)(2,1)S(1)}, u32[]{:S(2)}, u32[]{:S(2)}) collective-permute-start(bf16[512,1024]{1,0:T(8,128)(2,1)S(1)} %sample.1.refs_8_), channel_id=1, source_target_pairs={{0,8},{4,12},{8,0},{12,4},{1,9},{5,13},{9,1},{13,5},{2,10},{6,14},... | collective-permute-start | bytes 3145736 | tf_op jit(solution)/shard_map/ppermute | solution.py:36
  101.3 24.2 %collective-permute-start.17 = (bf16[512,1024]{1,0:T(8,128)(2,1)S(1)}, bf16[512,1024]{1,0:T(8,128)(2,1)S(1)}, u32[]{:S(2)}, u32[]{:S(2)}) collective-permute-start(bf16[512,1024]{1,0:T(8,128)(2,1)S(1)} %sample.1.refs_8_), channel_id=1, source_target_pairs={{0,4},{4,0},{8,12},{12,8},{1,5},{5,1},{9,13},{13,9},{2,6},{6,2},{1... | collective-permute-start | bytes 3145736 | tf_op jit(solution)/shard_map/ppermute | solution.py:36
  101.8 25.5 %collective-permute-start.22 = (bf16[256,1024]{1,0:T(8,128)(2,1)S(1)}, bf16[256,1024]{1,0:T(8,128)(2,1)S(1)}, u32[]{:S(2)}, u32[]{:S(2)}) collective-permute-start(bf16[256,1024]{1,0:T(8,128)(2,1)S(1)} %relay.3), channel_id=1, source_target_pairs={{0,16},{16,0},{1,17},{17,1},{2,18},{18,2},{3,19},{19,3},{4,20},{20... | collective-permute-start | bytes 1572872 | tf_op jit(solution)/shard_map/ppermute | solution.py:36
  125.5 13.7 %collective-permute-start.19 = (bf16[256,1024]{1,0:T(8,128)(2,1)S(1)}, bf16[256,1024]{1,0:T(8,128)(2,1)S(1)}, u32[]{:S(2)}, u32[]{:S(2)}) collective-permute-start(bf16[256,1024]{1,0:T(8,128)(2,1)S(1)} %slice.28), channel_id=1, source_target_pairs={{0,4},{4,0},{8,12},{12,8},{1,5},{5,1},{9,13},{13,9},{2,6},{6,2},{1... | collective-permute-start | bytes 1572872 | tf_op jit(solution)/shard_map/ppermute | solution.py:36
  126.1 13.1 %collective-permute-start.20 = (bf16[256,1024]{1,0:T(8,128)(2,1)S(1)}, bf16[256,1024]{1,0:T(8,128)(2,1)S(1)}, u32[]{:S(2)}, u32[]{:S(2)}) collective-permute-start(bf16[256,1024]{1,0:T(8,128)(2,1)S(1)} %slice.29), channel_id=1, source_target_pairs={{0,8},{4,12},{8,0},{12,4},{1,9},{5,13},{9,1},{13,5},{2,10},{6,14},... | collective-permute-start | bytes 1572872 | tf_op jit(solution)/shard_map/ppermute | solution.py:36
  127.7 28.7 %collective-permute-start.29 = (bf16[256,1152]{1,0:T(8,128)(2,1)S(1)}, bf16[256,1152]{1,0:T(8,128)(2,1)S(1)}, u32[]{:S(2)}, u32[]{:S(2)}) collective-permute-start(bf16[256,1152]{1,0:T(8,128)(2,1)S(1)} %relay.4), channel_id=1, source_target_pairs={{0,16},{16,0},{1,17},{17,1},{2,18},{18,2},{3,19},{19,3},{4,20},{20... | collective-permute-start | bytes 1769480 | tf_op jit(solution)/shard_map/ppermute | solution.py:36
  130.5 25.9 %collective-permute-start.32 = (bf16[256,1152]{1,0:T(8,128)(2,1)S(1)}, bf16[256,1152]{1,0:T(8,128)(2,1)S(1)}, u32[]{:S(2)}, u32[]{:S(2)}) collective-permute-start(bf16[256,1152]{1,0:T(8,128)(2,1)S(1)} %get-tuple-element.130), channel_id=1, source_target_pairs={{0,2},{2,0},{1,3},{3,1},{4,6},{6,4},{5,7},{7,5},{8,10},{10,8},{9,1... | collective-permute-start | bytes 1769480 | tf_op jit(solution)/shard_map/ppermute | solution.py:36
  156.4 18.6 %collective-permute-start.28 = (bf16[256,1024]{1,0:T(8,128)(2,1)}, bf16[256,1024]{1,0:T(8,128)(2,1)}, u32[]{:S(2)}, u32[]{:S(2)}) collective-permute-start(bf16[256,1024]{1,0:T(8,128)(2,1)} %get-tuple-element.125), channel_id=1, source_target_pairs={{0,2},{2,0},{1,3},{3,1},{4,6},{6,4},{5,7},{7,5},{8,10},{10,8},{9,1... | collective-permute-start | bytes 1572872 | tf_op jit(solution)/shard_map/ppermute | solution.py:36
  156.4 26.8 %collective-permute-start.30 = (bf16[256,1024]{1,0:T(8,128)(2,1)}, bf16[256,1024]{1,0:T(8,128)(2,1)}, u32[]{:S(2)}, u32[]{:S(2)}) collective-permute-start(bf16[256,1024]{1,0:T(8,128)(2,1)} %relay.5), channel_id=1, source_target_pairs={{0,16},{16,0},{1,17},{17,1},{2,18},{18,2},{3,19},{19,3},{4,20},{20... | collective-permute-start | bytes 1572872 | tf_op jit(solution)/shard_map/ppermute | solution.py:36
  172.6 14.3 %collective-permute-start.35 = (bf16[144,512]{1,0:T(8,128)(2,1)S(1)}, bf16[144,512]{1,0:T(8,128)(2,1)S(1)}, u32[]{:S(2)}, u32[]{:S(2)}) collective-permute-start(bf16[144,512]{1,0:T(8,128)(2,1)S(1)} %get-tuple-element.142), channel_id=1, source_target_pairs={{0,4},{2,6},{4,0},{6,2},{8,12},{10,14},{12,8},{14,10},{1,5},{3,7},... | collective-permute-start | bytes 442376 | tf_op jit(solution)/shard_map/ppermute | solution.py:36
  (42 other events, 258.7 us)
